TPU v7x, 128 devices: a whole 4x4x4 slice. The times are simulated.
128 devices in a mesh: req: 8 (over z, core), mlp: 16 (over x, y).
Axes of the slice: x: 4, y: 4, z: 4, core: 2. Of those that a mesh axis runs over, the one named last changes fastest.
Arguments:
- queries: bfloat16 [384, 7168], P(('req', 'mlp')), may hold values from -36 to 36
- keys_new: bfloat16 [384, 7168], P(('req', 'mlp')), may hold values from -6 to 6
- values_new: bfloat16 [384, 7168], P(('req', 'mlp')), may hold values from -6 to 6
- resid: bfloat16 [384, 7168], P(('req', 'mlp')), may hold values from -3 to 3
- tree_mask: int32 [24, 16, 16], P('req'), may hold values from 0 to 1, as said below
- tree_size: int32 [24], P('req'), may hold values from 8 to 16, as said below
- accepted: int32 [24, 16], P('req'), may hold values from -1 to 15, as said below
- dest_slot: int32 [24], P('req'), may hold values from 0 to 15, as said below
- page_table: int32 [24, 384], P('req'), may hold values from -1 to 383, as said below
- key_cache: bfloat16 [3072, 16, 7168], P(('req', 'mlp')), may hold values from -6 to 6
- value_cache: bfloat16 [3072, 16, 7168], P(('req', 'mlp')), may hold values from -6 to 6
- w_out: bfloat16 [7168, 7168], P(('req', 'mlp')), may hold values from -0.0625 to 0.0625
- w_up: bfloat16 [7168, 28672], P(None, ('req', 'mlp')), may hold values from -0.0625 to 0.0625
- w_down: bfloat16 [28672, 7168], P(('req', 'mlp')), may hold values from -0.03125 to 0.03125
- ln_gain: float32 [7168], replicated, may hold values from 0.1 to 1.9
Outputs:
- mixed: bfloat16 [384, 7168], P(('req', 'mlp'))
- new_keys: bfloat16 [128, 16, 7168], P(('req', 'mlp'))
- new_values: bfloat16 [128, 16, 7168], P(('req', 'mlp'))
Inputs may be any that keep to these rules, and one draw needn't show every extreme that they name: `tree_mask`: entry [r, i, j] is 1 where slot j is slot i or one of its ancestors in request r's draft tree, else 0; every slot's parent has a lower index, so slot 0 is the root. `tree_size`: draft slots at or beyond a request's size are padding. `accepted`: row r lists in increasing order the slots of one path from the root of request r's tree to a slot below tree_size[r], then -1. `dest_slot`: the new pages of one group's 3 requests are distinct. `page_table`: row r lists the pages of its group's pool that hold request r's cache, then -1; no page belongs to two requests, every request has 16 pages or more, and in some groups one request holds every page that the others leave.
All inputs are finite; a program needn't handle non-finite values.
Results may differ from a plain program's by a relative error of at most 0.017.
Values may be sent and summed in bfloat16 or wider, within the bound.
No kernel may reach another device: no remote copies, remote signals or barrier semaphores. Data moves between devices by JAX's collectives and lax.ppermute only.
A program may use at most 128 MiB of HBM per device.

v0:
```python
import math

import jax
import jax.numpy as jnp
from jax import lax
from jax.sharding import PartitionSpec as P

H = 56


def normalize_rows(hidden, ln_gain):
    row_mean = jnp.mean(hidden, axis=1, keepdims=True)
    centered = hidden - row_mean
    spread = jnp.mean(centered * centered, axis=1, keepdims=True)
    return (centered * lax.rsqrt(spread + 1e-05) * ln_gain).astype(jnp.bfloat16)


def spread_normed(hidden, ln_gain, w_up):
    normed = normalize_rows(hidden, ln_gain)
    return jnp.maximum(
        jnp.dot(
            lax.all_gather(normed, ("req", "mlp"), axis=0, tiled=True),
            w_up,
            preferred_element_type=jnp.float32,
        ),
        0.0,
    ).astype(jnp.bfloat16)


def regroup_rows(attended):
    return lax.all_to_all(attended, ("req", "mlp"), split_axis=1, concat_axis=0, tiled=True)


def local(
    queries,
    keys_new,
    values_new,
    resid,
    tree_mask,
    tree_size,
    accepted,
    dest_slot,
    page_table,
    key_cache,
    value_cache,
    w_out,
    w_up,
    w_down,
    ln_gain,
):
    member = lax.axis_index("mlp")
    rows_dev, model_width = queries.shape
    requests = tree_size.shape[0]
    tree_len = tree_mask.shape[1]
    group_rows = requests * tree_len
    pages_dev, page_len = (key_cache.shape[0], key_cache.shape[1])
    head_count = H
    head_dim = model_width // head_count
    scaling = 1.0 / math.sqrt(head_dim)
    group_q, group_k, group_v = (
        lax.all_gather(queries, "mlp", axis=0, tiled=True),
        lax.all_gather(keys_new, "mlp", axis=0, tiled=True),
        lax.all_gather(values_new, "mlp", axis=0, tiled=True),
    )
    page_ids = member * pages_dev + jnp.arange(pages_dev, dtype=jnp.int32)
    owners = jnp.any(page_table[:, :, None] == page_ids[None, None, :], axis=1)
    owner_tokens = jnp.repeat(owners, page_len, axis=1)
    row_req = jnp.arange(group_rows, dtype=jnp.int32) // tree_len
    req_ids = jnp.arange(requests, dtype=jnp.int32)
    pool_ok = jnp.any(
        (row_req[:, None, None] == req_ids[None, :, None]) & owner_tokens[None], axis=1
    )
    cache_keys = key_cache.reshape(pages_dev * page_len, head_count, head_dim)
    cache_vals = value_cache.reshape(pages_dev * page_len, head_count, head_dim)
    pool_scores = (
        jnp.einsum(
            "qhd,khd->hqk",
            group_q.reshape(group_rows, head_count, head_dim),
            cache_keys,
            preferred_element_type=jnp.float32,
        )
        * scaling
    )
    pool_scores = jnp.where(pool_ok[None], pool_scores, -jnp.inf)
    row_start = member * rows_dev
    own_req = lax.dynamic_slice_in_dim(row_req, row_start, rows_dev, 0)
    own_tree = lax.dynamic_slice_in_dim(
        tree_mask.reshape(group_rows, tree_len), row_start, rows_dev, 0
    )
    key_slot = jnp.arange(group_rows, dtype=jnp.int32) % tree_len
    draft_ok = (
        (own_req[:, None] == row_req[None, :])
        & (jnp.tile(own_tree, (1, requests)) == 1)
        & (key_slot[None, :] < jnp.repeat(tree_size, tree_len)[None, :])
    )
    draft_scores = (
        jnp.einsum(
            "qhd,khd->hqk",
            queries.reshape(rows_dev, head_count, head_dim),
            group_k.reshape(group_rows, head_count, head_dim),
            preferred_element_type=jnp.float32,
        )
        * scaling
    )
    draft_scores = jnp.where(draft_ok[None], draft_scores, -jnp.inf)
    local_max = jnp.max(pool_scores, axis=2)
    own_max = jnp.maximum(
        lax.dynamic_slice_in_dim(local_max, row_start, rows_dev, 1), jnp.max(draft_scores, axis=2)
    )
    local_max = lax.dynamic_update_slice_in_dim(local_max, own_max, row_start, 1)
    row_max = lax.pmax(local_max, "mlp")
    pool_weights = jnp.exp(pool_scores - row_max[:, :, None])
    pool_total = jnp.transpose(jnp.sum(pool_weights, axis=2))
    pool_weighted = jnp.einsum(
        "hqk,khd->qhd",
        pool_weights.astype(jnp.bfloat16),
        cache_vals,
        preferred_element_type=jnp.float32,
    ).reshape(group_rows, model_width)
    summed_weighted, summed_total = (
        lax.psum_scatter(
            pool_weighted.astype(jnp.bfloat16), "mlp", scatter_dimension=0, tiled=True
        ).astype(jnp.float32),
        lax.psum_scatter(
            pool_total.astype(jnp.bfloat16), "mlp", scatter_dimension=0, tiled=True
        ).astype(jnp.float32),
    )
    own_row_max = lax.dynamic_slice_in_dim(row_max, row_start, rows_dev, 1)
    draft_weights = jnp.exp(draft_scores - own_row_max[:, :, None])
    total = summed_total + jnp.transpose(jnp.sum(draft_weights, axis=2))
    draft_weighted = jnp.einsum(
        "hqk,khd->qhd",
        draft_weights.astype(jnp.bfloat16),
        group_v.reshape(group_rows, head_count, head_dim),
        preferred_element_type=jnp.float32,
    )
    weighted = summed_weighted.reshape(rows_dev, head_count, head_dim) + draft_weighted
    attended = (weighted / total[:, :, None]).reshape(rows_dev, model_width).astype(jnp.bfloat16)
    blocks = regroup_rows(attended)
    hidden = resid.astype(jnp.float32) + lax.psum_scatter(
        jnp.dot(blocks, w_out, preferred_element_type=jnp.float32),
        ("req", "mlp"),
        scatter_dimension=0,
        tiled=True,
    )
    activation = spread_normed(hidden, ln_gain, w_up)
    mixed = (
        hidden
        + lax.psum_scatter(
            jnp.dot(activation, w_down, preferred_element_type=jnp.float32),
            ("req", "mlp"),
            scatter_dimension=0,
            tiled=True,
        )
    ).astype(jnp.bfloat16)
    slot_match = dest_slot == member
    valid_rows = accepted >= 0
    target_rows = req_ids[:, None] * tree_len + jnp.maximum(accepted, 0)
    matches = (
        target_rows[:, :, None] == jnp.arange(group_rows, dtype=jnp.int32)[None, None, :]
    ) & (valid_rows & slot_match[:, None])[:, :, None]
    chooser = jnp.any(matches, axis=0).astype(jnp.bfloat16)
    picked = jnp.dot(
        chooser, jnp.concatenate([group_k, group_v], axis=1), preferred_element_type=jnp.float32
    ).astype(jnp.bfloat16)
    new_keys = picked[:, :model_width][None]
    new_values = picked[:, model_width:][None]
    return (mixed, new_keys, new_values)


def solution(mesh):
    in_specs = (
        P(("req", "mlp"), None),
        P(("req", "mlp"), None),
        P(("req", "mlp"), None),
        P(("req", "mlp"), None),
        P("req", None, None),
        P("req"),
        P("req", None),
        P("req"),
        P("req", None),
        P(("req", "mlp"), None, None),
        P(("req", "mlp"), None, None),
        P(("req", "mlp"), None),
        P(None, ("req", "mlp")),
        P(("req", "mlp"), None),
        P(),
    )
    out_specs = (
        P(("req", "mlp"), None),
        P(("req", "mlp"), None, None),
        P(("req", "mlp"), None, None),
    )
    return jax.shard_map(local, mesh=mesh, in_specs=in_specs, out_specs=out_specs, check_vma=False)
```

profile of v0, /device:TPU:1, one launch (start us, length us, event | category | flops | bytes accessed | tf_op | source)
XLA Modules:
  0.0 718.0 jit_solution(5104146724432790331)
XLA Ops:
  7.3 0.9 dynamic-slice_compare_fusion
  9.1 0.9 compare_reduce_fusion
  10.2 23.6 %all-gather.1 = bf16[16,3,7168]{2,1,0:T(4,128)(2,1)} all-gather(bf16[1,3,7168]{2,1,0:T(4,128)(2,1)} %bitcast.60), channel_id=1, replica_groups=mesh['req'=8,'mlp'=16] {'mlp'}, dimensions={0}, use_global_device_ids=true | all-gather | bytes 731136 | tf_op jit(solution)/shard_map/all_gather | solution.py:62
  33.8 3.0 reshape.197
  36.8 19.5 %all-gather = bf16[16,3,7168]{2,1,0:T(4,128)(2,1)} all-gather(bf16[1,3,7168]{2,1,0:T(4,128)(2,1)} %bitcast.61), channel_id=1, replica_groups=mesh['req'=8,'mlp'=16] {'mlp'}, dimensions={0}, use_global_device_ids=true | all-gather | bytes 731136 | tf_op jit(solution)/shard_map/all_gather | solution.py:61
  56.3 3.0 reshape.193
  59.4 4.1 copy.51
  64.2 4.7 fusion.4
  69.2 58.0 %pmax.7 = f32[56,48]{1,0:T(8,128)S(1)} all-reduce(f32[56,48]{1,0:T(8,128)S(1)} %dynamic_update_slice.3), channel_id=1, replica_groups=mesh['req'=8,'mlp'=16] {'mlp'}, use_global_device_ids=true, to_apply=%region_4.5 | all-reduce | flops 2688 | bytes 21504 | tf_op jit(solution)/shard_map/pmax | solution.py:111
  127.2 4.1 copy.52
  131.4 2.8 fusion.20
  134.1 1.0 copy.74
  135.2 19.1 %all-gather.2 = bf16[16,3,7168]{2,1,0:T(4,128)(2,1)} all-gather(bf16[1,3,7168]{2,1,0:T(4,128)(2,1)S(1)} %bitcast.62), channel_id=1, replica_groups=mesh['req'=8,'mlp'=16] {'mlp'}, dimensions={0}, use_global_device_ids=true | all-gather | bytes 731136 | tf_op jit(solution)/shard_map/all_gather | solution.py:63
  154.3 3.0 reshape.201
  158.6 2.9 fusion.5
  161.5 58.1 %all-reduce.1 = bf16[48,56]{0,1:T(8,128)(2,1)S(1)} all-reduce(bf16[48,56]{0,1:T(8,128)(2,1)S(1)} %bitcast.59), channel_id=3, replica_groups=mesh['req'=8,'mlp'=16] {'mlp'}, use_global_device_ids=true, to_apply=%region_7.8.clone | all-reduce | flops 2688 | bytes 10752
  219.9 20.9 %all-reduce.8.cloned.1.call-done = bf16[48,7168]{1,0:T(8,128)(2,1)} async-done(((bf16[48,7168]{1,0:T(8,128)(2,1)}), bf16[48,7168]{1,0:T(8,128)(2,1)}) %all-reduce.8.cloned.1.call-update) | async-done | bytes 688144
  240.8 1.5 fusion.30
  242.6 38.2 %all_to_all.16 = bf16[3,128,56]{2,0,1:T(4,128)(2,1)S(1)} all-to-all(bf16[3,128,56]{2,0,1:T(4,128)(2,1)S(1)} %copy.47), channel_id=1, replica_groups=mesh['req'=8,'mlp'=16] {'req','mlp'}, dimensions={1} | all-to-all | bytes 86016 | tf_op jit(solution)/shard_map/all_to_all | solution.py:31
  281.0 6.8 fusion.51
  287.8 161.9 %all-reduce.10.cloned.1.call-done = f32[384,7168]{1,0:T(8,128)} async-done(((f32[384,7168]{1,0:T(8,128)}), f32[384,7168]{1,0:T(8,128)}) %all-reduce.10.cloned.1.call-update) | async-done | bytes 11010064
  449.8 1.2 fusion.49
  451.0 1.3 multiply_reduce_fusion
  452.2 1.8 fusion.39
  454.1 68.1 %all-gather.6.cloned.1.call-done = bf16[128,3,7168]{2,1,0:T(4,128)(2,1)} async-done(((bf16[1,3,7168]{2,1,0:T(4,128)(2,1)}), bf16[128,3,7168]{2,1,0:T(4,128)(2,1)}) %all-gather.6.cloned.1.call-update) | async-done | bytes 5505040 | tf_op jit(solution)/shard_map/all_gather | solution.py:22
  522.1 13.1 %reshape.211 = bf16[384,7168]{1,0:T(8,128)(2,1)} reshape(bf16[128,3,7168]{2,1,0:T(4,128)(2,1)} %all-gather.6.cloned.1.call-done) | data formatting | bytes 11010048
  535.2 11.4 %fusion.26 = f32[384,7168]{1,0:T(8,128)} fusion(bf16[224,7168]{1,0:T(8,128)(2,1)S(1)} %copy-done, bf16[384,7168]{1,0:T(8,128)(2,1)} %reshape.211, bf16[7168,224]{0,1:T(8,128)(2,1)} %param.27), kind=kOutput, calls=%fused_computation.21 | convolution fusion | flops 2466422784 | bytes 22937600 | tf_op jit(solution)/shard_map/dot_general | solution.py:150
  546.7 2.3 reshape.207
  549.0 2.4 reshape.209
  551.6 2.0 convolution_convert_fusion
  554.4 155.2 %all-reduce.12.cloned.1.call-done = f32[384,7168]{1,0:T(8,128)} async-done(((f32[384,7168]{1,0:T(8,128)}), f32[384,7168]{1,0:T(8,128)}) %all-reduce.12.cloned.1.call-update) | async-done | bytes 11010064
  709.6 1.8 fusion.35
  (62 shorter events, 4.9 us)
Async XLA Ops:
  7.2 528.1 %copy-start = (bf16[224,7168]{1,0:T(8,128)(2,1)S(1)}, bf16[224,7168]{1,0:T(8,128)(2,1)}, u32[]{:S(2)}) copy-start(bf16[224,7168]{1,0:T(8,128)(2,1)} %param.28) | copy-start | bytes 9633796
  7.2 233.6 %all-reduce.8.cloned.1.call-start = ((), (), s32[]{:S(2)}) async-start(), calls=%async_computation.2 | async-start | bytes 1376256
  59.4 4.3 copy-start.4
  59.4 4.3 copy-start.5
  59.4 4.8 copy-start.2
  127.2 4.1 copy-start.1
  131.3 3.9 copy-start.6
  134.1 23.2 %copy-start.10 = (u32[128]{0:T(128)S(1)}, u32[128]{0:T(128)}, u32[]{:S(2)}) copy-start(u32[128]{0:T(128)} %constant.81) | copy-start | bytes 1540
  135.2 314.6 %all-reduce.10.cloned.1.call-start = ((), (), s32[]{:S(2)}) async-start(), calls=%async_computation.3 | async-start | bytes 22020096
  287.8 162.0 %copy-start.3 = (bf16[3,7168]{1,0:T(4,128)(2,1)S(1)}, bf16[3,7168]{1,0:T(4,128)(2,1)}, u32[]{:S(2)}) copy-start(bf16[3,7168]{1,0:T(4,128)(2,1)} %param.18) | copy-start | bytes 129028
  287.8 164.5 %copy-start.7 = (f32[7168]{0:T(1024)S(1)}, f32[7168]{0:T(1024)}, u32[]{:S(2)}) copy-start(f32[7168]{0:T(1024)} %param.29) | copy-start | bytes 86020
  287.8 234.4 %all-gather.6.cloned.1.call-start = ((), (), s32[]{:S(2)}) async-start(), calls=%async_computation.1 | async-start | bytes 7397376 | tf_op jit(solution)/shard_map/all_gather | solution.py:22
  454.0 255.6 %all-reduce.12.cloned.1.call-start = ((), (), s32[]{:S(2)}) async-start(), calls=%async_computation.4 | async-start | bytes 22020096
  546.6 4.7 copy-start.9
  546.6 4.7 copy-start.8
Sparse Core Ops, SparseCore 0:
  135.3 105.4 all-reduce.7
  287.9 161.8 all-reduce.9
  454.1 67.9 all-gather.5
  546.8 162.7 all-reduce.11
where the time goes:
time: 719 us; the launch traced here: 718 us
  waiting for transfers between devices  406 us (56%)
  blocking collectives  216 us (30%)
  local copies, waits for them, and re-layouts  39.3 us (5%)
  matrix products  29.7 us (4%)
  between operations  14.6 us (2%)
  other arithmetic  11.6 us (2%)
    unnamed x7, waiting for transfers between devices  338 us
    all_gather x1, waiting for transfers between devices, spread_normed(): lax.all_gather(normed, ('req', 'mlp'), axis=0, tiled=True)  68.1 us
    unnamed x1, blocking collectives  58.1 us
    pmax x1, blocking collectives, local(): row_max = lax.pmax(local_max, 'mlp')  58 us
    all_to_all x1, blocking collectives, regroup_rows(): lax.all_to_all(attended, ('req', 'mlp'), split_axis=1, concat_axis=0, til...  38.2 us
    unnamed x28, local copies, waits for them, and re-layouts  26.6 us
    all_gather x1, blocking collectives, local(): lax.all_gather(keys_new, 'mlp', axis=0, tiled=True)  23.6 us
    all_gather x1, blocking collectives, local(): lax.all_gather(queries, 'mlp', axis=0, tiled=True)  19.5 us
  transfers between devices with their start and end apart: 4, of which 4 were waited for; matrix products, arithmetic and copies ran while one was open for 2% of the time, Pallas kernels for 0%

commit v1 on v0

v1 whole, which is shorter than its diff:
```python
import math

import jax
import jax.numpy as jnp
from jax import lax
from jax.experimental import pallas as pl
from jax.experimental.pallas import tpu as pltpu
from jax.sharding import Mesh, PartitionSpec as P

HD = 128
NEG = -(2.0**100)
F32 = jnp.float32
BF16 = jnp.bfloat16
ALL = ("z", "c", "x", "y")
REQ = ("z", "c")
MLP = ("x", "y")
CHIPS = ("z", "x", "y")
DN = (((1,), (1,)), ((), ()))


def attend_kernel(heads, scaling, q, k, v, dk, dv, pool_mask, draft_mask, out):
    pm = pool_mask[...]
    dm = draft_mask[...]
    rows = q.shape[0]
    keys = k.shape[0] * k.shape[1]
    kk = k[...].reshape(keys, k.shape[2])
    vv = v[...].reshape(keys, v.shape[2])
    lane = lax.broadcasted_iota(jnp.int32, (rows, HD), 1)
    stats = jnp.zeros((rows, HD), F32)
    for h in range(heads):
        cols = slice(h * HD, (h + 1) * HD)
        qh = q[:, cols]
        s = lax.dot_general(qh, kk[:, cols], DN, preferred_element_type=F32) * scaling
        sd = lax.dot_general(qh, dk[:, cols], DN, preferred_element_type=F32) * scaling
        s = jnp.where(pm > 0, s, NEG)
        sd = jnp.where(dm > 0, sd, NEG)
        top = jnp.maximum(jnp.max(s, axis=1, keepdims=True), jnp.max(sd, axis=1, keepdims=True))
        top = top.astype(BF16).astype(F32)
        p = jnp.exp(s - top) * pm
        pd = jnp.exp(sd - top) * dm
        total = jnp.sum(p, axis=1, keepdims=True) + jnp.sum(pd, axis=1, keepdims=True)
        high = total.astype(BF16).astype(F32)
        stats = jnp.where(lane == h, top, stats)
        stats = jnp.where(lane == 8 + h, high, stats)
        stats = jnp.where(lane == 16 + h, total - high, stats)
        w = jnp.dot(p.astype(BF16), vv[:, cols], preferred_element_type=F32)
        w = w + jnp.dot(pd.astype(BF16), dv[:, cols], preferred_element_type=F32)
        out[:, cols] = w.astype(BF16)
    out[:, heads * HD :] = stats.astype(BF16)


def attend(q, key_cache, value_cache, dk, dv, pool_mask, draft_mask):
    rows, width = q.shape
    pages, page_len, _ = key_cache.shape
    heads = 7
    steps = width // (heads * HD)
    wide = heads * HD
    col = lambda i: (0, i)
    col3 = lambda i: (0, 0, i)
    fixed = lambda i: (0, 0)

    def body(*refs):
        attend_kernel(heads, 1.0 / math.sqrt(HD), *refs)

    return pl.pallas_call(
        body,
        grid=(steps,),
        in_specs=[
            pl.BlockSpec((rows, wide), col),
            pl.BlockSpec((pages, page_len, wide), col3),
            pl.BlockSpec((pages, page_len, wide), col3),
            pl.BlockSpec((dk.shape[0], wide), col),
            pl.BlockSpec((dv.shape[0], wide), col),
            pl.BlockSpec(pool_mask.shape, fixed),
            pl.BlockSpec(draft_mask.shape, fixed),
        ],
        out_specs=pl.BlockSpec((rows, wide + HD), col),
        out_shape=jax.ShapeDtypeStruct((rows, steps * (wide + HD)), BF16),
        compiler_params=pltpu.CompilerParams(vmem_limit_bytes=40 * 1024 * 1024),
        cost_estimate=pl.CostEstimate(
            flops=4 * rows * pages * page_len * width,
            bytes_accessed=4 * pages * page_len * width,
            transcendentals=rows * pages * page_len * width // HD,
        ),
    )(q, key_cache, value_cache, dk, dv, pool_mask, draft_mask)


def pair(x):
    return lax.ppermute(x, "c", [(0, 1), (1, 0)])


def spread(x, axes, count):
    return lax.all_to_all(
        jnp.broadcast_to(x[None], (count,) + x.shape), axes, split_axis=0, concat_axis=0
    )


def exchange(x, axes):
    return lax.all_to_all(x, axes, split_axis=0, concat_axis=0)


def local(
    queries,
    keys_new,
    values_new,
    resid,
    tree_mask,
    tree_size,
    accepted,
    dest_slot,
    page_table,
    key_cache,
    value_cache,
    w_out,
    w_up,
    w_down,
    ln_gain,
):
    zs, cs, xs, ys = (lax.axis_size(a) for a in ALL)
    members = xs * ys
    groups = zs * cs
    z = lax.axis_index("z")
    c = lax.axis_index("c")
    member = lax.axis_index(MLP)
    rows_dev, width = queries.shape
    requests, tree_len = tree_mask.shape[:2]
    group_rows = requests * tree_len
    pages_dev, page_len, _ = key_cache.shape
    tokens = group_rows * groups
    heads = width // HD
    half = width // cs
    chunk = half // zs
    block = tokens // members

    k_dev = w_out.shape[0]
    wo = w_out.reshape(k_dev, cs, zs, chunk)
    wo_parts = []
    for d in range(zs):
        piece = lax.dynamic_index_in_dim(wo, (z + d) % zs, 2, keepdims=False)
        if d:
            piece = lax.ppermute(piece, "z", [(i, (i + d) % zs) for i in range(zs)])
        wo_parts.append(piece)

    up_own = lax.dynamic_slice_in_dim(w_up, c * half, half, 0)
    up_pair = pair(lax.dynamic_slice_in_dim(w_up, (1 - c) * half, half, 0))
    down_own = lax.dynamic_slice_in_dim(w_down, c * half, half, 1)
    down_pair = pair(lax.dynamic_slice_in_dim(w_down, (1 - c) * half, half, 1))
    gain = lax.dynamic_slice_in_dim(ln_gain, c * half + z * chunk, chunk, 0)

    res = exchange(
        resid.reshape(rows_dev, cs, zs, chunk).transpose(2, 1, 0, 3).reshape(groups, rows_dev, chunk),
        REQ,
    ).reshape(block, chunk)

    group_q = spread(queries, MLP, members).reshape(group_rows, width)

    page_ids = member * pages_dev + jnp.arange(pages_dev, dtype=jnp.int32)
    owners = jnp.any(page_table[:, :, None] == page_ids[None, None, :], axis=1)
    pool_mask = jnp.repeat(jnp.repeat(owners, page_len, axis=1), tree_len, axis=0).astype(F32)
    draft_pad = 8
    slot_ids = member * rows_dev + jnp.arange(draft_pad, dtype=jnp.int32)
    row_ids = jnp.arange(group_rows, dtype=jnp.int32)
    tree_cols = jnp.tile(tree_mask.reshape(group_rows, tree_len), (1, requests))
    live = jnp.repeat(tree_size, tree_len) > (row_ids % tree_len)
    tree_ok = (
        (tree_cols == 1)
        & live[None, :]
        & ((row_ids // tree_len)[:, None] == (row_ids // tree_len)[None, :])
    ).astype(F32)
    pick = (row_ids[:, None] == slot_ids[None, :]) & (
        jnp.arange(draft_pad, dtype=jnp.int32) < rows_dev
    )[None, :]
    draft_mask = jnp.dot(tree_ok, pick.astype(F32))
    pad = ((0, draft_pad - rows_dev), (0, 0))
    parts = attend(
        group_q,
        key_cache,
        value_cache,
        jnp.pad(keys_new, pad),
        jnp.pad(values_new, pad),
        pool_mask,
        draft_mask,
    )

    parts = exchange(parts.reshape(members, rows_dev, parts.shape[1]), MLP)
    parts = parts.reshape(members, rows_dev, heads // 7, 8, HD).astype(F32)
    st = parts[:, :, :, 7]
    tops, highs, lows = st[..., 0:7], st[..., 8:15], st[..., 16:23]
    scale = jnp.exp(tops - jnp.max(tops, axis=0, keepdims=True))
    total = jnp.sum(scale * (highs + lows), axis=0)
    weighted = jnp.sum(scale[..., None] * parts[:, :, :, :7], axis=0)
    attended = (weighted / total[..., None]).astype(BF16).reshape(rows_dev, width)

    feats = (
        attended.reshape(rows_dev, zs, cs, members, k_dev)
        .transpose(2, 3, 0, 1, 4)
        .reshape(1, cs * members, rows_dev, zs * k_dev)
    )
    feats = jnp.broadcast_to(feats, (zs,) + feats.shape[1:]).reshape(
        groups * members, rows_dev, zs * k_dev
    )
    feats = exchange(feats, ALL)
    feats = (
        feats.reshape(groups, members, rows_dev, zs * k_dev)
        .transpose(1, 0, 2, 3)
        .reshape(tokens, zs * k_dev)
    )
    wo_all = jnp.concatenate([jnp.stack(wo_parts[::-1]), jnp.stack(wo_parts[::-1])])
    wo_all = lax.dynamic_slice_in_dim(wo_all, zs - 1 - z, zs, 0)
    wo_all = wo_all.reshape(zs * k_dev, cs, chunk)
    wo_own = lax.dynamic_index_in_dim(wo_all, c, 1, keepdims=False)
    wo_pair = lax.dynamic_index_in_dim(wo_all, 1 - c, 1, keepdims=False)
    sent = pair(jnp.dot(feats, wo_pair, preferred_element_type=F32).astype(BF16))
    part = jnp.dot(feats, wo_own, preferred_element_type=F32) + sent.astype(F32)
    part = exchange(part.astype(BF16).reshape(members, block, chunk), MLP)
    hidden = res.astype(F32) + jnp.sum(part.astype(F32), axis=0)

    mean = jnp.mean(hidden, axis=1)
    dev = jnp.sum(jnp.square(hidden - mean[:, None]), axis=1)
    stat = jnp.stack([mean, dev])
    stat = spread(jnp.pad(stat, ((0, 6), (0, 128 - block))), REQ, groups)[:, :2, :block]
    row_mean = jnp.mean(stat[:, 0], axis=0)
    spread_sum = jnp.sum(stat[:, 1] + chunk * jnp.square(stat[:, 0] - row_mean[None]), axis=0)
    inv = lax.rsqrt(spread_sum / width + 1e-05)
    normed = ((hidden - row_mean[:, None]) * inv[:, None] * gain[None, :]).astype(BF16)

    rows = spread(normed, CHIPS, zs * members).reshape(zs, tokens, chunk)

    def up(weight):
        out = None
        for i in range(zs):
            term = jnp.dot(
                rows[i], weight[i * chunk : (i + 1) * chunk], preferred_element_type=F32
            )
            out = term if out is None else out + term
        return out

    other = pair(up(up_pair))
    act = jnp.maximum(up(up_own) + other, 0.0).astype(BF16)
    act_pair = pair(act)
    down = []
    for i in range(zs):
        cols = slice(i * chunk, (i + 1) * chunk)
        down.append(
            (
                jnp.dot(act, down_own[:, cols], preferred_element_type=F32)
                + jnp.dot(act_pair, down_pair[:, cols], preferred_element_type=F32)
            )
            .astype(BF16)
            .reshape(members, block, chunk)
        )
    down = exchange(jnp.stack(down).reshape(zs * members, block, chunk), CHIPS)
    mixed = (hidden + jnp.sum(down.astype(F32), axis=0)).astype(BF16)
    mixed = exchange(mixed.reshape(groups, rows_dev, chunk), REQ)
    mixed = mixed.reshape(zs, cs, rows_dev, chunk).transpose(2, 1, 0, 3).reshape(rows_dev, width)

    both = lax.all_gather(
        jnp.concatenate([keys_new, values_new], axis=1), MLP, axis=0, tiled=True
    )
    valid = (accepted >= 0) & (dest_slot == member)[:, None]
    target = jnp.arange(requests, dtype=jnp.int32)[:, None] * tree_len + jnp.maximum(accepted, 0)
    chooser = jnp.any((target[:, :, None] == row_ids[None, None, :]) & valid[:, :, None], axis=0)
    picked = jnp.dot(chooser.astype(BF16), both, preferred_element_type=F32).astype(BF16)
    return (mixed, picked[:, :width][None], picked[:, width:][None])


def solution(mesh):
    groups, members = mesh.devices.shape
    side = math.isqrt(members)
    fine = Mesh(mesh.devices.reshape(groups // 2, 2, side, side), ALL)
    rows = P(ALL, None)
    pages = P(ALL, None, None)
    in_specs = (
        rows,
        rows,
        rows,
        rows,
        P(REQ, None, None),
        P(REQ),
        P(REQ, None),
        P(REQ),
        P(REQ, None),
        pages,
        pages,
        rows,
        P(None, ALL),
        rows,
        P(),
    )
    return jax.shard_map(
        local, mesh=fine, in_specs=in_specs, out_specs=(rows, pages, pages), check_vma=False
    )
```

time: 719 us -> 312 us (0.43)
  waiting for transfers between devices: 406 us -> 117 us
  blocking collectives: 216 us -> 0 us
  starting transfers between devices: 0.16 us -> 63.2 us
  local copies, waits for them, and re-layouts: 39.3 us -> 61.7 us
  Pallas kernels: 0 us -> 17.7 us
  matrix products: 29.7 us -> 21.7 us
    unnamed x7 -> x1, waiting for transfers between devices: 338 us -> 0.02 us
    all_to_all x0 -> x9, waiting for transfers between devices: none -> 74.2 us  [the longest x3 41.7 us: spread(): lax.all_to_all(jnp.broadcast_to(x[None], (count,) + x.shape), axes, split...]
    all_gather x3 -> x0, blocking collectives: 62.1 us -> none  [the longest x1 23.6 us: local(): lax.all_gather(keys_new, 'mlp', axis=0, tiled=True)]
    unnamed x1 -> x0, blocking collectives: 58.1 us -> none
    pmax x1 -> x0, blocking collectives: 58 us -> none  [local(): row_max = lax.pmax(local_max, 'mlp')]
    all_to_all x0 -> x9, starting transfers between devices: none -> 53.2 us  [the longest x6 36.3 us: exchange(): return lax.all_to_all(x, axes, split_axis=0, concat_axis=0)]
    all_to_all x1 -> x0, blocking collectives: 38.2 us -> none  [regroup_rows(): lax.all_to_all(attended, ('req', 'mlp'), split_axis=1, concat_axis=0, til...]
    all_gather x1, waiting for transfers between devices: 68.1 us -> 40.7 us  [local(): lax.all_gather(jnp.concatenate([keys_new, values_new], axis=1), MLP, axis...]
  transfers between devices with their start and end apart: 4 -> 18, of which waited for: 4 -> 11; matrix products, arithmetic and copies ran while one was open for 2% -> 17% of each run, Pallas kernels for 0% -> 0%
where the time goes in v1:
time: 312 us; the launch traced here: 310 us
  waiting for transfers between devices  117 us (38%)
  starting transfers between devices  63.2 us (20%)
  local copies, waits for them, and re-layouts  61.7 us (20%)
  matrix products  21.7 us (7%)
  Pallas kernels  17.7 us (6%)
  between operations  14.6 us (5%)
  other arithmetic  14.1 us (5%)
    all_to_all x3, waiting for transfers between devices, spread(): lax.all_to_all(jnp.broadcast_to(x[None], (count,) + x.shape), axes, split...  41.7 us
    all_gather x1, waiting for transfers between devices, local(): lax.all_gather(jnp.concatenate([keys_new, values_new], axis=1), MLP, axis...  40.7 us
    all_to_all x6, starting transfers between devices, exchange(): return lax.all_to_all(x, axes, split_axis=0, concat_axis=0)  36.3 us
    all_to_all x6, waiting for transfers between devices, exchange(): return lax.all_to_all(x, axes, split_axis=0, concat_axis=0)  32.5 us
    unnamed x51, local copies, waits for them, and re-layouts  22.8 us
    pallas_call x1, Pallas kernels, attend(): pl.pallas_call(body, grid=(steps,), in_specs=[pl.BlockSpec((rows, wide),...  17.7 us
    all_to_all x3, starting transfers between devices, spread(): lax.all_to_all(jnp.broadcast_to(x[None], (count,) + x.shape), axes, split...  17 us
    dot_general x8, matrix products, up(): jnp.dot(rows[i], weight[i * chunk:(i + 1) * chunk], preferred_element_typ...  7.26 us
  transfers between devices with their start and end apart: 18, of which 11 were waited for; matrix products, arithmetic and copies ran while one was open for 17% of the time, Pallas kernels for 0%

profile of v1, /device:TPU:1, one launch (start us, length us, event | category | flops | bytes accessed | tf_op | source)
XLA Modules:
  0.0 310.3 jit_solution(8635991396056043128)
XLA Ops:
  7.2 2.9 reshape.249
  10.1 4.6 %constant_dynamic-slice_fusion.3 = (bf16[56,2,1,896]{3,2,1,0:T(2,128)(2,1)}, bf16[56,2,1,896]{3,2,1,0:T(2,128)(2,1)S(1)}, bf16[56,2,1,896]{3,2,1,0:T(2,128)(2,1)S(1)}, bf16[56,2,1,896]{3,2,1,0:T(2,128)(2,1)S(1)}) fusion(bf16[56,2,4,896]{3,2,1,0:T(4,128)(2,1)} %reshape.249, s32[]{:T(128)S(6)} %select_n.86, s32[]{:T(128)S(6)} %select_n.84, s32[]{:T(128)S(6)} %select_n.82, ...), kind=kLoop, calls=%fused_computation.105 | loop fusion | bytes 1605648 | tf_op jit(solution)/shard_map/jit(dynamic_index_in_dim)/dynamic_slice | solution.py:139
  15.4 4.6 %collective-permute-start = (bf16[56,2,896]{2,0,1:T(8,128)(2,1)}, bf16[56,2,896]{2,0,1:T(8,128)(2,1)}, u32[]{:S(2)}, u32[]{:S(2)}) collective-permute-start(bf16[56,2,896]{2,0,1:T(8,128)(2,1)} %bitcast.94), channel_id=1, source_target_pairs={{0,96},{32,0},{64,32},{96,64},{1,97},{33,1},{65,33},{97,65},{2,98}... | collective-permute-start | bytes 602120 | tf_op jit(solution)/shard_map/ppermute | solution.py:141
  23.4 6.8 %all-to-all-start.1 = ((bf16[16,3,7168]{2,1,0:T(4,128)(2,1)}), bf16[16,3,7168]{2,1,0:T(4,128)(2,1)}, u32[]{:S(2)}, u32[]{:S(2)}) async-start(bf16[16,3,7168]{2,1,0:T(4,128)(2,1)} %broadcast_in_dim.20), calls=%async_computation.1 | async-start | bytes 1835008 | tf_op jit(solution)/shard_map/all_to_all | solution.py:93
  36.2 7.9 %all-to-all-done.1 = bf16[16,3,7168]{2,1,0:T(4,128)(2,1)} async-done(((bf16[16,3,7168]{2,1,0:T(4,128)(2,1)}), bf16[16,3,7168]{2,1,0:T(4,128)(2,1)}, u32[]{:S(2)}, u32[]{:S(2)}) %all-to-all-start.1) | async-done | bytes 688160 | tf_op jit(solution)/shard_map/all_to_all | solution.py:93
  44.1 2.3 reshape.243.refs_0_
  46.5 2.6 copy-done.1
  49.0 2.6 copy-done.2
  52.7 17.7 %shard_map.166 = bf16[48,8192]{1,0:T(8,128)(2,1)S(1)} custom-call(bf16[48,7168]{1,0:T(8,128)(2,1)S(1)} %copy-done.4, bf16[24,16,7168]{2,1,0:T(8,128)(2,1)S(1)} %copy-done.1, bf16[24,16,7168]{2,1,0:T(8,128)(2,1)S(1)} %copy-done.2, bf16[8,7168]{1,0:T(8,128)(2,1)S(1)} %pad.11.refs_3_, bf16[8,7168]{1,0:T(8,128)(2,1)S(1)} %pad.12.refs_4_, ...), custom_call_target="tpu_custom_call" | custom-call | flops 528482304 | bytes 11010048 | tf_op jit(solution)/shard_map/pallas_call | solution.py:65
  71.3 2.3 reshape.245
  73.6 4.4 %all-to-all-start.2 = ((bf16[16,3,8192]{2,1,0:T(4,128)(2,1)}), bf16[16,3,8192]{2,1,0:T(4,128)(2,1)}, u32[]{:S(2)}, u32[]{:S(2)}) async-start(bf16[16,3,8192]{2,1,0:T(4,128)(2,1)} %reshape.245), calls=%async_computation.2 | async-start | bytes 2097152 | tf_op jit(solution)/shard_map/all_to_all | solution.py:99
  84.5 7.7 %all-to-all-done.2 = bf16[16,3,8192]{2,1,0:T(4,128)(2,1)} async-done(((bf16[16,3,8192]{2,1,0:T(4,128)(2,1)}), bf16[16,3,8192]{2,1,0:T(4,128)(2,1)}, u32[]{:S(2)}, u32[]{:S(2)}) %all-to-all-start.2) | async-done | bytes 786464 | tf_op jit(solution)/shard_map/all_to_all | solution.py:99
  96.5 8.9 %all-to-all-start.3 = ((bf16[128,3,224]{2,1,0:T(4,128)(2,1)}), bf16[128,3,224]{2,1,0:T(4,128)(2,1)S(1)}, u32[]{:S(2)}, u32[]{:S(2)}) async-start(bf16[128,3,224]{2,1,0:T(4,128)(2,1)} %bitcast.119), calls=%async_computation.3 | async-start | bytes 524288 | tf_op jit(solution)/shard_map/all_to_all | solution.py:99
  109.3 7.3 %all-to-all-done.3 = bf16[128,3,224]{2,1,0:T(4,128)(2,1)S(1)} async-done(((bf16[128,3,224]{2,1,0:T(4,128)(2,1)}), bf16[128,3,224]{2,1,0:T(4,128)(2,1)S(1)}, u32[]{:S(2)}, u32[]{:S(2)}) %all-to-all-start.3) | async-done | bytes 172064 | tf_op jit(solution)/shard_map/all_to_all | solution.py:99
  123.7 2.4 add_convert_fusion
  126.1 4.3 %all-to-all-start.4 = ((bf16[16,24,896]{2,1,0:T(8,128)(2,1)}), bf16[16,24,896]{2,1,0:T(8,128)(2,1)}, u32[]{:S(2)}, u32[]{:S(2)}) async-start(bf16[16,24,896]{2,1,0:T(8,128)(2,1)} %bitcast.114), calls=%async_computation.4 | async-start | bytes 1376256 | tf_op jit(solution)/shard_map/all_to_all | solution.py:99
  131.2 11.0 %all-to-all-done.4 = bf16[16,24,896]{2,1,0:T(8,128)(2,1)} async-done(((bf16[16,24,896]{2,1,0:T(8,128)(2,1)}), bf16[16,24,896]{2,1,0:T(8,128)(2,1)}, u32[]{:S(2)}, u32[]{:S(2)}) %all-to-all-start.4) | async-done | bytes 688160 | tf_op jit(solution)/shard_map/all_to_all | solution.py:99
  142.2 6.1 %all-to-all-start = ((bf16[8,3,896]{2,1,0:T(4,128)(2,1)}), bf16[8,3,896]{2,1,0:T(4,128)(2,1)S(1)}, u32[]{:S(2)}, u32[]{:S(2)}) async-start(bf16[8,3,896]{2,1,0:T(4,128)(2,1)} %bitcast.1), calls=%async_computation | async-start | bytes 114688 | tf_op jit(solution)/shard_map/all_to_all | solution.py:99
  149.5 3.6 %all-to-all-done = bf16[8,3,896]{2,1,0:T(4,128)(2,1)S(1)} async-done(((bf16[8,3,896]{2,1,0:T(4,128)(2,1)}), bf16[8,3,896]{2,1,0:T(4,128)(2,1)S(1)}, u32[]{:S(2)}, u32[]{:S(2)}) %all-to-all-start) | async-done | bytes 43040 | tf_op jit(solution)/shard_map/all_to_all | solution.py:99
  154.2 4.6 %all-to-all-start.5 = ((f32[8,8,128]{2,1,0:T(8,128)}), f32[8,8,128]{2,1,0:T(8,128)}, u32[]{:S(2)}, u32[]{:S(2)}) async-start(f32[8,8,128]{2,1,0:T(8,128)} %broadcast_in_dim.26), calls=%async_computation.5 | async-start | bytes 65536 | tf_op jit(solution)/shard_map/all_to_all | solution.py:93
  160.2 3.4 %all-to-all-done.5 = f32[8,8,128]{2,1,0:T(8,128)} async-done(((f32[8,8,128]{2,1,0:T(8,128)}), f32[8,8,128]{2,1,0:T(8,128)}, u32[]{:S(2)}, u32[]{:S(2)}) %all-to-all-start.5) | async-done | bytes 32800 | tf_op jit(solution)/shard_map/all_to_all | solution.py:93
  170.2 5.6 %all-to-all-start.6 = ((bf16[64,24,896]{2,1,0:T(8,128)(2,1)}), bf16[64,24,896]{2,1,0:T(8,128)(2,1)}, u32[]{:S(2)}, u32[]{:S(2)}) async-start(bf16[64,24,896]{2,1,0:T(8,128)(2,1)} %broadcast_in_dim.27), calls=%async_computation.6 | async-start | bytes 5505024 | tf_op jit(solution)/shard_map/all_to_all | solution.py:93
  175.8 2.7 constant_dynamic-slice_fusion.1
  180.5 30.3 %all-to-all-done.6 = bf16[64,24,896]{2,1,0:T(8,128)(2,1)} async-done(((bf16[64,24,896]{2,1,0:T(8,128)(2,1)}), bf16[64,24,896]{2,1,0:T(8,128)(2,1)}, u32[]{:S(2)}, u32[]{:S(2)}) %all-to-all-start.6) | async-done | bytes 2752544 | tf_op jit(solution)/shard_map/all_to_all | solution.py:93
  219.7 2.6 collective-permute-start.5
  234.1 6.7 %all-to-all-start.7 = ((bf16[64,24,896]{2,1,0:T(8,128)(2,1)}), bf16[64,24,896]{2,1,0:T(8,128)(2,1)}, u32[]{:S(2)}, u32[]{:S(2)}) async-start(bf16[64,24,896]{2,1,0:T(8,128)(2,1)} %bitcast.98), calls=%async_computation.7 | async-start | bytes 5505024 | tf_op jit(solution)/shard_map/all_to_all | solution.py:99
  241.1 40.7 %all-gather.3.cloned.1.call-done = bf16[16,3,14336]{2,1,0:T(4,128)(2,1)} async-done(((bf16[1,3,14336]{2,1,0:T(4,128)(2,1)}), bf16[16,3,14336]{2,1,0:T(4,128)(2,1)}) %all-gather.3.cloned.1.call-update) | async-done | bytes 1376272 | tf_op jit(solution)/shard_map/all_gather | solution.py:257
  281.8 3.3 %reshape.258 = bf16[48,14336]{1,0:T(8,128)(2,1)} reshape(bf16[16,3,14336]{2,1,0:T(4,128)(2,1)} %all-gather.3.cloned.1.call-done) | data formatting | bytes 2752512
  285.1 2.4 convolution_convert_fusion
  287.5 2.9 convert_reduce_fusion
  292.0 5.9 %all-to-all-start.8 = ((bf16[8,3,896]{2,1,0:T(4,128)(2,1)}), bf16[8,3,896]{2,1,0:T(4,128)(2,1)S(1)}, u32[]{:S(2)}, u32[]{:S(2)}) async-start(bf16[8,3,896]{2,1,0:T(4,128)(2,1)} %add_convert_fusion.1), calls=%async_computation.8 | async-start | bytes 114688 | tf_op jit(solution)/shard_map/all_to_all | solution.py:99
  299.7 3.0 all-to-all-done.8
  (157 shorter events, 71.7 us)
Async XLA Ops:
  7.2 172.1 %copy-start = (bf16[224,7168]{1,0:T(8,128)(2,1)S(1)}, bf16[224,7168]{1,0:T(8,128)(2,1)}, u32[]{:S(2)}) copy-start(bf16[224,7168]{1,0:T(8,128)(2,1)} %param.28) | copy-start | bytes 9633796
  14.7 7.5 %copy-start.15 = (bf16[3,7168]{1,0:T(4,128)(2,1)S(1)}, bf16[3,7168]{1,0:T(4,128)(2,1)}, u32[]{:S(2)}) copy-start(bf16[3,7168]{1,0:T(4,128)(2,1)} %param.15) | copy-start | bytes 129028
  15.4 15.9 %collective-permute-start = (bf16[56,2,896]{2,0,1:T(8,128)(2,1)}, bf16[56,2,896]{2,0,1:T(8,128)(2,1)}, u32[]{:S(2)}, u32[]{:S(2)}) collective-permute-start(bf16[56,2,896]{2,0,1:T(8,128)(2,1)} %bitcast.94), channel_id=1, source_target_pairs={{0,96},{32,0},{64,32},{96,64},{1,97},{33,1},{65,33},{97,65},{2,98}... | collective-permute-start | bytes 602120 | tf_op jit(solution)/shard_map/ppermute | solution.py:141
  20.7 12.2 %collective-permute-start.1 = (bf16[56,2,896]{2,0,1:T(8,128)(2,1)}, bf16[56,2,896]{2,0,1:T(8,128)(2,1)}, u32[]{:S(2)}, u32[]{:S(2)}) collective-permute-start(bf16[56,2,896]{2,0,1:T(8,128)(2,1)} %bitcast.93), channel_id=1, source_target_pairs={{0,64},{32,96},{64,0},{96,32},{1,65},{33,97},{65,1},{97,33},{2,66}... | collective-permute-start | bytes 602120 | tf_op jit(solution)/shard_map/ppermute | solution.py:141
  20.7 9.6 %copy-start.18 = (s32[3,384]{1,0:T(4,128)S(1)}, s32[3,384]{1,0:T(4,128)}, u32[]{:S(2)}) copy-start(s32[3,384]{1,0:T(4,128)} %param.23) | copy-start | bytes 13828
  21.5 9.2 %copy-start.16 = (s32[3,16,16]{2,1,0:T(8,128)S(1)}, s32[3,16,16]{2,1,0:T(8,128)}, u32[]{:S(2)}) copy-start(s32[3,16,16]{2,1,0:T(8,128)} %param.19) | copy-start | bytes 9220
  21.5 9.4 %copy-start.19 = (s32[3]{0:T(128)S(1)}, s32[3]{0:T(128)}, u32[]{:S(2)}) copy-start(s32[3]{0:T(128)} %param.20) | copy-start | bytes 40
  21.5 9.5 %copy-start.10 = (bf16[3,7168]{1,0:T(4,128)(2,1)S(1)}, bf16[3,7168]{1,0:T(4,128)(2,1)}, u32[]{:S(2)}) copy-start(bf16[3,7168]{1,0:T(4,128)(2,1)} %param.16) | copy-start | bytes 129028
  21.5 9.6 %copy-start.12 = (bf16[3,7168]{1,0:T(4,128)(2,1)S(1)}, bf16[3,7168]{1,0:T(4,128)(2,1)}, u32[]{:S(2)}) copy-start(bf16[3,7168]{1,0:T(4,128)(2,1)} %param.17) | copy-start | bytes 129028
  21.5 13.1 %collective-permute-start.2 = (bf16[56,2,896]{2,0,1:T(8,128)(2,1)}, bf16[56,2,896]{2,0,1:T(8,128)(2,1)}, u32[]{:S(2)}, u32[]{:S(2)}) collective-permute-start(bf16[56,2,896]{2,0,1:T(8,128)(2,1)} %bitcast.92), channel_id=1, source_target_pairs={{0,32},{32,64},{64,96},{96,0},{1,33},{33,65},{65,97},{97,1},{2,34}... | collective-permute-start | bytes 602120 | tf_op jit(solution)/shard_map/ppermute | solution.py:141
  23.4 20.7 %all-to-all-start.1 = ((bf16[16,3,7168]{2,1,0:T(4,128)(2,1)}), bf16[16,3,7168]{2,1,0:T(4,128)(2,1)}, u32[]{:S(2)}, u32[]{:S(2)}) async-start(bf16[16,3,7168]{2,1,0:T(4,128)(2,1)} %broadcast_in_dim.20), calls=%async_computation.1 | async-start | bytes 1835008 | tf_op jit(solution)/shard_map/all_to_all | solution.py:93
  73.6 18.6 %all-to-all-start.2 = ((bf16[16,3,8192]{2,1,0:T(4,128)(2,1)}), bf16[16,3,8192]{2,1,0:T(4,128)(2,1)}, u32[]{:S(2)}, u32[]{:S(2)}) async-start(bf16[16,3,8192]{2,1,0:T(4,128)(2,1)} %reshape.245), calls=%async_computation.2 | async-start | bytes 2097152 | tf_op jit(solution)/shard_map/all_to_all | solution.py:99
  96.5 20.1 %all-to-all-start.3 = ((bf16[128,3,224]{2,1,0:T(4,128)(2,1)}), bf16[128,3,224]{2,1,0:T(4,128)(2,1)S(1)}, u32[]{:S(2)}, u32[]{:S(2)}) async-start(bf16[128,3,224]{2,1,0:T(4,128)(2,1)} %bitcast.119), calls=%async_computation.3 | async-start | bytes 524288 | tf_op jit(solution)/shard_map/all_to_all | solution.py:99
  120.8 2.9 collective-permute-start.3
  121.6 8.8 %copy-start.14 = (bf16[3,7168]{1,0:T(4,128)(2,1)S(1)}, bf16[3,7168]{1,0:T(4,128)(2,1)}, u32[]{:S(2)}) copy-start(bf16[3,7168]{1,0:T(4,128)(2,1)} %param.18) | copy-start | bytes 129028
  126.1 16.0 %all-to-all-start.4 = ((bf16[16,24,896]{2,1,0:T(8,128)(2,1)}), bf16[16,24,896]{2,1,0:T(8,128)(2,1)}, u32[]{:S(2)}, u32[]{:S(2)}) async-start(bf16[16,24,896]{2,1,0:T(8,128)(2,1)} %bitcast.114), calls=%async_computation.4 | async-start | bytes 1376256 | tf_op jit(solution)/shard_map/all_to_all | solution.py:99
  142.2 10.9 %all-to-all-start = ((bf16[8,3,896]{2,1,0:T(4,128)(2,1)}), bf16[8,3,896]{2,1,0:T(4,128)(2,1)S(1)}, u32[]{:S(2)}, u32[]{:S(2)}) async-start(bf16[8,3,896]{2,1,0:T(4,128)(2,1)} %bitcast.1), calls=%async_computation | async-start | bytes 114688 | tf_op jit(solution)/shard_map/all_to_all | solution.py:99
  149.5 20.7 %copy-start.6 = (f32[8,3,896]{2,1,0:T(4,128)}, f32[8,3,896]{2,1,0:T(4,128)S(1)}, u32[]{:S(2)}) copy-start(f32[8,3,896]{2,1,0:T(4,128)S(1)} %reduce_sum.79) | copy-start | bytes 258052
  153.1 17.1 %copy-start.8 = (bf16[8,3,896]{2,1,0:T(4,128)(2,1)}, bf16[8,3,896]{2,1,0:T(4,128)(2,1)S(1)}, u32[]{:S(2)}) copy-start(bf16[8,3,896]{2,1,0:T(4,128)(2,1)S(1)} %all-to-all-done) | copy-start | bytes 129028
  154.2 9.4 %all-to-all-start.5 = ((f32[8,8,128]{2,1,0:T(8,128)}), f32[8,8,128]{2,1,0:T(8,128)}, u32[]{:S(2)}, u32[]{:S(2)}) async-start(f32[8,8,128]{2,1,0:T(8,128)} %broadcast_in_dim.26), calls=%async_computation.5 | async-start | bytes 65536 | tf_op jit(solution)/shard_map/all_to_all | solution.py:93
  170.2 40.7 %all-to-all-start.6 = ((bf16[64,24,896]{2,1,0:T(8,128)(2,1)}), bf16[64,24,896]{2,1,0:T(8,128)(2,1)}, u32[]{:S(2)}, u32[]{:S(2)}) async-start(bf16[64,24,896]{2,1,0:T(8,128)(2,1)} %broadcast_in_dim.27), calls=%async_computation.6 | async-start | bytes 5505024 | tf_op jit(solution)/shard_map/all_to_all | solution.py:93
  175.8 106.0 %all-gather.3.cloned.1.call-start = ((), (), s32[]{:S(2)}) async-start(), calls=%async_computation.9 | async-start | bytes 1949696 | tf_op jit(solution)/shard_map/all_gather | solution.py:257
  178.5 35.5 %collective-permute-start.4 = (bf16[3584,224]{0,1:T(8,128)(2,1)}, bf16[3584,224]{0,1:T(8,128)(2,1)}, u32[]{:S(2)}, u32[]{:S(2)}) collective-permute-start(bf16[3584,224]{0,1:T(8,128)(2,1)} %constant_dynamic-slice_fusion.1), channel_id=1, source_target_pairs={{0,16},{16,0},{1,17},{17,1},{2,18},{18,2},{3,19},{19,3},{4,20},{20... | collective-permute-start | bytes 4816904 | tf_op jit(solution)/shard_map/ppermute | solution.py:89
  180.5 44.3 %collective-permute-start.7 = (bf16[224,3584]{1,0:T(8,128)(2,1)}, bf16[224,3584]{1,0:T(8,128)(2,1)}, u32[]{:S(2)}, u32[]{:S(2)}) collective-permute-start(bf16[224,3584]{1,0:T(8,128)(2,1)} %constant_dynamic-slice_fusion), channel_id=1, source_target_pairs={{0,16},{16,0},{1,17},{17,1},{2,18},{18,2},{3,19},{19,3},{4,20},{20... | collective-permute-start | bytes 4816904 | tf_op jit(solution)/shard_map/ppermute | solution.py:89
  219.7 3.9 %collective-permute-start.5 = (f32[384,224]{0,1:T(8,128)S(1)}, f32[384,224]{0,1:T(8,128)S(1)}, u32[]{:S(2)}, u32[]{:S(2)}) collective-permute-start(f32[384,224]{0,1:T(8,128)S(1)} %fusion.6), channel_id=1, source_target_pairs={{0,16},{16,0},{1,17},{17,1},{2,18},{18,2},{3,19},{19,3},{4,20},{20... | collective-permute-start | bytes 1032200 | tf_op jit(solution)/shard_map/ppermute | solution.py:89
  223.6 1.5 collective-permute-start.6
  234.1 6.7 %copy-start.20 = (s32[3]{0:T(128)S(1)}, s32[3]{0:T(128)}, u32[]{:S(2)}) copy-start(s32[3]{0:T(128)} %param.22) | copy-start | bytes 40
  234.1 6.8 %copy-start.17 = (s32[3,16]{1,0:T(4,128)S(1)}, s32[3,16]{1,0:T(4,128)}, u32[]{:S(2)}) copy-start(s32[3,16]{1,0:T(4,128)} %param.21) | copy-start | bytes 580
  234.1 53.4 %all-to-all-start.7 = ((bf16[64,24,896]{2,1,0:T(8,128)(2,1)}), bf16[64,24,896]{2,1,0:T(8,128)(2,1)}, u32[]{:S(2)}, u32[]{:S(2)}) async-start(bf16[64,24,896]{2,1,0:T(8,128)(2,1)} %bitcast.98), calls=%async_computation.7 | async-start | bytes 5505024 | tf_op jit(solution)/shard_map/all_to_all | solution.py:99
  287.5 3.8 %copy-start.7 = (f32[8,3,896]{2,1,0:T(4,128)S(1)}, f32[8,3,896]{2,1,0:T(4,128)}, u32[]{:S(2)}) copy-start(f32[8,3,896]{2,1,0:T(4,128)} %copy-done.6) | copy-start | bytes 258052
  287.5 3.8 %copy-start.9 = (bf16[8,3,896]{2,1,0:T(4,128)(2,1)S(1)}, bf16[8,3,896]{2,1,0:T(4,128)(2,1)}, u32[]{:S(2)}) copy-start(bf16[8,3,896]{2,1,0:T(4,128)(2,1)} %copy-done.8) | copy-start | bytes 129028
  292.0 10.8 %all-to-all-start.8 = ((bf16[8,3,896]{2,1,0:T(4,128)(2,1)}), bf16[8,3,896]{2,1,0:T(4,128)(2,1)S(1)}, u32[]{:S(2)}, u32[]{:S(2)}) async-start(bf16[8,3,896]{2,1,0:T(4,128)(2,1)} %add_convert_fusion.1), calls=%async_computation.8 | async-start | bytes 114688 | tf_op jit(solution)/shard_map/all_to_all | solution.py:99
  (7 other events, 11.8 us)
Sparse Core Ops, SparseCore 0:
  224.9 56.8 all-gather.2

commit v2 on v1

--- a/solution.py
+++ b/solution.py
@@ -14,7 +14,6 @@
 ALL = ("z", "c", "x", "y")
 REQ = ("z", "c")
 MLP = ("x", "y")
-CHIPS = ("z", "x", "y")
 DN = (((1,), (1,)), ((), ()))
 
 
@@ -87,6 +86,69 @@
 
 def pair(x):
     return lax.ppermute(x, "c", [(0, 1), (1, 0)])
+
+
+def shift(x, step, size):
+    return lax.ppermute(x, "z", [(i, (i + step) % size) for i in range(size)])
+
+
+def after(x, first):
+    return lax.optimization_barrier((x, first))[0]
+
+
+def up_kernel(n, *refs):
+    g = refs[0][...]
+    for d in range(n):
+        for e in range(2):
+            w = lax.dot_general(g, refs[1 + d][e], DN, preferred_element_type=F32)
+            if e:
+                refs[n + 2][d] = w.astype(BF16)
+            else:
+                refs[n + 1][d] = w
+
+
+def up_project(normed, weights):
+    n = len(weights)
+    rows = normed.shape[0]
+    units = weights[0].shape[1]
+    return pl.pallas_call(
+        lambda *refs: up_kernel(n, *refs),
+        out_shape=(
+            jax.ShapeDtypeStruct((n, rows, units), F32),
+            jax.ShapeDtypeStruct((n, rows, units), BF16),
+        ),
+        compiler_params=pltpu.CompilerParams(vmem_limit_bytes=40 * 1024 * 1024),
+        cost_estimate=pl.CostEstimate(
+            flops=4 * n * rows * normed.shape[1] * units,
+            bytes_accessed=4 * n * normed.shape[1] * units,
+            transcendentals=0,
+        ),
+    )(normed, *weights)
+
+
+def down_kernel(n, *refs):
+    total = None
+    for d in range(n):
+        for e in range(2):
+            term = jnp.dot(refs[e * n + d][...], refs[2 * n + d][e], preferred_element_type=F32)
+            total = term if total is None else total + term
+    refs[3 * n][...] = total.astype(BF16)
+
+
+def down_project(own, other, weights):
+    n = len(weights)
+    rows, units = own[0].shape
+    width = weights[0].shape[2]
+    return pl.pallas_call(
+        lambda *refs: down_kernel(n, *refs),
+        out_shape=jax.ShapeDtypeStruct((rows, width), BF16),
+        compiler_params=pltpu.CompilerParams(vmem_limit_bytes=40 * 1024 * 1024),
+        cost_estimate=pl.CostEstimate(
+            flops=4 * n * rows * width * units,
+            bytes_accessed=4 * n * width * units,
+            transcendentals=0,
+        ),
+    )(*own, *other, *weights)
 
 
 def spread(x, axes, count):
@@ -132,27 +194,22 @@
     chunk = half // zs
     block = tokens // members
 
+    group_q = spread(queries, MLP, members).reshape(group_rows, width)
+
+    def piece(w, core, d):
+        return lax.dynamic_slice_in_dim(w, core * half + ((z + d) % zs) * chunk, chunk, 1)
+
     k_dev = w_out.shape[0]
-    wo = w_out.reshape(k_dev, cs, zs, chunk)
+    wo = after(w_out, group_q)
     wo_parts = []
     for d in range(zs):
-        piece = lax.dynamic_index_in_dim(wo, (z + d) % zs, 2, keepdims=False)
-        if d:
-            piece = lax.ppermute(piece, "z", [(i, (i + d) % zs) for i in range(zs)])
-        wo_parts.append(piece)
-
-    up_own = lax.dynamic_slice_in_dim(w_up, c * half, half, 0)
-    up_pair = pair(lax.dynamic_slice_in_dim(w_up, (1 - c) * half, half, 0))
-    down_own = lax.dynamic_slice_in_dim(w_down, c * half, half, 1)
-    down_pair = pair(lax.dynamic_slice_in_dim(w_down, (1 - c) * half, half, 1))
-    gain = lax.dynamic_slice_in_dim(ln_gain, c * half + z * chunk, chunk, 0)
-
-    res = exchange(
-        resid.reshape(rows_dev, cs, zs, chunk).transpose(2, 1, 0, 3).reshape(groups, rows_dev, chunk),
-        REQ,
-    ).reshape(block, chunk)
-
-    group_q = spread(queries, MLP, members).reshape(group_rows, width)
+        part = jnp.stack([piece(wo, c, d), piece(wo, 1 - c, d)])
+        wo_parts.append(shift(part, d, zs) if d else part)
+    wo_parts = jnp.concatenate(wo_parts, axis=1)
+
+    both = spread(
+        after(jnp.concatenate([keys_new, values_new], axis=1), group_q), MLP, members
+    ).reshape(group_rows, 2 * width)
 
     page_ids = member * pages_dev + jnp.arange(pages_dev, dtype=jnp.int32)
     owners = jnp.any(page_table[:, :, None] == page_ids[None, None, :], axis=1)
@@ -182,6 +239,34 @@
         draft_mask,
     )
 
+    res = after(resid, parts)
+    res = jnp.stack(
+        [
+            lax.dynamic_slice_in_dim(res, c * half, half, 1),
+            pair(lax.dynamic_slice_in_dim(res, (1 - c) * half, half, 1)),
+        ]
+    ).reshape(cs * rows_dev, half)
+    res_parts = []
+    for d in range(zs):
+        part = lax.dynamic_slice_in_dim(res, ((z + d) % zs) * chunk, chunk, 1)
+        res_parts.append(shift(part, d, zs) if d else part)
+    res = jnp.concatenate(res_parts, axis=0)
+    at = jnp.arange(block, dtype=jnp.int32)
+    source = ((z - at // (cs * rows_dev)) % zs) * cs + (c + at // rows_dev) % cs
+    order = at[:, None] == (source * rows_dev + at % rows_dev)[None, :]
+    res = jnp.dot(order.astype(BF16), res, preferred_element_type=F32)
+
+    weights = []
+    for w in (w_up.T, w_down):
+        w = after(w, parts)
+        other = pair(lax.dynamic_slice_in_dim(w, (1 - c) * half, half, 1))
+        split = []
+        for d in range(zs):
+            at = ((z + d) % zs) * chunk
+            part = jnp.stack([piece(w, c, d), lax.dynamic_slice_in_dim(other, at, chunk, 1)])
+            split.append(shift(part, d, zs) if d else part)
+        weights.append(split)
+
     parts = exchange(parts.reshape(members, rows_dev, parts.shape[1]), MLP)
     parts = parts.reshape(members, rows_dev, heads // 7, 8, HD).astype(F32)
     st = parts[:, :, :, 7]
@@ -191,29 +276,26 @@
     weighted = jnp.sum(scale[..., None] * parts[:, :, :, :7], axis=0)
     attended = (weighted / total[..., None]).astype(BF16).reshape(rows_dev, width)
 
-    feats = (
-        attended.reshape(rows_dev, zs, cs, members, k_dev)
-        .transpose(2, 3, 0, 1, 4)
-        .reshape(1, cs * members, rows_dev, zs * k_dev)
-    )
-    feats = jnp.broadcast_to(feats, (zs,) + feats.shape[1:]).reshape(
-        groups * members, rows_dev, zs * k_dev
-    )
+    feats = attended.reshape(rows_dev, zs, cs, members, k_dev).transpose(1, 2, 3, 0, 4)
+    feats = jnp.stack(
+        [
+            jnp.concatenate([feats[(to - d) % zs] for d in range(zs)], axis=3)
+            for to in range(zs)
+        ]
+    ).reshape(groups * members, rows_dev, zs * k_dev)
     feats = exchange(feats, ALL)
     feats = (
         feats.reshape(groups, members, rows_dev, zs * k_dev)
         .transpose(1, 0, 2, 3)
         .reshape(tokens, zs * k_dev)
     )
-    wo_all = jnp.concatenate([jnp.stack(wo_parts[::-1]), jnp.stack(wo_parts[::-1])])
-    wo_all = lax.dynamic_slice_in_dim(wo_all, zs - 1 - z, zs, 0)
-    wo_all = wo_all.reshape(zs * k_dev, cs, chunk)
-    wo_own = lax.dynamic_index_in_dim(wo_all, c, 1, keepdims=False)
-    wo_pair = lax.dynamic_index_in_dim(wo_all, 1 - c, 1, keepdims=False)
+    wo_own, wo_pair = wo_parts[0], wo_parts[1]
     sent = pair(jnp.dot(feats, wo_pair, preferred_element_type=F32).astype(BF16))
     part = jnp.dot(feats, wo_own, preferred_element_type=F32) + sent.astype(F32)
     part = exchange(part.astype(BF16).reshape(members, block, chunk), MLP)
-    hidden = res.astype(F32) + jnp.sum(part.astype(F32), axis=0)
+    hidden = res + jnp.sum(part.astype(F32), axis=0)
+
+    gain = lax.dynamic_slice_in_dim(ln_gain, c * half + z * chunk, chunk, 0)
 
     mean = jnp.mean(hidden, axis=1)
     dev = jnp.sum(jnp.square(hidden - mean[:, None]), axis=1)
@@ -224,39 +306,23 @@
     inv = lax.rsqrt(spread_sum / width + 1e-05)
     normed = ((hidden - row_mean[:, None]) * inv[:, None] * gain[None, :]).astype(BF16)
 
-    rows = spread(normed, CHIPS, zs * members).reshape(zs, tokens, chunk)
-
-    def up(weight):
-        out = None
-        for i in range(zs):
-            term = jnp.dot(
-                rows[i], weight[i * chunk : (i + 1) * chunk], preferred_element_type=F32
-            )
-            out = term if out is None else out + term
-        return out
-
-    other = pair(up(up_pair))
-    act = jnp.maximum(up(up_own) + other, 0.0).astype(BF16)
-    act_pair = pair(act)
-    down = []
-    for i in range(zs):
-        cols = slice(i * chunk, (i + 1) * chunk)
-        down.append(
-            (
-                jnp.dot(act, down_own[:, cols], preferred_element_type=F32)
-                + jnp.dot(act_pair, down_pair[:, cols], preferred_element_type=F32)
-            )
-            .astype(BF16)
-            .reshape(members, block, chunk)
-        )
-    down = exchange(jnp.stack(down).reshape(zs * members, block, chunk), CHIPS)
+    rows = spread(normed, MLP, members).reshape(tokens, chunk)
+    mine, theirs = up_project(rows, weights[0])
+    theirs = pair(theirs)
+    act = None
+    for d in range(zs):
+        term = mine[d] + theirs[d].astype(F32)
+        if d:
+            term = shift(term.astype(BF16), -d, zs).astype(F32)
+        act = term if act is None else act + term
+    act = jnp.maximum(act, 0.0).astype(BF16)
+    acts = [shift(act, d, zs) if d else act for d in range(zs)]
+    down = down_project(acts, [pair(a) for a in acts], weights[1])
+    down = exchange(down.reshape(members, block, chunk), MLP)
     mixed = (hidden + jnp.sum(down.astype(F32), axis=0)).astype(BF16)
     mixed = exchange(mixed.reshape(groups, rows_dev, chunk), REQ)
     mixed = mixed.reshape(zs, cs, rows_dev, chunk).transpose(2, 1, 0, 3).reshape(rows_dev, width)
 
-    both = lax.all_gather(
-        jnp.concatenate([keys_new, values_new], axis=1), MLP, axis=0, tiled=True
-    )
     valid = (accepted >= 0) & (dest_slot == member)[:, None]
     target = jnp.arange(requests, dtype=jnp.int32)[:, None] * tree_len + jnp.maximum(accepted, 0)
     chooser = jnp.any((target[:, :, None] == row_ids[None, None, :]) & valid[:, :, None], axis=0)

time: 312 us -> 302 us (0.968)
  starting transfers between devices: 63.2 us -> 89 us
  matrix products: 21.7 us -> 3.38 us
  between operations: 14.6 us -> 1.45 us
  local copies, waits for them, and re-layouts: 61.7 us -> 49.4 us
  Pallas kernels: 17.7 us -> 23.3 us
  other arithmetic: 14.1 us -> 18.4 us
    ppermute x3 -> x18, waiting for transfers between devices: 0.01 us -> 48.1 us  [shift(): return lax.ppermute(x, 'z', [(i, (i + step) % size) for i in range(size)])]
    all_gather x1 -> x0, waiting for transfers between devices: 40.7 us -> none  [local(): lax.all_gather(jnp.concatenate([keys_new, values_new], axis=1), MLP, axis...]
    ppermute x3 -> x18, starting transfers between devices: 5.35 us -> 22.9 us  [shift(): return lax.ppermute(x, 'z', [(i, (i + step) % size) for i in range(size)])]
    dot_general x16 -> x1, matrix products: 14.4 us -> 0.27 us  [local(): res = jnp.dot(order.astype(BF16), res, preferred_element_type=F32)]
    all_to_all x6 -> x5, waiting for transfers between devices: 32.5 us -> 20.6 us  [exchange(): return lax.all_to_all(x, axes, split_axis=0, concat_axis=0)]
    dynamic_slice x8 -> x3, local copies, waits for them, and re-layouts: 12.9 us -> 4.02 us  [the longest x2 4 us: local(): other = pair(lax.dynamic_slice_in_dim(w, (1 - c) * half, half, 1))]
    another operation x1 -> x14, other arithmetic: 1.82 us -> 10.4 us  [the longest x8 7.23 us: local(): jnp.stack([piece(w, c, d), lax.dynamic_slice_in_dim(other, at, chunk, 1)])]
    another operation x1 -> x6, local copies, waits for them, and re-layouts: 0.08 us -> 8.6 us  [the longest x3 7.01 us: local(): jnp.stack([piece(w, c, d), lax.dynamic_slice_in_dim(other, at, chunk, 1)])]
  transfers between devices with their start and end apart: 18 -> 36, of which waited for: 11 -> 11; matrix products, arithmetic and copies ran while one was open for 17% -> 18% of each run, Pallas kernels for 0% -> 1%
where the time goes in v2:
time: 302 us; the launch traced here: 300 us
  waiting for transfers between devices  115 us (38%)
  starting transfers between devices  89 us (29%)
  local copies, waits for them, and re-layouts  49.4 us (16%)
  Pallas kernels  23.3 us (8%)
  other arithmetic  18.4 us (6%)
  matrix products  3.38 us (1%)
    ppermute x18, waiting for transfers between devices, shift(): return lax.ppermute(x, 'z', [(i, (i + step) % size) for i in range(size)])  48.1 us
    all_to_all x4, waiting for transfers between devices, spread(): lax.all_to_all(jnp.broadcast_to(x[None], (count,) + x.shape), axes, split...  45.9 us
    all_to_all x5, starting transfers between devices, exchange(): return lax.all_to_all(x, axes, split_axis=0, concat_axis=0)  29.5 us
    all_to_all x4, starting transfers between devices, spread(): lax.all_to_all(jnp.broadcast_to(x[None], (count,) + x.shape), axes, split...  23.7 us
    ppermute x18, starting transfers between devices, shift(): return lax.ppermute(x, 'z', [(i, (i + step) % size) for i in range(size)])  22.9 us
    all_to_all x5, waiting for transfers between devices, exchange(): return lax.all_to_all(x, axes, split_axis=0, concat_axis=0)  20.6 us
    pallas_call x1, Pallas kernels, attend(): pl.pallas_call(body, grid=(steps,), in_specs=[pl.BlockSpec((rows, wide),...  17.7 us
    unnamed x65, local copies, waits for them, and re-layouts  17.1 us
  transfers between devices with their start and end apart: 36, of which 11 were waited for; matrix products, arithmetic and copies ran while one was open for 18% of the time, Pallas kernels for 1%

profile of v2, /device:TPU:1, one launch (start us, length us, event | category | flops | bytes accessed | tf_op | source)
XLA Modules:
  0.0 300.4 jit_solution(8589992574841045983)
XLA Ops:
  2.7 7.6 %all-to-all-start = ((bf16[16,3,7168]{2,1,0:T(4,128)(2,1)}), bf16[16,3,7168]{2,1,0:T(4,128)(2,1)S(1)}, u32[]{:S(2)}, u32[]{:S(2)}) async-start(bf16[16,3,7168]{2,1,0:T(4,128)(2,1)} %broadcast_in_dim.18), calls=%async_computation | async-start | bytes 1835008 | tf_op jit(solution)/shard_map/all_to_all | solution.py:155
  12.3 12.1 %all-to-all-done = bf16[16,3,7168]{2,1,0:T(4,128)(2,1)S(1)} async-done(((bf16[16,3,7168]{2,1,0:T(4,128)(2,1)}), bf16[16,3,7168]{2,1,0:T(4,128)(2,1)S(1)}, u32[]{:S(2)}, u32[]{:S(2)}) %all-to-all-start) | async-done | bytes 688160 | tf_op jit(solution)/shard_map/all_to_all | solution.py:155
  25.0 2.6 copy-done
  27.6 2.6 copy-done.1
  30.1 17.7 %shard_map.166 = bf16[48,8192]{1,0:T(8,128)(2,1)S(1)} custom-call(bf16[48,7168]{1,0:T(8,128)(2,1)S(1)} %reshape.223.refs_0_, bf16[24,16,7168]{2,1,0:T(8,128)(2,1)S(1)} %copy-done, bf16[24,16,7168]{2,1,0:T(8,128)(2,1)S(1)} %copy-done.1, bf16[8,7168]{1,0:T(8,128)(2,1)S(1)} %pad.11.refs_3_, bf16[8,7168]{1,0:T(8,128)(2,1)S(1)} %pad.12.refs_4_, ...), custom_call_target="tpu_custom_call" | custom-call | flops 528482304 | bytes 11010048 | tf_op jit(solution)/shard_map/pallas_call | solution.py:64
  49.2 4.0 %all-to-all-start.1 = ((bf16[16,3,8192]{2,1,0:T(4,128)(2,1)}), bf16[16,3,8192]{2,1,0:T(4,128)(2,1)S(1)}, u32[]{:S(2)}, u32[]{:S(2)}) async-start(bf16[16,3,8192]{2,1,0:T(4,128)(2,1)} %reshape.226), calls=%async_computation.1 | async-start | bytes 2097152 | tf_op jit(solution)/shard_map/all_to_all | solution.py:161
  54.7 3.8 %collective-permute-start.6 = (bf16[2,56,896]{2,1,0:T(8,128)(2,1)}, bf16[2,56,896]{2,1,0:T(8,128)(2,1)}, u32[]{:S(2)}, u32[]{:S(2)}) collective-permute-start(bf16[2,56,896]{2,1,0:T(8,128)(2,1)} %pad_maximum_fusion.11), channel_id=1, source_target_pairs={{0,96},{32,0},{64,32},{96,64},{1,97},{33,1},{65,33},{97,65},{2,98}... | collective-permute-start | bytes 602120 | tf_op jit(solution)/shard_map/ppermute | solution.py:92
  60.6 2.7 constant_dynamic-slice_fusion
  63.3 3.4 %collective-permute-start.23 = (bf16[224,3584]{1,0:T(8,128)(2,1)}, bf16[224,3584]{1,0:T(8,128)(2,1)}, u32[]{:S(2)}, u32[]{:S(2)}) collective-permute-start(bf16[224,3584]{1,0:T(8,128)(2,1)} %constant_dynamic-slice_fusion), channel_id=1, source_target_pairs={{0,16},{16,0},{1,17},{17,1},{2,18},{18,2},{3,19},{19,3},{4,20},{20... | collective-permute-start | bytes 4816904 | tf_op jit(solution)/shard_map/ppermute | solution.py:88
  71.1 10.0 %all-to-all-start.2 = ((bf16[128,3,224]{2,1,0:T(4,128)(2,1)}), bf16[128,3,224]{2,1,0:T(4,128)(2,1)S(1)}, u32[]{:S(2)}, u32[]{:S(2)}) async-start(bf16[128,3,224]{2,1,0:T(4,128)(2,1)} %copy.104), calls=%async_computation.2 | async-start | bytes 524288 | tf_op jit(solution)/shard_map/all_to_all | solution.py:161
  85.6 6.6 %all-to-all-done.2 = bf16[128,3,224]{2,1,0:T(4,128)(2,1)S(1)} async-done(((bf16[128,3,224]{2,1,0:T(4,128)(2,1)}), bf16[128,3,224]{2,1,0:T(4,128)(2,1)S(1)}, u32[]{:S(2)}, u32[]{:S(2)}) %all-to-all-start.2) | async-done | bytes 172064 | tf_op jit(solution)/shard_map/all_to_all | solution.py:161
  99.9 3.6 %all-to-all-start.3 = ((bf16[16,24,896]{2,1,0:T(8,128)(2,1)}), bf16[16,24,896]{2,1,0:T(8,128)(2,1)S(1)}, u32[]{:S(2)}, u32[]{:S(2)}) async-start(bf16[16,24,896]{2,1,0:T(8,128)(2,1)} %bitcast.28), calls=%async_computation.3 | async-start | bytes 1376256 | tf_op jit(solution)/shard_map/all_to_all | solution.py:161
  106.8 3.3 %dynamic-slice_bitcast_fusion = (bf16[1,224,896]{2,1,0:T(8,128)(2,1)}, bf16[1,224,896]{2,1,0:T(8,128)(2,1)}, bf16[1,224,896]{2,1,0:T(8,128)(2,1)}, bf16[1,224,89...) fusion(bf16[224,3584]{1,0:T(8,128)(2,1)} %collective-permute-do, ...), kind=kLoop, calls=%fused_computation.21 | loop fusion | bytes 6422544 | tf_op jit(solution)/shard_map/stack | solution.py:266
  113.0 2.9 collective-permute-start.10
  117.2 5.1 %all-to-all-start.4 = ((f32[8,8,128]{2,1,0:T(8,128)}), f32[8,8,128]{2,1,0:T(8,128)S(1)}, u32[]{:S(2)}, u32[]{:S(2)}) async-start(f32[8,8,128]{2,1,0:T(8,128)} %broadcast_in_dim.22), calls=%async_computation.4 | async-start | bytes 65536 | tf_op jit(solution)/shard_map/all_to_all | solution.py:155
  123.3 2.6 collective-permute-start.11
  125.9 25.0 %all-to-all-done.4 = f32[8,8,128]{2,1,0:T(8,128)S(1)} async-done(((f32[8,8,128]{2,1,0:T(8,128)}), f32[8,8,128]{2,1,0:T(8,128)S(1)}, u32[]{:S(2)}, u32[]{:S(2)}) %all-to-all-start.4) | async-done | bytes 32800 | tf_op jit(solution)/shard_map/all_to_all | solution.py:155
  152.0 6.6 %all-to-all-start.5 = ((bf16[16,24,896]{2,1,0:T(8,128)(2,1)}), bf16[16,24,896]{2,1,0:T(8,128)(2,1)S(1)}, u32[]{:S(2)}, u32[]{:S(2)}) async-start(bf16[16,24,896]{2,1,0:T(8,128)(2,1)} %broadcast_in_dim.23), calls=%async_computation.5 | async-start | bytes 1376256 | tf_op jit(solution)/shard_map/all_to_all | solution.py:155
  161.6 8.8 %all-to-all-done.5 = bf16[16,24,896]{2,1,0:T(8,128)(2,1)S(1)} async-done(((bf16[16,24,896]{2,1,0:T(8,128)(2,1)}), bf16[16,24,896]{2,1,0:T(8,128)(2,1)S(1)}, u32[]{:S(2)}, u32[]{:S(2)}) %all-to-all-start.5) | async-done | bytes 688160 | tf_op jit(solution)/shard_map/all_to_all | solution.py:155
  174.7 2.9 shard_map.167
  183.2 4.4 %all-to-all-start.8 = ((bf16[16,3,14336]{2,1,0:T(4,128)(2,1)}), bf16[16,3,14336]{2,1,0:T(4,128)(2,1)}, u32[]{:S(2)}, u32[]{:S(2)}) async-start(bf16[16,3,14336]{2,1,0:T(4,128)(2,1)} %broadcast_in_dim.24), calls=%async_computation.8 | async-start | bytes 3670016 | tf_op jit(solution)/shard_map/all_to_all | solution.py:155
  187.6 2.5 dynamic-slice_bitcast_fusion.1
  208.3 29.4 %collective-permute-done.15 = bf16[384,224]{1,0:T(8,128)(2,1)} collective-permute-done((bf16[384,224]{1,0:T(8,128)(2,1)}, bf16[384,224]{1,0:T(8,128)(2,1)}, u32[]{:S(2)}, u32[]{:S(2)}) %collective-permute-start.15) | collective-permute-done | bytes 172064 | tf_op jit(solution)/shard_map/ppermute | solution.py:92
  240.6 2.5 collective-permute-start.18
  244.8 5.4 %collective-permute-done.16.refs_1_ = bf16[384,224]{1,0:T(8,128)(2,1)S(1)} collective-permute-done((bf16[384,224]{1,0:T(8,128)(2,1)S(1)}, bf16[384,224]{1,0:T(8,128)(2,1)S(1)}, u32[]{:S(2)}, u32[]{:S(2)}) %collective-permute-start.16) | collective-permute-done | bytes 172064 | tf_op jit(solution)/shard_map/ppermute | solution.py:92
  251.8 13.2 %collective-permute-done.18.refs_3_ = bf16[384,224]{1,0:T(8,128)(2,1)S(1)} collective-permute-done((bf16[384,224]{1,0:T(8,128)(2,1)S(1)}, bf16[384,224]{1,0:T(8,128)(2,1)S(1)}, u32[]{:S(2)}, u32[]{:S(2)}) %collective-permute-start.18) | collective-permute-done | bytes 172064 | tf_op jit(solution)/shard_map/ppermute | solution.py:92
  267.8 2.6 shard_map.168
  270.5 6.2 %all-to-all-start.6 = ((bf16[16,24,896]{2,1,0:T(8,128)(2,1)}), bf16[16,24,896]{2,1,0:T(8,128)(2,1)S(1)}, u32[]{:S(2)}, u32[]{:S(2)}) async-start(bf16[16,24,896]{2,1,0:T(8,128)(2,1)} %bitcast.55), calls=%async_computation.6 | async-start | bytes 1376256 | tf_op jit(solution)/shard_map/all_to_all | solution.py:161
  276.9 2.4 reshape.236
  279.6 8.9 %all-to-all-done.6 = bf16[16,24,896]{2,1,0:T(8,128)(2,1)S(1)} async-done(((bf16[16,24,896]{2,1,0:T(8,128)(2,1)}), bf16[16,24,896]{2,1,0:T(8,128)(2,1)S(1)}, u32[]{:S(2)}, u32[]{:S(2)}) %all-to-all-start.6) | async-done | bytes 688160 | tf_op jit(solution)/shard_map/all_to_all | solution.py:161
  289.2 5.7 %all-to-all-start.7 = ((bf16[8,3,896]{2,1,0:T(4,128)(2,1)}), bf16[8,3,896]{2,1,0:T(4,128)(2,1)S(1)}, u32[]{:S(2)}, u32[]{:S(2)}) async-start(bf16[8,3,896]{2,1,0:T(4,128)(2,1)} %reshape.233), calls=%async_computation.7 | async-start | bytes 114688 | tf_op jit(solution)/shard_map/all_to_all | solution.py:161
  295.7 4.0 %all-to-all-done.7 = bf16[8,3,896]{2,1,0:T(4,128)(2,1)S(1)} async-done(((bf16[8,3,896]{2,1,0:T(4,128)(2,1)}), bf16[8,3,896]{2,1,0:T(4,128)(2,1)S(1)}, u32[]{:S(2)}, u32[]{:S(2)}) %all-to-all-start.7) | async-done | bytes 43040 | tf_op jit(solution)/shard_map/all_to_all | solution.py:161
  (201 shorter events, 77.9 us)
Async XLA Ops:
  2.7 21.6 %all-to-all-start = ((bf16[16,3,7168]{2,1,0:T(4,128)(2,1)}), bf16[16,3,7168]{2,1,0:T(4,128)(2,1)S(1)}, u32[]{:S(2)}, u32[]{:S(2)}) async-start(bf16[16,3,7168]{2,1,0:T(4,128)(2,1)} %broadcast_in_dim.18), calls=%async_computation | async-start | bytes 1835008 | tf_op jit(solution)/shard_map/all_to_all | solution.py:155
  49.2 18.6 %all-to-all-start.1 = ((bf16[16,3,8192]{2,1,0:T(4,128)(2,1)}), bf16[16,3,8192]{2,1,0:T(4,128)(2,1)S(1)}, u32[]{:S(2)}, u32[]{:S(2)}) async-start(bf16[16,3,8192]{2,1,0:T(4,128)(2,1)} %reshape.226), calls=%async_computation.1 | async-start | bytes 2097152 | tf_op jit(solution)/shard_map/all_to_all | solution.py:161
  54.7 28.8 %collective-permute-start.6 = (bf16[2,56,896]{2,1,0:T(8,128)(2,1)}, bf16[2,56,896]{2,1,0:T(8,128)(2,1)}, u32[]{:S(2)}, u32[]{:S(2)}) collective-permute-start(bf16[2,56,896]{2,1,0:T(8,128)(2,1)} %pad_maximum_fusion.11), channel_id=1, source_target_pairs={{0,96},{32,0},{64,32},{96,64},{1,97},{33,1},{65,33},{97,65},{2,98}... | collective-permute-start | bytes 602120 | tf_op jit(solution)/shard_map/ppermute | solution.py:92
  59.1 24.3 %collective-permute-start.5 = (bf16[2,56,896]{2,1,0:T(8,128)(2,1)}, bf16[2,56,896]{2,1,0:T(8,128)(2,1)}, u32[]{:S(2)}, u32[]{:S(2)}) collective-permute-start(bf16[2,56,896]{2,1,0:T(8,128)(2,1)} %pad_maximum_fusion.10), channel_id=1, source_target_pairs={{0,64},{32,96},{64,0},{96,32},{1,65},{33,97},{65,1},{97,33},{2,66}... | collective-permute-start | bytes 602120 | tf_op jit(solution)/shard_map/ppermute | solution.py:92
  59.9 23.6 %collective-permute-start.4 = (bf16[2,56,896]{2,1,0:T(8,128)(2,1)}, bf16[2,56,896]{2,1,0:T(8,128)(2,1)}, u32[]{:S(2)}, u32[]{:S(2)}) collective-permute-start(bf16[2,56,896]{2,1,0:T(8,128)(2,1)} %pad_maximum_fusion.9), channel_id=1, source_target_pairs={{0,32},{32,64},{64,96},{96,0},{1,33},{33,65},{65,97},{97,1},{2,34}... | collective-permute-start | bytes 602120 | tf_op jit(solution)/shard_map/ppermute | solution.py:92
  63.3 43.5 %collective-permute-start.23 = (bf16[224,3584]{1,0:T(8,128)(2,1)}, bf16[224,3584]{1,0:T(8,128)(2,1)}, u32[]{:S(2)}, u32[]{:S(2)}) collective-permute-start(bf16[224,3584]{1,0:T(8,128)(2,1)} %constant_dynamic-slice_fusion), channel_id=1, source_target_pairs={{0,16},{16,0},{1,17},{17,1},{2,18},{18,2},{3,19},{19,3},{4,20},{20... | collective-permute-start | bytes 4816904 | tf_op jit(solution)/shard_map/ppermute | solution.py:88
  71.1 21.1 %all-to-all-start.2 = ((bf16[128,3,224]{2,1,0:T(4,128)(2,1)}), bf16[128,3,224]{2,1,0:T(4,128)(2,1)S(1)}, u32[]{:S(2)}, u32[]{:S(2)}) async-start(bf16[128,3,224]{2,1,0:T(4,128)(2,1)} %copy.104), calls=%async_computation.2 | async-start | bytes 524288 | tf_op jit(solution)/shard_map/all_to_all | solution.py:161
  82.4 24.4 %collective-permute-start.8 = (bf16[224,3584]{1,0:T(8,128)(2,1)}, bf16[224,3584]{1,0:T(8,128)(2,1)}, u32[]{:S(2)}, u32[]{:S(2)}) collective-permute-start(bf16[224,3584]{1,0:T(8,128)(2,1)} %constant_dynamic-slice_fusion.1), channel_id=1, source_target_pairs={{0,16},{16,0},{1,17},{17,1},{2,18},{18,2},{3,19},{19,3},{4,20},{20... | collective-permute-start | bytes 4816904 | tf_op jit(solution)/shard_map/ppermute | solution.py:88
  99.9 16.1 %all-to-all-start.3 = ((bf16[16,24,896]{2,1,0:T(8,128)(2,1)}), bf16[16,24,896]{2,1,0:T(8,128)(2,1)S(1)}, u32[]{:S(2)}, u32[]{:S(2)}) async-start(bf16[16,24,896]{2,1,0:T(8,128)(2,1)} %bitcast.28), calls=%async_computation.3 | async-start | bytes 1376256 | tf_op jit(solution)/shard_map/all_to_all | solution.py:161
  104.4 11.7 %collective-permute-start.3 = (bf16[6,896]{1,0:T(8,128)(2,1)S(1)}, bf16[6,896]{1,0:T(8,128)(2,1)S(1)}, u32[]{:S(2)}, u32[]{:S(2)}) collective-permute-start(bf16[6,896]{1,0:T(8,128)(2,1)S(1)} %get-tuple-element.61), channel_id=1, source_target_pairs={{0,96},{32,0},{64,32},{96,64},{1,97},{33,1},{65,33},{97,65},{2,98}... | collective-permute-start | bytes 32264 | tf_op jit(solution)/shard_map/ppermute | solution.py:92
  105.1 11.0 %collective-permute-start.2 = (bf16[6,896]{1,0:T(8,128)(2,1)S(1)}, bf16[6,896]{1,0:T(8,128)(2,1)S(1)}, u32[]{:S(2)}, u32[]{:S(2)}) collective-permute-start(bf16[6,896]{1,0:T(8,128)(2,1)S(1)} %get-tuple-element.62), channel_id=1, source_target_pairs={{0,64},{32,96},{64,0},{96,32},{1,65},{33,97},{65,1},{97,33},{2,66}... | collective-permute-start | bytes 32264 | tf_op jit(solution)/shard_map/ppermute | solution.py:92
  111.1 48.7 %collective-permute-start.9 = (bf16[2,224,896]{2,1,0:T(8,128)(2,1)}, bf16[2,224,896]{2,1,0:T(8,128)(2,1)S(1)}, u32[]{:S(2)}, u32[]{:S(2)}) collective-permute-start(bf16[2,224,896]{2,1,0:T(8,128)(2,1)} %pad_maximum_fusion.2), channel_id=1, source_target_pairs={{0,32},{32,64},{64,96},{96,0},{1,33},{33,65},{65,97},{97,1},{2,34}... | collective-permute-start | bytes 2408456 | tf_op jit(solution)/shard_map/ppermute | solution.py:92
  113.0 47.7 %collective-permute-start.10 = (bf16[2,224,896]{2,1,0:T(8,128)(2,1)}, bf16[2,224,896]{2,1,0:T(8,128)(2,1)S(1)}, u32[]{:S(2)}, u32[]{:S(2)}) collective-permute-start(bf16[2,224,896]{2,1,0:T(8,128)(2,1)} %pad_maximum_fusion.3), channel_id=1, source_target_pairs={{0,64},{32,96},{64,0},{96,32},{1,65},{33,97},{65,1},{97,33},{2,66}... | collective-permute-start | bytes 2408456 | tf_op jit(solution)/shard_map/ppermute | solution.py:92
  117.2 33.7 %all-to-all-start.4 = ((f32[8,8,128]{2,1,0:T(8,128)}), f32[8,8,128]{2,1,0:T(8,128)S(1)}, u32[]{:S(2)}, u32[]{:S(2)}) async-start(f32[8,8,128]{2,1,0:T(8,128)} %broadcast_in_dim.22), calls=%async_computation.4 | async-start | bytes 65536 | tf_op jit(solution)/shard_map/all_to_all | solution.py:155
  123.3 38.4 %collective-permute-start.11 = (bf16[2,224,896]{2,1,0:T(8,128)(2,1)}, bf16[2,224,896]{2,1,0:T(8,128)(2,1)}, u32[]{:S(2)}, u32[]{:S(2)}) collective-permute-start(bf16[2,224,896]{2,1,0:T(8,128)(2,1)} %pad_maximum_fusion.4), channel_id=1, source_target_pairs={{0,96},{32,0},{64,32},{96,64},{1,97},{33,1},{65,33},{97,65},{2,98}... | collective-permute-start | bytes 2408456 | tf_op jit(solution)/shard_map/ppermute | solution.py:92
  152.0 18.4 %all-to-all-start.5 = ((bf16[16,24,896]{2,1,0:T(8,128)(2,1)}), bf16[16,24,896]{2,1,0:T(8,128)(2,1)S(1)}, u32[]{:S(2)}, u32[]{:S(2)}) async-start(bf16[16,24,896]{2,1,0:T(8,128)(2,1)} %broadcast_in_dim.23), calls=%async_computation.5 | async-start | bytes 1376256 | tf_op jit(solution)/shard_map/all_to_all | solution.py:155
  178.8 14.9 %collective-permute-start.12 = (bf16[4,384,224]{1,2,0:T(8,128)(2,1)}, bf16[4,384,224]{1,2,0:T(8,128)(2,1)}, u32[]{:S(2)}, u32[]{:S(2)}) collective-permute-start(bf16[4,384,224]{1,2,0:T(8,128)(2,1)} %copy.107), channel_id=1, source_target_pairs={{0,16},{16,0},{1,17},{17,1},{2,18},{18,2},{3,19},{19,3},{4,20},{20... | collective-permute-start | bytes 2064392 | tf_op jit(solution)/shard_map/ppermute | solution.py:88
  183.2 87.3 %all-to-all-start.8 = ((bf16[16,3,14336]{2,1,0:T(4,128)(2,1)}), bf16[16,3,14336]{2,1,0:T(4,128)(2,1)}, u32[]{:S(2)}, u32[]{:S(2)}) async-start(bf16[16,3,14336]{2,1,0:T(4,128)(2,1)} %broadcast_in_dim.24), calls=%async_computation.8 | async-start | bytes 3670016 | tf_op jit(solution)/shard_map/all_to_all | solution.py:155
  191.1 49.5 %collective-permute-start.24 = (bf16[2,224,896]{2,1,0:T(8,128)(2,1)}, bf16[2,224,896]{2,1,0:T(8,128)(2,1)S(1)}, u32[]{:S(2)}, u32[]{:S(2)}) collective-permute-start(bf16[2,224,896]{2,1,0:T(8,128)(2,1)} %pad_maximum_fusion.6), channel_id=1, source_target_pairs={{0,32},{32,64},{64,96},{96,0},{1,33},{33,65},{65,97},{97,1},{2,34}... | collective-permute-start | bytes 2408456 | tf_op jit(solution)/shard_map/ppermute | solution.py:92
  192.1 51.0 %collective-permute-start.25 = (bf16[2,224,896]{2,1,0:T(8,128)(2,1)}, bf16[2,224,896]{2,1,0:T(8,128)(2,1)S(1)}, u32[]{:S(2)}, u32[]{:S(2)}) collective-permute-start(bf16[2,224,896]{2,1,0:T(8,128)(2,1)} %pad_maximum_fusion.7), channel_id=1, source_target_pairs={{0,64},{32,96},{64,0},{96,32},{1,65},{33,97},{65,1},{97,33},{2,66}... | collective-permute-start | bytes 2408456 | tf_op jit(solution)/shard_map/ppermute | solution.py:92
  202.3 35.5 %collective-permute-start.15 = (bf16[384,224]{1,0:T(8,128)(2,1)}, bf16[384,224]{1,0:T(8,128)(2,1)}, u32[]{:S(2)}, u32[]{:S(2)}) collective-permute-start(bf16[384,224]{1,0:T(8,128)(2,1)} %get-tuple-element.36), channel_id=1, source_target_pairs={{0,32},{32,64},{64,96},{96,0},{1,33},{33,65},{65,97},{97,1},{2,34}... | collective-permute-start | bytes 516104 | tf_op jit(solution)/shard_map/ppermute | solution.py:92
  203.9 33.9 %collective-permute-start.14 = (bf16[384,224]{1,0:T(8,128)(2,1)}, bf16[384,224]{1,0:T(8,128)(2,1)}, u32[]{:S(2)}, u32[]{:S(2)}) collective-permute-start(bf16[384,224]{1,0:T(8,128)(2,1)} %get-tuple-element.37), channel_id=1, source_target_pairs={{0,64},{32,96},{64,0},{96,32},{1,65},{33,97},{65,1},{97,33},{2,66}... | collective-permute-start | bytes 516104 | tf_op jit(solution)/shard_map/ppermute | solution.py:92
  204.5 33.3 %collective-permute-start.13 = (bf16[384,224]{1,0:T(8,128)(2,1)}, bf16[384,224]{1,0:T(8,128)(2,1)}, u32[]{:S(2)}, u32[]{:S(2)}) collective-permute-start(bf16[384,224]{1,0:T(8,128)(2,1)} %get-tuple-element.35), channel_id=1, source_target_pairs={{0,96},{32,0},{64,32},{96,64},{1,97},{33,1},{65,33},{97,65},{2,98}... | collective-permute-start | bytes 516104 | tf_op jit(solution)/shard_map/ppermute | solution.py:92
  237.8 29.2 %collective-permute-start.26 = (bf16[2,224,896]{2,1,0:T(8,128)(2,1)}, bf16[2,224,896]{2,1,0:T(8,128)(2,1)S(1)}, u32[]{:S(2)}, u32[]{:S(2)}) collective-permute-start(bf16[2,224,896]{2,1,0:T(8,128)(2,1)} %pad_maximum_fusion.8), channel_id=1, source_target_pairs={{0,96},{32,0},{64,32},{96,64},{1,97},{33,1},{65,33},{97,65},{2,98}... | collective-permute-start | bytes 2408456 | tf_op jit(solution)/shard_map/ppermute | solution.py:92
  239.0 11.1 %collective-permute-start.16 = (bf16[384,224]{1,0:T(8,128)(2,1)S(1)}, bf16[384,224]{1,0:T(8,128)(2,1)S(1)}, u32[]{:S(2)}, u32[]{:S(2)}) collective-permute-start(bf16[384,224]{1,0:T(8,128)(2,1)S(1)} %fusion.5.refs_0_), channel_id=1, source_target_pairs={{0,32},{32,64},{64,96},{96,0},{1,33},{33,65},{65,97},{97,1},{2,34}... | collective-permute-start | bytes 516104 | tf_op jit(solution)/shard_map/ppermute | solution.py:92
  240.6 11.3 %collective-permute-start.17 = (bf16[384,224]{1,0:T(8,128)(2,1)S(1)}, bf16[384,224]{1,0:T(8,128)(2,1)S(1)}, u32[]{:S(2)}, u32[]{:S(2)}) collective-permute-start(bf16[384,224]{1,0:T(8,128)(2,1)S(1)} %fusion.5.refs_0_), channel_id=1, source_target_pairs={{0,64},{32,96},{64,0},{96,32},{1,65},{33,97},{65,1},{97,33},{2,66}... | collective-permute-start | bytes 516104 | tf_op jit(solution)/shard_map/ppermute | solution.py:92
  240.6 24.5 %collective-permute-start.18 = (bf16[384,224]{1,0:T(8,128)(2,1)S(1)}, bf16[384,224]{1,0:T(8,128)(2,1)S(1)}, u32[]{:S(2)}, u32[]{:S(2)}) collective-permute-start(bf16[384,224]{1,0:T(8,128)(2,1)S(1)} %fusion.5.refs_0_), channel_id=1, source_target_pairs={{0,96},{32,0},{64,32},{96,64},{1,97},{33,1},{65,33},{97,65},{2,98}... | collective-permute-start | bytes 516104 | tf_op jit(solution)/shard_map/ppermute | solution.py:92
  243.1 23.9 %collective-permute-start.19 = (bf16[384,224]{1,0:T(8,128)(2,1)S(1)}, bf16[384,224]{1,0:T(8,128)(2,1)S(1)}, u32[]{:S(2)}, u32[]{:S(2)}) collective-permute-start(bf16[384,224]{1,0:T(8,128)(2,1)S(1)} %fusion.5.refs_0_), channel_id=1, source_target_pairs={{0,16},{16,0},{1,17},{17,1},{2,18},{18,2},{3,19},{19,3},{4,20},{20... | collective-permute-start | bytes 516104 | tf_op jit(solution)/shard_map/ppermute | solution.py:88
  250.2 16.8 %collective-permute-start.20 = (bf16[384,224]{1,0:T(8,128)(2,1)S(1)}, bf16[384,224]{1,0:T(8,128)(2,1)S(1)}, u32[]{:S(2)}, u32[]{:S(2)}) collective-permute-start(bf16[384,224]{1,0:T(8,128)(2,1)S(1)} %collective-permute-done.16.refs_1_), channel_id=1, source_target_pairs={{0,16},{16,0},{1,17},{17,1},{2,18},{18,2},{3,19},{19,3},{4,20},{20... | collective-permute-start | bytes 516104 | tf_op jit(solution)/shard_map/ppermute | solution.py:88
  251.8 15.1 %collective-permute-start.21 = (bf16[384,224]{1,0:T(8,128)(2,1)S(1)}, bf16[384,224]{1,0:T(8,128)(2,1)S(1)}, u32[]{:S(2)}, u32[]{:S(2)}) collective-permute-start(bf16[384,224]{1,0:T(8,128)(2,1)S(1)} %collective-permute-done.17.refs_2_), channel_id=1, source_target_pairs={{0,16},{16,0},{1,17},{17,1},{2,18},{18,2},{3,19},{19,3},{4,20},{20... | collective-permute-start | bytes 516104 | tf_op jit(solution)/shard_map/ppermute | solution.py:88
  270.5 18.0 %all-to-all-start.6 = ((bf16[16,24,896]{2,1,0:T(8,128)(2,1)}), bf16[16,24,896]{2,1,0:T(8,128)(2,1)S(1)}, u32[]{:S(2)}, u32[]{:S(2)}) async-start(bf16[16,24,896]{2,1,0:T(8,128)(2,1)} %bitcast.55), calls=%async_computation.6 | async-start | bytes 1376256 | tf_op jit(solution)/shard_map/all_to_all | solution.py:161
  289.2 10.6 %all-to-all-start.7 = ((bf16[8,3,896]{2,1,0:T(4,128)(2,1)}), bf16[8,3,896]{2,1,0:T(4,128)(2,1)S(1)}, u32[]{:S(2)}, u32[]{:S(2)}) async-start(bf16[8,3,896]{2,1,0:T(4,128)(2,1)} %reshape.233), calls=%async_computation.7 | async-start | bytes 114688 | tf_op jit(solution)/shard_map/all_to_all | solution.py:161
  (34 other events, 359.0 us)

commit v3 on v2

--- a/solution.py
+++ b/solution.py
@@ -14,6 +14,7 @@
 ALL = ("z", "c", "x", "y")
 REQ = ("z", "c")
 MLP = ("x", "y")
+CHIPS = ("z", "x", "y")
 DN = (((1,), (1,)), ((), ()))
 
 
@@ -75,7 +76,7 @@
         ],
         out_specs=pl.BlockSpec((rows, wide + HD), col),
         out_shape=jax.ShapeDtypeStruct((rows, steps * (wide + HD)), BF16),
-        compiler_params=pltpu.CompilerParams(vmem_limit_bytes=40 * 1024 * 1024),
+        compiler_params=pltpu.CompilerParams(vmem_limit_bytes=58 * 1024 * 1024),
         cost_estimate=pl.CostEstimate(
             flops=4 * rows * pages * page_len * width,
             bytes_accessed=4 * pages * page_len * width,
@@ -96,59 +97,206 @@
     return lax.optimization_barrier((x, first))[0]
 
 
-def up_kernel(n, *refs):
-    g = refs[0][...]
-    for d in range(n):
-        for e in range(2):
-            w = lax.dot_general(g, refs[1 + d][e], DN, preferred_element_type=F32)
-            if e:
-                refs[n + 2][d] = w.astype(BF16)
-            else:
-                refs[n + 1][d] = w
-
-
-def up_project(normed, weights):
-    n = len(weights)
-    rows = normed.shape[0]
-    units = weights[0].shape[1]
+def gain_kernel(gain, own, other, out):
+    high = gain[...].astype(BF16).astype(F32)
+    row = lax.broadcasted_iota(jnp.int32, (8, gain.shape[1]), 0)
+    low = gain[...] - high
+    both = jnp.where(row == 0, high, jnp.where(row == 1, low, 0.0)).astype(BF16)
+    for e, w in enumerate((own, other)):
+        out[e] = lax.dot_general(both, w[...], DN, preferred_element_type=F32)
+
+
+def hidden_kernel(parts, res, gain, hidden_out, row_out):
+    hidden = res[...] + jnp.sum(parts[...].astype(F32), axis=0)
+    hidden_out[...] = hidden
+    rows, chunk = hidden.shape
+    mean = jnp.mean(hidden, axis=1, keepdims=True)
+    centered = hidden - mean
+    dev = jnp.sum(centered * centered, axis=1, keepdims=True)
+    row_out[:, :chunk] = (centered * gain[...]).astype(BF16)
+    lane = lax.broadcasted_iota(jnp.int32, (rows, HD), 1)
+    stats = jnp.zeros((rows, HD), F32)
+    at = 0
+    for value in (mean, dev):
+        for _ in range(3):
+            high = value.astype(BF16).astype(F32)
+            stats = jnp.where(lane == at, high, stats)
+            value = value - high
+            at += 1
+    row_out[:, chunk:] = stats.astype(BF16)
+
+
+def up_kernel(place, rows, own, other, gain_own, gain_other, mine, theirs, stats_out):
+    step = pl.program_id(0)
+    chunk = own.shape[1]
+    g = rows[0, :, :chunk]
+    st = rows[0, :, chunk:].astype(F32)
+    mean = st[:, 0:1] + st[:, 1:2] + st[:, 2:3]
+    dev = st[:, 3:4] + st[:, 4:5] + st[:, 5:6]
+    lane = lax.broadcasted_iota(jnp.int32, st.shape, 1)
+    stats = jnp.where(lane == step, mean, 0.0) + jnp.where(lane == 8, dev, 0.0)
+
+    @pl.when(step == 0)
+    def _():
+        mine[...] = jnp.zeros_like(mine)
+        theirs[...] = jnp.zeros_like(theirs)
+        stats_out[...] = jnp.zeros_like(stats_out)
+
+    stats_out[...] += stats
+    for w, gw, out in ((own, gain_own, mine), (other, gain_other, theirs)):
+        term = lax.dot_general(g, w[...], DN, preferred_element_type=F32)
+        out[...] += term + mean * (gw[0, 0:1, :] + gw[0, 1:2, :])
+
+
+def act_kernel(width, mine, theirs, stats, stats_pair, gain_own, gain_pair, out):
+    n = gain_own.shape[0]
+    a = stats[...]
+    b = stats_pair[...]
+    lane = lax.broadcasted_iota(jnp.int32, a.shape, 1)
+    chunk = width // (2 * n)
+    mean = (
+        jnp.sum(jnp.where(lane < n, a, 0.0), axis=1, keepdims=True)
+        + jnp.sum(jnp.where(lane < n, b, 0.0), axis=1, keepdims=True)
+    ) / (2 * n)
+
+    def spread_of(v):
+        part = jnp.where(lane < n, chunk * jnp.square(v - mean), jnp.where(lane == 8, v, 0.0))
+        return jnp.sum(part, axis=1, keepdims=True)
+
+    inv = lax.rsqrt((spread_of(a) + spread_of(b)) / width + 1e-05)
+    gw = jnp.zeros((1, out.shape[1]), F32)
+    for k in range(n):
+        for ref in (gain_own, gain_pair):
+            gw = gw + ref[k, 0:1, :] + ref[k, 1:2, :]
+    pre = inv * (mine[...] + theirs[...] - mean * gw)
+    out[...] = jnp.maximum(pre, 0.0).astype(BF16)
+
+
+def down_kernel(place, act, act_pair, own, other, out):
+    out[0] = (
+        jnp.dot(act[...], own[...], preferred_element_type=F32)
+        + jnp.dot(act_pair[...], other[...], preferred_element_type=F32)
+    ).astype(BF16)
+
+
+def finish_kernel(parts, hidden, out, total):
+    step = pl.program_id(0)
+
+    @pl.when(step == 0)
+    def _():
+        total[...] = hidden[...]
+
+    total[...] += jnp.sum(parts[...].astype(F32), axis=0)
+
+    @pl.when(step == pl.num_programs(0) - 1)
+    def _():
+        out[...] = total[...].astype(BF16)
+
+
+def params():
+    return pltpu.CompilerParams(vmem_limit_bytes=32 * 1024 * 1024)
+
+
+def own_spec(units, chunk, n):
+    return pl.BlockSpec((units, chunk), lambda i, place: (0, place[0] * n + i))
+
+
+def other_spec(units, chunk):
+    return pl.BlockSpec((units, chunk), lambda i, place: (0, i))
+
+
+def gain_products(place, gain, own, other, n, chunk):
+    units = own.shape[0]
+
+    def body(place, gain, own, other, out):
+        gain_kernel(gain, own, other, out.at[0])
+
     return pl.pallas_call(
-        lambda *refs: up_kernel(n, *refs),
+        body,
+        grid_spec=pltpu.PrefetchScalarGridSpec(
+            num_scalar_prefetch=1,
+            grid=(n,),
+            in_specs=[
+                pl.BlockSpec((1, chunk), lambda i, place: (0, place[0] * n + i)),
+                own_spec(units, chunk, n),
+                other_spec(units, chunk),
+            ],
+            out_specs=pl.BlockSpec((1, 2, 8, units), lambda i, place: (i, 0, 0, 0)),
+        ),
+        out_shape=jax.ShapeDtypeStruct((n, 2, 8, units), F32),
+        compiler_params=params(),
+    )(place, gain, own, other)
+
+
+def up_project(place, rows, own, other, gain_own, gain_other):
+    n, tokens, wide = rows.shape
+    units = own.shape[0]
+    chunk = wide - HD
+    fixed = lambda i, place: (0, 0)
+    turn = lambda i, place: (i, 0, 0)
+    return pl.pallas_call(
+        up_kernel,
+        grid_spec=pltpu.PrefetchScalarGridSpec(
+            num_scalar_prefetch=1,
+            grid=(n,),
+            in_specs=[
+                pl.BlockSpec((1, tokens, wide), turn),
+                own_spec(units, chunk, n),
+                other_spec(units, chunk),
+                pl.BlockSpec((1, 8, units), turn),
+                pl.BlockSpec((1, 8, units), turn),
+            ],
+            out_specs=[
+                pl.BlockSpec((tokens, units), fixed),
+                pl.BlockSpec((tokens, units), fixed),
+                pl.BlockSpec((tokens, HD), fixed),
+            ],
+        ),
         out_shape=(
-            jax.ShapeDtypeStruct((n, rows, units), F32),
-            jax.ShapeDtypeStruct((n, rows, units), BF16),
-        ),
-        compiler_params=pltpu.CompilerParams(vmem_limit_bytes=40 * 1024 * 1024),
-        cost_estimate=pl.CostEstimate(
-            flops=4 * n * rows * normed.shape[1] * units,
-            bytes_accessed=4 * n * normed.shape[1] * units,
-            transcendentals=0,
-        ),
-    )(normed, *weights)
-
-
-def down_kernel(n, *refs):
-    total = None
-    for d in range(n):
-        for e in range(2):
-            term = jnp.dot(refs[e * n + d][...], refs[2 * n + d][e], preferred_element_type=F32)
-            total = term if total is None else total + term
-    refs[3 * n][...] = total.astype(BF16)
-
-
-def down_project(own, other, weights):
-    n = len(weights)
-    rows, units = own[0].shape
-    width = weights[0].shape[2]
+            jax.ShapeDtypeStruct((tokens, units), F32),
+            jax.ShapeDtypeStruct((tokens, units), F32),
+            jax.ShapeDtypeStruct((tokens, HD), F32),
+        ),
+        compiler_params=params(),
+    )(place, rows, own, other, gain_own, gain_other)
+
+
+def down_project(place, act, act_pair, own, other, n, chunk):
+    tokens, units = act.shape
+    fixed = lambda i, place: (0, 0)
     return pl.pallas_call(
-        lambda *refs: down_kernel(n, *refs),
-        out_shape=jax.ShapeDtypeStruct((rows, width), BF16),
-        compiler_params=pltpu.CompilerParams(vmem_limit_bytes=40 * 1024 * 1024),
-        cost_estimate=pl.CostEstimate(
-            flops=4 * n * rows * width * units,
-            bytes_accessed=4 * n * width * units,
-            transcendentals=0,
-        ),
-    )(*own, *other, *weights)
+        down_kernel,
+        grid_spec=pltpu.PrefetchScalarGridSpec(
+            num_scalar_prefetch=1,
+            grid=(n,),
+            in_specs=[
+                pl.BlockSpec((tokens, units), fixed),
+                pl.BlockSpec((tokens, units), fixed),
+                own_spec(units, chunk, n),
+                other_spec(units, chunk),
+            ],
+            out_specs=pl.BlockSpec((1, tokens, chunk), lambda i, place: (i, 0, 0)),
+        ),
+        out_shape=jax.ShapeDtypeStruct((n, tokens, chunk), BF16),
+        compiler_params=params(),
+    )(place, act, act_pair, own, other)
+
+
+def finish(parts, hidden):
+    count, block, chunk = parts.shape
+    per = count // 4
+    return pl.pallas_call(
+        finish_kernel,
+        grid=(4,),
+        in_specs=[
+            pl.BlockSpec((per, block, chunk), lambda i: (i, 0, 0)),
+            pl.BlockSpec((block, chunk), lambda i: (0, 0)),
+        ],
+        out_specs=pl.BlockSpec((block, chunk), lambda i: (0, 0)),
+        out_shape=jax.ShapeDtypeStruct((block, chunk), BF16),
+        scratch_shapes=[pltpu.VMEM((block, chunk), F32)],
+        compiler_params=params(),
+    )(parts, hidden)
 
 
 def spread(x, axes, count):
@@ -239,6 +387,8 @@
         draft_mask,
     )
 
+    parts, both = lax.optimization_barrier((parts, both))
+
     res = after(resid, parts)
     res = jnp.stack(
         [
@@ -256,16 +406,14 @@
     order = at[:, None] == (source * rows_dev + at % rows_dev)[None, :]
     res = jnp.dot(order.astype(BF16), res, preferred_element_type=F32)
 
-    weights = []
-    for w in (w_up.T, w_down):
-        w = after(w, parts)
-        other = pair(lax.dynamic_slice_in_dim(w, (1 - c) * half, half, 1))
-        split = []
-        for d in range(zs):
-            at = ((z + d) % zs) * chunk
-            part = jnp.stack([piece(w, c, d), lax.dynamic_slice_in_dim(other, at, chunk, 1)])
-            split.append(shift(part, d, zs) if d else part)
-        weights.append(split)
+    place = c.reshape(1).astype(jnp.int32)
+    up_w = w_up.T
+    up_other = pair(lax.dynamic_slice_in_dim(after(up_w, parts), (1 - c) * half, half, 1))
+    down_other = pair(lax.dynamic_slice_in_dim(after(w_down, parts), (1 - c) * half, half, 1))
+    gw = gain_products(place, ln_gain[None], up_w, up_other, zs, chunk)
+    gain_own = gw[:, 0]
+    gain_other = gw[:, 1]
+    gain_pair = pair(gain_other)
 
     parts = exchange(parts.reshape(members, rows_dev, parts.shape[1]), MLP)
     parts = parts.reshape(members, rows_dev, heads // 7, 8, HD).astype(F32)
@@ -293,33 +441,26 @@
     sent = pair(jnp.dot(feats, wo_pair, preferred_element_type=F32).astype(BF16))
     part = jnp.dot(feats, wo_own, preferred_element_type=F32) + sent.astype(F32)
     part = exchange(part.astype(BF16).reshape(members, block, chunk), MLP)
-    hidden = res + jnp.sum(part.astype(F32), axis=0)
-
     gain = lax.dynamic_slice_in_dim(ln_gain, c * half + z * chunk, chunk, 0)
 
-    mean = jnp.mean(hidden, axis=1)
-    dev = jnp.sum(jnp.square(hidden - mean[:, None]), axis=1)
-    stat = jnp.stack([mean, dev])
-    stat = spread(jnp.pad(stat, ((0, 6), (0, 128 - block))), REQ, groups)[:, :2, :block]
-    row_mean = jnp.mean(stat[:, 0], axis=0)
-    spread_sum = jnp.sum(stat[:, 1] + chunk * jnp.square(stat[:, 0] - row_mean[None]), axis=0)
-    inv = lax.rsqrt(spread_sum / width + 1e-05)
-    normed = ((hidden - row_mean[:, None]) * inv[:, None] * gain[None, :]).astype(BF16)
-
-    rows = spread(normed, MLP, members).reshape(tokens, chunk)
-    mine, theirs = up_project(rows, weights[0])
-    theirs = pair(theirs)
-    act = None
-    for d in range(zs):
-        term = mine[d] + theirs[d].astype(F32)
-        if d:
-            term = shift(term.astype(BF16), -d, zs).astype(F32)
-        act = term if act is None else act + term
-    act = jnp.maximum(act, 0.0).astype(BF16)
-    acts = [shift(act, d, zs) if d else act for d in range(zs)]
-    down = down_project(acts, [pair(a) for a in acts], weights[1])
-    down = exchange(down.reshape(members, block, chunk), MLP)
-    mixed = (hidden + jnp.sum(down.astype(F32), axis=0)).astype(BF16)
+    hidden, row = pl.pallas_call(
+        hidden_kernel,
+        out_shape=(
+            jax.ShapeDtypeStruct((block, chunk), F32),
+            jax.ShapeDtypeStruct((block, chunk + HD), BF16),
+        ),
+        compiler_params=params(),
+    )(part, res, gain[None])
+    rows = spread(row, CHIPS, zs * members).reshape(zs, tokens, chunk + HD)
+    mine, theirs, stats = up_project(place, rows, up_w, up_other, gain_own, gain_other)
+    act = pl.pallas_call(
+        lambda *refs: act_kernel(width, *refs),
+        out_shape=jax.ShapeDtypeStruct(mine.shape, BF16),
+        compiler_params=params(),
+    )(mine, pair(theirs), stats, pair(stats), gain_own, gain_pair)
+    down = down_project(place, act, pair(act), w_down, down_other, zs, chunk)
+    down = exchange(down.reshape(zs * members, block, chunk), CHIPS)
+    mixed = finish(down, hidden)
     mixed = exchange(mixed.reshape(groups, rows_dev, chunk), REQ)
     mixed = mixed.reshape(zs, cs, rows_dev, chunk).transpose(2, 1, 0, 3).reshape(rows_dev, width)
 

time: 302 us -> 245 us (0.81)
  local copies, waits for them, and re-layouts: 49.4 us -> 21.7 us
  starting transfers between devices: 89 us -> 70.1 us
  other arithmetic: 18.4 us -> 2.49 us
  Pallas kernels: 23.3 us -> 31.1 us
    ppermute x18 -> x6, waiting for transfers between devices: 48.1 us -> 1.77 us  [shift(): return lax.ppermute(x, 'z', [(i, (i + step) % size) for i in range(size)])]
    all_to_all x5, waiting for transfers between devices: 20.6 us -> 63 us  [exchange(): return lax.all_to_all(x, axes, split_axis=0, concat_axis=0)]
    ppermute x18 -> x6, starting transfers between devices: 22.9 us -> 9 us  [shift(): return lax.ppermute(x, 'z', [(i, (i + step) % size) for i in range(size)])]
    unnamed x65 -> x35, local copies, waits for them, and re-layouts: 17.1 us -> 3.28 us
    another operation x9 -> x0, other arithmetic: 7.24 us -> none  [the longest x8 7.23 us: local(): jnp.stack([piece(w, c, d), lax.dynamic_slice_in_dim(other, at, chunk, 1)])]
    another operation x3 -> x0, local copies, waits for them, and re-layouts: 7.01 us -> none  [local(): jnp.stack([piece(w, c, d), lax.dynamic_slice_in_dim(other, at, chunk, 1)])]
    pallas_call x2 -> x6, Pallas kernels: 5.59 us -> 12.1 us  [the longest x1 5.44 us: up_project(): pl.pallas_call(up_kernel, grid_spec=pltpu.PrefetchScalarGridSpec(num_scal...]
    all_to_all x4 -> x3, starting transfers between devices: 23.7 us -> 18.1 us  [spread(): lax.all_to_all(jnp.broadcast_to(x[None], (count,) + x.shape), axes, split...]
  transfers between devices with their start and end apart: 36 -> 22, of which waited for: 11 -> 14; matrix products, arithmetic and copies ran while one was open for 18% -> 5% of each run, Pallas kernels for 1% -> 11%
where the time goes in v3:
time: 245 us; the launch traced here: 244 us
  waiting for transfers between devices  113 us (46%)
  starting transfers between devices  70.1 us (29%)
  Pallas kernels  31.1 us (13%)
  local copies, waits for them, and re-layouts  21.7 us (9%)
  matrix products  4.17 us (2%)
  other arithmetic  2.49 us (1%)
    all_to_all x5, waiting for transfers between devices, exchange(): return lax.all_to_all(x, axes, split_axis=0, concat_axis=0)  63 us
    all_to_all x3, waiting for transfers between devices, spread(): lax.all_to_all(jnp.broadcast_to(x[None], (count,) + x.shape), axes, split...  44.8 us
    all_to_all x5, starting transfers between devices, exchange(): return lax.all_to_all(x, axes, split_axis=0, concat_axis=0)  33.2 us
    pallas_call x1, Pallas kernels, attend(): pl.pallas_call(body, grid=(steps,), in_specs=[pl.BlockSpec((rows, wide),...  18.9 us
    all_to_all x3, starting transfers between devices, spread(): lax.all_to_all(jnp.broadcast_to(x[None], (count,) + x.shape), axes, split...  18.1 us
    ppermute x8, starting transfers between devices, pair(): return lax.ppermute(x, 'c', [(0, 1), (1, 0)])  9.76 us
    ppermute x6, starting transfers between devices, shift(): return lax.ppermute(x, 'z', [(i, (i + step) % size) for i in range(size)])  9 us
    broadcast_in_dim x3, local copies, waits for them, and re-layouts, spread(): jnp.broadcast_to(x[None], (count,) + x.shape)  6.1 us
  transfers between devices with their start and end apart: 22, of which 14 were waited for; matrix products, arithmetic and copies ran while one was open for 5% of the time, Pallas kernels for 11%

profile of v3, /device:TPU:1, one launch (start us, length us, event | category | flops | bytes accessed | tf_op | source)
XLA Modules:
  0.0 244.3 jit_solution(14189368354849716355)
XLA Ops:
  0.7 2.0 broadcast_in_dim.20
  2.7 7.6 %all-to-all-start = ((bf16[16,3,7168]{2,1,0:T(4,128)(2,1)}), bf16[16,3,7168]{2,1,0:T(4,128)(2,1)S(1)}, u32[]{:S(2)}, u32[]{:S(2)}) async-start(bf16[16,3,7168]{2,1,0:T(4,128)(2,1)} %broadcast_in_dim.20), calls=%async_computation | async-start | bytes 1835008 | tf_op jit(solution)/shard_map/all_to_all | solution.py:303
  10.4 14.0 %all-to-all-done = bf16[16,3,7168]{2,1,0:T(4,128)(2,1)S(1)} async-done(((bf16[16,3,7168]{2,1,0:T(4,128)(2,1)}), bf16[16,3,7168]{2,1,0:T(4,128)(2,1)S(1)}, u32[]{:S(2)}, u32[]{:S(2)}) %all-to-all-start) | async-done | bytes 688160 | tf_op jit(solution)/shard_map/all_to_all | solution.py:303
  25.6 2.0 broadcast_in_dim.24
  27.6 4.1 %all-to-all-start.1 = ((bf16[16,3,14336]{2,1,0:T(4,128)(2,1)}), bf16[16,3,14336]{2,1,0:T(4,128)(2,1)S(1)}, u32[]{:S(2)}, u32[]{:S(2)}) async-start(bf16[16,3,14336]{2,1,0:T(4,128)(2,1)} %broadcast_in_dim.24), calls=%async_computation.1 | async-start | bytes 3670016 | tf_op jit(solution)/shard_map/all_to_all | solution.py:303
  35.3 18.9 %shard_map.166 = bf16[48,8192]{1,0:T(8,128)(2,1)} custom-call(bf16[48,7168]{1,0:T(8,128)(2,1)} %reshape.191.refs_0_, bf16[24,16,7168]{2,1,0:T(8,128)(2,1)} %refs_1_.1, bf16[24,16,7168]{2,1,0:T(8,128)(2,1)} %refs_2_.1, bf16[8,7168]{1,0:T(8,128)(2,1)} %pad.7.refs_3_, bf16[8,7168]{1,0:T(8,128)(2,1)} %pad.8.refs_4_, f32[48,384]{1,0:T(8,128)} %bitcast.106, ...), custom_call_target="tpu_custom_call" | custom-call | flops 528482304 | bytes 11010048 | tf_op jit(solution)/shard_map/pallas_call | solution.py:65
  54.5 2.0 reshape.193
  57.9 6.4 %all-to-all-start.2 = ((bf16[16,3,8192]{2,1,0:T(4,128)(2,1)}), bf16[16,3,8192]{2,1,0:T(4,128)(2,1)S(1)}, u32[]{:S(2)}, u32[]{:S(2)}) async-start(bf16[16,3,8192]{2,1,0:T(4,128)(2,1)} %reshape.194), calls=%async_computation.2 | async-start | bytes 2097152 | tf_op jit(solution)/shard_map/all_to_all | solution.py:309
  64.5 1.7 collective-permute-start
  66.3 3.4 %collective-permute-start.1 = (bf16[2,56,896]{2,1,0:T(8,128)(2,1)S(1)}, bf16[2,56,896]{2,1,0:T(8,128)(2,1)S(1)}, u32[]{:S(2)}, u32[]{:S(2)}) collective-permute-start(bf16[2,56,896]{2,1,0:T(8,128)(2,1)S(1)} %pad_maximum_fusion.2), channel_id=1, source_target_pairs={{0,64},{32,96},{64,0},{96,32},{1,65},{33,97},{65,1},{97,33},{2,66}... | collective-permute-start | bytes 602120 | tf_op jit(solution)/shard_map/ppermute | solution.py:93
  70.5 8.1 %all-to-all-done.2 = bf16[16,3,8192]{2,1,0:T(4,128)(2,1)S(1)} async-done(((bf16[16,3,8192]{2,1,0:T(4,128)(2,1)}), bf16[16,3,8192]{2,1,0:T(4,128)(2,1)S(1)}, u32[]{:S(2)}, u32[]{:S(2)}) %all-to-all-start.2) | async-done | bytes 786464 | tf_op jit(solution)/shard_map/all_to_all | solution.py:309
  81.8 10.4 %all-to-all-start.3 = ((bf16[128,3,224]{2,1,0:T(4,128)(2,1)}), bf16[128,3,224]{2,1,0:T(4,128)(2,1)S(1)}, u32[]{:S(2)}, u32[]{:S(2)}) async-start(bf16[128,3,224]{2,1,0:T(4,128)(2,1)} %copy.79), calls=%async_computation.3 | async-start | bytes 524288 | tf_op jit(solution)/shard_map/all_to_all | solution.py:309
  92.3 11.0 %all-to-all-done.3 = bf16[128,3,224]{2,1,0:T(4,128)(2,1)S(1)} async-done(((bf16[128,3,224]{2,1,0:T(4,128)(2,1)}), bf16[128,3,224]{2,1,0:T(4,128)(2,1)S(1)}, u32[]{:S(2)}, u32[]{:S(2)}) %all-to-all-start.3) | async-done | bytes 172064 | tf_op jit(solution)/shard_map/all_to_all | solution.py:309
  105.1 1.6 collective-permute-done.3
  107.9 3.6 %all-to-all-start.4 = ((bf16[16,24,896]{2,1,0:T(8,128)(2,1)}), bf16[16,24,896]{2,1,0:T(8,128)(2,1)S(1)}, u32[]{:S(2)}, u32[]{:S(2)}) async-start(bf16[16,24,896]{2,1,0:T(8,128)(2,1)} %bitcast.27), calls=%async_computation.4 | async-start | bytes 1376256 | tf_op jit(solution)/shard_map/all_to_all | solution.py:309
  116.8 6.4 %all-to-all-done.4.parts = bf16[16,24,896]{2,1,0:T(8,128)(2,1)S(1)} async-done(((bf16[16,24,896]{2,1,0:T(8,128)(2,1)}), bf16[16,24,896]{2,1,0:T(8,128)(2,1)S(1)}, u32[]{:S(2)}, u32[]{:S(2)}) %all-to-all-start.4) | async-done | bytes 688160 | tf_op jit(solution)/shard_map/all_to_all | solution.py:309
  123.4 2.1 broadcast_in_dim.26
  125.5 6.4 %all-to-all-start.5 = ((bf16[64,24,1024]{2,1,0:T(8,128)(2,1)}), bf16[64,24,1024]{2,1,0:T(8,128)(2,1)}, u32[]{:S(2)}, u32[]{:S(2)}) async-start(bf16[64,24,1024]{2,1,0:T(8,128)(2,1)} %broadcast_in_dim.26), calls=%async_computation.5 | async-start | bytes 6291456 | tf_op jit(solution)/shard_map/all_to_all | solution.py:303
  132.1 2.2 collective-permute-start.8
  135.6 1.7 collective-permute-start.13
  137.3 1.7 shard_map.168
  139.1 30.6 %all-to-all-done.5 = bf16[64,24,1024]{2,1,0:T(8,128)(2,1)} async-done(((bf16[64,24,1024]{2,1,0:T(8,128)(2,1)}), bf16[64,24,1024]{2,1,0:T(8,128)(2,1)}, u32[]{:S(2)}, u32[]{:S(2)}) %all-to-all-start.5) | async-done | bytes 3145760 | tf_op jit(solution)/shard_map/all_to_all | solution.py:303
  169.6 1.4 copy-done.5
  171.1 5.4 %shard_map.169 = (f32[384,224]{1,0:T(8,128)S(1)}, f32[384,224]{1,0:T(8,128)S(1)}, f32[384,128]{1,0:T(8,128)S(1)}) custom-call(s32[1]{0:T(128)} %bitcast.place, bf16[4,384,1024]{2,1,0:T(8,128)(2,1)} %bitcast.30.rows, bf16[224,7168]{1,0:T(8,128)(2,1)S(1)} %bitcast.94, bf16[224,3584]{1,0:T(8,128)(2,1)S(1)} %copy-done.5, ...), custom_call_target="tpu_custom_call" | custom-call | tf_op jit(solution)/shard_map/pallas_call | solution.py:237
  176.5 3.9 %collective-permute-start.9 = (f32[384,224]{1,0:T(8,128)S(1)}, f32[384,224]{1,0:T(8,128)S(1)}, u32[]{:S(2)}, u32[]{:S(2)}) collective-permute-start(f32[384,224]{1,0:T(8,128)S(1)} %get-tuple-element.22), channel_id=1, source_target_pairs={{0,16},{16,0},{1,17},{17,1},{2,18},{18,2},{3,19},{19,3},{4,20},{20... | collective-permute-start | bytes 1032200 | tf_op jit(solution)/shard_map/ppermute | solution.py:89
  184.0 3.9 %shard_map.171 = bf16[4,384,896]{2,1,0:T(8,128)(2,1)S(1)} custom-call(s32[1]{0:T(128)} %bitcast.place, bf16[384,224]{1,0:T(8,128)(2,1)S(1)} %shard_map.170.act, bf16[384,224]{1,0:T(8,128)(2,1)S(1)} %collective-permute-done.12.act_pair, bf16[224,7168]{1,0:T(8,128)(2,1)S(1)} %copy-done.3, bf16[224,3584]{1,0:T(8,128)(2,1)} %collective-permute-done.13.other), custom_call_target="tpu_custom_call" | custom-call | tf_op jit(solution)/shard_map/pallas_call | solution.py:267
  187.9 1.5 copy-done.1
  189.5 7.1 %all-to-all-start.6 = ((bf16[64,24,896]{2,1,0:T(8,128)(2,1)}), bf16[64,24,896]{2,1,0:T(8,128)(2,1)S(1)}, u32[]{:S(2)}, u32[]{:S(2)}) async-start(bf16[64,24,896]{2,1,0:T(8,128)(2,1)} %bitcast.95), calls=%async_computation.6 | async-start | bytes 5505024 | tf_op jit(solution)/shard_map/all_to_all | solution.py:309
  196.8 1.6 convolution_convert_fusion
  198.5 33.5 %all-to-all-done.6.parts = bf16[64,24,896]{2,1,0:T(8,128)(2,1)S(1)} async-done(((bf16[64,24,896]{2,1,0:T(8,128)(2,1)}), bf16[64,24,896]{2,1,0:T(8,128)(2,1)S(1)}, u32[]{:S(2)}, u32[]{:S(2)}) %all-to-all-start.6) | async-done | bytes 2752544 | tf_op jit(solution)/shard_map/all_to_all | solution.py:309
  233.0 5.7 %all-to-all-start.7 = ((bf16[8,3,896]{2,1,0:T(4,128)(2,1)}), bf16[8,3,896]{2,1,0:T(4,128)(2,1)S(1)}, u32[]{:S(2)}, u32[]{:S(2)}) async-start(bf16[8,3,896]{2,1,0:T(4,128)(2,1)} %reshape.202), calls=%async_computation.7 | async-start | bytes 114688 | tf_op jit(solution)/shard_map/all_to_all | solution.py:309
  239.6 4.0 %all-to-all-done.7 = bf16[8,3,896]{2,1,0:T(4,128)(2,1)S(1)} async-done(((bf16[8,3,896]{2,1,0:T(4,128)(2,1)}), bf16[8,3,896]{2,1,0:T(4,128)(2,1)S(1)}, u32[]{:S(2)}, u32[]{:S(2)}) %all-to-all-start.7) | async-done | bytes 43040 | tf_op jit(solution)/shard_map/all_to_all | solution.py:309
  (121 shorter events, 27.0 us)
Async XLA Ops:
  0.6 9.6 %copy-start.9 = (bf16[3,7168]{1,0:T(4,128)(2,1)S(1)}, bf16[3,7168]{1,0:T(4,128)(2,1)}, u32[]{:S(2)}) copy-start(bf16[3,7168]{1,0:T(4,128)(2,1)} %param.16) | copy-start | bytes 129028
  0.6 9.6 %copy-start.10 = (bf16[3,7168]{1,0:T(4,128)(2,1)S(1)}, bf16[3,7168]{1,0:T(4,128)(2,1)}, u32[]{:S(2)}) copy-start(bf16[3,7168]{1,0:T(4,128)(2,1)} %param.17) | copy-start | bytes 129028
  2.7 21.6 %all-to-all-start = ((bf16[16,3,7168]{2,1,0:T(4,128)(2,1)}), bf16[16,3,7168]{2,1,0:T(4,128)(2,1)S(1)}, u32[]{:S(2)}, u32[]{:S(2)}) async-start(bf16[16,3,7168]{2,1,0:T(4,128)(2,1)} %broadcast_in_dim.20), calls=%async_computation | async-start | bytes 1835008 | tf_op jit(solution)/shard_map/all_to_all | solution.py:303
  27.6 6.0 %copy-start.15 = (s32[3]{0:T(128)S(1)}, s32[3]{0:T(128)}, u32[]{:S(2)}) copy-start(s32[3]{0:T(128)} %param.20) | copy-start | bytes 40
  27.6 26.9 %all-to-all-start.1 = ((bf16[16,3,14336]{2,1,0:T(4,128)(2,1)}), bf16[16,3,14336]{2,1,0:T(4,128)(2,1)S(1)}, u32[]{:S(2)}, u32[]{:S(2)}) async-start(bf16[16,3,14336]{2,1,0:T(4,128)(2,1)} %broadcast_in_dim.24), calls=%async_computation.1 | async-start | bytes 3670016 | tf_op jit(solution)/shard_map/all_to_all | solution.py:303
  56.6 7.8 %copy-start.8 = (bf16[56,7168]{1,0:T(8,128)(2,1)S(1)}, bf16[56,7168]{1,0:T(8,128)(2,1)}, u32[]{:S(2)}) copy-start(bf16[56,7168]{1,0:T(8,128)(2,1)} %param.26) | copy-start | bytes 2408452
  57.9 20.7 %all-to-all-start.2 = ((bf16[16,3,8192]{2,1,0:T(4,128)(2,1)}), bf16[16,3,8192]{2,1,0:T(4,128)(2,1)S(1)}, u32[]{:S(2)}, u32[]{:S(2)}) async-start(bf16[16,3,8192]{2,1,0:T(4,128)(2,1)} %reshape.194), calls=%async_computation.2 | async-start | bytes 2097152 | tf_op jit(solution)/shard_map/all_to_all | solution.py:309
  64.5 27.6 %collective-permute-start = (bf16[2,56,896]{2,1,0:T(8,128)(2,1)S(1)}, bf16[2,56,896]{2,1,0:T(8,128)(2,1)S(1)}, u32[]{:S(2)}, u32[]{:S(2)}) collective-permute-start(bf16[2,56,896]{2,1,0:T(8,128)(2,1)S(1)} %pad_maximum_fusion.1), channel_id=1, source_target_pairs={{0,32},{32,64},{64,96},{96,0},{1,33},{33,65},{65,97},{97,1},{2,34}... | collective-permute-start | bytes 602120 | tf_op jit(solution)/shard_map/ppermute | solution.py:93
  66.3 25.9 %collective-permute-start.1 = (bf16[2,56,896]{2,1,0:T(8,128)(2,1)S(1)}, bf16[2,56,896]{2,1,0:T(8,128)(2,1)S(1)}, u32[]{:S(2)}, u32[]{:S(2)}) collective-permute-start(bf16[2,56,896]{2,1,0:T(8,128)(2,1)S(1)} %pad_maximum_fusion.2), channel_id=1, source_target_pairs={{0,64},{32,96},{64,0},{96,32},{1,65},{33,97},{65,1},{97,33},{2,66}... | collective-permute-start | bytes 602120 | tf_op jit(solution)/shard_map/ppermute | solution.py:93
  69.7 22.5 %collective-permute-start.2 = (bf16[2,56,896]{2,1,0:T(8,128)(2,1)S(1)}, bf16[2,56,896]{2,1,0:T(8,128)(2,1)S(1)}, u32[]{:S(2)}, u32[]{:S(2)}) collective-permute-start(bf16[2,56,896]{2,1,0:T(8,128)(2,1)S(1)} %pad_maximum_fusion.3), channel_id=1, source_target_pairs={{0,96},{32,0},{64,32},{96,64},{1,97},{33,1},{65,33},{97,65},{2,98}... | collective-permute-start | bytes 602120 | tf_op jit(solution)/shard_map/ppermute | solution.py:93
  81.8 21.5 %all-to-all-start.3 = ((bf16[128,3,224]{2,1,0:T(4,128)(2,1)}), bf16[128,3,224]{2,1,0:T(4,128)(2,1)S(1)}, u32[]{:S(2)}, u32[]{:S(2)}) async-start(bf16[128,3,224]{2,1,0:T(4,128)(2,1)} %copy.79), calls=%async_computation.3 | async-start | bytes 524288 | tf_op jit(solution)/shard_map/all_to_all | solution.py:309
  92.2 12.7 %copy-start.11 = (bf16[3,7168]{1,0:T(4,128)(2,1)S(1)}, bf16[3,7168]{1,0:T(4,128)(2,1)}, u32[]{:S(2)}) copy-start(bf16[3,7168]{1,0:T(4,128)(2,1)} %param.18) | copy-start | bytes 129028
  104.0 2.6 %collective-permute-start.3 = (bf16[384,896]{1,0:T(8,128)(2,1)S(1)}, bf16[384,896]{1,0:T(8,128)(2,1)S(1)}, u32[]{:S(2)}, u32[]{:S(2)}) collective-permute-start(bf16[384,896]{1,0:T(8,128)(2,1)S(1)} %convolution_convert_fusion.1), channel_id=1, source_target_pairs={{0,16},{16,0},{1,17},{17,1},{2,18},{18,2},{3,19},{19,3},{4,20},{20... | collective-permute-start | bytes 2064392 | tf_op jit(solution)/shard_map/ppermute | solution.py:89
  104.9 9.8 %copy-start.6 = (f32[7168]{0:T(1024)S(1)}, f32[7168]{0:T(1024)}, u32[]{:S(2)}) copy-start(f32[7168]{0:T(1024)} %param.29) | copy-start | bytes 86020
  104.9 6.6 %collective-permute-start.4 = (bf16[3,3584]{1,0:T(4,128)(2,1)S(1)}, bf16[3,3584]{1,0:T(4,128)(2,1)S(1)}, u32[]{:S(2)}, u32[]{:S(2)}) collective-permute-start(bf16[3,3584]{1,0:T(4,128)(2,1)S(1)} %get-tuple-element.54), channel_id=1, source_target_pairs={{0,16},{16,0},{1,17},{17,1},{2,18},{18,2},{3,19},{19,3},{4,20},{20... | collective-permute-start | bytes 64520 | tf_op jit(solution)/shard_map/ppermute | solution.py:89
  107.9 15.3 %all-to-all-start.4 = ((bf16[16,24,896]{2,1,0:T(8,128)(2,1)}), bf16[16,24,896]{2,1,0:T(8,128)(2,1)S(1)}, u32[]{:S(2)}, u32[]{:S(2)}) async-start(bf16[16,24,896]{2,1,0:T(8,128)(2,1)} %bitcast.27), calls=%async_computation.4 | async-start | bytes 1376256 | tf_op jit(solution)/shard_map/all_to_all | solution.py:309
  111.6 3.8 %collective-permute-start.5 = (bf16[6,896]{1,0:T(8,128)(2,1)S(1)}, bf16[6,896]{1,0:T(8,128)(2,1)S(1)}, u32[]{:S(2)}, u32[]{:S(2)}) collective-permute-start(bf16[6,896]{1,0:T(8,128)(2,1)S(1)} %get-tuple-element.52), channel_id=1, source_target_pairs={{0,32},{32,64},{64,96},{96,0},{1,33},{33,65},{65,97},{97,1},{2,34}... | collective-permute-start | bytes 32264 | tf_op jit(solution)/shard_map/ppermute | solution.py:93
  112.2 4.4 %collective-permute-start.6 = (bf16[6,896]{1,0:T(8,128)(2,1)S(1)}, bf16[6,896]{1,0:T(8,128)(2,1)S(1)}, u32[]{:S(2)}, u32[]{:S(2)}) collective-permute-start(bf16[6,896]{1,0:T(8,128)(2,1)S(1)} %get-tuple-element.51), channel_id=1, source_target_pairs={{0,64},{32,96},{64,0},{96,32},{1,65},{33,97},{65,1},{97,33},{2,66}... | collective-permute-start | bytes 32264 | tf_op jit(solution)/shard_map/ppermute | solution.py:93
  113.5 3.1 %collective-permute-start.7 = (bf16[6,896]{1,0:T(8,128)(2,1)S(1)}, bf16[6,896]{1,0:T(8,128)(2,1)S(1)}, u32[]{:S(2)}, u32[]{:S(2)}) collective-permute-start(bf16[6,896]{1,0:T(8,128)(2,1)S(1)} %get-tuple-element.50), channel_id=1, source_target_pairs={{0,96},{32,0},{64,32},{96,64},{1,97},{33,1},{65,33},{97,65},{2,98}... | collective-permute-start | bytes 32264 | tf_op jit(solution)/shard_map/ppermute | solution.py:93
  125.5 6.4 %copy-start = (bf16[7168,224]{0,1:T(8,128)(2,1)S(1)}, bf16[7168,224]{0,1:T(8,128)(2,1)}, u32[]{:S(2)}) copy-start(bf16[7168,224]{0,1:T(8,128)(2,1)} %param.27) | copy-start | bytes 9633796
  125.5 44.1 %all-to-all-start.5 = ((bf16[64,24,1024]{2,1,0:T(8,128)(2,1)}), bf16[64,24,1024]{2,1,0:T(8,128)(2,1)}, u32[]{:S(2)}, u32[]{:S(2)}) async-start(bf16[64,24,1024]{2,1,0:T(8,128)(2,1)} %broadcast_in_dim.26), calls=%async_computation.5 | async-start | bytes 6291456 | tf_op jit(solution)/shard_map/all_to_all | solution.py:303
  132.1 5.3 %collective-permute-start.8 = (bf16[224,3584]{1,0:T(8,128)(2,1)S(1)}, bf16[224,3584]{1,0:T(8,128)(2,1)S(1)}, u32[]{:S(2)}, u32[]{:S(2)}) collective-permute-start(bf16[224,3584]{1,0:T(8,128)(2,1)S(1)} %constant_dynamic-slice_fusion.1), channel_id=1, source_target_pairs={{0,16},{16,0},{1,17},{17,1},{2,18},{18,2},{3,19},{19,3},{4,20},{20... | collective-permute-start | bytes 4816904 | tf_op jit(solution)/shard_map/ppermute | solution.py:89
  135.6 47.4 %collective-permute-start.13 = (bf16[224,3584]{1,0:T(8,128)(2,1)}, bf16[224,3584]{1,0:T(8,128)(2,1)}, u32[]{:S(2)}, u32[]{:S(2)}) collective-permute-start(bf16[224,3584]{1,0:T(8,128)(2,1)} %constant_dynamic-slice_fusion), channel_id=1, source_target_pairs={{0,16},{16,0},{1,17},{17,1},{2,18},{18,2},{3,19},{19,3},{4,20},{20... | collective-permute-start | bytes 4816904 | tf_op jit(solution)/shard_map/ppermute | solution.py:89
  171.1 13.0 %copy-start.3 = (bf16[224,7168]{1,0:T(8,128)(2,1)S(1)}, bf16[224,7168]{1,0:T(8,128)(2,1)}, u32[]{:S(2)}) copy-start(bf16[224,7168]{1,0:T(8,128)(2,1)} %own.1) | copy-start | bytes 9633796
  176.5 5.6 %collective-permute-start.9 = (f32[384,224]{1,0:T(8,128)S(1)}, f32[384,224]{1,0:T(8,128)S(1)}, u32[]{:S(2)}, u32[]{:S(2)}) collective-permute-start(f32[384,224]{1,0:T(8,128)S(1)} %get-tuple-element.22), channel_id=1, source_target_pairs={{0,16},{16,0},{1,17},{17,1},{2,18},{18,2},{3,19},{19,3},{4,20},{20... | collective-permute-start | bytes 1032200 | tf_op jit(solution)/shard_map/ppermute | solution.py:89
  180.4 1.7 collective-permute-start.10
  180.5 1.6 collective-permute-start.11
  182.5 1.5 collective-permute-start.12
  189.4 7.1 %copy-start.16 = (s32[3]{0:T(128)S(1)}, s32[3]{0:T(128)}, u32[]{:S(2)}) copy-start(s32[3]{0:T(128)} %param.22) | copy-start | bytes 40
  189.4 7.1 %copy-start.13 = (s32[3,16]{1,0:T(4,128)S(1)}, s32[3,16]{1,0:T(4,128)}, u32[]{:S(2)}) copy-start(s32[3,16]{1,0:T(4,128)} %param.21) | copy-start | bytes 580
  189.5 42.5 %all-to-all-start.6 = ((bf16[64,24,896]{2,1,0:T(8,128)(2,1)}), bf16[64,24,896]{2,1,0:T(8,128)(2,1)S(1)}, u32[]{:S(2)}, u32[]{:S(2)}) async-start(bf16[64,24,896]{2,1,0:T(8,128)(2,1)} %bitcast.95), calls=%async_computation.6 | async-start | bytes 5505024 | tf_op jit(solution)/shard_map/all_to_all | solution.py:309
  233.0 10.6 %all-to-all-start.7 = ((bf16[8,3,896]{2,1,0:T(4,128)(2,1)}), bf16[8,3,896]{2,1,0:T(4,128)(2,1)S(1)}, u32[]{:S(2)}, u32[]{:S(2)}) async-start(bf16[8,3,896]{2,1,0:T(4,128)(2,1)} %reshape.202), calls=%async_computation.7 | async-start | bytes 114688 | tf_op jit(solution)/shard_map/all_to_all | solution.py:309
  (7 other events, 20.7 us)

commit v4 on v3

--- a/solution.py
+++ b/solution.py
@@ -11,53 +11,54 @@
 NEG = -(2.0**100)
 F32 = jnp.float32
 BF16 = jnp.bfloat16
-ALL = ("z", "c", "x", "y")
+ALL = ("z", "c", "x", "u", "v")
 REQ = ("z", "c")
-MLP = ("x", "y")
-CHIPS = ("z", "x", "y")
+MLP = ("x", "u", "v")
+HEADS = ("x", "u")
+CHIPS = ("z", "x", "u", "v")
 DN = (((1,), (1,)), ((), ()))
 
 
-def attend_kernel(heads, scaling, q, k, v, dk, dv, pool_mask, draft_mask, out):
-    pm = pool_mask[...]
-    dm = draft_mask[...]
+def attend_kernel(heads, scaling, q, k, v, dk, dv, mask, out):
     rows = q.shape[0]
     keys = k.shape[0] * k.shape[1]
-    kk = k[...].reshape(keys, k.shape[2])
-    vv = v[...].reshape(keys, v.shape[2])
+    kk = jnp.concatenate([k[...].reshape(keys, k.shape[2]), dk[...]], axis=0)
+    vv = jnp.concatenate([v[...].reshape(keys, v.shape[2]), dv[...]], axis=0)
+    m = mask[...]
+    span = [slice(h * HD, (h + 1) * HD) for h in range(heads)]
+    scores = [
+        jnp.where(
+            m > 0,
+            lax.dot_general(q[:, cols], kk[:, cols], DN, preferred_element_type=F32) * scaling,
+            NEG,
+        )
+        for cols in span
+    ]
+    tops = [jnp.max(s, axis=1, keepdims=True).astype(BF16).astype(F32) for s in scores]
+    weights = [jnp.exp(s - top) * m for s, top in zip(scores, tops)]
+    totals = [jnp.sum(p, axis=1, keepdims=True) for p in weights]
+    half = out.shape[1]
     lane = lax.broadcasted_iota(jnp.int32, (rows, HD), 1)
     stats = jnp.zeros((rows, HD), F32)
-    for h in range(heads):
-        cols = slice(h * HD, (h + 1) * HD)
-        qh = q[:, cols]
-        s = lax.dot_general(qh, kk[:, cols], DN, preferred_element_type=F32) * scaling
-        sd = lax.dot_general(qh, dk[:, cols], DN, preferred_element_type=F32) * scaling
-        s = jnp.where(pm > 0, s, NEG)
-        sd = jnp.where(dm > 0, sd, NEG)
-        top = jnp.maximum(jnp.max(s, axis=1, keepdims=True), jnp.max(sd, axis=1, keepdims=True))
-        top = top.astype(BF16).astype(F32)
-        p = jnp.exp(s - top) * pm
-        pd = jnp.exp(sd - top) * dm
-        total = jnp.sum(p, axis=1, keepdims=True) + jnp.sum(pd, axis=1, keepdims=True)
-        high = total.astype(BF16).astype(F32)
-        stats = jnp.where(lane == h, top, stats)
+    for h, cols in enumerate(span):
+        w = jnp.dot(weights[h].astype(BF16), vv[:, cols], preferred_element_type=F32)
+        for i in range(rows // half):
+            out[i, :, cols] = w[i * half : (i + 1) * half].astype(BF16)
+        high = totals[h].astype(BF16).astype(F32)
+        stats = jnp.where(lane == h, tops[h], stats)
         stats = jnp.where(lane == 8 + h, high, stats)
-        stats = jnp.where(lane == 16 + h, total - high, stats)
-        w = jnp.dot(p.astype(BF16), vv[:, cols], preferred_element_type=F32)
-        w = w + jnp.dot(pd.astype(BF16), dv[:, cols], preferred_element_type=F32)
-        out[:, cols] = w.astype(BF16)
-    out[:, heads * HD :] = stats.astype(BF16)
-
-
-def attend(q, key_cache, value_cache, dk, dv, pool_mask, draft_mask):
+        stats = jnp.where(lane == 16 + h, totals[h] - high, stats)
+    for i in range(rows // half):
+        out[i, :, heads * HD :] = stats[i * half : (i + 1) * half].astype(BF16)
+
+
+def attend(q, key_cache, value_cache, dk, dv, mask, steps, split):
     rows, width = q.shape
     pages, page_len, _ = key_cache.shape
-    heads = 7
-    steps = width // (heads * HD)
-    wide = heads * HD
+    wide = width // steps
+    heads = wide // HD
     col = lambda i: (0, i)
     col3 = lambda i: (0, 0, i)
-    fixed = lambda i: (0, 0)
 
     def body(*refs):
         attend_kernel(heads, 1.0 / math.sqrt(HD), *refs)
@@ -71,26 +72,44 @@
             pl.BlockSpec((pages, page_len, wide), col3),
             pl.BlockSpec((dk.shape[0], wide), col),
             pl.BlockSpec((dv.shape[0], wide), col),
-            pl.BlockSpec(pool_mask.shape, fixed),
-            pl.BlockSpec(draft_mask.shape, fixed),
+            pl.BlockSpec(mask.shape, lambda i: (0, 0)),
         ],
-        out_specs=pl.BlockSpec((rows, wide + HD), col),
-        out_shape=jax.ShapeDtypeStruct((rows, steps * (wide + HD)), BF16),
+        out_specs=pl.BlockSpec((split, rows // split, wide + HD), lambda i: (i, 0, 0)),
+        out_shape=jax.ShapeDtypeStruct((steps * split, rows // split, wide + HD), BF16),
         compiler_params=pltpu.CompilerParams(vmem_limit_bytes=58 * 1024 * 1024),
         cost_estimate=pl.CostEstimate(
             flops=4 * rows * pages * page_len * width,
             bytes_accessed=4 * pages * page_len * width,
             transcendentals=rows * pages * page_len * width // HD,
         ),
-    )(q, key_cache, value_cache, dk, dv, pool_mask, draft_mask)
+    )(q, key_cache, value_cache, dk, dv, mask)
+
+
+def combine_kernel(heads, parts, out):
+    count, rows, _ = parts.shape
+    st = parts[:, :, heads * HD :].astype(F32).reshape(count * rows, HD)
+    sums = pltpu.roll(st, HD - 8, 1) + pltpu.roll(st, HD - 16, 1)
+    st = st.reshape(count, rows, HD)
+    scale = jnp.exp(st - jnp.max(st, axis=0, keepdims=True))
+    total = jnp.sum(scale * sums.reshape(count, rows, HD), axis=0)
+    for h in range(heads):
+        cols = slice(h * HD, (h + 1) * HD)
+        acc = jnp.zeros((rows, HD), F32)
+        for i in range(count):
+            acc = acc + scale[i, :, h : h + 1] * parts[i, :, cols].astype(F32)
+        out[:, cols] = (acc / total[:, h : h + 1]).astype(BF16)
 
 
 def pair(x):
     return lax.ppermute(x, "c", [(0, 1), (1, 0)])
 
 
-def shift(x, step, size):
-    return lax.ppermute(x, "z", [(i, (i + step) % size) for i in range(size)])
+def shift(x, step, size, axes="z"):
+    return lax.ppermute(x, axes, [(i, (i + step) % size) for i in range(size)])
+
+
+def move(x, count, to):
+    return lax.ppermute(x, ALL, [(i, to(i)) for i in range(count)])
 
 
 def after(x, first):
@@ -326,11 +345,14 @@
     w_down,
     ln_gain,
 ):
-    zs, cs, xs, ys = (lax.axis_size(a) for a in ALL)
+    zs, cs, xs, us, vs = (lax.axis_size(a) for a in ALL)
+    ys = us * vs
     members = xs * ys
     groups = zs * cs
+    hosts = xs * us
     z = lax.axis_index("z")
     c = lax.axis_index("c")
+    v = lax.axis_index("v")
     member = lax.axis_index(MLP)
     rows_dev, width = queries.shape
     requests, tree_len = tree_mask.shape[:2]
@@ -342,27 +364,55 @@
     chunk = half // zs
     block = tokens // members
 
-    group_q = spread(queries, MLP, members).reshape(group_rows, width)
-
-    def piece(w, core, d):
-        return lax.dynamic_slice_in_dim(w, core * half + ((z + d) % zs) * chunk, chunk, 1)
+    wide_q = jnp.broadcast_to(queries[None], (members,) + queries.shape)
+    group_q = exchange(wide_q, MLP).reshape(group_rows, width)
+
+    def piece(w, d):
+        return lax.dynamic_slice_in_dim(w, ((z + d) % zs) * chunk, chunk, w.ndim - 1)
+
+    def regroup(x):
+        x = jnp.stack(
+            [
+                lax.dynamic_slice_in_dim(x, c * half, half, 1),
+                pair(lax.dynamic_slice_in_dim(x, (1 - c) * half, half, 1)),
+            ]
+        )
+        got = [shift(piece(x, d), d, zs) if d else piece(x, 0) for d in range(zs)]
+        got = jnp.concatenate(got)
+        at = [((z - k // cs) % zs) * cs + (c + k) % cs for k in range(groups)]
+        return jnp.stack([lax.dynamic_index_in_dim(got, i, 0, keepdims=False) for i in at])
 
     k_dev = w_out.shape[0]
-    wo = after(w_out, group_q)
-    wo_parts = []
-    for d in range(zs):
-        part = jnp.stack([piece(wo, c, d), piece(wo, 1 - c, d)])
-        wo_parts.append(shift(part, d, zs) if d else part)
-    wo_parts = jnp.concatenate(wo_parts, axis=1)
-
-    both = spread(
-        after(jnp.concatenate([keys_new, values_new], axis=1), group_q), MLP, members
-    ).reshape(group_rows, 2 * width)
+    lanes = groups * members
+
+    def to_host(i):
+        r, a, b = i // members, i % members // vs, i % vs
+        return a * members + r * vs + b
+
+    def to_other(i):
+        return to_host(i) // vs * vs + (vs - 1 - i % vs)
+
+    wo = after(w_out, wide_q)
+    wo_same, wo_other = move(wo, lanes, to_host), move(wo, lanes, to_other)
+
+    def to_block(i):
+        r, s, k = i // members, i % members // groups, i % groups
+        return k * members + r * vs + s
+
+    def from_block(i):
+        k, r, s = i // members, i % members // vs, i % vs
+        return r * members + s * groups + k
+
+    res = regroup(move(after(resid, wide_q), lanes, to_block)).reshape(block, chunk)
+    res = res.astype(F32)
+
+    both = after(jnp.concatenate([keys_new, values_new], axis=1), wide_q)
+    both = jnp.stack([shift(both, d, xs, "x") if d else both for d in range(xs)])
 
     page_ids = member * pages_dev + jnp.arange(pages_dev, dtype=jnp.int32)
     owners = jnp.any(page_table[:, :, None] == page_ids[None, None, :], axis=1)
     pool_mask = jnp.repeat(jnp.repeat(owners, page_len, axis=1), tree_len, axis=0).astype(F32)
-    draft_pad = 8
+    draft_pad = 16
     slot_ids = member * rows_dev + jnp.arange(draft_pad, dtype=jnp.int32)
     row_ids = jnp.arange(group_rows, dtype=jnp.int32)
     tree_cols = jnp.tile(tree_mask.reshape(group_rows, tree_len), (1, requests))
@@ -383,28 +433,18 @@
         value_cache,
         jnp.pad(keys_new, pad),
         jnp.pad(values_new, pad),
-        pool_mask,
-        draft_mask,
+        jnp.concatenate([pool_mask, draft_mask], axis=1),
+        hosts,
+        vs,
     )
 
-    parts, both = lax.optimization_barrier((parts, both))
-
-    res = after(resid, parts)
-    res = jnp.stack(
-        [
-            lax.dynamic_slice_in_dim(res, c * half, half, 1),
-            pair(lax.dynamic_slice_in_dim(res, (1 - c) * half, half, 1)),
-        ]
-    ).reshape(cs * rows_dev, half)
-    res_parts = []
-    for d in range(zs):
-        part = lax.dynamic_slice_in_dim(res, ((z + d) % zs) * chunk, chunk, 1)
-        res_parts.append(shift(part, d, zs) if d else part)
-    res = jnp.concatenate(res_parts, axis=0)
-    at = jnp.arange(block, dtype=jnp.int32)
-    source = ((z - at // (cs * rows_dev)) % zs) * cs + (c + at // rows_dev) % cs
-    order = at[:, None] == (source * rows_dev + at % rows_dev)[None, :]
-    res = jnp.dot(order.astype(BF16), res, preferred_element_type=F32)
+    parts, wo_same, wo_other, res, both = lax.optimization_barrier(
+        (parts, wo_same, wo_other, res, both)
+    )
+    wo = jnp.where(v == 0, jnp.stack([wo_same, wo_other]), jnp.stack([wo_other, wo_same]))
+    wo = regroup(wo.reshape(vs * k_dev, width)).reshape(groups * vs * k_dev, chunk)
+
+    both = jnp.stack([shift(both, d, ys, ("u", "v")) if d else both for d in range(ys)])
 
     place = c.reshape(1).astype(jnp.int32)
     up_w = w_up.T
@@ -415,32 +455,16 @@
     gain_other = gw[:, 1]
     gain_pair = pair(gain_other)
 
-    parts = exchange(parts.reshape(members, rows_dev, parts.shape[1]), MLP)
-    parts = parts.reshape(members, rows_dev, heads // 7, 8, HD).astype(F32)
-    st = parts[:, :, :, 7]
-    tops, highs, lows = st[..., 0:7], st[..., 8:15], st[..., 16:23]
-    scale = jnp.exp(tops - jnp.max(tops, axis=0, keepdims=True))
-    total = jnp.sum(scale * (highs + lows), axis=0)
-    weighted = jnp.sum(scale[..., None] * parts[:, :, :, :7], axis=0)
-    attended = (weighted / total[..., None]).astype(BF16).reshape(rows_dev, width)
-
-    feats = attended.reshape(rows_dev, zs, cs, members, k_dev).transpose(1, 2, 3, 0, 4)
-    feats = jnp.stack(
-        [
-            jnp.concatenate([feats[(to - d) % zs] for d in range(zs)], axis=3)
-            for to in range(zs)
-        ]
-    ).reshape(groups * members, rows_dev, zs * k_dev)
-    feats = exchange(feats, ALL)
-    feats = (
-        feats.reshape(groups, members, rows_dev, zs * k_dev)
-        .transpose(1, 0, 2, 3)
-        .reshape(tokens, zs * k_dev)
-    )
-    wo_own, wo_pair = wo_parts[0], wo_parts[1]
-    sent = pair(jnp.dot(feats, wo_pair, preferred_element_type=F32).astype(BF16))
-    part = jnp.dot(feats, wo_own, preferred_element_type=F32) + sent.astype(F32)
-    part = exchange(part.astype(BF16).reshape(members, block, chunk), MLP)
+    parts = exchange(parts, MLP)
+    attended = pl.pallas_call(
+        lambda *refs: combine_kernel(heads // hosts, *refs),
+        out_shape=jax.ShapeDtypeStruct((block, width // hosts), BF16),
+        compiler_params=params(),
+    )(parts)
+
+    feats = spread(attended, REQ, groups).reshape(groups * block, width // hosts)
+    part = jnp.dot(feats, wo, preferred_element_type=F32).astype(BF16)
+    part = exchange(part.reshape(groups, block, chunk), HEADS)
     gain = lax.dynamic_slice_in_dim(ln_gain, c * half + z * chunk, chunk, 0)
 
     hidden, row = pl.pallas_call(
@@ -451,6 +475,7 @@
         ),
         compiler_params=params(),
     )(part, res, gain[None])
+    row, both = lax.optimization_barrier((row, both))
     rows = spread(row, CHIPS, zs * members).reshape(zs, tokens, chunk + HD)
     mine, theirs, stats = up_project(place, rows, up_w, up_other, gain_own, gain_other)
     act = pl.pallas_call(
@@ -463,10 +488,17 @@
     mixed = finish(down, hidden)
     mixed = exchange(mixed.reshape(groups, rows_dev, chunk), REQ)
     mixed = mixed.reshape(zs, cs, rows_dev, chunk).transpose(2, 1, 0, 3).reshape(rows_dev, width)
+    mixed = move(mixed, lanes, from_block)
 
     valid = (accepted >= 0) & (dest_slot == member)[:, None]
     target = jnp.arange(requests, dtype=jnp.int32)[:, None] * tree_len + jnp.maximum(accepted, 0)
-    chooser = jnp.any((target[:, :, None] == row_ids[None, None, :]) & valid[:, :, None], axis=0)
+    x = lax.axis_index("x")
+    y = lax.axis_index(("u", "v"))
+    at = jnp.arange(group_rows, dtype=jnp.int32)
+    near = at // rows_dev
+    slots = (((x - near % xs) % xs) * ys + (y - near // xs) % ys) * rows_dev + at % rows_dev
+    chooser = jnp.any((target[:, :, None] == slots[None, None, :]) & valid[:, :, None], axis=0)
+    both = both.reshape(group_rows, 2 * width)
     picked = jnp.dot(chooser.astype(BF16), both, preferred_element_type=F32).astype(BF16)
     return (mixed, picked[:, :width][None], picked[:, width:][None])
 
@@ -474,7 +506,7 @@
 def solution(mesh):
     groups, members = mesh.devices.shape
     side = math.isqrt(members)
-    fine = Mesh(mesh.devices.reshape(groups // 2, 2, side, side), ALL)
+    fine = Mesh(mesh.devices.reshape(groups // 2, 2, side, side // 2, 2), ALL)
     rows = P(ALL, None)
     pages = P(ALL, None, None)
     in_specs = (

time: 245 us -> 313 us (1.28); the launches traced: 244 us -> 309 us
  waiting for transfers between devices: 113 us -> 151 us
  starting transfers between devices: 70.1 us -> 103 us
  Pallas kernels: 31.1 us -> 22.8 us
  other arithmetic: 2.49 us -> 8.08 us
    ppermute x6 -> x16, waiting for transfers between devices: 1.77 us -> 69.8 us  [the longest x4 68.5 us: move(): return lax.ppermute(x, ALL, [(i, to(i)) for i in range(count)])]
    ppermute x6 -> x16, starting transfers between devices: 9 us -> 40.3 us  [the longest x12 25.7 us: shift(): return lax.ppermute(x, axes, [(i, (i + step) % size) for i in range(size)])]
    all_to_all x5, waiting for transfers between devices: 63 us -> 44.9 us  [exchange(): return lax.all_to_all(x, axes, split_axis=0, concat_axis=0)]
    all_to_all x3 -> x2, waiting for transfers between devices: 44.8 us -> 33.6 us  [spread(): lax.all_to_all(jnp.broadcast_to(x[None], (count,) + x.shape), axes, split...]
    ppermute x8, starting transfers between devices: 9.76 us -> 20.4 us  [pair(): return lax.ppermute(x, 'c', [(0, 1), (1, 0)])]
    pallas_call x1, Pallas kernels: 18.9 us -> 10.2 us  [attend(): pl.pallas_call(body, grid=(steps,), in_specs=[pl.BlockSpec((rows, wide),...]
    all_to_all x3 -> x2, starting transfers between devices: 18.1 us -> 12.8 us  [spread(): lax.all_to_all(jnp.broadcast_to(x[None], (count,) + x.shape), axes, split...]
    another operation x6 -> x4, other arithmetic: 0.39 us -> 5.22 us  [the longest x1 3.7 us: local(): jnp.stack([shift(both, d, ys, ('u', 'v')) if d else both for d in range(y...]
  transfers between devices with their start and end apart: 22 -> 31, of which waited for: 14 -> 15; matrix products, arithmetic and copies ran while one was open for 5% -> 7% of each run, Pallas kernels for 11% -> 6%
where the time goes in v4:
time: 313 us; the launch traced here: 309 us
  waiting for transfers between devices  151 us (48%)
  starting transfers between devices  103 us (33%)
  Pallas kernels  22.8 us (7%)
  local copies, waits for them, and re-layouts  19.4 us (6%)
  other arithmetic  8.08 us (3%)
  matrix products  3.14 us (1%)
    ppermute x4, waiting for transfers between devices, move(): return lax.ppermute(x, ALL, [(i, to(i)) for i in range(count)])  68.5 us
    all_to_all x5, waiting for transfers between devices, exchange(): return lax.all_to_all(x, axes, split_axis=0, concat_axis=0)  44.9 us
    all_to_all x2, waiting for transfers between devices, spread(): lax.all_to_all(jnp.broadcast_to(x[None], (count,) + x.shape), axes, split...  33.6 us
    all_to_all x5, starting transfers between devices, exchange(): return lax.all_to_all(x, axes, split_axis=0, concat_axis=0)  29.4 us
    ppermute x12, starting transfers between devices, shift(): return lax.ppermute(x, axes, [(i, (i + step) % size) for i in range(size)])  25.7 us
    ppermute x8, starting transfers between devices, pair(): return lax.ppermute(x, 'c', [(0, 1), (1, 0)])  20.4 us
    ppermute x4, starting transfers between devices, move(): return lax.ppermute(x, ALL, [(i, to(i)) for i in range(count)])  14.6 us
    all_to_all x2, starting transfers between devices, spread(): lax.all_to_all(jnp.broadcast_to(x[None], (count,) + x.shape), axes, split...  12.8 us
  transfers between devices with their start and end apart: 31, of which 15 were waited for; matrix products, arithmetic and copies ran while one was open for 7% of the time, Pallas kernels for 6%

profile of v4, /device:TPU:1, one launch (start us, length us, event | category | flops | bytes accessed | tf_op | source)
XLA Modules:
  0.0 308.9 jit_solution(1205822222836280084)
XLA Ops:
  2.8 7.6 %all-to-all-start = ((bf16[16,3,7168]{2,1,0:T(4,128)(2,1)}), bf16[16,3,7168]{2,1,0:T(4,128)(2,1)S(1)}, u32[]{:S(2)}, u32[]{:S(2)}) async-start(bf16[16,3,7168]{2,1,0:T(4,128)(2,1)} %broadcast_in_dim.20), calls=%async_computation | async-start | bytes 1835008 | tf_op jit(solution)/shard_map/all_to_all | solution.py:328
  11.9 2.4 collective-permute-start.8
  14.3 6.3 %collective-permute-start.2 = (bf16[3,7168]{1,0:T(4,128)(2,1)S(1)}, bf16[3,7168]{1,0:T(4,128)(2,1)S(1)}, u32[]{:S(2)}, u32[]{:S(2)}) collective-permute-start(bf16[3,7168]{1,0:T(4,128)(2,1)S(1)} %copy-done.13), channel_id=1, source_target_pairs={{0,0},{1,16},{2,32},{3,48},{4,64},{5,80},{6,96},{7,112},{8,1},{9,1... | collective-permute-start | bytes 129032 | tf_op jit(solution)/shard_map/ppermute | solution.py:112
  21.2 3.1 %collective-permute-done.2 = bf16[3,7168]{1,0:T(4,128)(2,1)S(1)} collective-permute-done((bf16[3,7168]{1,0:T(4,128)(2,1)S(1)}, bf16[3,7168]{1,0:T(4,128)(2,1)S(1)}, u32[]{:S(2)}, u32[]{:S(2)}) %collective-permute-start.2) | collective-permute-done | bytes 43040 | tf_op jit(solution)/shard_map/ppermute | solution.py:112
  25.6 4.4 %collective-permute-start.4 = (bf16[2,3,896]{2,1,0:T(4,128)(2,1)S(1)}, bf16[2,3,896]{2,1,0:T(4,128)(2,1)S(1)}, u32[]{:S(2)}, u32[]{:S(2)}) collective-permute-start(bf16[2,3,896]{2,1,0:T(4,128)(2,1)S(1)} %get-tuple-element.48), channel_id=1, source_target_pairs={{0,32},{32,64},{64,96},{96,0},{1,33},{33,65},{65,97},{97,1},{2,34}... | collective-permute-start | bytes 32264 | tf_op jit(solution)/shard_map/ppermute | solution.py:108
  30.1 4.4 %collective-permute-start.5 = (bf16[2,3,896]{2,1,0:T(4,128)(2,1)S(1)}, bf16[2,3,896]{2,1,0:T(4,128)(2,1)S(1)}, u32[]{:S(2)}, u32[]{:S(2)}) collective-permute-start(bf16[2,3,896]{2,1,0:T(4,128)(2,1)S(1)} %get-tuple-element.49), channel_id=1, source_target_pairs={{0,64},{32,96},{64,0},{96,32},{1,65},{33,97},{65,1},{97,33},{2,66}... | collective-permute-start | bytes 32264 | tf_op jit(solution)/shard_map/ppermute | solution.py:108
  36.6 5.9 %collective-permute-start.9 = (bf16[3,14336]{1,0:T(4,128)(2,1)S(1)}, bf16[3,14336]{1,0:T(4,128)(2,1)S(1)}, u32[]{:S(2)}, u32[]{:S(2)}) collective-permute-start(bf16[3,14336]{1,0:T(4,128)(2,1)S(1)} %pad_maximum_fusion.3), channel_id=1, source_target_pairs={{0,12},{4,0},{8,4},{12,8},{1,13},{5,1},{9,5},{13,9},{2,14},{6,2},{... | collective-permute-start | bytes 258056 | tf_op jit(solution)/shard_map/ppermute | solution.py:108
  44.5 3.5 %collective-permute-start.1 = (bf16[56,7168]{1,0:T(8,128)(2,1)}, bf16[56,7168]{1,0:T(8,128)(2,1)S(1)}, u32[]{:S(2)}, u32[]{:S(2)}) collective-permute-start(bf16[56,7168]{1,0:T(8,128)(2,1)} %param.26), channel_id=1, source_target_pairs={{0,1},{1,0},{2,17},{3,16},{4,33},{5,32},{6,49},{7,48},{8,65},{9,64... | collective-permute-start | bytes 2408456 | tf_op jit(solution)/shard_map/ppermute | solution.py:112
  50.2 10.2 %shard_map.166 = bf16[16,24,1024]{2,1,0:T(8,128)(2,1)} custom-call(bf16[48,7168]{1,0:T(8,128)(2,1)} %reshape.200.refs_0_, bf16[24,16,7168]{2,1,0:T(8,128)(2,1)} %refs_1_.1, bf16[24,16,7168]{2,1,0:T(8,128)(2,1)} %refs_2_.1, bf16[16,7168]{1,0:T(8,128)(2,1)} %pad.7.refs_3_, bf16[16,7168]{1,0:T(8,128)(2,1)} %pad.8.refs_4_, f32[48,400]{1,0:T(8,128)} %pad_maximum_fusion.4.refs_5_), custom_call_target="tpu_custom_call" | custom-call | flops 528482304 | bytes 11010048 | tf_op jit(solution)/shard_map/pallas_call | solution.py:66
  60.4 62.0 %collective-permute-done = bf16[56,7168]{1,0:T(8,128)(2,1)S(1)} collective-permute-done((bf16[56,7168]{1,0:T(8,128)(2,1)}, bf16[56,7168]{1,0:T(8,128)(2,1)S(1)}, u32[]{:S(2)}, u32[]{:S(2)}) %collective-permute-start) | collective-permute-done | bytes 802848 | tf_op jit(solution)/shard_map/ppermute | solution.py:112
  123.7 10.2 %collective-permute-start.10 = (bf16[112,3584]{1,0:T(8,128)(2,1)}, bf16[112,3584]{1,0:T(8,128)(2,1)S(1)}, u32[]{:S(2)}, u32[]{:S(2)}) collective-permute-start(bf16[112,3584]{1,0:T(8,128)(2,1)} %get-tuple-element.41), channel_id=1, source_target_pairs={{0,16},{16,0},{1,17},{17,1},{2,18},{18,2},{3,19},{19,3},{4,20},{20... | collective-permute-start | bytes 2408456 | tf_op jit(solution)/shard_map/ppermute | solution.py:104
  133.8 5.8 %all-to-all-start.1 = ((bf16[16,24,1024]{2,1,0:T(8,128)(2,1)}), bf16[16,24,1024]{2,1,0:T(8,128)(2,1)S(1)}, u32[]{:S(2)}, u32[]{:S(2)}) async-start(bf16[16,24,1024]{2,1,0:T(8,128)(2,1)} %shard_map.166), calls=%async_computation.1 | async-start | bytes 1572864 | tf_op jit(solution)/shard_map/all_to_all | solution.py:328
  144.8 2.4 collective-permute-start.15
  147.2 5.9 %all-to-all-done.1.refs_0_ = bf16[16,24,1024]{2,1,0:T(8,128)(2,1)S(1)} async-done(((bf16[16,24,1024]{2,1,0:T(8,128)(2,1)}), bf16[16,24,1024]{2,1,0:T(8,128)(2,1)S(1)}, u32[]{:S(2)}, u32[]{:S(2)}) %all-to-all-start.1) | async-done | bytes 786464 | tf_op jit(solution)/shard_map/all_to_all | solution.py:328
  154.4 5.5 %all-to-all-start.2 = ((bf16[8,24,896]{2,1,0:T(8,128)(2,1)}), bf16[8,24,896]{2,1,0:T(8,128)(2,1)S(1)}, u32[]{:S(2)}, u32[]{:S(2)}) async-start(bf16[8,24,896]{2,1,0:T(8,128)(2,1)} %broadcast_in_dim.24), calls=%async_computation.2 | async-start | bytes 688128 | tf_op jit(solution)/shard_map/all_to_all | solution.py:322
  163.3 4.3 %all-to-all-done.2 = bf16[8,24,896]{2,1,0:T(8,128)(2,1)S(1)} async-done(((bf16[8,24,896]{2,1,0:T(8,128)(2,1)}), bf16[8,24,896]{2,1,0:T(8,128)(2,1)S(1)}, u32[]{:S(2)}, u32[]{:S(2)}) %all-to-all-start.2) | async-done | bytes 344096 | tf_op jit(solution)/shard_map/all_to_all | solution.py:322
  168.9 4.0 %all-to-all-start.3 = ((bf16[8,24,896]{2,1,0:T(8,128)(2,1)}), bf16[8,24,896]{2,1,0:T(8,128)(2,1)S(1)}, u32[]{:S(2)}, u32[]{:S(2)}) async-start(bf16[8,24,896]{2,1,0:T(8,128)(2,1)} %bitcast.17), calls=%async_computation.3 | async-start | bytes 688128 | tf_op jit(solution)/shard_map/all_to_all | solution.py:328
  172.9 3.7 %pad_maximum_fusion = bf16[4,4,3,14336]{3,2,1,0:T(4,128)(2,1)} fusion(bf16[1,4,3,14336]{3,2,1,0:T(4,128)(2,1)} %bitcast.21, bf16[1,4,3,14336]{3,2,1,0:T(4,128)(2,1)} %bitcast.20, bf16[1,4,3,14336]{3,2,1,0:T(4,128)(2,1)S(1)} %bitcast.63, bf16[1,4,3,14336]{3,2,1,0:T(4,128)(2,1)S(1)} %bitcast.58), kind=kLoop, calls=%fused_computation.9 | loop fusion | flops 2064384 | bytes 2752512 | tf_op jit(solution)/shard_map/stack | solution.py:447
  176.6 3.9 %all-to-all-done.3.parts = bf16[8,24,896]{2,1,0:T(8,128)(2,1)S(1)} async-done(((bf16[8,24,896]{2,1,0:T(8,128)(2,1)}), bf16[8,24,896]{2,1,0:T(8,128)(2,1)S(1)}, u32[]{:S(2)}, u32[]{:S(2)}) %all-to-all-start.3) | async-done | bytes 344096 | tf_op jit(solution)/shard_map/all_to_all | solution.py:328
  182.7 7.3 %all-to-all-start.4 = ((bf16[64,24,1024]{2,1,0:T(8,128)(2,1)}), bf16[64,24,1024]{2,1,0:T(8,128)(2,1)}, u32[]{:S(2)}, u32[]{:S(2)}) async-start(bf16[64,24,1024]{2,1,0:T(8,128)(2,1)} %broadcast_in_dim.26), calls=%async_computation.4 | async-start | bytes 6291456 | tf_op jit(solution)/shard_map/all_to_all | solution.py:322
  190.2 2.8 collective-permute-start.17
  197.8 29.3 %all-to-all-done.4 = bf16[64,24,1024]{2,1,0:T(8,128)(2,1)} async-done(((bf16[64,24,1024]{2,1,0:T(8,128)(2,1)}), bf16[64,24,1024]{2,1,0:T(8,128)(2,1)}, u32[]{:S(2)}, u32[]{:S(2)}) %all-to-all-start.4) | async-done | bytes 3145760 | tf_op jit(solution)/shard_map/all_to_all | solution.py:322
  228.5 5.4 %shard_map.170 = (f32[384,224]{1,0:T(8,128)S(1)}, f32[384,224]{1,0:T(8,128)S(1)}, f32[384,128]{1,0:T(8,128)S(1)}) custom-call(s32[1]{0:T(128)} %bitcast.place, bf16[4,384,1024]{2,1,0:T(8,128)(2,1)} %bitcast.22.rows, bf16[224,7168]{1,0:T(8,128)(2,1)S(1)} %bitcast.53, bf16[224,3584]{1,0:T(8,128)(2,1)S(1)} %copy-done.5, ...), custom_call_target="tpu_custom_call" | custom-call | tf_op jit(solution)/shard_map/pallas_call | solution.py:256
  234.0 4.7 %collective-permute-start.18 = (f32[384,224]{1,0:T(8,128)S(1)}, f32[384,224]{1,0:T(8,128)S(1)}, u32[]{:S(2)}, u32[]{:S(2)}) collective-permute-start(f32[384,224]{1,0:T(8,128)S(1)} %get-tuple-element.32), channel_id=1, source_target_pairs={{0,16},{16,0},{1,17},{17,1},{2,18},{18,2},{3,19},{19,3},{4,20},{20... | collective-permute-start | bytes 1032200 | tf_op jit(solution)/shard_map/ppermute | solution.py:104
  242.3 3.9 %shard_map.172 = bf16[4,384,896]{2,1,0:T(8,128)(2,1)S(1)} custom-call(s32[1]{0:T(128)} %bitcast.place, bf16[384,224]{1,0:T(8,128)(2,1)S(1)} %shard_map.171.act, bf16[384,224]{1,0:T(8,128)(2,1)S(1)} %collective-permute-done.21.act_pair, bf16[224,7168]{1,0:T(8,128)(2,1)S(1)} %copy-done.3, bf16[224,3584]{1,0:T(8,128)(2,1)} %collective-permute-done.22.other), custom_call_target="tpu_custom_call" | custom-call | tf_op jit(solution)/shard_map/pallas_call | solution.py:286
  247.7 6.4 %all-to-all-start.5 = ((bf16[64,24,896]{2,1,0:T(8,128)(2,1)}), bf16[64,24,896]{2,1,0:T(8,128)(2,1)S(1)}, u32[]{:S(2)}, u32[]{:S(2)}) async-start(bf16[64,24,896]{2,1,0:T(8,128)(2,1)} %bitcast.54), calls=%async_computation.5 | async-start | bytes 5505024 | tf_op jit(solution)/shard_map/all_to_all | solution.py:328
  254.4 3.2 %reshape.210 = bf16[48,14336]{1,0:T(8,128)(2,1)} reshape(bf16[4,4,3,14336]{3,2,1,0:T(4,128)(2,1)} %pad_maximum_fusion) | data formatting | bytes 2752512 | tf_op jit(solution)/shard_map/reshape | solution.py:501
  257.6 31.9 %all-to-all-done.5.parts = bf16[64,24,896]{2,1,0:T(8,128)(2,1)S(1)} async-done(((bf16[64,24,896]{2,1,0:T(8,128)(2,1)}), bf16[64,24,896]{2,1,0:T(8,128)(2,1)S(1)}, u32[]{:S(2)}, u32[]{:S(2)}) %all-to-all-start.5) | async-done | bytes 2752544 | tf_op jit(solution)/shard_map/all_to_all | solution.py:328
  290.6 5.7 %all-to-all-start.6 = ((bf16[8,3,896]{2,1,0:T(4,128)(2,1)}), bf16[8,3,896]{2,1,0:T(4,128)(2,1)S(1)}, u32[]{:S(2)}, u32[]{:S(2)}) async-start(bf16[8,3,896]{2,1,0:T(4,128)(2,1)} %reshape.207), calls=%async_computation.6 | async-start | bytes 114688 | tf_op jit(solution)/shard_map/all_to_all | solution.py:328
  298.0 3.2 %all-to-all-done.6 = bf16[8,3,896]{2,1,0:T(4,128)(2,1)S(1)} async-done(((bf16[8,3,896]{2,1,0:T(4,128)(2,1)}), bf16[8,3,896]{2,1,0:T(4,128)(2,1)S(1)}, u32[]{:S(2)}, u32[]{:S(2)}) %all-to-all-start.6) | async-done | bytes 43040 | tf_op jit(solution)/shard_map/all_to_all | solution.py:328
  301.2 2.8 collective-permute-start.23
  304.8 3.4 %collective-permute-done.23 = bf16[3,7168]{1,0:T(4,128)(2,1)S(1)} collective-permute-done((bf16[3,7168]{1,0:T(4,128)(2,1)S(1)}, bf16[3,7168]{1,0:T(4,128)(2,1)S(1)}, u32[]{:S(2)}, u32[]{:S(2)}) %collective-permute-start.23) | collective-permute-done | bytes 43040 | tf_op jit(solution)/shard_map/ppermute | solution.py:112
  (136 shorter events, 42.2 us)
Async XLA Ops:
  0.7 23.7 %copy-start.11 = (s32[3,384]{1,0:T(4,128)S(1)}, s32[3,384]{1,0:T(4,128)}, u32[]{:S(2)}) copy-start(s32[3,384]{1,0:T(4,128)} %param.23) | copy-start | bytes 13828
  2.8 46.0 %all-to-all-start = ((bf16[16,3,7168]{2,1,0:T(4,128)(2,1)}), bf16[16,3,7168]{2,1,0:T(4,128)(2,1)S(1)}, u32[]{:S(2)}, u32[]{:S(2)}) async-start(bf16[16,3,7168]{2,1,0:T(4,128)(2,1)} %broadcast_in_dim.20), calls=%async_computation | async-start | bytes 1835008 | tf_op jit(solution)/shard_map/all_to_all | solution.py:328
  10.5 37.9 %collective-permute-start.7 = (bf16[3,14336]{1,0:T(4,128)(2,1)S(1)}, bf16[3,14336]{1,0:T(4,128)(2,1)S(1)}, u32[]{:S(2)}, u32[]{:S(2)}) collective-permute-start(bf16[3,14336]{1,0:T(4,128)(2,1)S(1)} %pad_maximum_fusion.3), channel_id=1, source_target_pairs={{0,4},{4,8},{8,12},{12,0},{1,5},{5,9},{9,13},{13,1},{2,6},{6,10},{... | collective-permute-start | bytes 258056 | tf_op jit(solution)/shard_map/ppermute | solution.py:108
  11.9 36.5 %collective-permute-start.8 = (bf16[3,14336]{1,0:T(4,128)(2,1)S(1)}, bf16[3,14336]{1,0:T(4,128)(2,1)S(1)}, u32[]{:S(2)}, u32[]{:S(2)}) collective-permute-start(bf16[3,14336]{1,0:T(4,128)(2,1)S(1)} %pad_maximum_fusion.3), channel_id=1, source_target_pairs={{0,8},{4,12},{8,0},{12,4},{1,9},{5,13},{9,1},{13,5},{2,10},{6,14},... | collective-permute-start | bytes 258056 | tf_op jit(solution)/shard_map/ppermute | solution.py:108
  14.3 10.0 %collective-permute-start.2 = (bf16[3,7168]{1,0:T(4,128)(2,1)S(1)}, bf16[3,7168]{1,0:T(4,128)(2,1)S(1)}, u32[]{:S(2)}, u32[]{:S(2)}) collective-permute-start(bf16[3,7168]{1,0:T(4,128)(2,1)S(1)} %copy-done.13), channel_id=1, source_target_pairs={{0,0},{1,16},{2,32},{3,48},{4,64},{5,80},{6,96},{7,112},{8,1},{9,1... | collective-permute-start | bytes 129032 | tf_op jit(solution)/shard_map/ppermute | solution.py:112
  24.3 1.3 collective-permute-start.3
  25.6 11.0 %collective-permute-start.4 = (bf16[2,3,896]{2,1,0:T(4,128)(2,1)S(1)}, bf16[2,3,896]{2,1,0:T(4,128)(2,1)S(1)}, u32[]{:S(2)}, u32[]{:S(2)}) collective-permute-start(bf16[2,3,896]{2,1,0:T(4,128)(2,1)S(1)} %get-tuple-element.48), channel_id=1, source_target_pairs={{0,32},{32,64},{64,96},{96,0},{1,33},{33,65},{65,97},{97,1},{2,34}... | collective-permute-start | bytes 32264 | tf_op jit(solution)/shard_map/ppermute | solution.py:108
  30.1 12.4 %collective-permute-start.5 = (bf16[2,3,896]{2,1,0:T(4,128)(2,1)S(1)}, bf16[2,3,896]{2,1,0:T(4,128)(2,1)S(1)}, u32[]{:S(2)}, u32[]{:S(2)}) collective-permute-start(bf16[2,3,896]{2,1,0:T(4,128)(2,1)S(1)} %get-tuple-element.49), channel_id=1, source_target_pairs={{0,64},{32,96},{64,0},{96,32},{1,65},{33,97},{65,1},{97,33},{2,66}... | collective-permute-start | bytes 32264 | tf_op jit(solution)/shard_map/ppermute | solution.py:108
  34.5 10.0 %collective-permute-start.6 = (bf16[2,3,896]{2,1,0:T(4,128)(2,1)S(1)}, bf16[2,3,896]{2,1,0:T(4,128)(2,1)S(1)}, u32[]{:S(2)}, u32[]{:S(2)}) collective-permute-start(bf16[2,3,896]{2,1,0:T(4,128)(2,1)S(1)} %get-tuple-element.50), channel_id=1, source_target_pairs={{0,96},{32,0},{64,32},{96,64},{1,97},{33,1},{65,33},{97,65},{2,98}... | collective-permute-start | bytes 32264 | tf_op jit(solution)/shard_map/ppermute | solution.py:108
  36.6 11.8 %collective-permute-start.9 = (bf16[3,14336]{1,0:T(4,128)(2,1)S(1)}, bf16[3,14336]{1,0:T(4,128)(2,1)S(1)}, u32[]{:S(2)}, u32[]{:S(2)}) collective-permute-start(bf16[3,14336]{1,0:T(4,128)(2,1)S(1)} %pad_maximum_fusion.3), channel_id=1, source_target_pairs={{0,12},{4,0},{8,4},{12,8},{1,13},{5,1},{9,5},{13,9},{2,14},{6,2},{... | collective-permute-start | bytes 258056 | tf_op jit(solution)/shard_map/ppermute | solution.py:108
  42.5 79.8 %collective-permute-start = (bf16[56,7168]{1,0:T(8,128)(2,1)}, bf16[56,7168]{1,0:T(8,128)(2,1)S(1)}, u32[]{:S(2)}, u32[]{:S(2)}) collective-permute-start(bf16[56,7168]{1,0:T(8,128)(2,1)} %param.26), channel_id=1, source_target_pairs={{0,0},{1,1},{2,16},{3,17},{4,32},{5,33},{6,48},{7,49},{8,64},{9,65... | collective-permute-start | bytes 2408456 | tf_op jit(solution)/shard_map/ppermute | solution.py:112
  44.5 77.8 %collective-permute-start.1 = (bf16[56,7168]{1,0:T(8,128)(2,1)}, bf16[56,7168]{1,0:T(8,128)(2,1)S(1)}, u32[]{:S(2)}, u32[]{:S(2)}) collective-permute-start(bf16[56,7168]{1,0:T(8,128)(2,1)} %param.26), channel_id=1, source_target_pairs={{0,1},{1,0},{2,17},{3,16},{4,33},{5,32},{6,49},{7,48},{8,65},{9,64... | collective-permute-start | bytes 2408456 | tf_op jit(solution)/shard_map/ppermute | solution.py:112
  123.7 16.0 %collective-permute-start.10 = (bf16[112,3584]{1,0:T(8,128)(2,1)}, bf16[112,3584]{1,0:T(8,128)(2,1)S(1)}, u32[]{:S(2)}, u32[]{:S(2)}) collective-permute-start(bf16[112,3584]{1,0:T(8,128)(2,1)} %get-tuple-element.41), channel_id=1, source_target_pairs={{0,16},{16,0},{1,17},{17,1},{2,18},{18,2},{3,19},{19,3},{4,20},{20... | collective-permute-start | bytes 2408456 | tf_op jit(solution)/shard_map/ppermute | solution.py:104
  133.8 19.3 %all-to-all-start.1 = ((bf16[16,24,1024]{2,1,0:T(8,128)(2,1)}), bf16[16,24,1024]{2,1,0:T(8,128)(2,1)S(1)}, u32[]{:S(2)}, u32[]{:S(2)}) async-start(bf16[16,24,1024]{2,1,0:T(8,128)(2,1)} %shard_map.166), calls=%async_computation.1 | async-start | bytes 1572864 | tf_op jit(solution)/shard_map/all_to_all | solution.py:328
  140.7 19.2 %collective-permute-start.11 = (bf16[2,112,896]{2,1,0:T(8,128)(2,1)}, bf16[2,112,896]{2,1,0:T(8,128)(2,1)S(1)}, u32[]{:S(2)}, u32[]{:S(2)}) collective-permute-start(bf16[2,112,896]{2,1,0:T(8,128)(2,1)} %get-tuple-element.38), channel_id=1, source_target_pairs={{0,32},{32,64},{64,96},{96,0},{1,33},{33,65},{65,97},{97,1},{2,34}... | collective-permute-start | bytes 1204232 | tf_op jit(solution)/shard_map/ppermute | solution.py:108
  140.7 20.3 %collective-permute-start.12 = (bf16[2,112,896]{2,1,0:T(8,128)(2,1)}, bf16[2,112,896]{2,1,0:T(8,128)(2,1)S(1)}, u32[]{:S(2)}, u32[]{:S(2)}) collective-permute-start(bf16[2,112,896]{2,1,0:T(8,128)(2,1)} %get-tuple-element.39), channel_id=1, source_target_pairs={{0,64},{32,96},{64,0},{96,32},{1,65},{33,97},{65,1},{97,33},{2,66}... | collective-permute-start | bytes 1204232 | tf_op jit(solution)/shard_map/ppermute | solution.py:108
  143.0 18.7 %collective-permute-start.13 = (bf16[2,112,896]{2,1,0:T(8,128)(2,1)}, bf16[2,112,896]{2,1,0:T(8,128)(2,1)}, u32[]{:S(2)}, u32[]{:S(2)}) collective-permute-start(bf16[2,112,896]{2,1,0:T(8,128)(2,1)} %get-tuple-element.40), channel_id=1, source_target_pairs={{0,96},{32,0},{64,32},{96,64},{1,97},{33,1},{65,33},{97,65},{2,98}... | collective-permute-start | bytes 1204232 | tf_op jit(solution)/shard_map/ppermute | solution.py:108
  143.5 29.4 %collective-permute-start.14 = (bf16[4,3,14336]{2,1,0:T(4,128)(2,1)S(1)}, bf16[4,3,14336]{2,1,0:T(4,128)(2,1)S(1)}, u32[]{:S(2)}, u32[]{:S(2)}) collective-permute-start(bf16[4,3,14336]{2,1,0:T(4,128)(2,1)S(1)} %pad_maximum_fusion.2), channel_id=1, source_target_pairs={{0,1},{1,2},{2,3},{3,0},{4,5},{5,6},{6,7},{7,4},{8,9},{9,10},{10,1... | collective-permute-start | bytes 1032200 | tf_op jit(solution)/shard_map/ppermute | solution.py:108
  144.8 28.0 %collective-permute-start.15 = (bf16[4,3,14336]{2,1,0:T(4,128)(2,1)S(1)}, bf16[4,3,14336]{2,1,0:T(4,128)(2,1)}, u32[]{:S(2)}, u32[]{:S(2)}) collective-permute-start(bf16[4,3,14336]{2,1,0:T(4,128)(2,1)S(1)} %pad_maximum_fusion.2), channel_id=1, source_target_pairs={{0,2},{1,3},{2,0},{3,1},{4,6},{5,7},{6,4},{7,5},{8,10},{9,11},{10,... | collective-permute-start | bytes 1032200 | tf_op jit(solution)/shard_map/ppermute | solution.py:108
  154.4 13.2 %all-to-all-start.2 = ((bf16[8,24,896]{2,1,0:T(8,128)(2,1)}), bf16[8,24,896]{2,1,0:T(8,128)(2,1)S(1)}, u32[]{:S(2)}, u32[]{:S(2)}) async-start(bf16[8,24,896]{2,1,0:T(8,128)(2,1)} %broadcast_in_dim.24), calls=%async_computation.2 | async-start | bytes 688128 | tf_op jit(solution)/shard_map/all_to_all | solution.py:322
  159.9 13.0 %collective-permute-start.16 = (bf16[4,3,14336]{2,1,0:T(4,128)(2,1)S(1)}, bf16[4,3,14336]{2,1,0:T(4,128)(2,1)}, u32[]{:S(2)}, u32[]{:S(2)}) collective-permute-start(bf16[4,3,14336]{2,1,0:T(4,128)(2,1)S(1)} %pad_maximum_fusion.2), channel_id=1, source_target_pairs={{0,3},{1,0},{2,1},{3,2},{4,7},{5,4},{6,5},{7,6},{8,11},{9,8},{10,9... | collective-permute-start | bytes 1032200 | tf_op jit(solution)/shard_map/ppermute | solution.py:108
  168.9 11.6 %all-to-all-start.3 = ((bf16[8,24,896]{2,1,0:T(8,128)(2,1)}), bf16[8,24,896]{2,1,0:T(8,128)(2,1)S(1)}, u32[]{:S(2)}, u32[]{:S(2)}) async-start(bf16[8,24,896]{2,1,0:T(8,128)(2,1)} %bitcast.17), calls=%async_computation.3 | async-start | bytes 688128 | tf_op jit(solution)/shard_map/all_to_all | solution.py:328
  182.7 44.4 %all-to-all-start.4 = ((bf16[64,24,1024]{2,1,0:T(8,128)(2,1)}), bf16[64,24,1024]{2,1,0:T(8,128)(2,1)}, u32[]{:S(2)}, u32[]{:S(2)}) async-start(bf16[64,24,1024]{2,1,0:T(8,128)(2,1)} %broadcast_in_dim.26), calls=%async_computation.4 | async-start | bytes 6291456 | tf_op jit(solution)/shard_map/all_to_all | solution.py:322
  190.2 5.9 %collective-permute-start.17 = (bf16[224,3584]{1,0:T(8,128)(2,1)S(1)}, bf16[224,3584]{1,0:T(8,128)(2,1)S(1)}, u32[]{:S(2)}, u32[]{:S(2)}) collective-permute-start(bf16[224,3584]{1,0:T(8,128)(2,1)S(1)} %constant_dynamic-slice_fusion.1), channel_id=1, source_target_pairs={{0,16},{16,0},{1,17},{17,1},{2,18},{18,2},{3,19},{19,3},{4,20},{20... | collective-permute-start | bytes 4816904 | tf_op jit(solution)/shard_map/ppermute | solution.py:104
  194.3 46.9 %collective-permute-start.22 = (bf16[224,3584]{1,0:T(8,128)(2,1)}, bf16[224,3584]{1,0:T(8,128)(2,1)}, u32[]{:S(2)}, u32[]{:S(2)}) collective-permute-start(bf16[224,3584]{1,0:T(8,128)(2,1)} %constant_dynamic-slice_fusion), channel_id=1, source_target_pairs={{0,16},{16,0},{1,17},{17,1},{2,18},{18,2},{3,19},{19,3},{4,20},{20... | collective-permute-start | bytes 4816904 | tf_op jit(solution)/shard_map/ppermute | solution.py:104
  234.0 6.4 %collective-permute-start.18 = (f32[384,224]{1,0:T(8,128)S(1)}, f32[384,224]{1,0:T(8,128)S(1)}, u32[]{:S(2)}, u32[]{:S(2)}) collective-permute-start(f32[384,224]{1,0:T(8,128)S(1)} %get-tuple-element.32), channel_id=1, source_target_pairs={{0,16},{16,0},{1,17},{17,1},{2,18},{18,2},{3,19},{19,3},{4,20},{20... | collective-permute-start | bytes 1032200 | tf_op jit(solution)/shard_map/ppermute | solution.py:104
  238.7 1.7 collective-permute-start.19
  238.8 1.6 collective-permute-start.20
  240.7 1.5 collective-permute-start.21
  247.7 41.8 %all-to-all-start.5 = ((bf16[64,24,896]{2,1,0:T(8,128)(2,1)}), bf16[64,24,896]{2,1,0:T(8,128)(2,1)S(1)}, u32[]{:S(2)}, u32[]{:S(2)}) async-start(bf16[64,24,896]{2,1,0:T(8,128)(2,1)} %bitcast.54), calls=%async_computation.5 | async-start | bytes 5505024 | tf_op jit(solution)/shard_map/all_to_all | solution.py:328
  290.6 10.6 %all-to-all-start.6 = ((bf16[8,3,896]{2,1,0:T(4,128)(2,1)}), bf16[8,3,896]{2,1,0:T(4,128)(2,1)S(1)}, u32[]{:S(2)}, u32[]{:S(2)}) async-start(bf16[8,3,896]{2,1,0:T(4,128)(2,1)} %reshape.207), calls=%async_computation.6 | async-start | bytes 114688 | tf_op jit(solution)/shard_map/all_to_all | solution.py:328
  301.2 7.0 %collective-permute-start.23 = (bf16[3,7168]{1,0:T(4,128)(2,1)S(1)}, bf16[3,7168]{1,0:T(4,128)(2,1)S(1)}, u32[]{:S(2)}, u32[]{:S(2)}) collective-permute-start(bf16[3,7168]{1,0:T(4,128)(2,1)S(1)} %reshape.209), channel_id=1, source_target_pairs={{0,0},{1,8},{2,16},{3,24},{4,32},{5,40},{6,48},{7,56},{8,64},{9,72... | collective-permute-start | bytes 129032 | tf_op jit(solution)/shard_map/ppermute | solution.py:112
  (14 other events, 118.4 us)

commit v5 on v2

v5 whole, which is shorter than its diff:
```python
import math

import jax
import jax.numpy as jnp
from jax import lax
from jax.experimental import pallas as pl
from jax.experimental.pallas import tpu as pltpu
from jax.sharding import Mesh, PartitionSpec as P

HD = 128
NEG = -(2.0**100)
F32 = jnp.float32
BF16 = jnp.bfloat16
ALL = ("z", "c", "x", "y")
REQ = ("z", "c")
MLP = ("x", "y")
DN = (((1,), (1,)), ((), ()))


def attend_kernel(heads, scaling, q, k, v, dk, dv, mask, out):
    rows = q.shape[0]
    keys = k.shape[0] * k.shape[1]
    kk = jnp.concatenate([k[...].reshape(keys, k.shape[2]), dk[...]], axis=0)
    vv = jnp.concatenate([v[...].reshape(keys, v.shape[2]), dv[...]], axis=0)
    m = mask[...]
    span = [slice(h * HD, (h + 1) * HD) for h in range(heads)]
    scores = [
        jnp.where(
            m > 0,
            lax.dot_general(q[:, cols], kk[:, cols], DN, preferred_element_type=F32) * scaling,
            NEG,
        )
        for cols in span
    ]
    tops = [jnp.max(s, axis=1, keepdims=True).astype(BF16).astype(F32) for s in scores]
    weights = [jnp.exp(s - top) * m for s, top in zip(scores, tops)]
    totals = [jnp.sum(p, axis=1, keepdims=True) for p in weights]
    lane = lax.broadcasted_iota(jnp.int32, (rows, HD), 1)
    stats = jnp.zeros((rows, HD), F32)
    for h, cols in enumerate(span):
        w = jnp.dot(weights[h].astype(BF16), vv[:, cols], preferred_element_type=F32)
        out[:, cols] = w.astype(BF16)
        high = totals[h].astype(BF16).astype(F32)
        stats = jnp.where(lane == h, tops[h], stats)
        stats = jnp.where(lane == 8 + h, high, stats)
        stats = jnp.where(lane == 16 + h, totals[h] - high, stats)
    out[:, heads * HD :] = stats.astype(BF16)


def attend(q, key_cache, value_cache, dk, dv, mask, steps):
    rows, width = q.shape
    pages, page_len, _ = key_cache.shape
    wide = width // steps
    heads = wide // HD
    col = lambda i: (0, i)
    col3 = lambda i: (0, 0, i)

    def body(*refs):
        attend_kernel(heads, 1.0 / math.sqrt(HD), *refs)

    return pl.pallas_call(
        body,
        grid=(steps,),
        in_specs=[
            pl.BlockSpec((rows, wide), col),
            pl.BlockSpec((pages, page_len, wide), col3),
            pl.BlockSpec((pages, page_len, wide), col3),
            pl.BlockSpec((dk.shape[0], wide), col),
            pl.BlockSpec((dv.shape[0], wide), col),
            pl.BlockSpec(mask.shape, lambda i: (0, 0)),
        ],
        out_specs=pl.BlockSpec((rows, wide + HD), col),
        out_shape=jax.ShapeDtypeStruct((rows, steps * (wide + HD)), BF16),
        compiler_params=pltpu.CompilerParams(vmem_limit_bytes=58 * 1024 * 1024),
        cost_estimate=pl.CostEstimate(
            flops=4 * rows * pages * page_len * width,
            bytes_accessed=4 * pages * page_len * width,
            transcendentals=rows * pages * page_len * width // HD,
        ),
    )(q, key_cache, value_cache, dk, dv, mask)


def pair(x):
    return lax.ppermute(x, "c", [(0, 1), (1, 0)])


def shift(x, step, size):
    return lax.ppermute(x, "z", [(i, (i + step) % size) for i in range(size)])


def after(x, first):
    return lax.optimization_barrier((x, first))[0]


def gain_kernel(place, gain, weight, out):
    high = gain[...].astype(BF16).astype(F32)
    row = lax.broadcasted_iota(jnp.int32, (8, gain.shape[1]), 0)
    both = jnp.where(row == 0, high, jnp.where(row == 1, gain[...] - high, 0.0)).astype(BF16)
    got = lax.dot_general(both, weight[...], DN, preferred_element_type=F32)
    out[0] = jnp.broadcast_to(got[0:1] + got[1:2], got.shape)


def hidden_kernel(parts, res, gain, hidden_out, row_out):
    hidden = res[...] + jnp.sum(parts[...].astype(F32), axis=0)
    hidden_out[...] = hidden
    rows, chunk = hidden.shape
    mean = jnp.mean(hidden, axis=1, keepdims=True)
    centered = hidden - mean
    dev = jnp.sum(centered * centered, axis=1, keepdims=True)
    row_out[:, :chunk] = (centered * gain[...]).astype(BF16)
    lane = lax.broadcasted_iota(jnp.int32, (rows, HD), 1)
    stats = jnp.zeros((rows, HD), F32)
    at = 0
    for value in (mean, dev):
        for _ in range(3):
            high = value.astype(BF16).astype(F32)
            stats = jnp.where(lane == at, high, stats)
            value = value - high
            at += 1
    row_out[:, chunk:] = stats.astype(BF16)


def up_kernel(n, *refs):
    rows = refs[0]
    chunk = refs[1].shape[2]
    g = rows[:, :chunk]
    st = rows[:, chunk:].astype(F32)
    lane = lax.broadcasted_iota(jnp.int32, st.shape, 1)
    st = jnp.where(lane < 6, st, 0.0)
    none = jnp.zeros_like(st)
    for d in range(n):
        for e in range(2):
            w = refs[1 + d][e]
            wide = refs[n + 1].shape[2]
            w = jnp.concatenate([w, jnp.zeros((wide - w.shape[0], chunk), BF16)], axis=0)
            got = lax.dot_general(g, w, DN, preferred_element_type=F32)
            beside = jnp.concatenate([none, pltpu.roll(st, 96 if e else 102, 1)], axis=1)
            refs[n + 1 + e][d] = (got + beside).astype(refs[n + 1 + e].dtype)


def act_kernel(width, units, n, *refs):
    terms = [refs[d][...].astype(F32) for d in range(n)]
    gain = refs[n]
    out = refs[n + 1]
    chunk = width // (2 * n)
    pre = terms[0]
    for d in range(1, n):
        pre = pre + terms[d]
    pre = pre[:, :units]
    means, devs = [], []
    for t in terms:
        for at in (units + 6, units):
            means.append(t[:, at : at + 1] + t[:, at + 1 : at + 2] + t[:, at + 2 : at + 3])
            devs.append(t[:, at + 3 : at + 4] + t[:, at + 4 : at + 5] + t[:, at + 5 : at + 6])
    mean = sum(means[1:], means[0]) / (2 * n)
    var = sum(devs[1:], devs[0])
    for k, value in enumerate(means):
        off = value - mean
        var = var + chunk * off * off
        pre = pre + off * gain[k, 0:1, :]
    out[...] = jnp.maximum(lax.rsqrt(var / width + 1e-05) * pre, 0.0).astype(BF16)


def down_kernel(n, *refs):
    total = None
    for d in range(n):
        for e in range(2):
            term = jnp.dot(refs[e * n + d][...], refs[2 * n + d][e], preferred_element_type=F32)
            total = term if total is None else total + term
    refs[3 * n][...] = total.astype(BF16)


def finish_kernel(parts, hidden, out, total):
    step = pl.program_id(0)

    @pl.when(step == 0)
    def _():
        total[...] = hidden[...]

    total[...] += jnp.sum(parts[...].astype(F32), axis=0)

    @pl.when(step == pl.num_programs(0) - 1)
    def _():
        out[...] = total[...].astype(BF16)


def params():
    return pltpu.CompilerParams(vmem_limit_bytes=32 * 1024 * 1024)


def gain_products(order, gain, weight, chunk):
    units = weight.shape[0]
    n = order.shape[0]
    return pl.pallas_call(
        gain_kernel,
        grid_spec=pltpu.PrefetchScalarGridSpec(
            num_scalar_prefetch=1,
            grid=(n,),
            in_specs=[
                pl.BlockSpec((1, chunk), lambda i, order: (0, order[i])),
                pl.BlockSpec((units, chunk), lambda i, order: (0, order[i])),
            ],
            out_specs=pl.BlockSpec((1, 8, units), lambda i, order: (i, 0, 0)),
        ),
        out_shape=jax.ShapeDtypeStruct((n, 8, units), F32),
        compiler_params=params(),
    )(order, gain, weight)


def up_project(rows, weights):
    n = len(weights)
    tokens = rows.shape[0]
    return pl.pallas_call(
        lambda *refs: up_kernel(n, *refs),
        out_shape=(
            jax.ShapeDtypeStruct((n, tokens, 256), F32),
            jax.ShapeDtypeStruct((n, tokens, 256), BF16),
        ),
        compiler_params=params(),
    )(rows, *weights)


def down_project(own, other, weights):
    n = len(weights)
    return pl.pallas_call(
        lambda *refs: down_kernel(n, *refs),
        out_shape=jax.ShapeDtypeStruct((own[0].shape[0], weights[0].shape[2]), BF16),
        compiler_params=params(),
    )(*own, *other, *weights)


def finish(parts, hidden):
    count, block, chunk = parts.shape
    per = count // 4
    return pl.pallas_call(
        finish_kernel,
        grid=(4,),
        in_specs=[
            pl.BlockSpec((per, block, chunk), lambda i: (i, 0, 0)),
            pl.BlockSpec((block, chunk), lambda i: (0, 0)),
        ],
        out_specs=pl.BlockSpec((block, chunk), lambda i: (0, 0)),
        out_shape=jax.ShapeDtypeStruct((block, chunk), BF16),
        scratch_shapes=[pltpu.VMEM((block, chunk), F32)],
        compiler_params=params(),
    )(parts, hidden)


def spread(x, axes, count):
    return lax.all_to_all(
        jnp.broadcast_to(x[None], (count,) + x.shape), axes, split_axis=0, concat_axis=0
    )


def exchange(x, axes):
    return lax.all_to_all(x, axes, split_axis=0, concat_axis=0)


def local(
    queries,
    keys_new,
    values_new,
    resid,
    tree_mask,
    tree_size,
    accepted,
    dest_slot,
    page_table,
    key_cache,
    value_cache,
    w_out,
    w_up,
    w_down,
    ln_gain,
):
    zs, cs, xs, ys = (lax.axis_size(a) for a in ALL)
    members = xs * ys
    groups = zs * cs
    z = lax.axis_index("z")
    c = lax.axis_index("c")
    member = lax.axis_index(MLP)
    rows_dev, width = queries.shape
    requests, tree_len = tree_mask.shape[:2]
    group_rows = requests * tree_len
    pages_dev, page_len, _ = key_cache.shape
    tokens = group_rows * groups
    heads = width // HD
    half = width // cs
    chunk = half // zs
    block = tokens // members

    wide_q = jnp.broadcast_to(queries[None], (members,) + queries.shape)
    group_q = exchange(wide_q, MLP).reshape(group_rows, width)

    def piece(w, core, d):
        return lax.dynamic_slice_in_dim(w, core * half + ((z + d) % zs) * chunk, chunk, 1)

    k_dev = w_out.shape[0]
    wo = after(w_out, wide_q)
    wo_parts = []
    for d in range(zs):
        part = jnp.stack([piece(wo, c, d), piece(wo, 1 - c, d)])
        wo_parts.append(shift(part, d, zs) if d else part)
    wo_parts = jnp.concatenate(wo_parts, axis=1)

    def swap(w):
        return pair(lax.dynamic_slice_in_dim(w, (1 - c) * half, half, 1))

    def reshard(w, other):
        split = []
        for d in range(zs):
            at = ((z + d) % zs) * chunk
            part = jnp.stack([piece(w, c, d), lax.dynamic_slice_in_dim(other, at, chunk, 1)])
            split.append(shift(part, d, zs) if d else part)
        return split

    up_w = w_up.T
    up_w = after(up_w, wide_q)
    ups = reshard(up_w, swap(up_w))
    order = jnp.stack(
        [(c + e) % cs * zs + (z + d) % zs for d in range(zs) for e in range(cs)]
    ).astype(jnp.int32)
    gain_up = gain_products(order, ln_gain[None], up_w, chunk)

    page_ids = member * pages_dev + jnp.arange(pages_dev, dtype=jnp.int32)
    owners = jnp.any(page_table[:, :, None] == page_ids[None, None, :], axis=1)
    pool_mask = jnp.repeat(jnp.repeat(owners, page_len, axis=1), tree_len, axis=0).astype(F32)
    draft_pad = 16
    slot_ids = member * rows_dev + jnp.arange(draft_pad, dtype=jnp.int32)
    row_ids = jnp.arange(group_rows, dtype=jnp.int32)
    tree_cols = jnp.tile(tree_mask.reshape(group_rows, tree_len), (1, requests))
    live = jnp.repeat(tree_size, tree_len) > (row_ids % tree_len)
    tree_ok = (
        (tree_cols == 1)
        & live[None, :]
        & ((row_ids // tree_len)[:, None] == (row_ids // tree_len)[None, :])
    ).astype(F32)
    pick = (row_ids[:, None] == slot_ids[None, :]) & (
        jnp.arange(draft_pad, dtype=jnp.int32) < rows_dev
    )[None, :]
    draft_mask = jnp.dot(tree_ok, pick.astype(F32))
    pad = ((0, draft_pad - rows_dev), (0, 0))
    parts = attend(
        group_q,
        key_cache,
        value_cache,
        jnp.pad(keys_new, pad),
        jnp.pad(values_new, pad),
        jnp.concatenate([pool_mask, draft_mask], axis=1),
        heads // 7,
    )

    parts, ups[1], ups[3], wo_parts = lax.optimization_barrier((parts, ups[1], ups[3], wo_parts))
    down_other = swap(after(w_down, parts))

    res = after(resid, parts)
    res = jnp.stack(
        [
            lax.dynamic_slice_in_dim(res, c * half, half, 1),
            pair(lax.dynamic_slice_in_dim(res, (1 - c) * half, half, 1)),
        ]
    ).reshape(cs * rows_dev, half)
    res_parts = []
    for d in range(zs):
        part = lax.dynamic_slice_in_dim(res, ((z + d) % zs) * chunk, chunk, 1)
        res_parts.append(shift(part, d, zs) if d else part)
    res = jnp.concatenate(res_parts, axis=0)
    at = jnp.arange(block, dtype=jnp.int32)
    source = ((z - at // (cs * rows_dev)) % zs) * cs + (c + at // rows_dev) % cs
    order = at[:, None] == (source * rows_dev + at % rows_dev)[None, :]
    res = jnp.dot(order.astype(BF16), res, preferred_element_type=F32)

    parts = exchange(parts.reshape(members, rows_dev, parts.shape[1]), MLP)
    parts = parts.reshape(members, rows_dev, heads // 7, 8, HD).astype(F32)
    st = parts[:, :, :, 7]
    tops, highs, lows = st[..., 0:7], st[..., 8:15], st[..., 16:23]
    scale = jnp.exp(tops - jnp.max(tops, axis=0, keepdims=True))
    total = jnp.sum(scale * (highs + lows), axis=0)
    weighted = jnp.sum(scale[..., None] * parts[:, :, :, :7], axis=0)
    attended = (weighted / total[..., None]).astype(BF16).reshape(rows_dev, width)

    feats = attended.reshape(rows_dev, zs, cs, members, k_dev).transpose(1, 2, 3, 0, 4)
    feats = jnp.stack(
        [
            jnp.concatenate([feats[(to - d) % zs] for d in range(zs)], axis=3)
            for to in range(zs)
        ]
    ).reshape(groups * members, rows_dev, zs * k_dev)
    feats, ups[2], down_other = lax.optimization_barrier((feats, ups[2], down_other))
    feats = exchange(feats, ALL)
    downs = reshard(*after((w_down, down_other), feats))
    feats = (
        feats.reshape(groups, members, rows_dev, zs * k_dev)
        .transpose(1, 0, 2, 3)
        .reshape(tokens, zs * k_dev)
    )
    wo_own, wo_pair = wo_parts[0], wo_parts[1]
    sent = pair(jnp.dot(feats, wo_pair, preferred_element_type=F32).astype(BF16))
    part = jnp.dot(feats, wo_own, preferred_element_type=F32) + sent.astype(F32)
    part = exchange(part.astype(BF16).reshape(members, block, chunk), MLP)
    gain = lax.dynamic_slice_in_dim(ln_gain, c * half + z * chunk, chunk, 0)

    hidden, row = pl.pallas_call(
        hidden_kernel,
        out_shape=(
            jax.ShapeDtypeStruct((block, chunk), F32),
            jax.ShapeDtypeStruct((block, chunk + HD), BF16),
        ),
        compiler_params=params(),
    )(part, res, gain[None])
    row, downs[1], downs[3] = lax.optimization_barrier((row, downs[1], downs[3]))
    rows = spread(row, MLP, members).reshape(tokens, chunk + HD)
    rows, downs[2] = lax.optimization_barrier((rows, downs[2]))

    both = jnp.broadcast_to(
        jnp.concatenate([keys_new, values_new], axis=1)[None], (members, rows_dev, 2 * width)
    )
    both = exchange(after(both, rows), MLP).reshape(group_rows, 2 * width)

    mine, theirs = up_project(rows, ups)
    theirs = pair(theirs)
    terms = []
    for d in range(zs):
        term = mine[d] + theirs[d].astype(F32)
        terms.append(shift(term.astype(BF16), -d, zs) if d else term)
    units = w_down.shape[0]
    act = pl.pallas_call(
        lambda *refs: act_kernel(width, units, zs, *refs),
        out_shape=jax.ShapeDtypeStruct((tokens, units), BF16),
        compiler_params=params(),
    )(*terms, gain_up)
    acts = [shift(act, d, zs) if d else act for d in range(zs)]
    down = down_project(acts, [pair(a) for a in acts], downs)
    down, both = lax.optimization_barrier((down, both))
    down = exchange(down.reshape(members, block, chunk), MLP)
    mixed = finish(down, hidden)
    mixed = exchange(mixed.reshape(groups, rows_dev, chunk), REQ)
    mixed = mixed.reshape(zs, cs, rows_dev, chunk).transpose(2, 1, 0, 3).reshape(rows_dev, width)

    valid = (accepted >= 0) & (dest_slot == member)[:, None]
    target = jnp.arange(requests, dtype=jnp.int32)[:, None] * tree_len + jnp.maximum(accepted, 0)
    chooser = jnp.any((target[:, :, None] == row_ids[None, None, :]) & valid[:, :, None], axis=0)
    picked = jnp.dot(chooser.astype(BF16), both, preferred_element_type=F32).astype(BF16)
    return (mixed, picked[:, :width][None], picked[:, width:][None])


def solution(mesh):
    groups, members = mesh.devices.shape
    side = math.isqrt(members)
    fine = Mesh(mesh.devices.reshape(groups // 2, 2, side, side), ALL)
    rows = P(ALL, None)
    pages = P(ALL, None, None)
    in_specs = (
        rows,
        rows,
        rows,
        rows,
        P(REQ, None, None),
        P(REQ),
        P(REQ, None),
        P(REQ),
        P(REQ, None),
        pages,
        pages,
        rows,
        P(None, ALL),
        rows,
        P(),
    )
    return jax.shard_map(
        local, mesh=fine, in_specs=in_specs, out_specs=(rows, pages, pages), check_vma=False
    )
```

time: 302 us -> 254 us (0.84)
  waiting for transfers between devices: 115 us -> 72.5 us
  starting transfers between devices: 89 us -> 79 us
  other arithmetic: 18.4 us -> 22 us
    all_to_all x4 -> x1, waiting for transfers between devices: 45.9 us -> 2.28 us  [spread(): lax.all_to_all(jnp.broadcast_to(x[None], (count,) + x.shape), axes, split...]
    all_to_all x4 -> x1, starting transfers between devices: 23.7 us -> 4.28 us  [spread(): lax.all_to_all(jnp.broadcast_to(x[None], (count,) + x.shape), axes, split...]
    all_to_all x5 -> x7, starting transfers between devices: 29.5 us -> 44.1 us  [exchange(): return lax.all_to_all(x, axes, split_axis=0, concat_axis=0)]
    all_to_all x5 -> x7, waiting for transfers between devices: 20.6 us -> 34.5 us  [exchange(): return lax.all_to_all(x, axes, split_axis=0, concat_axis=0)]
    ppermute x18, waiting for transfers between devices: 48.1 us -> 35.7 us  [shift(): return lax.ppermute(x, 'z', [(i, (i + step) % size) for i in range(size)])]
    pallas_call x1, Pallas kernels: 17.7 us -> 10.2 us  [attend(): pl.pallas_call(body, grid=(steps,), in_specs=[pl.BlockSpec((rows, wide),...]
    pallas_call x0 -> x4, Pallas kernels: none -> 6.95 us  [the longest x1 2.76 us: gain_products(): pl.pallas_call(gain_kernel, grid_spec=pltpu.PrefetchScalarGridSpec(num_sc...]
    broadcast_in_dim x4 -> x1, local copies, waits for them, and re-layouts: 5.55 us -> 0.98 us  [spread(): jnp.broadcast_to(x[None], (count,) + x.shape)]
  transfers between devices with their start and end apart: 36 -> 35, of which waited for: 11 -> 14; matrix products, arithmetic and copies ran while one was open for 18% -> 19% of each run, Pallas kernels for 1% -> 7%
where the time goes in v5:
time: 254 us; the launch traced here: 253 us
  starting transfers between devices  79 us (31%)
  waiting for transfers between devices  72.5 us (29%)
  local copies, waits for them, and re-layouts  48.6 us (19%)
  Pallas kernels  26 us (10%)
  other arithmetic  22 us (9%)
  matrix products  3.25 us (1%)
    all_to_all x7, starting transfers between devices, exchange(): return lax.all_to_all(x, axes, split_axis=0, concat_axis=0)  44.1 us
    ppermute x18, waiting for transfers between devices, shift(): return lax.ppermute(x, 'z', [(i, (i + step) % size) for i in range(size)])  35.7 us
    all_to_all x7, waiting for transfers between devices, exchange(): return lax.all_to_all(x, axes, split_axis=0, concat_axis=0)  34.5 us
    ppermute x18, starting transfers between devices, shift(): return lax.ppermute(x, 'z', [(i, (i + step) % size) for i in range(size)])  20 us
    unnamed x75, local copies, waits for them, and re-layouts  13.5 us
    ppermute x9, starting transfers between devices, pair(): return lax.ppermute(x, 'c', [(0, 1), (1, 0)])  10.6 us
    another operation x8, other arithmetic, reshard(): jnp.stack([piece(w, c, d), lax.dynamic_slice_in_dim(other, at, chunk, 1)])  10.5 us
    pallas_call x1, Pallas kernels, attend(): pl.pallas_call(body, grid=(steps,), in_specs=[pl.BlockSpec((rows, wide),...  10.2 us
  transfers between devices with their start and end apart: 35, of which 14 were waited for; matrix products, arithmetic and copies ran while one was open for 19% of the time, Pallas kernels for 7%

profile of v5, /device:TPU:1, one launch (start us, length us, event | category | flops | bytes accessed | tf_op | source)
XLA Modules:
  0.0 252.6 jit_solution(7907302177964091836)
XLA Ops:
  2.6 2.7 %constant_dynamic-slice_fusion.6 = bf16[224,3584]{1,0:T(8,128)(2,1)} fusion(bf16[224,7168]{1,0:T(8,128)(2,1)} %bitcast.133, s32[]{:T(128)S(6)} %select_n.236), kind=kLoop, calls=%fused_computation.103 | loop fusion | bytes 3211268 | tf_op jit(solution)/shard_map/dynamic_slice | solution.py:307
  6.8 7.1 %all-to-all-start = ((bf16[16,3,7168]{2,1,0:T(4,128)(2,1)}), bf16[16,3,7168]{2,1,0:T(4,128)(2,1)}, u32[]{:S(2)}, u32[]{:S(2)}) async-start(bf16[16,3,7168]{2,1,0:T(4,128)(2,1)} %broadcast_in_dim.20), calls=%async_computation | async-start | bytes 1835008 | tf_op jit(solution)/shard_map/all_to_all | solution.py:256
  16.1 3.8 %collective-permute-start.5 = (bf16[2,56,896]{2,1,0:T(8,128)(2,1)}, bf16[2,56,896]{2,1,0:T(8,128)(2,1)}, u32[]{:S(2)}, u32[]{:S(2)}) collective-permute-start(bf16[2,56,896]{2,1,0:T(8,128)(2,1)} %pad_maximum_fusion.11), channel_id=1, source_target_pairs={{0,96},{32,0},{64,32},{96,64},{1,97},{33,1},{65,33},{97,65},{2,98}... | collective-permute-start | bytes 602120 | tf_op jit(solution)/shard_map/ppermute | solution.py:88
  23.3 2.4 dynamic-slice_bitcast_fusion.2
  35.6 2.4 reshape.198.refs_0_
  38.0 10.2 %shard_map.166 = bf16[48,8192]{1,0:T(8,128)(2,1)} custom-call(bf16[48,7168]{1,0:T(8,128)(2,1)} %reshape.198.refs_0_, bf16[24,16,7168]{2,1,0:T(8,128)(2,1)} %refs_1_.1, bf16[24,16,7168]{2,1,0:T(8,128)(2,1)} %refs_2_.1, bf16[16,7168]{1,0:T(8,128)(2,1)} %pad.7.refs_3_, bf16[16,7168]{1,0:T(8,128)(2,1)} %pad.8.refs_4_, f32[48,400]{1,0:T(8,128)} %pad_maximum_fusion.14.refs_5_), custom_call_target="tpu_custom_call" | custom-call | flops 528482304 | bytes 11010048 | tf_op jit(solution)/shard_map/pallas_call | solution.py:61
  48.2 2.6 %collective-permute-done.1.refs_2_ = bf16[2,224,896]{2,1,0:T(8,128)(2,1)} collective-permute-done((bf16[2,224,896]{2,1,0:T(8,128)(2,1)}, bf16[2,224,896]{2,1,0:T(8,128)(2,1)}, u32[]{:S(2)}, u32[]{:S(2)}) %collective-permute-start.1) | collective-permute-done | bytes 802848 | tf_op jit(solution)/shard_map/ppermute | solution.py:88
  53.1 6.7 %all-to-all-start.1 = ((bf16[16,3,8192]{2,1,0:T(4,128)(2,1)}), bf16[16,3,8192]{2,1,0:T(4,128)(2,1)}, u32[]{:S(2)}, u32[]{:S(2)}) async-start(bf16[16,3,8192]{2,1,0:T(4,128)(2,1)} %reshape.200), calls=%async_computation.1 | async-start | bytes 2097152 | tf_op jit(solution)/shard_map/all_to_all | solution.py:256
  61.8 2.7 %constant_dynamic-slice_fusion.5 = bf16[224,3584]{1,0:T(8,128)(2,1)} fusion(bf16[224,7168]{1,0:T(8,128)(2,1)} %param.28, s32[]{:T(128)S(6)} %select_n.236), kind=kLoop, calls=%fused_computation.102 | loop fusion | bytes 3211268 | tf_op jit(solution)/shard_map/dynamic_slice | solution.py:307
  65.9 9.2 %all-to-all-done.1 = bf16[16,3,8192]{2,1,0:T(4,128)(2,1)} async-done(((bf16[16,3,8192]{2,1,0:T(4,128)(2,1)}), bf16[16,3,8192]{2,1,0:T(4,128)(2,1)}, u32[]{:S(2)}, u32[]{:S(2)}) %all-to-all-start.1) | async-done | bytes 786464 | tf_op jit(solution)/shard_map/all_to_all | solution.py:256
  78.6 3.6 %collective-permute-done.6.refs_3_ = bf16[2,224,896]{2,1,0:T(8,128)(2,1)} collective-permute-done((bf16[2,224,896]{2,1,0:T(8,128)(2,1)}, bf16[2,224,896]{2,1,0:T(8,128)(2,1)}, u32[]{:S(2)}, u32[]{:S(2)}) %collective-permute-start.6) | collective-permute-done | bytes 802848 | tf_op jit(solution)/shard_map/ppermute | solution.py:88
  83.2 8.5 %all-to-all-start.2 = ((bf16[128,3,224]{2,1,0:T(4,128)(2,1)}), bf16[128,3,224]{2,1,0:T(4,128)(2,1)}, u32[]{:S(2)}, u32[]{:S(2)}) async-start(bf16[128,3,224]{2,1,0:T(4,128)(2,1)} %copy.69), calls=%async_computation.2 | async-start | bytes 524288 | tf_op jit(solution)/shard_map/all_to_all | solution.py:256
  92.3 10.2 %all-to-all-done.2 = bf16[128,3,224]{2,1,0:T(4,128)(2,1)} async-done(((bf16[128,3,224]{2,1,0:T(4,128)(2,1)}), bf16[128,3,224]{2,1,0:T(4,128)(2,1)}, u32[]{:S(2)}, u32[]{:S(2)}) %all-to-all-start.2) | async-done | bytes 172064 | tf_op jit(solution)/shard_map/all_to_all | solution.py:256
  107.7 2.6 %dynamic-slice_bitcast_fusion = (bf16[1,224,896]{2,1,0:T(8,128)(2,1)}, bf16[1,224,896]{2,1,0:T(8,128)(2,1)}, bf16[1,224,896]{2,1,0:T(8,128)(2,1)S(1)}, bf16[1,224,896]{2,1,0:T(8,128)(2,1)S(1)}) fusion(bf16[224,3584]{1,0:T(8,128)(2,1)} %collective-permute-done.7, s32[]{:T(128)S(6)} %select_n.256, s32[]{:T(128)S(6)} %select_n.249, s32[]{:T(128)S(6)} %select_n.240, ...), kind=kLoop, calls=%fused_computation.18 | loop fusion | bytes 3211280 | tf_op jit(solution)/shard_map/stack | solution.py:313
  117.3 4.4 %all-to-all-start.3 = ((bf16[16,24,896]{2,1,0:T(8,128)(2,1)}), bf16[16,24,896]{2,1,0:T(8,128)(2,1)}, u32[]{:S(2)}, u32[]{:S(2)}) async-start(bf16[16,24,896]{2,1,0:T(8,128)(2,1)} %bitcast.142), calls=%async_computation.3 | async-start | bytes 1376256 | tf_op jit(solution)/shard_map/all_to_all | solution.py:256
  125.6 7.5 %collective-permute-done.12 = bf16[6,896]{1,0:T(8,128)(2,1)S(1)} collective-permute-done((bf16[6,896]{1,0:T(8,128)(2,1)S(1)}, bf16[6,896]{1,0:T(8,128)(2,1)S(1)}, u32[]{:S(2)}, u32[]{:S(2)}) %collective-permute-start.12) | collective-permute-done | bytes 10784 | tf_op jit(solution)/shard_map/ppermute | solution.py:88
  137.8 4.3 %all-to-all-start.4 = ((bf16[16,24,1024]{2,1,0:T(8,128)(2,1)}), bf16[16,24,1024]{2,1,0:T(8,128)(2,1)}, u32[]{:S(2)}, u32[]{:S(2)}) async-start(bf16[16,24,1024]{2,1,0:T(8,128)(2,1)} %broadcast_in_dim.25), calls=%async_computation.4 | async-start | bytes 1572864 | tf_op jit(solution)/shard_map/all_to_all | solution.py:250
  144.2 8.1 %collective-permute-done.15.refs_10_ = bf16[2,224,896]{2,1,0:T(8,128)(2,1)} collective-permute-done((bf16[2,224,896]{2,1,0:T(8,128)(2,1)}, bf16[2,224,896]{2,1,0:T(8,128)(2,1)}, u32[]{:S(2)}, u32[]{:S(2)}) %collective-permute-start.15) | collective-permute-done | bytes 802848 | tf_op jit(solution)/shard_map/ppermute | solution.py:88
  155.8 4.6 %shard_map.168 = (f32[4,384,256]{2,1,0:T(8,128)S(1)}, bf16[4,384,256]{2,1,0:T(8,128)(2,1)}) custom-call(bf16[384,1024]{1,0:T(8,128)(2,1)} %bitcast.40.refs_0_, bf16[2,224,896]{2,1,0:T(8,128)(2,1)S(1)} %copy-done.1, bf16[2,224,896]{2,1,0:T(8,128)(2,1)} %collective-permute-done.1.refs_2_, bf16[2,224,896]{2,1,0:T(8,128)(2,1)} %collective-permute-done.6.refs_3_, ...), custom_call_target="tpu_custom_call" | custom-call | tf_op jit(solution)/shard_map/pallas_call | solution.py:213
  161.6 2.7 %collective-permute-start.16 = (bf16[4,384,256]{2,1,0:T(8,128)(2,1)}, bf16[4,384,256]{2,1,0:T(8,128)(2,1)}, u32[]{:S(2)}, u32[]{:S(2)}) collective-permute-start(bf16[4,384,256]{2,1,0:T(8,128)(2,1)} %get-tuple-element.45), channel_id=1, source_target_pairs={{0,16},{16,0},{1,17},{17,1},{2,18},{18,2},{3,19},{19,3},{4,20},{20... | collective-permute-start | bytes 2359304 | tf_op jit(solution)/shard_map/ppermute | solution.py:84
  166.3 4.4 %all-to-all-start.5 = ((bf16[16,3,14336]{2,1,0:T(4,128)(2,1)}), bf16[16,3,14336]{2,1,0:T(4,128)(2,1)}, u32[]{:S(2)}, u32[]{:S(2)}) async-start(bf16[16,3,14336]{2,1,0:T(4,128)(2,1)} %broadcast_in_dim.27), calls=%async_computation.5 | async-start | bytes 3670016 | tf_op jit(solution)/shard_map/all_to_all | solution.py:256
  170.8 2.6 %fusion.10 = (bf16[384,256]{1,0:T(8,128)(2,1)}, bf16[384,256]{1,0:T(8,128)(2,1)}, bf16[384,256]{1,0:T(8,128)(2,1)}, f32[384,256]{1,0:T(8,128)}) fusion(f32[4,384,256]{2,1,0:T(8,128)} %copy-done.3, bf16[4,384,256]{2,1,0:T(8,128)(2,1)} %collective-permute-done.16), kind=kLoop, calls=%fused_computation.48 | loop fusion | flops 1081344 | bytes 3342336 | tf_op jit(solution)/shard_map/convert_element_type | solution.py:425
  177.2 2.8 %shard_map.169.refs_4_ = f32[8,8,224]{2,1,0:T(8,128)S(1)} custom-call(s32[8]{0:T(128)S(1)} %stack.208.place, f32[1,7168]{1,0:T(1,128)S(1)} %bitcast.136, bf16[224,7168]{1,0:T(8,128)(2,1)S(1)} %bitcast.135), custom_call_target="tpu_custom_call" | custom-call | tf_op jit(solution)/shard_map/pallas_call | solution.py:194
  182.8 4.8 %collective-permute-done.19.refs_3_ = bf16[384,256]{1,0:T(8,128)(2,1)} collective-permute-done((bf16[384,256]{1,0:T(8,128)(2,1)}, bf16[384,256]{1,0:T(8,128)(2,1)}, u32[]{:S(2)}, u32[]{:S(2)}) %collective-permute-start.19) | collective-permute-done | bytes 196640 | tf_op jit(solution)/shard_map/ppermute | solution.py:88
  188.5 2.7 %shard_map.170.refs_0_ = bf16[384,224]{1,0:T(8,128)(2,1)S(1)} custom-call(f32[384,256]{1,0:T(8,128)S(1)} %copy-done.2, bf16[384,256]{1,0:T(8,128)(2,1)S(1)} %copy-done.5, bf16[384,256]{1,0:T(8,128)(2,1)} %collective-permute-done.18.refs_2_, bf16[384,256]{1,0:T(8,128)(2,1)} %collective-permute-done.19.refs_3_, f32[8,8,224]{2,1,0:T(8,128)S(1)} %shard_map.169.refs_4_), custom_call_target="tpu_custom_call" | custom-call | tf_op jit(solution)/shard_map/pallas_call | solution.py:427
  196.2 6.5 %collective-permute-done.20.refs_1_ = bf16[384,224]{1,0:T(8,128)(2,1)S(1)} collective-permute-done((bf16[384,224]{1,0:T(8,128)(2,1)S(1)}, bf16[384,224]{1,0:T(8,128)(2,1)S(1)}, u32[]{:S(2)}, u32[]{:S(2)}) %collective-permute-start.20) | collective-permute-done | bytes 172064 | tf_op jit(solution)/shard_map/ppermute | solution.py:88
  204.9 3.2 %reshape.207 = bf16[48,14336]{1,0:T(8,128)(2,1)} reshape(bf16[16,3,14336]{2,1,0:T(4,128)(2,1)} %all-to-all-done.5) | data formatting | bytes 2752512 | tf_op jit(solution)/shard_map/reshape | solution.py:418
  217.3 4.3 %shard_map.171 = bf16[384,896]{1,0:T(8,128)(2,1)} custom-call(bf16[384,224]{1,0:T(8,128)(2,1)S(1)} %shard_map.170.refs_0_, bf16[384,224]{1,0:T(8,128)(2,1)S(1)} %copy-done.7, bf16[384,224]{1,0:T(8,128)(2,1)S(1)} %copy-done.9, bf16[384,224]{1,0:T(8,128)(2,1)S(1)} %copy-done.11, bf16[384,224]{1,0:T(8,128)(2,1)S(1)} %copy-done.13, ...), custom_call_target="tpu_custom_call" | custom-call | tf_op jit(solution)/shard_map/pallas_call | solution.py:225
  221.6 6.7 %all-to-all-start.6 = ((bf16[16,24,896]{2,1,0:T(8,128)(2,1)}), bf16[16,24,896]{2,1,0:T(8,128)(2,1)S(1)}, u32[]{:S(2)}, u32[]{:S(2)}) async-start(bf16[16,24,896]{2,1,0:T(8,128)(2,1)} %bitcast.60), calls=%async_computation.6 | async-start | bytes 1376256 | tf_op jit(solution)/shard_map/all_to_all | solution.py:256
  228.7 11.2 %all-to-all-done.6.parts = bf16[16,24,896]{2,1,0:T(8,128)(2,1)S(1)} async-done(((bf16[16,24,896]{2,1,0:T(8,128)(2,1)}), bf16[16,24,896]{2,1,0:T(8,128)(2,1)S(1)}, u32[]{:S(2)}, u32[]{:S(2)}) %all-to-all-start.6) | async-done | bytes 688160 | tf_op jit(solution)/shard_map/all_to_all | solution.py:256
  240.7 6.3 %all-to-all-start.7 = ((bf16[8,3,896]{2,1,0:T(4,128)(2,1)}), bf16[8,3,896]{2,1,0:T(4,128)(2,1)S(1)}, u32[]{:S(2)}, u32[]{:S(2)}) async-start(bf16[8,3,896]{2,1,0:T(4,128)(2,1)} %reshape.209), calls=%async_computation.7 | async-start | bytes 114688 | tf_op jit(solution)/shard_map/all_to_all | solution.py:256
  247.9 4.0 %all-to-all-done.7 = bf16[8,3,896]{2,1,0:T(4,128)(2,1)S(1)} async-done(((bf16[8,3,896]{2,1,0:T(4,128)(2,1)}), bf16[8,3,896]{2,1,0:T(4,128)(2,1)S(1)}, u32[]{:S(2)}, u32[]{:S(2)}) %all-to-all-start.7) | async-done | bytes 43040 | tf_op jit(solution)/shard_map/all_to_all | solution.py:256
  (201 shorter events, 85.6 us)
Async XLA Ops:
  5.3 17.9 %collective-permute-start = (bf16[224,3584]{1,0:T(8,128)(2,1)}, bf16[224,3584]{1,0:T(8,128)(2,1)}, u32[]{:S(2)}, u32[]{:S(2)}) collective-permute-start(bf16[224,3584]{1,0:T(8,128)(2,1)} %constant_dynamic-slice_fusion.6), channel_id=1, source_target_pairs={{0,16},{16,0},{1,17},{17,1},{2,18},{18,2},{3,19},{19,3},{4,20},{20... | collective-permute-start | bytes 4816904 | tf_op jit(solution)/shard_map/ppermute | solution.py:84
  6.8 28.9 %all-to-all-start = ((bf16[16,3,7168]{2,1,0:T(4,128)(2,1)}), bf16[16,3,7168]{2,1,0:T(4,128)(2,1)}, u32[]{:S(2)}, u32[]{:S(2)}) async-start(bf16[16,3,7168]{2,1,0:T(4,128)(2,1)} %broadcast_in_dim.20), calls=%async_computation | async-start | bytes 1835008 | tf_op jit(solution)/shard_map/all_to_all | solution.py:256
  16.1 17.3 %collective-permute-start.5 = (bf16[2,56,896]{2,1,0:T(8,128)(2,1)}, bf16[2,56,896]{2,1,0:T(8,128)(2,1)}, u32[]{:S(2)}, u32[]{:S(2)}) collective-permute-start(bf16[2,56,896]{2,1,0:T(8,128)(2,1)} %pad_maximum_fusion.11), channel_id=1, source_target_pairs={{0,96},{32,0},{64,32},{96,64},{1,97},{33,1},{65,33},{97,65},{2,98}... | collective-permute-start | bytes 602120 | tf_op jit(solution)/shard_map/ppermute | solution.py:88
  20.5 12.8 %collective-permute-start.4 = (bf16[2,56,896]{2,1,0:T(8,128)(2,1)}, bf16[2,56,896]{2,1,0:T(8,128)(2,1)}, u32[]{:S(2)}, u32[]{:S(2)}) collective-permute-start(bf16[2,56,896]{2,1,0:T(8,128)(2,1)} %pad_maximum_fusion.10), channel_id=1, source_target_pairs={{0,64},{32,96},{64,0},{96,32},{1,65},{33,97},{65,1},{97,33},{2,66}... | collective-permute-start | bytes 602120 | tf_op jit(solution)/shard_map/ppermute | solution.py:88
  21.2 12.3 %collective-permute-start.3 = (bf16[2,56,896]{2,1,0:T(8,128)(2,1)}, bf16[2,56,896]{2,1,0:T(8,128)(2,1)}, u32[]{:S(2)}, u32[]{:S(2)}) collective-permute-start(bf16[2,56,896]{2,1,0:T(8,128)(2,1)} %pad_maximum_fusion.9), channel_id=1, source_target_pairs={{0,32},{32,64},{64,96},{96,0},{1,33},{33,65},{65,97},{97,1},{2,34}... | collective-permute-start | bytes 602120 | tf_op jit(solution)/shard_map/ppermute | solution.py:88
  26.7 24.1 %collective-permute-start.1 = (bf16[2,224,896]{2,1,0:T(8,128)(2,1)}, bf16[2,224,896]{2,1,0:T(8,128)(2,1)}, u32[]{:S(2)}, u32[]{:S(2)}) collective-permute-start(bf16[2,224,896]{2,1,0:T(8,128)(2,1)} %pad_maximum_fusion), channel_id=1, source_target_pairs={{0,32},{32,64},{64,96},{96,0},{1,33},{33,65},{65,97},{97,1},{2,34}... | collective-permute-start | bytes 2408456 | tf_op jit(solution)/shard_map/ppermute | solution.py:88
  29.7 21.1 %collective-permute-start.2 = (bf16[2,224,896]{2,1,0:T(8,128)(2,1)}, bf16[2,224,896]{2,1,0:T(8,128)(2,1)}, u32[]{:S(2)}, u32[]{:S(2)}) collective-permute-start(bf16[2,224,896]{2,1,0:T(8,128)(2,1)} %pad_maximum_fusion.1), channel_id=1, source_target_pairs={{0,96},{32,0},{64,32},{96,64},{1,97},{33,1},{65,33},{97,65},{2,98}... | collective-permute-start | bytes 2408456 | tf_op jit(solution)/shard_map/ppermute | solution.py:88
  53.1 21.9 %all-to-all-start.1 = ((bf16[16,3,8192]{2,1,0:T(4,128)(2,1)}), bf16[16,3,8192]{2,1,0:T(4,128)(2,1)}, u32[]{:S(2)}, u32[]{:S(2)}) async-start(bf16[16,3,8192]{2,1,0:T(4,128)(2,1)} %reshape.200), calls=%async_computation.1 | async-start | bytes 2097152 | tf_op jit(solution)/shard_map/all_to_all | solution.py:256
  61.8 20.5 %collective-permute-start.6 = (bf16[2,224,896]{2,1,0:T(8,128)(2,1)}, bf16[2,224,896]{2,1,0:T(8,128)(2,1)}, u32[]{:S(2)}, u32[]{:S(2)}) collective-permute-start(bf16[2,224,896]{2,1,0:T(8,128)(2,1)} %pad_maximum_fusion.3), channel_id=1, source_target_pairs={{0,64},{32,96},{64,0},{96,32},{1,65},{33,97},{65,1},{97,33},{2,66}... | collective-permute-start | bytes 2408456 | tf_op jit(solution)/shard_map/ppermute | solution.py:88
  64.5 17.8 %collective-permute-start.7 = (bf16[224,3584]{1,0:T(8,128)(2,1)}, bf16[224,3584]{1,0:T(8,128)(2,1)}, u32[]{:S(2)}, u32[]{:S(2)}) collective-permute-start(bf16[224,3584]{1,0:T(8,128)(2,1)} %constant_dynamic-slice_fusion.5), channel_id=1, source_target_pairs={{0,16},{16,0},{1,17},{17,1},{2,18},{18,2},{3,19},{19,3},{4,20},{20... | collective-permute-start | bytes 4816904 | tf_op jit(solution)/shard_map/ppermute | solution.py:84
  83.2 19.3 %all-to-all-start.2 = ((bf16[128,3,224]{2,1,0:T(4,128)(2,1)}), bf16[128,3,224]{2,1,0:T(4,128)(2,1)}, u32[]{:S(2)}, u32[]{:S(2)}) async-start(bf16[128,3,224]{2,1,0:T(4,128)(2,1)} %copy.69), calls=%async_computation.2 | async-start | bytes 524288 | tf_op jit(solution)/shard_map/all_to_all | solution.py:256
  106.7 9.4 %collective-permute-start.8 = (bf16[384,896]{1,0:T(8,128)(2,1)S(1)}, bf16[384,896]{1,0:T(8,128)(2,1)S(1)}, u32[]{:S(2)}, u32[]{:S(2)}) collective-permute-start(bf16[384,896]{1,0:T(8,128)(2,1)S(1)} %convolution_convert_fusion.1), channel_id=1, source_target_pairs={{0,16},{16,0},{1,17},{17,1},{2,18},{18,2},{3,19},{19,3},{4,20},{20... | collective-permute-start | bytes 2064392 | tf_op jit(solution)/shard_map/ppermute | solution.py:84
  107.6 14.1 %collective-permute-start.9 = (bf16[3,3584]{1,0:T(4,128)(2,1)S(1)}, bf16[3,3584]{1,0:T(4,128)(2,1)S(1)}, u32[]{:S(2)}, u32[]{:S(2)}) collective-permute-start(bf16[3,3584]{1,0:T(4,128)(2,1)S(1)} %get-tuple-element.98), channel_id=1, source_target_pairs={{0,16},{16,0},{1,17},{17,1},{2,18},{18,2},{3,19},{19,3},{4,20},{20... | collective-permute-start | bytes 64520 | tf_op jit(solution)/shard_map/ppermute | solution.py:84
  112.4 24.3 %collective-permute-start.13 = (bf16[2,224,896]{2,1,0:T(8,128)(2,1)}, bf16[2,224,896]{2,1,0:T(8,128)(2,1)}, u32[]{:S(2)}, u32[]{:S(2)}) collective-permute-start(bf16[2,224,896]{2,1,0:T(8,128)(2,1)} %pad_maximum_fusion.4), channel_id=1, source_target_pairs={{0,32},{32,64},{64,96},{96,0},{1,33},{33,65},{65,97},{97,1},{2,34}... | collective-permute-start | bytes 2408456 | tf_op jit(solution)/shard_map/ppermute | solution.py:88
  113.9 22.9 %collective-permute-start.14 = (bf16[2,224,896]{2,1,0:T(8,128)(2,1)}, bf16[2,224,896]{2,1,0:T(8,128)(2,1)}, u32[]{:S(2)}, u32[]{:S(2)}) collective-permute-start(bf16[2,224,896]{2,1,0:T(8,128)(2,1)} %pad_maximum_fusion.5), channel_id=1, source_target_pairs={{0,96},{32,0},{64,32},{96,64},{1,97},{33,1},{65,33},{97,65},{2,98}... | collective-permute-start | bytes 2408456 | tf_op jit(solution)/shard_map/ppermute | solution.py:88
  117.3 18.1 %all-to-all-start.3 = ((bf16[16,24,896]{2,1,0:T(8,128)(2,1)}), bf16[16,24,896]{2,1,0:T(8,128)(2,1)}, u32[]{:S(2)}, u32[]{:S(2)}) async-start(bf16[16,24,896]{2,1,0:T(8,128)(2,1)} %bitcast.142), calls=%async_computation.3 | async-start | bytes 1376256 | tf_op jit(solution)/shard_map/all_to_all | solution.py:256
  121.9 11.2 %collective-permute-start.12 = (bf16[6,896]{1,0:T(8,128)(2,1)S(1)}, bf16[6,896]{1,0:T(8,128)(2,1)S(1)}, u32[]{:S(2)}, u32[]{:S(2)}) collective-permute-start(bf16[6,896]{1,0:T(8,128)(2,1)S(1)} %get-tuple-element.94), channel_id=1, source_target_pairs={{0,96},{32,0},{64,32},{96,64},{1,97},{33,1},{65,33},{97,65},{2,98}... | collective-permute-start | bytes 32264 | tf_op jit(solution)/shard_map/ppermute | solution.py:88
  121.9 13.3 %collective-permute-start.11 = (bf16[6,896]{1,0:T(8,128)(2,1)S(1)}, bf16[6,896]{1,0:T(8,128)(2,1)S(1)}, u32[]{:S(2)}, u32[]{:S(2)}) collective-permute-start(bf16[6,896]{1,0:T(8,128)(2,1)S(1)} %get-tuple-element.95), channel_id=1, source_target_pairs={{0,64},{32,96},{64,0},{96,32},{1,65},{33,97},{65,1},{97,33},{2,66}... | collective-permute-start | bytes 32264 | tf_op jit(solution)/shard_map/ppermute | solution.py:88
  123.0 12.2 %collective-permute-start.10 = (bf16[6,896]{1,0:T(8,128)(2,1)S(1)}, bf16[6,896]{1,0:T(8,128)(2,1)S(1)}, u32[]{:S(2)}, u32[]{:S(2)}) collective-permute-start(bf16[6,896]{1,0:T(8,128)(2,1)S(1)} %get-tuple-element.96), channel_id=1, source_target_pairs={{0,32},{32,64},{64,96},{96,0},{1,33},{33,65},{65,97},{97,1},{2,34}... | collective-permute-start | bytes 32264 | tf_op jit(solution)/shard_map/ppermute | solution.py:88
  133.1 19.3 %collective-permute-start.15 = (bf16[2,224,896]{2,1,0:T(8,128)(2,1)}, bf16[2,224,896]{2,1,0:T(8,128)(2,1)}, u32[]{:S(2)}, u32[]{:S(2)}) collective-permute-start(bf16[2,224,896]{2,1,0:T(8,128)(2,1)} %pad_maximum_fusion.6), channel_id=1, source_target_pairs={{0,64},{32,96},{64,0},{96,32},{1,65},{33,97},{65,1},{97,33},{2,66}... | collective-permute-start | bytes 2408456 | tf_op jit(solution)/shard_map/ppermute | solution.py:88
  137.8 16.8 %all-to-all-start.4 = ((bf16[16,24,1024]{2,1,0:T(8,128)(2,1)}), bf16[16,24,1024]{2,1,0:T(8,128)(2,1)}, u32[]{:S(2)}, u32[]{:S(2)}) async-start(bf16[16,24,1024]{2,1,0:T(8,128)(2,1)} %broadcast_in_dim.25), calls=%async_computation.4 | async-start | bytes 1572864 | tf_op jit(solution)/shard_map/all_to_all | solution.py:250
  161.6 9.2 %collective-permute-start.16 = (bf16[4,384,256]{2,1,0:T(8,128)(2,1)}, bf16[4,384,256]{2,1,0:T(8,128)(2,1)}, u32[]{:S(2)}, u32[]{:S(2)}) collective-permute-start(bf16[4,384,256]{2,1,0:T(8,128)(2,1)} %get-tuple-element.45), channel_id=1, source_target_pairs={{0,16},{16,0},{1,17},{17,1},{2,18},{18,2},{3,19},{19,3},{4,20},{20... | collective-permute-start | bytes 2359304 | tf_op jit(solution)/shard_map/ppermute | solution.py:84
  166.3 38.5 %all-to-all-start.5 = ((bf16[16,3,14336]{2,1,0:T(4,128)(2,1)}), bf16[16,3,14336]{2,1,0:T(4,128)(2,1)}, u32[]{:S(2)}, u32[]{:S(2)}) async-start(bf16[16,3,14336]{2,1,0:T(4,128)(2,1)} %broadcast_in_dim.27), calls=%async_computation.5 | async-start | bytes 3670016 | tf_op jit(solution)/shard_map/all_to_all | solution.py:256
  173.4 7.5 %collective-permute-start.17 = (bf16[384,256]{1,0:T(8,128)(2,1)}, bf16[384,256]{1,0:T(8,128)(2,1)S(1)}, u32[]{:S(2)}, u32[]{:S(2)}) collective-permute-start(bf16[384,256]{1,0:T(8,128)(2,1)} %get-tuple-element.65), channel_id=1, source_target_pairs={{0,96},{32,0},{64,32},{96,64},{1,97},{33,1},{65,33},{97,65},{2,98}... | collective-permute-start | bytes 589832 | tf_op jit(solution)/shard_map/ppermute | solution.py:88
  174.8 8.0 %collective-permute-start.18 = (bf16[384,256]{1,0:T(8,128)(2,1)}, bf16[384,256]{1,0:T(8,128)(2,1)}, u32[]{:S(2)}, u32[]{:S(2)}) collective-permute-start(bf16[384,256]{1,0:T(8,128)(2,1)} %get-tuple-element.64), channel_id=1, source_target_pairs={{0,64},{32,96},{64,0},{96,32},{1,65},{33,97},{65,1},{97,33},{2,66}... | collective-permute-start | bytes 589832 | tf_op jit(solution)/shard_map/ppermute | solution.py:88
  177.1 10.5 %collective-permute-start.19 = (bf16[384,256]{1,0:T(8,128)(2,1)}, bf16[384,256]{1,0:T(8,128)(2,1)}, u32[]{:S(2)}, u32[]{:S(2)}) collective-permute-start(bf16[384,256]{1,0:T(8,128)(2,1)} %get-tuple-element.63), channel_id=1, source_target_pairs={{0,32},{32,64},{64,96},{96,0},{1,33},{33,65},{65,97},{97,1},{2,34}... | collective-permute-start | bytes 589832 | tf_op jit(solution)/shard_map/ppermute | solution.py:88
  191.2 11.5 %collective-permute-start.20 = (bf16[384,224]{1,0:T(8,128)(2,1)S(1)}, bf16[384,224]{1,0:T(8,128)(2,1)S(1)}, u32[]{:S(2)}, u32[]{:S(2)}) collective-permute-start(bf16[384,224]{1,0:T(8,128)(2,1)S(1)} %shard_map.170.refs_0_), channel_id=1, source_target_pairs={{0,32},{32,64},{64,96},{96,0},{1,33},{33,65},{65,97},{97,1},{2,34}... | collective-permute-start | bytes 516104 | tf_op jit(solution)/shard_map/ppermute | solution.py:88
  191.6 12.5 %collective-permute-start.21 = (bf16[384,224]{1,0:T(8,128)(2,1)S(1)}, bf16[384,224]{1,0:T(8,128)(2,1)S(1)}, u32[]{:S(2)}, u32[]{:S(2)}) collective-permute-start(bf16[384,224]{1,0:T(8,128)(2,1)S(1)} %shard_map.170.refs_0_), channel_id=1, source_target_pairs={{0,64},{32,96},{64,0},{96,32},{1,65},{33,97},{65,1},{97,33},{2,66}... | collective-permute-start | bytes 516104 | tf_op jit(solution)/shard_map/ppermute | solution.py:88
  192.4 11.8 %collective-permute-start.22 = (bf16[384,224]{1,0:T(8,128)(2,1)S(1)}, bf16[384,224]{1,0:T(8,128)(2,1)S(1)}, u32[]{:S(2)}, u32[]{:S(2)}) collective-permute-start(bf16[384,224]{1,0:T(8,128)(2,1)S(1)} %shard_map.170.refs_0_), channel_id=1, source_target_pairs={{0,96},{32,0},{64,32},{96,64},{1,97},{33,1},{65,33},{97,65},{2,98}... | collective-permute-start | bytes 516104 | tf_op jit(solution)/shard_map/ppermute | solution.py:88
  194.0 14.0 %collective-permute-start.23 = (bf16[384,224]{1,0:T(8,128)(2,1)S(1)}, bf16[384,224]{1,0:T(8,128)(2,1)S(1)}, u32[]{:S(2)}, u32[]{:S(2)}) collective-permute-start(bf16[384,224]{1,0:T(8,128)(2,1)S(1)} %shard_map.170.refs_0_), channel_id=1, source_target_pairs={{0,16},{16,0},{1,17},{17,1},{2,18},{18,2},{3,19},{19,3},{4,20},{20... | collective-permute-start | bytes 516104 | tf_op jit(solution)/shard_map/ppermute | solution.py:84
  221.6 18.3 %all-to-all-start.6 = ((bf16[16,24,896]{2,1,0:T(8,128)(2,1)}), bf16[16,24,896]{2,1,0:T(8,128)(2,1)S(1)}, u32[]{:S(2)}, u32[]{:S(2)}) async-start(bf16[16,24,896]{2,1,0:T(8,128)(2,1)} %bitcast.60), calls=%async_computation.6 | async-start | bytes 1376256 | tf_op jit(solution)/shard_map/all_to_all | solution.py:256
  240.7 11.2 %all-to-all-start.7 = ((bf16[8,3,896]{2,1,0:T(4,128)(2,1)}), bf16[8,3,896]{2,1,0:T(4,128)(2,1)S(1)}, u32[]{:S(2)}, u32[]{:S(2)}) async-start(bf16[8,3,896]{2,1,0:T(4,128)(2,1)} %reshape.209), calls=%async_computation.7 | async-start | bytes 114688 | tf_op jit(solution)/shard_map/all_to_all | solution.py:256
  (40 other events, 283.4 us)

commit v6 on v5

--- a/solution.py
+++ b/solution.py
@@ -120,22 +120,34 @@
     row_out[:, chunk:] = stats.astype(BF16)
 
 
+def fetch(sources, buffer, sems):
+    copies = []
+    for d, source in enumerate(sources):
+        copies.append(pltpu.make_async_copy(source, buffer.at[d], sems.at[d]))
+        copies[-1].start()
+    return copies
+
+
 def up_kernel(n, *refs):
     rows = refs[0]
-    chunk = refs[1].shape[2]
+    outs = refs[n + 1 : n + 3]
+    buffer = refs[n + 3]
+    copies = fetch(refs[1 : n + 1], buffer, refs[n + 4])
+    chunk = buffer.shape[3]
+    wide = outs[0].shape[2]
     g = rows[:, :chunk]
     st = rows[:, chunk:].astype(F32)
     lane = lax.broadcasted_iota(jnp.int32, st.shape, 1)
     st = jnp.where(lane < 6, st, 0.0)
     none = jnp.zeros_like(st)
+    beside = [jnp.concatenate([none, pltpu.roll(st, by, 1)], axis=1) for by in (102, 96)]
     for d in range(n):
+        copies[d].wait()
         for e in range(2):
-            w = refs[1 + d][e]
-            wide = refs[n + 1].shape[2]
+            w = buffer[d, e]
             w = jnp.concatenate([w, jnp.zeros((wide - w.shape[0], chunk), BF16)], axis=0)
             got = lax.dot_general(g, w, DN, preferred_element_type=F32)
-            beside = jnp.concatenate([none, pltpu.roll(st, 96 if e else 102, 1)], axis=1)
-            refs[n + 1 + e][d] = (got + beside).astype(refs[n + 1 + e].dtype)
+            outs[e][d] = (got + beside[e]).astype(BF16)
 
 
 def act_kernel(width, units, n, *refs):
@@ -162,10 +174,13 @@
 
 
 def down_kernel(n, *refs):
+    buffer = refs[3 * n + 1]
+    copies = fetch(refs[2 * n : 3 * n], buffer, refs[3 * n + 2])
     total = None
     for d in range(n):
+        copies[d].wait()
         for e in range(2):
-            term = jnp.dot(refs[e * n + d][...], refs[2 * n + d][e], preferred_element_type=F32)
+            term = jnp.dot(refs[e * n + d][...], buffer[d, e], preferred_element_type=F32)
             total = term if total is None else total + term
     refs[3 * n][...] = total.astype(BF16)
 
@@ -184,8 +199,36 @@
         out[...] = total[...].astype(BF16)
 
 
-def params():
-    return pltpu.CompilerParams(vmem_limit_bytes=32 * 1024 * 1024)
+def params(mib=32):
+    return pltpu.CompilerParams(vmem_limit_bytes=mib * 1024 * 1024)
+
+
+def cut_kernel(n, spots, a, b, *outs):
+    for d in range(n):
+
+        @pl.when(pl.program_id(0) == d)
+        def _():
+            outs[d][0] = a[...]
+            outs[d][1] = b[...]
+
+
+def cut(spots, a, b, n, chunk):
+    rows = a.shape[0]
+    whole = pl.BlockSpec((2, rows, chunk), lambda i, spots: (0, 0, 0))
+    return pl.pallas_call(
+        lambda *refs: cut_kernel(n, *refs),
+        grid_spec=pltpu.PrefetchScalarGridSpec(
+            num_scalar_prefetch=1,
+            grid=(n,),
+            in_specs=[
+                pl.BlockSpec((rows, chunk), lambda i, spots: (0, spots[i])),
+                pl.BlockSpec((rows, chunk), lambda i, spots: (0, spots[n + i])),
+            ],
+            out_specs=[whole] * n,
+        ),
+        out_shape=[jax.ShapeDtypeStruct((2, rows, chunk), BF16)] * n,
+        compiler_params=params(),
+    )(spots, a, b)
 
 
 def gain_products(order, gain, weight, chunk):
@@ -207,25 +250,36 @@
     )(order, gain, weight)
 
 
+def weight_specs(weights):
+    n = len(weights)
+    return (
+        [pl.BlockSpec(memory_space=pltpu.HBM)] * n,
+        [pltpu.VMEM((n,) + weights[0].shape, BF16), pltpu.SemaphoreType.DMA((n,))],
+    )
+
+
 def up_project(rows, weights):
     n = len(weights)
     tokens = rows.shape[0]
+    specs, scratch = weight_specs(weights)
     return pl.pallas_call(
         lambda *refs: up_kernel(n, *refs),
-        out_shape=(
-            jax.ShapeDtypeStruct((n, tokens, 256), F32),
-            jax.ShapeDtypeStruct((n, tokens, 256), BF16),
-        ),
-        compiler_params=params(),
+        in_specs=[pl.BlockSpec(memory_space=pltpu.VMEM)] + specs,
+        out_shape=[jax.ShapeDtypeStruct((n, tokens, 256), BF16)] * 2,
+        scratch_shapes=scratch,
+        compiler_params=params(24),
     )(rows, *weights)
 
 
 def down_project(own, other, weights):
     n = len(weights)
+    specs, scratch = weight_specs(weights)
     return pl.pallas_call(
         lambda *refs: down_kernel(n, *refs),
+        in_specs=[pl.BlockSpec(memory_space=pltpu.VMEM)] * (2 * n) + specs,
         out_shape=jax.ShapeDtypeStruct((own[0].shape[0], weights[0].shape[2]), BF16),
-        compiler_params=params(),
+        scratch_shapes=scratch,
+        compiler_params=params(24),
     )(*own, *other, *weights)
 
 
@@ -292,30 +346,27 @@
     wide_q = jnp.broadcast_to(queries[None], (members,) + queries.shape)
     group_q = exchange(wide_q, MLP).reshape(group_rows, width)
 
-    def piece(w, core, d):
-        return lax.dynamic_slice_in_dim(w, core * half + ((z + d) % zs) * chunk, chunk, 1)
+    turn = (z + jnp.arange(zs, dtype=jnp.int32)) % zs
+    own_turn, other_turn = c * zs + turn, (1 - c) * zs + turn
+
+    def send(pieces):
+        return [shift(p, d, zs) if d else p for d, p in enumerate(pieces)]
 
     k_dev = w_out.shape[0]
     wo = after(w_out, wide_q)
-    wo_parts = []
-    for d in range(zs):
-        part = jnp.stack([piece(wo, c, d), piece(wo, 1 - c, d)])
-        wo_parts.append(shift(part, d, zs) if d else part)
+    wo_parts = send(cut(jnp.concatenate([own_turn, other_turn]), wo, wo, zs, chunk))
     wo_parts = jnp.concatenate(wo_parts, axis=1)
 
     def swap(w):
         return pair(lax.dynamic_slice_in_dim(w, (1 - c) * half, half, 1))
 
     def reshard(w, other):
-        split = []
-        for d in range(zs):
-            at = ((z + d) % zs) * chunk
-            part = jnp.stack([piece(w, c, d), lax.dynamic_slice_in_dim(other, at, chunk, 1)])
-            split.append(shift(part, d, zs) if d else part)
-        return split
-
-    up_w = w_up.T
-    up_w = after(up_w, wide_q)
+        return send(cut(jnp.concatenate([own_turn, turn]), w, other, zs, chunk))
+
+    def swap(w):
+        return pair(lax.dynamic_slice_in_dim(w, (1 - c) * half, half, 1))
+
+    up_w = after(w_up.T, wide_q)
     ups = reshard(up_w, swap(up_w))
     order = jnp.stack(
         [(c + e) % cs * zs + (z + d) % zs for d in range(zs) for e in range(cs)]
@@ -350,7 +401,9 @@
         heads // 7,
     )
 
-    parts, ups[1], ups[3], wo_parts = lax.optimization_barrier((parts, ups[1], ups[3], wo_parts))
+    parts, ups[1], ups[3], wo_parts, gain_up = lax.optimization_barrier(
+        (parts, ups[1], ups[3], wo_parts, gain_up)
+    )
     down_other = swap(after(w_down, parts))
 
     res = after(resid, parts)
@@ -386,9 +439,13 @@
             for to in range(zs)
         ]
     ).reshape(groups * members, rows_dev, zs * k_dev)
-    feats, ups[2], down_other = lax.optimization_barrier((feats, ups[2], down_other))
+    both = jnp.broadcast_to(
+        jnp.concatenate([keys_new, values_new], axis=1)[None], (members, rows_dev, 2 * width)
+    )
+    feats, ups[2], down_other, res, both = lax.optimization_barrier(
+        (feats, ups[2], down_other, res, both)
+    )
     feats = exchange(feats, ALL)
-    downs = reshard(*after((w_down, down_other), feats))
     feats = (
         feats.reshape(groups, members, rows_dev, zs * k_dev)
         .transpose(1, 0, 2, 3)
@@ -397,7 +454,9 @@
     wo_own, wo_pair = wo_parts[0], wo_parts[1]
     sent = pair(jnp.dot(feats, wo_pair, preferred_element_type=F32).astype(BF16))
     part = jnp.dot(feats, wo_own, preferred_element_type=F32) + sent.astype(F32)
-    part = exchange(part.astype(BF16).reshape(members, block, chunk), MLP)
+    part = part.astype(BF16).reshape(members, block, chunk)
+    downs = reshard(*after((w_down, down_other), part))
+    part = exchange(part, MLP)
     gain = lax.dynamic_slice_in_dim(ln_gain, c * half + z * chunk, chunk, 0)
 
     hidden, row = pl.pallas_call(
@@ -408,20 +467,16 @@
         ),
         compiler_params=params(),
     )(part, res, gain[None])
-    row, downs[1], downs[3] = lax.optimization_barrier((row, downs[1], downs[3]))
     rows = spread(row, MLP, members).reshape(tokens, chunk + HD)
-    rows, downs[2] = lax.optimization_barrier((rows, downs[2]))
-
-    both = jnp.broadcast_to(
-        jnp.concatenate([keys_new, values_new], axis=1)[None], (members, rows_dev, 2 * width)
-    )
-    both = exchange(after(both, rows), MLP).reshape(group_rows, 2 * width)
+    rows, downs = lax.optimization_barrier((rows, downs))
+
+    both = exchange(after(both, rows), MLP)
 
     mine, theirs = up_project(rows, ups)
     theirs = pair(theirs)
     terms = []
     for d in range(zs):
-        term = mine[d] + theirs[d].astype(F32)
+        term = mine[d].astype(F32) + theirs[d].astype(F32)
         terms.append(shift(term.astype(BF16), -d, zs) if d else term)
     units = w_down.shape[0]
     act = pl.pallas_call(
@@ -440,6 +495,7 @@
     valid = (accepted >= 0) & (dest_slot == member)[:, None]
     target = jnp.arange(requests, dtype=jnp.int32)[:, None] * tree_len + jnp.maximum(accepted, 0)
     chooser = jnp.any((target[:, :, None] == row_ids[None, None, :]) & valid[:, :, None], axis=0)
+    both = both.reshape(group_rows, 2 * width)
     picked = jnp.dot(chooser.astype(BF16), both, preferred_element_type=F32).astype(BF16)
     return (mixed, picked[:, :width][None], picked[:, width:][None])
 

time: 254 us -> 243 us (0.957)
  blocking collectives: 0 us -> 19.1 us
  local copies, waits for them, and re-layouts: 48.6 us -> 30.2 us
  other arithmetic: 22 us -> 8.68 us
  Pallas kernels: 26 us -> 33.8 us
  starting transfers between devices: 79 us -> 72.1 us
    all_to_all x0 -> x1, blocking collectives: none -> 19.1 us  [exchange(): return lax.all_to_all(x, axes, split_axis=0, concat_axis=0)]
    all_to_all x7 -> x6, waiting for transfers between devices: 34.5 us -> 19.9 us  [exchange(): return lax.all_to_all(x, axes, split_axis=0, concat_axis=0)]
    ppermute x18, waiting for transfers between devices: 35.7 us -> 49.6 us  [shift(): return lax.ppermute(x, 'z', [(i, (i + step) % size) for i in range(size)])]
    another operation x11 -> x0, other arithmetic: 12.6 us -> none  [the longest x8 10.5 us: reshard(): jnp.stack([piece(w, c, d), lax.dynamic_slice_in_dim(other, at, chunk, 1)])]
    unnamed x75 -> x39, local copies, waits for them, and re-layouts: 13.5 us -> 4.26 us
    pallas_call x2 -> x5, Pallas kernels: 8.84 us -> 17.6 us  [the longest x3 10.6 us: cut(): pl.pallas_call(lambda *refs: cut_kernel(n, *refs), grid_spec=pltpu.Prefet...]
    another operation x5 -> x0, local copies, waits for them, and re-layouts: 8.5 us -> none  [the longest x4 7.19 us: reshard(): jnp.stack([piece(w, c, d), lax.dynamic_slice_in_dim(other, at, chunk, 1)])]
    all_to_all x7 -> x6, starting transfers between devices: 44.1 us -> 38.1 us  [exchange(): return lax.all_to_all(x, axes, split_axis=0, concat_axis=0)]
  transfers between devices with their start and end apart: 35 -> 34, of which waited for: 14 -> 18; matrix products, arithmetic and copies ran while one was open for 19% -> 11% of each run, Pallas kernels for 7% -> 12%
where the time goes in v6:
time: 243 us; the launch traced here: 242 us
  waiting for transfers between devices  72.3 us (30%)
  starting transfers between devices  72.1 us (30%)
  Pallas kernels  33.8 us (14%)
  local copies, waits for them, and re-layouts  30.2 us (12%)
  blocking collectives  19.1 us (8%)
  other arithmetic  8.68 us (4%)
  matrix products  4.44 us (2%)
    ppermute x18, waiting for transfers between devices, shift(): return lax.ppermute(x, 'z', [(i, (i + step) % size) for i in range(size)])  49.6 us
    all_to_all x6, starting transfers between devices, exchange(): return lax.all_to_all(x, axes, split_axis=0, concat_axis=0)  38.1 us
    all_to_all x6, waiting for transfers between devices, exchange(): return lax.all_to_all(x, axes, split_axis=0, concat_axis=0)  19.9 us
    ppermute x18, starting transfers between devices, shift(): return lax.ppermute(x, 'z', [(i, (i + step) % size) for i in range(size)])  19.9 us
    all_to_all x1, blocking collectives, exchange(): return lax.all_to_all(x, axes, split_axis=0, concat_axis=0)  19.1 us
    pallas_call x3, Pallas kernels, cut(): pl.pallas_call(lambda *refs: cut_kernel(n, *refs), grid_spec=pltpu.Prefet...  10.6 us
    pallas_call x1, Pallas kernels, attend(): pl.pallas_call(body, grid=(steps,), in_specs=[pl.BlockSpec((rows, wide),...  10.2 us
    ppermute x9, starting transfers between devices, pair(): return lax.ppermute(x, 'c', [(0, 1), (1, 0)])  9.4 us
  transfers between devices with their start and end apart: 34, of which 18 were waited for; matrix products, arithmetic and copies ran while one was open for 11% of the time, Pallas kernels for 12%

profile of v6, /device:TPU:1, one launch (start us, length us, event | category | flops | bytes accessed | tf_op | source)
XLA Modules:
  0.0 241.7 jit_solution(16724677882744874716)
XLA Ops:
  2.6 7.6 %all-to-all-start = ((bf16[16,3,7168]{2,1,0:T(4,128)(2,1)}), bf16[16,3,7168]{2,1,0:T(4,128)(2,1)}, u32[]{:S(2)}, u32[]{:S(2)}) async-start(bf16[16,3,7168]{2,1,0:T(4,128)(2,1)} %broadcast_in_dim.20), calls=%async_computation | async-start | bytes 1835008 | tf_op jit(solution)/shard_map/all_to_all | solution.py:310
  10.3 2.8 %constant_dynamic-slice_fusion.6 = bf16[224,3584]{1,0:T(8,128)(2,1)} fusion(bf16[224,7168]{1,0:T(8,128)(2,1)} %bitcast.85, s32[]{:T(128)S(6)} %select_n.153), kind=kLoop, calls=%fused_computation.76 | loop fusion | bytes 3211268 | tf_op jit(solution)/shard_map/dynamic_slice | solution.py:367
  17.1 3.8 %collective-permute-start.5 = (bf16[2,56,896]{2,1,0:T(8,128)(2,1)}, bf16[2,56,896]{2,1,0:T(8,128)(2,1)}, u32[]{:S(2)}, u32[]{:S(2)}) collective-permute-start(bf16[2,56,896]{2,1,0:T(8,128)(2,1)} %get-tuple-element.50), channel_id=1, source_target_pairs={{0,96},{32,0},{64,32},{96,64},{1,97},{33,1},{65,33},{97,65},{2,98}... | collective-permute-start | bytes 602120 | tf_op jit(solution)/shard_map/ppermute | solution.py:88
  23.3 4.4 %shard_map.167 = (bf16[2,224,896]{2,1,0:T(8,128)(2,1)S(1)}, bf16[2,224,896]{2,1,0:T(8,128)(2,1)}, bf16[2,224,896]{2,1,0:T(8,128)(2,1)}, bf16[2,224,896]{2,1,0:T(8,128)(2,1)}) custom-call(s32[8]{0:T(128)S(1)} %get-tuple-element.106.refs_0_, bf16[224,7168]{1,0:T(8,128)(2,1)S(1)} %bitcast.86, bf16[224,3584]{1,0:T(8,128)(2,1)} %collective-permute-done.refs_2_), custom_call_target="tpu_custom_call" | custom-call | tf_op jit(solution)/shard_map/pallas_call | solution.py:218
  33.7 2.8 %shard_map.169.refs_4_ = f32[8,8,224]{2,1,0:T(8,128)S(1)} custom-call(s32[8]{0:T(128)S(1)} %stack.59.place, f32[1,7168]{1,0:T(1,128)S(1)} %bitcast.89, bf16[224,7168]{1,0:T(8,128)(2,1)S(1)} %bitcast.87), custom_call_target="tpu_custom_call" | custom-call | tf_op jit(solution)/shard_map/pallas_call | solution.py:237
  39.2 2.4 reshape.202.refs_0_
  41.6 10.2 %shard_map.166 = bf16[48,8192]{1,0:T(8,128)(2,1)} custom-call(bf16[48,7168]{1,0:T(8,128)(2,1)} %reshape.202.refs_0_, bf16[24,16,7168]{2,1,0:T(8,128)(2,1)} %refs_1_.1, bf16[24,16,7168]{2,1,0:T(8,128)(2,1)} %refs_2_.1, bf16[16,7168]{1,0:T(8,128)(2,1)} %pad.7.refs_3_, bf16[16,7168]{1,0:T(8,128)(2,1)} %pad.8.refs_4_, f32[48,400]{1,0:T(8,128)} %pad_maximum_fusion.3.refs_5_), custom_call_target="tpu_custom_call" | custom-call | flops 528482304 | bytes 11010048 | tf_op jit(solution)/shard_map/pallas_call | solution.py:61
  54.3 2.4 reshape.204
  56.7 6.9 %all-to-all-start.1 = ((bf16[16,3,8192]{2,1,0:T(4,128)(2,1)}), bf16[16,3,8192]{2,1,0:T(4,128)(2,1)}, u32[]{:S(2)}, u32[]{:S(2)}) async-start(bf16[16,3,8192]{2,1,0:T(4,128)(2,1)} %reshape.204), calls=%async_computation.1 | async-start | bytes 2097152 | tf_op jit(solution)/shard_map/all_to_all | solution.py:310
  63.8 2.4 collective-permute-start.11
  69.6 3.7 %collective-permute-done.11 = bf16[6,896]{1,0:T(8,128)(2,1)S(1)} collective-permute-done((bf16[6,896]{1,0:T(8,128)(2,1)S(1)}, bf16[6,896]{1,0:T(8,128)(2,1)S(1)}, u32[]{:S(2)}, u32[]{:S(2)}) %collective-permute-start.11) | collective-permute-done | bytes 10784 | tf_op jit(solution)/shard_map/ppermute | solution.py:88
  75.7 3.7 %all-to-all-done.1 = bf16[16,3,8192]{2,1,0:T(4,128)(2,1)} async-done(((bf16[16,3,8192]{2,1,0:T(4,128)(2,1)}), bf16[16,3,8192]{2,1,0:T(4,128)(2,1)}, u32[]{:S(2)}, u32[]{:S(2)}) %all-to-all-start.1) | async-done | bytes 786464 | tf_op jit(solution)/shard_map/all_to_all | solution.py:310
  88.1 19.1 %all_to_all.40 = bf16[128,3,224]{2,1,0:T(4,128)(2,1)S(1)} all-to-all(bf16[128,3,224]{2,1,0:T(4,128)(2,1)S(1)} %copy.69), channel_id=1, replica_groups=mesh['z'=4,'c'=2,'x'=4,'y'=4] {'z','c','x','y'}, dimensions={0} | all-to-all | bytes 344064 | tf_op jit(solution)/shard_map/all_to_all | solution.py:310
  116.2 4.3 %all-to-all-start.3 = ((bf16[16,24,896]{2,1,0:T(8,128)(2,1)}), bf16[16,24,896]{2,1,0:T(8,128)(2,1)}, u32[]{:S(2)}, u32[]{:S(2)}) async-start(bf16[16,24,896]{2,1,0:T(8,128)(2,1)} %bitcast.95), calls=%async_computation.3 | async-start | bytes 1376256 | tf_op jit(solution)/shard_map/all_to_all | solution.py:310
  120.5 4.4 %shard_map.171 = (bf16[2,224,896]{2,1,0:T(8,128)(2,1)S(1)}, bf16[2,224,896]{2,1,0:T(8,128)(2,1)}, bf16[2,224,896]{2,1,0:T(8,128)(2,1)}, bf16[2,224,896]{2,1,0:T(8,128)(2,1)}) custom-call(s32[8]{0:T(128)S(1)} %get-tuple-element.106.refs_0_, bf16[224,7168]{1,0:T(8,128)(2,1)S(1)} %copy-done.1, bf16[224,3584]{1,0:T(8,128)(2,1)} %collective-permute-done.7.refs_2_), custom_call_target="tpu_custom_call" | custom-call | tf_op jit(solution)/shard_map/pallas_call | solution.py:218
  128.9 3.4 %all-to-all-done.3.parts = bf16[16,24,896]{2,1,0:T(8,128)(2,1)} async-done(((bf16[16,24,896]{2,1,0:T(8,128)(2,1)}), bf16[16,24,896]{2,1,0:T(8,128)(2,1)}, u32[]{:S(2)}, u32[]{:S(2)}) %all-to-all-start.3) | async-done | bytes 688160 | tf_op jit(solution)/shard_map/all_to_all | solution.py:310
  134.6 4.7 %all-to-all-start.4 = ((bf16[16,24,1024]{2,1,0:T(8,128)(2,1)}), bf16[16,24,1024]{2,1,0:T(8,128)(2,1)S(1)}, u32[]{:S(2)}, u32[]{:S(2)}) async-start(bf16[16,24,1024]{2,1,0:T(8,128)(2,1)} %broadcast_in_dim.27), calls=%async_computation.4 | async-start | bytes 1572864 | tf_op jit(solution)/shard_map/all_to_all | solution.py:304
  139.3 7.9 %collective-permute-done.13.refs_9_ = bf16[2,224,896]{2,1,0:T(8,128)(2,1)S(1)} collective-permute-done((bf16[2,224,896]{2,1,0:T(8,128)(2,1)}, bf16[2,224,896]{2,1,0:T(8,128)(2,1)S(1)}, u32[]{:S(2)}, u32[]{:S(2)}) %collective-permute-start.13) | collective-permute-done | bytes 802848 | tf_op jit(solution)/shard_map/ppermute | solution.py:88
  147.1 15.6 %collective-permute-done.14.refs_10_ = bf16[2,224,896]{2,1,0:T(8,128)(2,1)S(1)} collective-permute-done((bf16[2,224,896]{2,1,0:T(8,128)(2,1)}, bf16[2,224,896]{2,1,0:T(8,128)(2,1)S(1)}, u32[]{:S(2)}, u32[]{:S(2)}) %collective-permute-start.14) | collective-permute-done | bytes 802848 | tf_op jit(solution)/shard_map/ppermute | solution.py:88
  164.0 4.0 %shard_map.172 = (bf16[4,384,256]{2,1,0:T(8,128)(2,1)S(1)}, bf16[4,384,256]{2,1,0:T(8,128)(2,1)}) custom-call(bf16[384,1024]{1,0:T(8,128)(2,1)S(1)} %bitcast.88, bf16[2,224,896]{2,1,0:T(8,128)(2,1)S(1)} %copy-done.4, bf16[2,224,896]{2,1,0:T(8,128)(2,1)} %collective-permute-done.1.refs_2_, bf16[2,224,896]{2,1,0:T(8,128)(2,1)} %collective-permute-done.6.refs_3_, ...), custom_call_target="tpu_custom_call" | custom-call | tf_op jit(solution)/shard_map/pallas_call | solution.py:265
  170.5 6.6 %all-to-all-start.5 = ((bf16[16,3,14336]{2,1,0:T(4,128)(2,1)}), bf16[16,3,14336]{2,1,0:T(4,128)(2,1)}, u32[]{:S(2)}, u32[]{:S(2)}) async-start(bf16[16,3,14336]{2,1,0:T(4,128)(2,1)} %broadcast_in_dim.25), calls=%async_computation.5 | async-start | bytes 3670016 | tf_op jit(solution)/shard_map/all_to_all | solution.py:310
  177.3 2.4 collective-permute-start.17
  180.4 3.8 %collective-permute-done.17.refs_1_ = bf16[384,256]{1,0:T(8,128)(2,1)S(1)} collective-permute-done((bf16[384,256]{1,0:T(8,128)(2,1)S(1)}, bf16[384,256]{1,0:T(8,128)(2,1)S(1)}, u32[]{:S(2)}, u32[]{:S(2)}) %collective-permute-start.17) | collective-permute-done | bytes 196640 | tf_op jit(solution)/shard_map/ppermute | solution.py:88
  184.2 2.8 %collective-permute-done.18.refs_2_ = bf16[384,256]{1,0:T(8,128)(2,1)S(1)} collective-permute-done((bf16[384,256]{1,0:T(8,128)(2,1)S(1)}, bf16[384,256]{1,0:T(8,128)(2,1)S(1)}, u32[]{:S(2)}, u32[]{:S(2)}) %collective-permute-start.18) | collective-permute-done | bytes 196640 | tf_op jit(solution)/shard_map/ppermute | solution.py:88
  187.0 4.7 %collective-permute-done.19.refs_3_ = bf16[384,256]{1,0:T(8,128)(2,1)S(1)} collective-permute-done((bf16[384,256]{1,0:T(8,128)(2,1)S(1)}, bf16[384,256]{1,0:T(8,128)(2,1)S(1)}, u32[]{:S(2)}, u32[]{:S(2)}) %collective-permute-start.19) | collective-permute-done | bytes 196640 | tf_op jit(solution)/shard_map/ppermute | solution.py:88
  197.4 7.5 %collective-permute-done.20.refs_1_ = bf16[384,224]{1,0:T(8,128)(2,1)S(1)} collective-permute-done((bf16[384,224]{1,0:T(8,128)(2,1)S(1)}, bf16[384,224]{1,0:T(8,128)(2,1)S(1)}, u32[]{:S(2)}, u32[]{:S(2)}) %collective-permute-start.20) | collective-permute-done | bytes 172064 | tf_op jit(solution)/shard_map/ppermute | solution.py:88
  208.0 3.0 %shard_map.174 = bf16[384,896]{1,0:T(8,128)(2,1)} custom-call(bf16[384,224]{1,0:T(8,128)(2,1)S(1)} %shard_map.173.refs_0_, bf16[384,224]{1,0:T(8,128)(2,1)S(1)} %collective-permute-done.20.refs_1_, bf16[384,224]{1,0:T(8,128)(2,1)S(1)} %collective-permute-done.21.refs_2_, bf16[384,224]{1,0:T(8,128)(2,1)S(1)} %collective-permute-done.22.refs_3_, ...), custom_call_target="tpu_custom_call" | custom-call | tf_op jit(solution)/shard_map/pallas_call | solution.py:277
  211.0 6.5 %all-to-all-start.6 = ((bf16[16,24,896]{2,1,0:T(8,128)(2,1)}), bf16[16,24,896]{2,1,0:T(8,128)(2,1)S(1)}, u32[]{:S(2)}, u32[]{:S(2)}) async-start(bf16[16,24,896]{2,1,0:T(8,128)(2,1)} %bitcast.36), calls=%async_computation.6 | async-start | bytes 1376256 | tf_op jit(solution)/shard_map/all_to_all | solution.py:310
  217.7 2.4 reshape.215
  220.4 8.8 %all-to-all-done.6.parts = bf16[16,24,896]{2,1,0:T(8,128)(2,1)S(1)} async-done(((bf16[16,24,896]{2,1,0:T(8,128)(2,1)}), bf16[16,24,896]{2,1,0:T(8,128)(2,1)S(1)}, u32[]{:S(2)}, u32[]{:S(2)}) %all-to-all-start.6) | async-done | bytes 688160 | tf_op jit(solution)/shard_map/all_to_all | solution.py:310
  230.0 6.2 %all-to-all-start.7 = ((bf16[8,3,896]{2,1,0:T(4,128)(2,1)}), bf16[8,3,896]{2,1,0:T(4,128)(2,1)S(1)}, u32[]{:S(2)}, u32[]{:S(2)}) async-start(bf16[8,3,896]{2,1,0:T(4,128)(2,1)} %reshape.212), calls=%async_computation.7 | async-start | bytes 114688 | tf_op jit(solution)/shard_map/all_to_all | solution.py:310
  237.0 4.0 %all-to-all-done.7 = bf16[8,3,896]{2,1,0:T(4,128)(2,1)S(1)} async-done(((bf16[8,3,896]{2,1,0:T(4,128)(2,1)}), bf16[8,3,896]{2,1,0:T(4,128)(2,1)S(1)}, u32[]{:S(2)}, u32[]{:S(2)}) %all-to-all-start.7) | async-done | bytes 43040 | tf_op jit(solution)/shard_map/all_to_all | solution.py:310
  (154 shorter events, 65.4 us)
Async XLA Ops:
  2.6 36.6 %all-to-all-start = ((bf16[16,3,7168]{2,1,0:T(4,128)(2,1)}), bf16[16,3,7168]{2,1,0:T(4,128)(2,1)}, u32[]{:S(2)}, u32[]{:S(2)}) async-start(bf16[16,3,7168]{2,1,0:T(4,128)(2,1)} %broadcast_in_dim.20), calls=%async_computation | async-start | bytes 1835008 | tf_op jit(solution)/shard_map/all_to_all | solution.py:310
  13.1 10.1 %collective-permute-start = (bf16[224,3584]{1,0:T(8,128)(2,1)}, bf16[224,3584]{1,0:T(8,128)(2,1)}, u32[]{:S(2)}, u32[]{:S(2)}) collective-permute-start(bf16[224,3584]{1,0:T(8,128)(2,1)} %constant_dynamic-slice_fusion.6), channel_id=1, source_target_pairs={{0,16},{16,0},{1,17},{17,1},{2,18},{18,2},{3,19},{19,3},{4,20},{20... | collective-permute-start | bytes 4816904 | tf_op jit(solution)/shard_map/ppermute | solution.py:84
  17.1 20.1 %collective-permute-start.5 = (bf16[2,56,896]{2,1,0:T(8,128)(2,1)}, bf16[2,56,896]{2,1,0:T(8,128)(2,1)}, u32[]{:S(2)}, u32[]{:S(2)}) collective-permute-start(bf16[2,56,896]{2,1,0:T(8,128)(2,1)} %get-tuple-element.50), channel_id=1, source_target_pairs={{0,96},{32,0},{64,32},{96,64},{1,97},{33,1},{65,33},{97,65},{2,98}... | collective-permute-start | bytes 602120 | tf_op jit(solution)/shard_map/ppermute | solution.py:88
  20.8 16.3 %collective-permute-start.4 = (bf16[2,56,896]{2,1,0:T(8,128)(2,1)}, bf16[2,56,896]{2,1,0:T(8,128)(2,1)}, u32[]{:S(2)}, u32[]{:S(2)}) collective-permute-start(bf16[2,56,896]{2,1,0:T(8,128)(2,1)} %get-tuple-element.49), channel_id=1, source_target_pairs={{0,64},{32,96},{64,0},{96,32},{1,65},{33,97},{65,1},{97,33},{2,66}... | collective-permute-start | bytes 602120 | tf_op jit(solution)/shard_map/ppermute | solution.py:88
  20.8 16.3 %collective-permute-start.3 = (bf16[2,56,896]{2,1,0:T(8,128)(2,1)}, bf16[2,56,896]{2,1,0:T(8,128)(2,1)}, u32[]{:S(2)}, u32[]{:S(2)}) collective-permute-start(bf16[2,56,896]{2,1,0:T(8,128)(2,1)} %get-tuple-element.48), channel_id=1, source_target_pairs={{0,32},{32,64},{64,96},{96,0},{1,33},{33,65},{65,97},{97,1},{2,34}... | collective-permute-start | bytes 602120 | tf_op jit(solution)/shard_map/ppermute | solution.py:88
  28.7 23.1 %collective-permute-start.1 = (bf16[2,224,896]{2,1,0:T(8,128)(2,1)}, bf16[2,224,896]{2,1,0:T(8,128)(2,1)}, u32[]{:S(2)}, u32[]{:S(2)}) collective-permute-start(bf16[2,224,896]{2,1,0:T(8,128)(2,1)} %get-tuple-element.44), channel_id=1, source_target_pairs={{0,32},{32,64},{64,96},{96,0},{1,33},{33,65},{65,97},{97,1},{2,34}... | collective-permute-start | bytes 2408456 | tf_op jit(solution)/shard_map/ppermute | solution.py:88
  30.6 21.2 %collective-permute-start.2 = (bf16[2,224,896]{2,1,0:T(8,128)(2,1)}, bf16[2,224,896]{2,1,0:T(8,128)(2,1)}, u32[]{:S(2)}, u32[]{:S(2)}) collective-permute-start(bf16[2,224,896]{2,1,0:T(8,128)(2,1)} %get-tuple-element.45), channel_id=1, source_target_pairs={{0,96},{32,0},{64,32},{96,64},{1,97},{33,1},{65,33},{97,65},{2,98}... | collective-permute-start | bytes 2408456 | tf_op jit(solution)/shard_map/ppermute | solution.py:88
  51.9 11.8 %collective-permute-start.8 = (bf16[3,3584]{1,0:T(4,128)(2,1)S(1)}, bf16[3,3584]{1,0:T(4,128)(2,1)S(1)}, u32[]{:S(2)}, u32[]{:S(2)}) collective-permute-start(bf16[3,3584]{1,0:T(4,128)(2,1)S(1)} %get-tuple-element.104), channel_id=1, source_target_pairs={{0,16},{16,0},{1,17},{17,1},{2,18},{18,2},{3,19},{19,3},{4,20},{20... | collective-permute-start | bytes 64520 | tf_op jit(solution)/shard_map/ppermute | solution.py:84
  53.4 32.5 %collective-permute-start.6 = (bf16[2,224,896]{2,1,0:T(8,128)(2,1)}, bf16[2,224,896]{2,1,0:T(8,128)(2,1)}, u32[]{:S(2)}, u32[]{:S(2)}) collective-permute-start(bf16[2,224,896]{2,1,0:T(8,128)(2,1)} %get-tuple-element.52), channel_id=1, source_target_pairs={{0,64},{32,96},{64,0},{96,32},{1,65},{33,97},{65,1},{97,33},{2,66}... | collective-permute-start | bytes 2408456 | tf_op jit(solution)/shard_map/ppermute | solution.py:88
  56.7 22.7 %all-to-all-start.1 = ((bf16[16,3,8192]{2,1,0:T(4,128)(2,1)}), bf16[16,3,8192]{2,1,0:T(4,128)(2,1)}, u32[]{:S(2)}, u32[]{:S(2)}) async-start(bf16[16,3,8192]{2,1,0:T(4,128)(2,1)} %reshape.204), calls=%async_computation.1 | async-start | bytes 2097152 | tf_op jit(solution)/shard_map/all_to_all | solution.py:310
  63.8 9.5 %collective-permute-start.11 = (bf16[6,896]{1,0:T(8,128)(2,1)S(1)}, bf16[6,896]{1,0:T(8,128)(2,1)S(1)}, u32[]{:S(2)}, u32[]{:S(2)}) collective-permute-start(bf16[6,896]{1,0:T(8,128)(2,1)S(1)} %get-tuple-element.100), channel_id=1, source_target_pairs={{0,96},{32,0},{64,32},{96,64},{1,97},{33,1},{65,33},{97,65},{2,98}... | collective-permute-start | bytes 32264 | tf_op jit(solution)/shard_map/ppermute | solution.py:88
  66.2 9.0 %collective-permute-start.10 = (bf16[6,896]{1,0:T(8,128)(2,1)S(1)}, bf16[6,896]{1,0:T(8,128)(2,1)S(1)}, u32[]{:S(2)}, u32[]{:S(2)}) collective-permute-start(bf16[6,896]{1,0:T(8,128)(2,1)S(1)} %get-tuple-element.101), channel_id=1, source_target_pairs={{0,64},{32,96},{64,0},{96,32},{1,65},{33,97},{65,1},{97,33},{2,66}... | collective-permute-start | bytes 32264 | tf_op jit(solution)/shard_map/ppermute | solution.py:88
  66.2 9.4 %collective-permute-start.9 = (bf16[6,896]{1,0:T(8,128)(2,1)S(1)}, bf16[6,896]{1,0:T(8,128)(2,1)S(1)}, u32[]{:S(2)}, u32[]{:S(2)}) collective-permute-start(bf16[6,896]{1,0:T(8,128)(2,1)S(1)} %get-tuple-element.102), channel_id=1, source_target_pairs={{0,32},{32,64},{64,96},{96,0},{1,33},{33,65},{65,97},{97,1},{2,34}... | collective-permute-start | bytes 32264 | tf_op jit(solution)/shard_map/ppermute | solution.py:88
  68.2 17.7 %collective-permute-start.7 = (bf16[224,3584]{1,0:T(8,128)(2,1)}, bf16[224,3584]{1,0:T(8,128)(2,1)}, u32[]{:S(2)}, u32[]{:S(2)}) collective-permute-start(bf16[224,3584]{1,0:T(8,128)(2,1)} %constant_dynamic-slice_fusion.5), channel_id=1, source_target_pairs={{0,16},{16,0},{1,17},{17,1},{2,18},{18,2},{3,19},{19,3},{4,20},{20... | collective-permute-start | bytes 4816904 | tf_op jit(solution)/shard_map/ppermute | solution.py:84
  111.3 2.6 %collective-permute-start.12 = (bf16[384,896]{1,0:T(8,128)(2,1)S(1)}, bf16[384,896]{1,0:T(8,128)(2,1)S(1)}, u32[]{:S(2)}, u32[]{:S(2)}) collective-permute-start(bf16[384,896]{1,0:T(8,128)(2,1)S(1)} %convolution_convert_fusion.1), channel_id=1, source_target_pairs={{0,16},{16,0},{1,17},{17,1},{2,18},{18,2},{3,19},{19,3},{4,20},{20... | collective-permute-start | bytes 2064392 | tf_op jit(solution)/shard_map/ppermute | solution.py:84
  116.2 16.0 %all-to-all-start.3 = ((bf16[16,24,896]{2,1,0:T(8,128)(2,1)}), bf16[16,24,896]{2,1,0:T(8,128)(2,1)}, u32[]{:S(2)}, u32[]{:S(2)}) async-start(bf16[16,24,896]{2,1,0:T(8,128)(2,1)} %bitcast.95), calls=%async_computation.3 | async-start | bytes 1376256 | tf_op jit(solution)/shard_map/all_to_all | solution.py:310
  125.8 21.3 %collective-permute-start.13 = (bf16[2,224,896]{2,1,0:T(8,128)(2,1)}, bf16[2,224,896]{2,1,0:T(8,128)(2,1)S(1)}, u32[]{:S(2)}, u32[]{:S(2)}) collective-permute-start(bf16[2,224,896]{2,1,0:T(8,128)(2,1)} %get-tuple-element.63), channel_id=1, source_target_pairs={{0,32},{32,64},{64,96},{96,0},{1,33},{33,65},{65,97},{97,1},{2,34}... | collective-permute-start | bytes 2408456 | tf_op jit(solution)/shard_map/ppermute | solution.py:88
  126.4 36.3 %collective-permute-start.14 = (bf16[2,224,896]{2,1,0:T(8,128)(2,1)}, bf16[2,224,896]{2,1,0:T(8,128)(2,1)S(1)}, u32[]{:S(2)}, u32[]{:S(2)}) collective-permute-start(bf16[2,224,896]{2,1,0:T(8,128)(2,1)} %get-tuple-element.64), channel_id=1, source_target_pairs={{0,64},{32,96},{64,0},{96,32},{1,65},{33,97},{65,1},{97,33},{2,66}... | collective-permute-start | bytes 2408456 | tf_op jit(solution)/shard_map/ppermute | solution.py:88
  127.6 36.4 %collective-permute-start.15 = (bf16[2,224,896]{2,1,0:T(8,128)(2,1)}, bf16[2,224,896]{2,1,0:T(8,128)(2,1)}, u32[]{:S(2)}, u32[]{:S(2)}) collective-permute-start(bf16[2,224,896]{2,1,0:T(8,128)(2,1)} %get-tuple-element.65), channel_id=1, source_target_pairs={{0,96},{32,0},{64,32},{96,64},{1,97},{33,1},{65,33},{97,65},{2,98}... | collective-permute-start | bytes 2408456 | tf_op jit(solution)/shard_map/ppermute | solution.py:88
  134.6 29.4 %all-to-all-start.4 = ((bf16[16,24,1024]{2,1,0:T(8,128)(2,1)}), bf16[16,24,1024]{2,1,0:T(8,128)(2,1)S(1)}, u32[]{:S(2)}, u32[]{:S(2)}) async-start(bf16[16,24,1024]{2,1,0:T(8,128)(2,1)} %broadcast_in_dim.27), calls=%async_computation.4 | async-start | bytes 1572864 | tf_op jit(solution)/shard_map/all_to_all | solution.py:304
  169.0 8.1 %collective-permute-start.16 = (bf16[4,384,256]{2,1,0:T(8,128)(2,1)}, bf16[4,384,256]{2,1,0:T(8,128)(2,1)S(1)}, u32[]{:S(2)}, u32[]{:S(2)}) collective-permute-start(bf16[4,384,256]{2,1,0:T(8,128)(2,1)} %get-tuple-element.72), channel_id=1, source_target_pairs={{0,16},{16,0},{1,17},{17,1},{2,18},{18,2},{3,19},{19,3},{4,20},{20... | collective-permute-start | bytes 2359304 | tf_op jit(solution)/shard_map/ppermute | solution.py:84
  170.5 40.5 %all-to-all-start.5 = ((bf16[16,3,14336]{2,1,0:T(4,128)(2,1)}), bf16[16,3,14336]{2,1,0:T(4,128)(2,1)}, u32[]{:S(2)}, u32[]{:S(2)}) async-start(bf16[16,3,14336]{2,1,0:T(4,128)(2,1)} %broadcast_in_dim.25), calls=%async_computation.5 | async-start | bytes 3670016 | tf_op jit(solution)/shard_map/all_to_all | solution.py:310
  177.3 6.9 %collective-permute-start.17 = (bf16[384,256]{1,0:T(8,128)(2,1)S(1)}, bf16[384,256]{1,0:T(8,128)(2,1)S(1)}, u32[]{:S(2)}, u32[]{:S(2)}) collective-permute-start(bf16[384,256]{1,0:T(8,128)(2,1)S(1)} %get-tuple-element.87), channel_id=1, source_target_pairs={{0,96},{32,0},{64,32},{96,64},{1,97},{33,1},{65,33},{97,65},{2,98}... | collective-permute-start | bytes 589832 | tf_op jit(solution)/shard_map/ppermute | solution.py:88
  179.7 7.3 %collective-permute-start.18 = (bf16[384,256]{1,0:T(8,128)(2,1)S(1)}, bf16[384,256]{1,0:T(8,128)(2,1)S(1)}, u32[]{:S(2)}, u32[]{:S(2)}) collective-permute-start(bf16[384,256]{1,0:T(8,128)(2,1)S(1)} %get-tuple-element.86), channel_id=1, source_target_pairs={{0,64},{32,96},{64,0},{96,32},{1,65},{33,97},{65,1},{97,33},{2,66}... | collective-permute-start | bytes 589832 | tf_op jit(solution)/shard_map/ppermute | solution.py:88
  179.7 12.0 %collective-permute-start.19 = (bf16[384,256]{1,0:T(8,128)(2,1)S(1)}, bf16[384,256]{1,0:T(8,128)(2,1)S(1)}, u32[]{:S(2)}, u32[]{:S(2)}) collective-permute-start(bf16[384,256]{1,0:T(8,128)(2,1)S(1)} %get-tuple-element.85), channel_id=1, source_target_pairs={{0,32},{32,64},{64,96},{96,0},{1,33},{33,65},{65,97},{97,1},{2,34}... | collective-permute-start | bytes 589832 | tf_op jit(solution)/shard_map/ppermute | solution.py:88
  193.4 11.5 %collective-permute-start.20 = (bf16[384,224]{1,0:T(8,128)(2,1)S(1)}, bf16[384,224]{1,0:T(8,128)(2,1)S(1)}, u32[]{:S(2)}, u32[]{:S(2)}) collective-permute-start(bf16[384,224]{1,0:T(8,128)(2,1)S(1)} %shard_map.173.refs_0_), channel_id=1, source_target_pairs={{0,32},{32,64},{64,96},{96,0},{1,33},{33,65},{65,97},{97,1},{2,34}... | collective-permute-start | bytes 516104 | tf_op jit(solution)/shard_map/ppermute | solution.py:88
  193.5 12.7 %collective-permute-start.21 = (bf16[384,224]{1,0:T(8,128)(2,1)S(1)}, bf16[384,224]{1,0:T(8,128)(2,1)S(1)}, u32[]{:S(2)}, u32[]{:S(2)}) collective-permute-start(bf16[384,224]{1,0:T(8,128)(2,1)S(1)} %shard_map.173.refs_0_), channel_id=1, source_target_pairs={{0,64},{32,96},{64,0},{96,32},{1,65},{33,97},{65,1},{97,33},{2,66}... | collective-permute-start | bytes 516104 | tf_op jit(solution)/shard_map/ppermute | solution.py:88
  194.6 11.7 %collective-permute-start.22 = (bf16[384,224]{1,0:T(8,128)(2,1)S(1)}, bf16[384,224]{1,0:T(8,128)(2,1)S(1)}, u32[]{:S(2)}, u32[]{:S(2)}) collective-permute-start(bf16[384,224]{1,0:T(8,128)(2,1)S(1)} %shard_map.173.refs_0_), channel_id=1, source_target_pairs={{0,96},{32,0},{64,32},{96,64},{1,97},{33,1},{65,33},{97,65},{2,98}... | collective-permute-start | bytes 516104 | tf_op jit(solution)/shard_map/ppermute | solution.py:88
  196.2 10.8 %collective-permute-start.23 = (bf16[384,224]{1,0:T(8,128)(2,1)S(1)}, bf16[384,224]{1,0:T(8,128)(2,1)S(1)}, u32[]{:S(2)}, u32[]{:S(2)}) collective-permute-start(bf16[384,224]{1,0:T(8,128)(2,1)S(1)} %shard_map.173.refs_0_), channel_id=1, source_target_pairs={{0,16},{16,0},{1,17},{17,1},{2,18},{18,2},{3,19},{19,3},{4,20},{20... | collective-permute-start | bytes 516104 | tf_op jit(solution)/shard_map/ppermute | solution.py:84
  204.9 2.4 collective-permute-start.24
  211.0 18.2 %all-to-all-start.6 = ((bf16[16,24,896]{2,1,0:T(8,128)(2,1)}), bf16[16,24,896]{2,1,0:T(8,128)(2,1)S(1)}, u32[]{:S(2)}, u32[]{:S(2)}) async-start(bf16[16,24,896]{2,1,0:T(8,128)(2,1)} %bitcast.36), calls=%async_computation.6 | async-start | bytes 1376256 | tf_op jit(solution)/shard_map/all_to_all | solution.py:310
  230.0 11.0 %all-to-all-start.7 = ((bf16[8,3,896]{2,1,0:T(4,128)(2,1)}), bf16[8,3,896]{2,1,0:T(4,128)(2,1)S(1)}, u32[]{:S(2)}, u32[]{:S(2)}) async-start(bf16[8,3,896]{2,1,0:T(4,128)(2,1)} %reshape.212), calls=%async_computation.7 | async-start | bytes 114688 | tf_op jit(solution)/shard_map/all_to_all | solution.py:310
  (21 other events, 228.0 us)

commit v7 on v6

--- a/solution.py
+++ b/solution.py
@@ -84,8 +84,8 @@
     return lax.ppermute(x, "c", [(0, 1), (1, 0)])
 
 
-def shift(x, step, size):
-    return lax.ppermute(x, "z", [(i, (i + step) % size) for i in range(size)])
+def shift(x, step, size, axis="z"):
+    return lax.ppermute(x, axis, [(i, (i + step) % size) for i in range(size)])
 
 
 def after(x, first):
@@ -353,25 +353,18 @@
         return [shift(p, d, zs) if d else p for d, p in enumerate(pieces)]
 
     k_dev = w_out.shape[0]
-    wo = after(w_out, wide_q)
-    wo_parts = send(cut(jnp.concatenate([own_turn, other_turn]), wo, wo, zs, chunk))
-    wo_parts = jnp.concatenate(wo_parts, axis=1)
 
     def swap(w):
         return pair(lax.dynamic_slice_in_dim(w, (1 - c) * half, half, 1))
 
     def reshard(w, other):
-        return send(cut(jnp.concatenate([own_turn, turn]), w, other, zs, chunk))
+        return cut(jnp.concatenate([own_turn, turn]), w, other, zs, chunk)
 
     def swap(w):
         return pair(lax.dynamic_slice_in_dim(w, (1 - c) * half, half, 1))
 
     up_w = after(w_up.T, wide_q)
-    ups = reshard(up_w, swap(up_w))
-    order = jnp.stack(
-        [(c + e) % cs * zs + (z + d) % zs for d in range(zs) for e in range(cs)]
-    ).astype(jnp.int32)
-    gain_up = gain_products(order, ln_gain[None], up_w, chunk)
+    ups = send(reshard(up_w, swap(up_w)))
 
     page_ids = member * pages_dev + jnp.arange(pages_dev, dtype=jnp.int32)
     owners = jnp.any(page_table[:, :, None] == page_ids[None, None, :], axis=1)
@@ -401,9 +394,11 @@
         heads // 7,
     )
 
-    parts, ups[1], ups[3], wo_parts, gain_up = lax.optimization_barrier(
-        (parts, ups[1], ups[3], wo_parts, gain_up)
-    )
+    parts, ups[1], ups[3] = lax.optimization_barrier((parts, ups[1], ups[3]))
+
+    wo = after(w_out, parts)
+    wo_parts = send(cut(jnp.concatenate([own_turn, other_turn]), wo, wo, zs, chunk))
+    wo_parts = jnp.concatenate(wo_parts, axis=1)
     down_other = swap(after(w_down, parts))
 
     res = after(resid, parts)
@@ -439,12 +434,11 @@
             for to in range(zs)
         ]
     ).reshape(groups * members, rows_dev, zs * k_dev)
-    both = jnp.broadcast_to(
-        jnp.concatenate([keys_new, values_new], axis=1)[None], (members, rows_dev, 2 * width)
-    )
-    feats, ups[2], down_other, res, both = lax.optimization_barrier(
-        (feats, ups[2], down_other, res, both)
-    )
+    feats, ups[2], down_other, res = lax.optimization_barrier((feats, ups[2], down_other, res))
+    downs = reshard(*after((w_down, down_other), feats))
+    draft_k, draft_v = after((keys_new, values_new), feats)
+    both = jnp.concatenate([draft_k, draft_v], axis=1)
+    both = [shift(both, d, xs, "x") if d else both for d in range(xs)]
     feats = exchange(feats, ALL)
     feats = (
         feats.reshape(groups, members, rows_dev, zs * k_dev)
@@ -455,7 +449,8 @@
     sent = pair(jnp.dot(feats, wo_pair, preferred_element_type=F32).astype(BF16))
     part = jnp.dot(feats, wo_own, preferred_element_type=F32) + sent.astype(F32)
     part = part.astype(BF16).reshape(members, block, chunk)
-    downs = reshard(*after((w_down, down_other), part))
+    part, downs = lax.optimization_barrier((part, downs))
+    downs = send(downs)
     part = exchange(part, MLP)
     gain = lax.dynamic_slice_in_dim(ln_gain, c * half + z * chunk, chunk, 0)
 
@@ -467,10 +462,15 @@
         ),
         compiler_params=params(),
     )(part, res, gain[None])
+    row, downs[1], downs[3] = lax.optimization_barrier((row, downs[1], downs[3]))
     rows = spread(row, MLP, members).reshape(tokens, chunk + HD)
-    rows, downs = lax.optimization_barrier((rows, downs))
-
-    both = exchange(after(both, rows), MLP)
+
+    order = jnp.stack(
+        [(c + e) % cs * zs + (z + d) % zs for d in range(zs) for e in range(cs)]
+    ).astype(jnp.int32)
+    gain_up = gain_products(order, ln_gain[None], after(w_up.T, row), chunk)
+    both = jnp.stack(both)
+    rows, downs, gain_up, both = lax.optimization_barrier((rows, downs, gain_up, both))
 
     mine, theirs = up_project(rows, ups)
     theirs = pair(theirs)
@@ -478,6 +478,8 @@
     for d in range(zs):
         term = mine[d].astype(F32) + theirs[d].astype(F32)
         terms.append(shift(term.astype(BF16), -d, zs) if d else term)
+    both = after(both, terms[1])
+    both = jnp.stack([shift(both, d, ys, "y") if d else both for d in range(ys)])
     units = w_down.shape[0]
     act = pl.pallas_call(
         lambda *refs: act_kernel(width, units, zs, *refs),
@@ -486,7 +488,6 @@
     )(*terms, gain_up)
     acts = [shift(act, d, zs) if d else act for d in range(zs)]
     down = down_project(acts, [pair(a) for a in acts], downs)
-    down, both = lax.optimization_barrier((down, both))
     down = exchange(down.reshape(members, block, chunk), MLP)
     mixed = finish(down, hidden)
     mixed = exchange(mixed.reshape(groups, rows_dev, chunk), REQ)
@@ -494,7 +495,11 @@
 
     valid = (accepted >= 0) & (dest_slot == member)[:, None]
     target = jnp.arange(requests, dtype=jnp.int32)[:, None] * tree_len + jnp.maximum(accepted, 0)
-    chooser = jnp.any((target[:, :, None] == row_ids[None, None, :]) & valid[:, :, None], axis=0)
+    x, y = lax.axis_index("x"), lax.axis_index("y")
+    at = jnp.arange(group_rows, dtype=jnp.int32)
+    near = at // rows_dev
+    slots = (((x - near % xs) % xs) * ys + (y - near // xs) % ys) * rows_dev + at % rows_dev
+    chooser = jnp.any((target[:, :, None] == slots[None, None, :]) & valid[:, :, None], axis=0)
     both = both.reshape(group_rows, 2 * width)
     picked = jnp.dot(chooser.astype(BF16), both, preferred_element_type=F32).astype(BF16)
     return (mixed, picked[:, :width][None], picked[:, width:][None])

time: 243 us -> 262 us (1.078)
  starting transfers between devices: 72.1 us -> 104 us
  blocking collectives: 19.1 us -> 0 us
  local copies, waits for them, and re-layouts: 30.2 us -> 42.7 us
  waiting for transfers between devices: 72.3 us -> 64.6 us
    all_to_all x1 -> x0, blocking collectives: 19.1 us -> none  [exchange(): return lax.all_to_all(x, axes, split_axis=0, concat_axis=0)]
    ppermute x9, starting transfers between devices: 9.4 us -> 28 us  [pair(): return lax.ppermute(x, 'c', [(0, 1), (1, 0)])]
    ppermute x18 -> x24, starting transfers between devices: 19.9 us -> 31.4 us  [shift(): return lax.ppermute(x, axis, [(i, (i + step) % size) for i in range(size)])]
    unnamed x39 -> x53, local copies, waits for them, and re-layouts: 4.26 us -> 15.3 us
    all_to_all x6, waiting for transfers between devices: 19.9 us -> 9.96 us  [exchange(): return lax.all_to_all(x, axes, split_axis=0, concat_axis=0)]
    another operation x0 -> x2, other arithmetic: none -> 5.19 us  [the longest x1 2.99 us: local(): jnp.stack([shift(both, d, ys, 'y') if d else both for d in range(ys)])]
    concatenate x2 -> x0, other arithmetic: 3.6 us -> none  [the longest x1 2.08 us: local(): wo_parts = jnp.concatenate(wo_parts, axis=1)]
    concatenate x0 -> x2, local copies, waits for them, and re-layouts: none -> 3.1 us  [the longest x1 1.64 us: local(): wo_parts = jnp.concatenate(wo_parts, axis=1)]
  transfers between devices with their start and end apart: 34 -> 40, of which waited for: 18 -> 16; matrix products, arithmetic and copies ran while one was open for 11% -> 14% of each run, Pallas kernels for 12% -> 10%
where the time goes in v7:
time: 262 us; the launch traced here: 260 us
  starting transfers between devices  104 us (40%)
  waiting for transfers between devices  64.6 us (25%)
  local copies, waits for them, and re-layouts  42.7 us (16%)
  Pallas kernels  31.3 us (12%)
  other arithmetic  10.3 us (4%)
  matrix products  5.55 us (2%)
    ppermute x24, waiting for transfers between devices, shift(): return lax.ppermute(x, axis, [(i, (i + step) % size) for i in range(size)])  50.6 us
    all_to_all x6, starting transfers between devices, exchange(): return lax.all_to_all(x, axes, split_axis=0, concat_axis=0)  38.7 us
    ppermute x24, starting transfers between devices, shift(): return lax.ppermute(x, axis, [(i, (i + step) % size) for i in range(size)])  31.4 us
    ppermute x9, starting transfers between devices, pair(): return lax.ppermute(x, 'c', [(0, 1), (1, 0)])  28 us
    unnamed x53, local copies, waits for them, and re-layouts  15.3 us
    pallas_call x1, Pallas kernels, attend(): pl.pallas_call(body, grid=(steps,), in_specs=[pl.BlockSpec((rows, wide),...  10.2 us
    all_to_all x6, waiting for transfers between devices, exchange(): return lax.all_to_all(x, axes, split_axis=0, concat_axis=0)  9.96 us
    pallas_call x3, Pallas kernels, cut(): pl.pallas_call(lambda *refs: cut_kernel(n, *refs), grid_spec=pltpu.Prefet...  8.26 us
  transfers between devices with their start and end apart: 40, of which 16 were waited for; matrix products, arithmetic and copies ran while one was open for 14% of the time, Pallas kernels for 10%

profile of v7, /device:TPU:1, one launch (start us, length us, event | category | flops | bytes accessed | tf_op | source)
XLA Modules:
  0.0 260.1 jit_solution(14446778579731278478)
XLA Ops:
  2.6 2.8 %constant_dynamic-slice_fusion.6 = bf16[224,3584]{1,0:T(8,128)(2,1)} fusion(bf16[224,7168]{1,0:T(8,128)(2,1)} %bitcast.91, s32[]{:T(128)S(6)} %select_n.201), kind=kLoop, calls=%fused_computation.82 | loop fusion | bytes 3211268 | tf_op jit(solution)/shard_map/dynamic_slice | solution.py:364
  7.0 6.9 %all-to-all-start = ((bf16[16,3,7168]{2,1,0:T(4,128)(2,1)}), bf16[16,3,7168]{2,1,0:T(4,128)(2,1)}, u32[]{:S(2)}, u32[]{:S(2)}) async-start(bf16[16,3,7168]{2,1,0:T(4,128)(2,1)} %broadcast_in_dim.18), calls=%async_computation | async-start | bytes 1835008 | tf_op jit(solution)/shard_map/all_to_all | solution.py:310
  16.2 4.4 %shard_map.167 = (bf16[2,224,896]{2,1,0:T(8,128)(2,1)S(1)}, bf16[2,224,896]{2,1,0:T(8,128)(2,1)}, bf16[2,224,896]{2,1,0:T(8,128)(2,1)}, bf16[2,224,896]{2,1,0:T(8,128)(2,1)}) custom-call(s32[8]{0:T(128)S(1)} %get-tuple-element.122.refs_0_, bf16[224,7168]{1,0:T(8,128)(2,1)S(1)} %bitcast.92, bf16[224,3584]{1,0:T(8,128)(2,1)} %collective-permute-done.refs_2_), custom_call_target="tpu_custom_call" | custom-call | tf_op jit(solution)/shard_map/pallas_call | solution.py:218
  26.3 2.8 %all-to-all-done = bf16[16,3,7168]{2,1,0:T(4,128)(2,1)} async-done(((bf16[16,3,7168]{2,1,0:T(4,128)(2,1)}), bf16[16,3,7168]{2,1,0:T(4,128)(2,1)}, u32[]{:S(2)}, u32[]{:S(2)}) %all-to-all-start) | async-done | bytes 688160 | tf_op jit(solution)/shard_map/all_to_all | solution.py:310
  31.4 10.2 %shard_map.166 = bf16[48,8192]{1,0:T(8,128)(2,1)} custom-call(bf16[48,7168]{1,0:T(8,128)(2,1)} %reshape.274.refs_0_, bf16[24,16,7168]{2,1,0:T(8,128)(2,1)} %refs_1_.1, bf16[24,16,7168]{2,1,0:T(8,128)(2,1)} %refs_2_.1, bf16[16,7168]{1,0:T(8,128)(2,1)} %pad.7.refs_3_, bf16[16,7168]{1,0:T(8,128)(2,1)} %pad.8.refs_4_, f32[48,400]{1,0:T(8,128)} %pad_maximum_fusion.3.refs_5_), custom_call_target="tpu_custom_call" | custom-call | flops 528482304 | bytes 11010048 | tf_op jit(solution)/shard_map/pallas_call | solution.py:61
  41.6 3.6 %collective-permute-start.3 = (bf16[2,224,896]{2,1,0:T(8,128)(2,1)}, bf16[2,224,896]{2,1,0:T(8,128)(2,1)}, u32[]{:S(2)}, u32[]{:S(2)}) collective-permute-start(bf16[2,224,896]{2,1,0:T(8,128)(2,1)} %get-tuple-element.55), channel_id=1, source_target_pairs={{0,64},{32,96},{64,0},{96,32},{1,65},{33,97},{65,1},{97,33},{2,66}... | collective-permute-start | bytes 2408456 | tf_op jit(solution)/shard_map/ppermute | solution.py:88
  47.5 4.7 %all-to-all-start.1 = ((bf16[16,3,8192]{2,1,0:T(4,128)(2,1)}), bf16[16,3,8192]{2,1,0:T(4,128)(2,1)}, u32[]{:S(2)}, u32[]{:S(2)}) async-start(bf16[16,3,8192]{2,1,0:T(4,128)(2,1)} %reshape.276), calls=%async_computation.1 | async-start | bytes 2097152 | tf_op jit(solution)/shard_map/all_to_all | solution.py:310
  52.2 17.7 %collective-permute-start.5 = (bf16[3,3584]{1,0:T(4,128)(2,1)S(1)}, bf16[3,3584]{1,0:T(4,128)(2,1)S(1)}, u32[]{:S(2)}, u32[]{:S(2)}) collective-permute-start(bf16[3,3584]{1,0:T(4,128)(2,1)S(1)} %get-tuple-element.120), channel_id=1, source_target_pairs={{0,16},{16,0},{1,17},{17,1},{2,18},{18,2},{3,19},{19,3},{4,20},{20... | collective-permute-start | bytes 64520 | tf_op jit(solution)/shard_map/ppermute | solution.py:84
  69.9 2.7 %constant_dynamic-slice_fusion.5 = bf16[224,3584]{1,0:T(8,128)(2,1)} fusion(bf16[224,7168]{1,0:T(8,128)(2,1)} %refs_1_.3, s32[]{:T(128)S(6)} %select_n.201), kind=kLoop, calls=%fused_computation.81 | loop fusion | bytes 3211268 | tf_op jit(solution)/shard_map/dynamic_slice | solution.py:364
  77.2 3.4 %collective-permute-start.8 = (bf16[6,896]{1,0:T(8,128)(2,1)S(1)}, bf16[6,896]{1,0:T(8,128)(2,1)S(1)}, u32[]{:S(2)}, u32[]{:S(2)}) collective-permute-start(bf16[6,896]{1,0:T(8,128)(2,1)S(1)} %get-tuple-element.116), channel_id=1, source_target_pairs={{0,96},{32,0},{64,32},{96,64},{1,97},{33,1},{65,33},{97,65},{2,98}... | collective-permute-start | bytes 32264 | tf_op jit(solution)/shard_map/ppermute | solution.py:88
  86.6 2.5 collective-permute-done.9
  94.4 11.8 %all-to-all-start.2 = ((bf16[128,3,224]{2,1,0:T(4,128)(2,1)}), bf16[128,3,224]{2,1,0:T(4,128)(2,1)}, u32[]{:S(2)}, u32[]{:S(2)}) async-start(bf16[128,3,224]{2,1,0:T(4,128)(2,1)} %copy.69), calls=%async_computation.2 | async-start | bytes 524288 | tf_op jit(solution)/shard_map/all_to_all | solution.py:310
  111.4 3.0 %shard_map.169 = (bf16[2,224,896]{2,1,0:T(8,128)(2,1)S(1)}, bf16[2,224,896]{2,1,0:T(8,128)(2,1)S(1)}, bf16[2,224,896]{2,1,0:T(8,128)(2,1)S(1)}, bf16[2,224,896]{2,1,0:T(8,128)(2,1)S(1)}) custom-call(s32[8]{0:T(128)S(1)} %get-tuple-element.122.refs_0_, bf16[224,7168]{1,0:T(8,128)(2,1)S(1)} %copy-done.1, bf16[224,3584]{1,0:T(8,128)(2,1)} %collective-permute-done.4.refs_2_), custom_call_target="tpu_custom_call" | custom-call | tf_op jit(solution)/shard_map/pallas_call | solution.py:218
  127.6 6.0 %all-to-all-start.3 = ((bf16[16,24,896]{2,1,0:T(8,128)(2,1)}), bf16[16,24,896]{2,1,0:T(8,128)(2,1)}, u32[]{:S(2)}, u32[]{:S(2)}) async-start(bf16[16,24,896]{2,1,0:T(8,128)(2,1)} %bitcast.101), calls=%async_computation.3 | async-start | bytes 1376256 | tf_op jit(solution)/shard_map/all_to_all | solution.py:310
  138.4 2.5 collective-permute-start.18
  142.2 3.1 %all-to-all-done.3.parts = bf16[16,24,896]{2,1,0:T(8,128)(2,1)} async-done(((bf16[16,24,896]{2,1,0:T(8,128)(2,1)}), bf16[16,24,896]{2,1,0:T(8,128)(2,1)}, u32[]{:S(2)}, u32[]{:S(2)}) %all-to-all-start.3) | async-done | bytes 688160 | tf_op jit(solution)/shard_map/all_to_all | solution.py:310
  146.7 8.2 %collective-permute-done.13.refs_9_ = bf16[2,224,896]{2,1,0:T(8,128)(2,1)} collective-permute-done((bf16[2,224,896]{2,1,0:T(8,128)(2,1)}, bf16[2,224,896]{2,1,0:T(8,128)(2,1)}, u32[]{:S(2)}, u32[]{:S(2)}) %collective-permute-start.13) | collective-permute-done | bytes 802848 | tf_op jit(solution)/shard_map/ppermute | solution.py:88
  157.0 6.3 %all-to-all-start.4 = ((bf16[16,24,1024]{2,1,0:T(8,128)(2,1)}), bf16[16,24,1024]{2,1,0:T(8,128)(2,1)}, u32[]{:S(2)}, u32[]{:S(2)}) async-start(bf16[16,24,1024]{2,1,0:T(8,128)(2,1)} %broadcast_in_dim.23), calls=%async_computation.4 | async-start | bytes 1572864 | tf_op jit(solution)/shard_map/all_to_all | solution.py:304
  165.5 2.8 %shard_map.171.refs_4_ = f32[8,8,224]{2,1,0:T(8,128)S(1)} custom-call(s32[8]{0:T(128)S(1)} %stack.97.place, f32[1,7168]{1,0:T(1,128)S(1)} %bitcast.95, bf16[224,7168]{1,0:T(8,128)(2,1)S(1)} %bitcast.93), custom_call_target="tpu_custom_call" | custom-call | tf_op jit(solution)/shard_map/pallas_call | solution.py:237
  168.3 6.6 %collective-permute-done.15.refs_10_ = bf16[2,224,896]{2,1,0:T(8,128)(2,1)} collective-permute-done((bf16[2,224,896]{2,1,0:T(8,128)(2,1)}, bf16[2,224,896]{2,1,0:T(8,128)(2,1)}, u32[]{:S(2)}, u32[]{:S(2)}) %collective-permute-start.15) | collective-permute-done | bytes 802848 | tf_op jit(solution)/shard_map/ppermute | solution.py:88
  176.0 4.2 %shard_map.172 = (bf16[4,384,256]{2,1,0:T(8,128)(2,1)S(1)}, bf16[4,384,256]{2,1,0:T(8,128)(2,1)S(1)}) custom-call(bf16[384,1024]{1,0:T(8,128)(2,1)} %bitcast.22.refs_0_, bf16[2,224,896]{2,1,0:T(8,128)(2,1)S(1)} %copy-done.5, bf16[2,224,896]{2,1,0:T(8,128)(2,1)} %collective-permute-done.1.refs_2_, bf16[2,224,896]{2,1,0:T(8,128)(2,1)} %collective-permute-done.3.refs_3_, ...), custom_call_target="tpu_custom_call" | custom-call | tf_op jit(solution)/shard_map/pallas_call | solution.py:265
  180.2 3.8 %collective-permute-start.19 = (bf16[4,384,256]{2,1,0:T(8,128)(2,1)S(1)}, bf16[4,384,256]{2,1,0:T(8,128)(2,1)S(1)}, u32[]{:S(2)}, u32[]{:S(2)}) collective-permute-start(bf16[4,384,256]{2,1,0:T(8,128)(2,1)S(1)} %get-tuple-element.90), channel_id=1, source_target_pairs={{0,16},{16,0},{1,17},{17,1},{2,18},{18,2},{3,19},{19,3},{4,20},{20... | collective-permute-start | bytes 2359304 | tf_op jit(solution)/shard_map/ppermute | solution.py:84
  189.0 3.4 %collective-permute-done.20.refs_1_ = bf16[384,256]{1,0:T(8,128)(2,1)S(1)} collective-permute-done((bf16[384,256]{1,0:T(8,128)(2,1)S(1)}, bf16[384,256]{1,0:T(8,128)(2,1)S(1)}, u32[]{:S(2)}, u32[]{:S(2)}) %collective-permute-start.20) | collective-permute-done | bytes 196640 | tf_op jit(solution)/shard_map/ppermute | solution.py:88
  192.3 2.5 collective-permute-done.21.refs_2_
  194.8 5.2 %collective-permute-done.22.refs_3_ = bf16[384,256]{1,0:T(8,128)(2,1)S(1)} collective-permute-done((bf16[384,256]{1,0:T(8,128)(2,1)S(1)}, bf16[384,256]{1,0:T(8,128)(2,1)S(1)}, u32[]{:S(2)}, u32[]{:S(2)}) %collective-permute-start.22) | collective-permute-done | bytes 196640 | tf_op jit(solution)/shard_map/ppermute | solution.py:88
  207.0 6.2 %collective-permute-done.23.refs_1_ = bf16[384,224]{1,0:T(8,128)(2,1)S(1)} collective-permute-done((bf16[384,224]{1,0:T(8,128)(2,1)S(1)}, bf16[384,224]{1,0:T(8,128)(2,1)S(1)}, u32[]{:S(2)}, u32[]{:S(2)}) %collective-permute-start.23) | collective-permute-done | bytes 172064 | tf_op jit(solution)/shard_map/ppermute | solution.py:88
  218.9 2.7 %shard_map.174 = bf16[384,896]{1,0:T(8,128)(2,1)S(1)} custom-call(bf16[384,224]{1,0:T(8,128)(2,1)S(1)} %shard_map.173.refs_0_, bf16[384,224]{1,0:T(8,128)(2,1)S(1)} %collective-permute-done.23.refs_1_, bf16[384,224]{1,0:T(8,128)(2,1)S(1)} %collective-permute-done.24.refs_2_, bf16[384,224]{1,0:T(8,128)(2,1)S(1)} %collective-permute-done.25.refs_3_, ...), custom_call_target="tpu_custom_call" | custom-call | tf_op jit(solution)/shard_map/pallas_call | solution.py:277
  222.4 5.5 %all-to-all-start.5 = ((bf16[16,24,896]{2,1,0:T(8,128)(2,1)}), bf16[16,24,896]{2,1,0:T(8,128)(2,1)S(1)}, u32[]{:S(2)}, u32[]{:S(2)}) async-start(bf16[16,24,896]{2,1,0:T(8,128)(2,1)} %bitcast.94), calls=%async_computation.5 | async-start | bytes 1376256 | tf_op jit(solution)/shard_map/all_to_all | solution.py:310
  228.0 15.3 %collective-permute-done.30 = bf16[4,3,14336]{2,1,0:T(4,128)(2,1)} collective-permute-done((bf16[4,3,14336]{2,1,0:T(4,128)(2,1)}, bf16[4,3,14336]{2,1,0:T(4,128)(2,1)}, u32[]{:S(2)}, u32[]{:S(2)}) %collective-permute-start.30) | collective-permute-done | bytes 344096 | tf_op jit(solution)/shard_map/ppermute | solution.py:88
  243.3 3.0 %pad_maximum_fusion = bf16[4,4,3,14336]{3,2,1,0:T(4,128)(2,1)S(1)} fusion(bf16[1,4,3,14336]{3,2,1,0:T(4,128)(2,1)} %bitcast.46, bf16[1,4,3,14336]{3,2,1,0:T(4,128)(2,1)} %bitcast.45, bf16[1,4,3,14336]{3,2,1,0:T(4,128)(2,1)} %bitcast.44, bf16[1,4,3,14336]{3,2,1,0:T(4,128)(2,1)} %bitcast.43), kind=kLoop, calls=%fused_computation.1 | loop fusion | flops 2064384 | bytes 2752512 | tf_op jit(solution)/shard_map/stack | solution.py:482
  250.8 3.8 %all-to-all-start.6 = ((bf16[8,3,896]{2,1,0:T(4,128)(2,1)}), bf16[8,3,896]{2,1,0:T(4,128)(2,1)S(1)}, u32[]{:S(2)}, u32[]{:S(2)}) async-start(bf16[8,3,896]{2,1,0:T(4,128)(2,1)} %reshape.284), calls=%async_computation.6 | async-start | bytes 114688 | tf_op jit(solution)/shard_map/all_to_all | solution.py:310
  255.4 4.0 %all-to-all-done.6 = bf16[8,3,896]{2,1,0:T(4,128)(2,1)S(1)} async-done(((bf16[8,3,896]{2,1,0:T(4,128)(2,1)}), bf16[8,3,896]{2,1,0:T(4,128)(2,1)S(1)}, u32[]{:S(2)}, u32[]{:S(2)}) %all-to-all-start.6) | async-done | bytes 43040 | tf_op jit(solution)/shard_map/all_to_all | solution.py:310
  (181 shorter events, 87.4 us)
Async XLA Ops:
  5.5 10.7 %collective-permute-start = (bf16[224,3584]{1,0:T(8,128)(2,1)}, bf16[224,3584]{1,0:T(8,128)(2,1)}, u32[]{:S(2)}, u32[]{:S(2)}) collective-permute-start(bf16[224,3584]{1,0:T(8,128)(2,1)} %constant_dynamic-slice_fusion.6), channel_id=1, source_target_pairs={{0,16},{16,0},{1,17},{17,1},{2,18},{18,2},{3,19},{19,3},{4,20},{20... | collective-permute-start | bytes 4816904 | tf_op jit(solution)/shard_map/ppermute | solution.py:84
  7.0 22.0 %all-to-all-start = ((bf16[16,3,7168]{2,1,0:T(4,128)(2,1)}), bf16[16,3,7168]{2,1,0:T(4,128)(2,1)}, u32[]{:S(2)}, u32[]{:S(2)}) async-start(bf16[16,3,7168]{2,1,0:T(4,128)(2,1)} %broadcast_in_dim.18), calls=%async_computation | async-start | bytes 1835008 | tf_op jit(solution)/shard_map/all_to_all | solution.py:310
  21.5 23.7 %collective-permute-start.1 = (bf16[2,224,896]{2,1,0:T(8,128)(2,1)}, bf16[2,224,896]{2,1,0:T(8,128)(2,1)}, u32[]{:S(2)}, u32[]{:S(2)}) collective-permute-start(bf16[2,224,896]{2,1,0:T(8,128)(2,1)} %get-tuple-element.52), channel_id=1, source_target_pairs={{0,32},{32,64},{64,96},{96,0},{1,33},{33,65},{65,97},{97,1},{2,34}... | collective-permute-start | bytes 2408456 | tf_op jit(solution)/shard_map/ppermute | solution.py:88
  23.2 22.1 %collective-permute-start.2 = (bf16[2,224,896]{2,1,0:T(8,128)(2,1)}, bf16[2,224,896]{2,1,0:T(8,128)(2,1)}, u32[]{:S(2)}, u32[]{:S(2)}) collective-permute-start(bf16[2,224,896]{2,1,0:T(8,128)(2,1)} %get-tuple-element.53), channel_id=1, source_target_pairs={{0,96},{32,0},{64,32},{96,64},{1,97},{33,1},{65,33},{97,65},{2,98}... | collective-permute-start | bytes 2408456 | tf_op jit(solution)/shard_map/ppermute | solution.py:88
  41.6 51.8 %collective-permute-start.3 = (bf16[2,224,896]{2,1,0:T(8,128)(2,1)}, bf16[2,224,896]{2,1,0:T(8,128)(2,1)}, u32[]{:S(2)}, u32[]{:S(2)}) collective-permute-start(bf16[2,224,896]{2,1,0:T(8,128)(2,1)} %get-tuple-element.55), channel_id=1, source_target_pairs={{0,64},{32,96},{64,0},{96,32},{1,65},{33,97},{65,1},{97,33},{2,66}... | collective-permute-start | bytes 2408456 | tf_op jit(solution)/shard_map/ppermute | solution.py:88
  47.5 42.4 %all-to-all-start.1 = ((bf16[16,3,8192]{2,1,0:T(4,128)(2,1)}), bf16[16,3,8192]{2,1,0:T(4,128)(2,1)}, u32[]{:S(2)}, u32[]{:S(2)}) async-start(bf16[16,3,8192]{2,1,0:T(4,128)(2,1)} %reshape.276), calls=%async_computation.1 | async-start | bytes 2097152 | tf_op jit(solution)/shard_map/all_to_all | solution.py:310
  52.2 23.4 %collective-permute-start.5 = (bf16[3,3584]{1,0:T(4,128)(2,1)S(1)}, bf16[3,3584]{1,0:T(4,128)(2,1)S(1)}, u32[]{:S(2)}, u32[]{:S(2)}) collective-permute-start(bf16[3,3584]{1,0:T(4,128)(2,1)S(1)} %get-tuple-element.120), channel_id=1, source_target_pairs={{0,16},{16,0},{1,17},{17,1},{2,18},{18,2},{3,19},{19,3},{4,20},{20... | collective-permute-start | bytes 64520 | tf_op jit(solution)/shard_map/ppermute | solution.py:84
  72.6 20.9 %collective-permute-start.4 = (bf16[224,3584]{1,0:T(8,128)(2,1)}, bf16[224,3584]{1,0:T(8,128)(2,1)}, u32[]{:S(2)}, u32[]{:S(2)}) collective-permute-start(bf16[224,3584]{1,0:T(8,128)(2,1)} %constant_dynamic-slice_fusion.5), channel_id=1, source_target_pairs={{0,16},{16,0},{1,17},{17,1},{2,18},{18,2},{3,19},{19,3},{4,20},{20... | collective-permute-start | bytes 4816904 | tf_op jit(solution)/shard_map/ppermute | solution.py:84
  82.0 7.1 %collective-permute-start.9 = (bf16[2,56,896]{2,1,0:T(8,128)(2,1)}, bf16[2,56,896]{2,1,0:T(8,128)(2,1)S(1)}, u32[]{:S(2)}, u32[]{:S(2)}) collective-permute-start(bf16[2,56,896]{2,1,0:T(8,128)(2,1)} %copy-done.14), channel_id=1, source_target_pairs={{0,32},{32,64},{64,96},{96,0},{1,33},{33,65},{65,97},{97,1},{2,34}... | collective-permute-start | bytes 602120 | tf_op jit(solution)/shard_map/ppermute | solution.py:88
  84.7 21.5 %collective-permute-start.10 = (bf16[2,56,896]{2,1,0:T(8,128)(2,1)}, bf16[2,56,896]{2,1,0:T(8,128)(2,1)}, u32[]{:S(2)}, u32[]{:S(2)}) collective-permute-start(bf16[2,56,896]{2,1,0:T(8,128)(2,1)} %copy-done.13), channel_id=1, source_target_pairs={{0,64},{32,96},{64,0},{96,32},{1,65},{33,97},{65,1},{97,33},{2,66}... | collective-permute-start | bytes 602120 | tf_op jit(solution)/shard_map/ppermute | solution.py:88
  86.0 21.8 %collective-permute-start.11 = (bf16[2,56,896]{2,1,0:T(8,128)(2,1)}, bf16[2,56,896]{2,1,0:T(8,128)(2,1)}, u32[]{:S(2)}, u32[]{:S(2)}) collective-permute-start(bf16[2,56,896]{2,1,0:T(8,128)(2,1)} %copy-done.12), channel_id=1, source_target_pairs={{0,96},{32,0},{64,32},{96,64},{1,97},{33,1},{65,33},{97,65},{2,98}... | collective-permute-start | bytes 602120 | tf_op jit(solution)/shard_map/ppermute | solution.py:88
  94.4 23.6 %all-to-all-start.2 = ((bf16[128,3,224]{2,1,0:T(4,128)(2,1)}), bf16[128,3,224]{2,1,0:T(4,128)(2,1)}, u32[]{:S(2)}, u32[]{:S(2)}) async-start(bf16[128,3,224]{2,1,0:T(4,128)(2,1)} %copy.69), calls=%async_computation.2 | async-start | bytes 524288 | tf_op jit(solution)/shard_map/all_to_all | solution.py:310
  127.6 17.7 %all-to-all-start.3 = ((bf16[16,24,896]{2,1,0:T(8,128)(2,1)}), bf16[16,24,896]{2,1,0:T(8,128)(2,1)}, u32[]{:S(2)}, u32[]{:S(2)}) async-start(bf16[16,24,896]{2,1,0:T(8,128)(2,1)} %bitcast.101), calls=%async_computation.3 | async-start | bytes 1376256 | tf_op jit(solution)/shard_map/all_to_all | solution.py:310
  133.6 21.3 %collective-permute-start.13 = (bf16[2,224,896]{2,1,0:T(8,128)(2,1)}, bf16[2,224,896]{2,1,0:T(8,128)(2,1)}, u32[]{:S(2)}, u32[]{:S(2)}) collective-permute-start(bf16[2,224,896]{2,1,0:T(8,128)(2,1)} %copy-done.11), channel_id=1, source_target_pairs={{0,32},{32,64},{64,96},{96,0},{1,33},{33,65},{65,97},{97,1},{2,34}... | collective-permute-start | bytes 2408456 | tf_op jit(solution)/shard_map/ppermute | solution.py:88
  135.1 20.9 %collective-permute-start.14 = (bf16[2,224,896]{2,1,0:T(8,128)(2,1)}, bf16[2,224,896]{2,1,0:T(8,128)(2,1)}, u32[]{:S(2)}, u32[]{:S(2)}) collective-permute-start(bf16[2,224,896]{2,1,0:T(8,128)(2,1)} %copy-done.10), channel_id=1, source_target_pairs={{0,96},{32,0},{64,32},{96,64},{1,97},{33,1},{65,33},{97,65},{2,98}... | collective-permute-start | bytes 2408456 | tf_op jit(solution)/shard_map/ppermute | solution.py:88
  138.4 24.9 %collective-permute-start.18 = (bf16[3,14336]{1,0:T(4,128)(2,1)}, bf16[3,14336]{1,0:T(4,128)(2,1)}, u32[]{:S(2)}, u32[]{:S(2)}) collective-permute-start(bf16[3,14336]{1,0:T(4,128)(2,1)} %constant_dynamic-update-slice_fusion.4), channel_id=1, source_target_pairs={{0,12},{4,0},{8,4},{12,8},{1,13},{5,1},{9,5},{13,9},{2,14},{6,2},{... | collective-permute-start | bytes 258056 | tf_op jit(solution)/shard_map/ppermute | solution.py:88
  140.9 22.4 %collective-permute-start.17 = (bf16[3,14336]{1,0:T(4,128)(2,1)}, bf16[3,14336]{1,0:T(4,128)(2,1)}, u32[]{:S(2)}, u32[]{:S(2)}) collective-permute-start(bf16[3,14336]{1,0:T(4,128)(2,1)} %constant_dynamic-update-slice_fusion.4), channel_id=1, source_target_pairs={{0,8},{4,12},{8,0},{12,4},{1,9},{5,13},{9,1},{13,5},{2,10},{6,14},... | collective-permute-start | bytes 258056 | tf_op jit(solution)/shard_map/ppermute | solution.py:88
  141.5 21.8 %collective-permute-start.16 = (bf16[3,14336]{1,0:T(4,128)(2,1)}, bf16[3,14336]{1,0:T(4,128)(2,1)}, u32[]{:S(2)}, u32[]{:S(2)}) collective-permute-start(bf16[3,14336]{1,0:T(4,128)(2,1)} %constant_dynamic-update-slice_fusion.4), channel_id=1, source_target_pairs={{0,4},{4,8},{8,12},{12,0},{1,5},{5,9},{9,13},{13,1},{2,6},{6,10},{... | collective-permute-start | bytes 258056 | tf_op jit(solution)/shard_map/ppermute | solution.py:88
  154.9 20.0 %collective-permute-start.15 = (bf16[2,224,896]{2,1,0:T(8,128)(2,1)}, bf16[2,224,896]{2,1,0:T(8,128)(2,1)}, u32[]{:S(2)}, u32[]{:S(2)}) collective-permute-start(bf16[2,224,896]{2,1,0:T(8,128)(2,1)} %copy-done.9), channel_id=1, source_target_pairs={{0,64},{32,96},{64,0},{96,32},{1,65},{33,97},{65,1},{97,33},{2,66}... | collective-permute-start | bytes 2408456 | tf_op jit(solution)/shard_map/ppermute | solution.py:88
  157.0 17.9 %all-to-all-start.4 = ((bf16[16,24,1024]{2,1,0:T(8,128)(2,1)}), bf16[16,24,1024]{2,1,0:T(8,128)(2,1)}, u32[]{:S(2)}, u32[]{:S(2)}) async-start(bf16[16,24,1024]{2,1,0:T(8,128)(2,1)} %broadcast_in_dim.23), calls=%async_computation.4 | async-start | bytes 1572864 | tf_op jit(solution)/shard_map/all_to_all | solution.py:304
  186.2 6.2 %collective-permute-start.20 = (bf16[384,256]{1,0:T(8,128)(2,1)S(1)}, bf16[384,256]{1,0:T(8,128)(2,1)S(1)}, u32[]{:S(2)}, u32[]{:S(2)}) collective-permute-start(bf16[384,256]{1,0:T(8,128)(2,1)S(1)} %get-tuple-element.103), channel_id=1, source_target_pairs={{0,96},{32,0},{64,32},{96,64},{1,97},{33,1},{65,33},{97,65},{2,98}... | collective-permute-start | bytes 589832 | tf_op jit(solution)/shard_map/ppermute | solution.py:88
  187.5 7.3 %collective-permute-start.21 = (bf16[384,256]{1,0:T(8,128)(2,1)S(1)}, bf16[384,256]{1,0:T(8,128)(2,1)S(1)}, u32[]{:S(2)}, u32[]{:S(2)}) collective-permute-start(bf16[384,256]{1,0:T(8,128)(2,1)S(1)} %get-tuple-element.102), channel_id=1, source_target_pairs={{0,64},{32,96},{64,0},{96,32},{1,65},{33,97},{65,1},{97,33},{2,66}... | collective-permute-start | bytes 589832 | tf_op jit(solution)/shard_map/ppermute | solution.py:88
  188.6 11.5 %collective-permute-start.22 = (bf16[384,256]{1,0:T(8,128)(2,1)S(1)}, bf16[384,256]{1,0:T(8,128)(2,1)S(1)}, u32[]{:S(2)}, u32[]{:S(2)}) collective-permute-start(bf16[384,256]{1,0:T(8,128)(2,1)S(1)} %get-tuple-element.101), channel_id=1, source_target_pairs={{0,32},{32,64},{64,96},{96,0},{1,33},{33,65},{65,97},{97,1},{2,34}... | collective-permute-start | bytes 589832 | tf_op jit(solution)/shard_map/ppermute | solution.py:88
  201.7 11.5 %collective-permute-start.23 = (bf16[384,224]{1,0:T(8,128)(2,1)S(1)}, bf16[384,224]{1,0:T(8,128)(2,1)S(1)}, u32[]{:S(2)}, u32[]{:S(2)}) collective-permute-start(bf16[384,224]{1,0:T(8,128)(2,1)S(1)} %shard_map.173.refs_0_), channel_id=1, source_target_pairs={{0,32},{32,64},{64,96},{96,0},{1,33},{33,65},{65,97},{97,1},{2,34}... | collective-permute-start | bytes 516104 | tf_op jit(solution)/shard_map/ppermute | solution.py:88
  201.8 12.2 %collective-permute-start.24 = (bf16[384,224]{1,0:T(8,128)(2,1)S(1)}, bf16[384,224]{1,0:T(8,128)(2,1)S(1)}, u32[]{:S(2)}, u32[]{:S(2)}) collective-permute-start(bf16[384,224]{1,0:T(8,128)(2,1)S(1)} %shard_map.173.refs_0_), channel_id=1, source_target_pairs={{0,64},{32,96},{64,0},{96,32},{1,65},{33,97},{65,1},{97,33},{2,66}... | collective-permute-start | bytes 516104 | tf_op jit(solution)/shard_map/ppermute | solution.py:88
  203.0 11.6 %collective-permute-start.25 = (bf16[384,224]{1,0:T(8,128)(2,1)S(1)}, bf16[384,224]{1,0:T(8,128)(2,1)S(1)}, u32[]{:S(2)}, u32[]{:S(2)}) collective-permute-start(bf16[384,224]{1,0:T(8,128)(2,1)S(1)} %shard_map.173.refs_0_), channel_id=1, source_target_pairs={{0,96},{32,0},{64,32},{96,64},{1,97},{33,1},{65,33},{97,65},{2,98}... | collective-permute-start | bytes 516104 | tf_op jit(solution)/shard_map/ppermute | solution.py:88
  204.9 11.5 %collective-permute-start.26 = (bf16[384,224]{1,0:T(8,128)(2,1)S(1)}, bf16[384,224]{1,0:T(8,128)(2,1)S(1)}, u32[]{:S(2)}, u32[]{:S(2)}) collective-permute-start(bf16[384,224]{1,0:T(8,128)(2,1)S(1)} %shard_map.173.refs_0_), channel_id=1, source_target_pairs={{0,16},{16,0},{1,17},{17,1},{2,18},{18,2},{3,19},{19,3},{4,20},{20... | collective-permute-start | bytes 516104 | tf_op jit(solution)/shard_map/ppermute | solution.py:84
  206.3 21.7 %collective-permute-start.32 = (bf16[4,3,14336]{2,1,0:T(4,128)(2,1)}, bf16[4,3,14336]{2,1,0:T(4,128)(2,1)}, u32[]{:S(2)}, u32[]{:S(2)}) collective-permute-start(bf16[4,3,14336]{2,1,0:T(4,128)(2,1)} %pad_maximum_fusion.1), channel_id=1, source_target_pairs={{0,3},{1,0},{2,1},{3,2},{4,7},{5,4},{6,5},{7,6},{8,11},{9,8},{10,9... | collective-permute-start | bytes 1032200 | tf_op jit(solution)/shard_map/ppermute | solution.py:88
  213.2 14.8 %collective-permute-start.31 = (bf16[4,3,14336]{2,1,0:T(4,128)(2,1)}, bf16[4,3,14336]{2,1,0:T(4,128)(2,1)}, u32[]{:S(2)}, u32[]{:S(2)}) collective-permute-start(bf16[4,3,14336]{2,1,0:T(4,128)(2,1)} %pad_maximum_fusion.1), channel_id=1, source_target_pairs={{0,2},{1,3},{2,0},{3,1},{4,6},{5,7},{6,4},{7,5},{8,10},{9,11},{10,... | collective-permute-start | bytes 1032200 | tf_op jit(solution)/shard_map/ppermute | solution.py:88
  214.0 29.2 %collective-permute-start.30 = (bf16[4,3,14336]{2,1,0:T(4,128)(2,1)}, bf16[4,3,14336]{2,1,0:T(4,128)(2,1)}, u32[]{:S(2)}, u32[]{:S(2)}) collective-permute-start(bf16[4,3,14336]{2,1,0:T(4,128)(2,1)} %pad_maximum_fusion.1), channel_id=1, source_target_pairs={{0,1},{1,2},{2,3},{3,0},{4,5},{5,6},{6,7},{7,4},{8,9},{9,10},{10,1... | collective-permute-start | bytes 1032200 | tf_op jit(solution)/shard_map/ppermute | solution.py:88
  222.4 27.5 %all-to-all-start.5 = ((bf16[16,24,896]{2,1,0:T(8,128)(2,1)}), bf16[16,24,896]{2,1,0:T(8,128)(2,1)S(1)}, u32[]{:S(2)}, u32[]{:S(2)}) async-start(bf16[16,24,896]{2,1,0:T(8,128)(2,1)} %bitcast.94), calls=%async_computation.5 | async-start | bytes 1376256 | tf_op jit(solution)/shard_map/all_to_all | solution.py:310
  250.8 8.7 %all-to-all-start.6 = ((bf16[8,3,896]{2,1,0:T(4,128)(2,1)}), bf16[8,3,896]{2,1,0:T(4,128)(2,1)S(1)}, u32[]{:S(2)}, u32[]{:S(2)}) async-start(bf16[8,3,896]{2,1,0:T(4,128)(2,1)} %reshape.284), calls=%async_computation.6 | async-start | bytes 114688 | tf_op jit(solution)/shard_map/all_to_all | solution.py:310
  (32 other events, 230.5 us)

commit v8 on v7

--- a/solution.py
+++ b/solution.py
@@ -84,8 +84,8 @@
     return lax.ppermute(x, "c", [(0, 1), (1, 0)])
 
 
-def shift(x, step, size, axis="z"):
-    return lax.ppermute(x, axis, [(i, (i + step) % size) for i in range(size)])
+def shift(x, step, size):
+    return lax.ppermute(x, "z", [(i, (i + step) % size) for i in range(size)])
 
 
 def after(x, first):
@@ -366,6 +366,23 @@
     up_w = after(w_up.T, wide_q)
     ups = send(reshard(up_w, swap(up_w)))
 
+    res = after(resid, wide_q)
+    res = jnp.stack(
+        [
+            lax.dynamic_slice_in_dim(res, c * half, half, 1),
+            pair(lax.dynamic_slice_in_dim(res, (1 - c) * half, half, 1)),
+        ]
+    ).reshape(cs * rows_dev, half)
+    res_parts = []
+    for d in range(zs):
+        part = lax.dynamic_slice_in_dim(res, ((z + d) % zs) * chunk, chunk, 1)
+        res_parts.append(shift(part, d, zs) if d else part)
+    res = jnp.concatenate(res_parts, axis=0)
+    at = jnp.arange(block, dtype=jnp.int32)
+    source = ((z - at // (cs * rows_dev)) % zs) * cs + (c + at // rows_dev) % cs
+    order = at[:, None] == (source * rows_dev + at % rows_dev)[None, :]
+    res = jnp.dot(order.astype(BF16), res, preferred_element_type=F32)
+
     page_ids = member * pages_dev + jnp.arange(pages_dev, dtype=jnp.int32)
     owners = jnp.any(page_table[:, :, None] == page_ids[None, None, :], axis=1)
     pool_mask = jnp.repeat(jnp.repeat(owners, page_len, axis=1), tree_len, axis=0).astype(F32)
@@ -394,29 +411,12 @@
         heads // 7,
     )
 
-    parts, ups[1], ups[3] = lax.optimization_barrier((parts, ups[1], ups[3]))
+    parts, ups[1], ups[3], res = lax.optimization_barrier((parts, ups[1], ups[3], res))
 
     wo = after(w_out, parts)
     wo_parts = send(cut(jnp.concatenate([own_turn, other_turn]), wo, wo, zs, chunk))
     wo_parts = jnp.concatenate(wo_parts, axis=1)
     down_other = swap(after(w_down, parts))
-
-    res = after(resid, parts)
-    res = jnp.stack(
-        [
-            lax.dynamic_slice_in_dim(res, c * half, half, 1),
-            pair(lax.dynamic_slice_in_dim(res, (1 - c) * half, half, 1)),
-        ]
-    ).reshape(cs * rows_dev, half)
-    res_parts = []
-    for d in range(zs):
-        part = lax.dynamic_slice_in_dim(res, ((z + d) % zs) * chunk, chunk, 1)
-        res_parts.append(shift(part, d, zs) if d else part)
-    res = jnp.concatenate(res_parts, axis=0)
-    at = jnp.arange(block, dtype=jnp.int32)
-    source = ((z - at // (cs * rows_dev)) % zs) * cs + (c + at // rows_dev) % cs
-    order = at[:, None] == (source * rows_dev + at % rows_dev)[None, :]
-    res = jnp.dot(order.astype(BF16), res, preferred_element_type=F32)
 
     parts = exchange(parts.reshape(members, rows_dev, parts.shape[1]), MLP)
     parts = parts.reshape(members, rows_dev, heads // 7, 8, HD).astype(F32)
@@ -434,12 +434,12 @@
             for to in range(zs)
         ]
     ).reshape(groups * members, rows_dev, zs * k_dev)
-    feats, ups[2], down_other, res = lax.optimization_barrier((feats, ups[2], down_other, res))
+    feats, ups[2], down_other, wo_parts = lax.optimization_barrier(
+        (feats, ups[2], down_other, wo_parts)
+    )
     downs = reshard(*after((w_down, down_other), feats))
-    draft_k, draft_v = after((keys_new, values_new), feats)
-    both = jnp.concatenate([draft_k, draft_v], axis=1)
-    both = [shift(both, d, xs, "x") if d else both for d in range(xs)]
-    feats = exchange(feats, ALL)
+    feats, downs = lax.optimization_barrier((exchange(feats, ALL), downs))
+    downs = send(downs)
     feats = (
         feats.reshape(groups, members, rows_dev, zs * k_dev)
         .transpose(1, 0, 2, 3)
@@ -449,8 +449,6 @@
     sent = pair(jnp.dot(feats, wo_pair, preferred_element_type=F32).astype(BF16))
     part = jnp.dot(feats, wo_own, preferred_element_type=F32) + sent.astype(F32)
     part = part.astype(BF16).reshape(members, block, chunk)
-    part, downs = lax.optimization_barrier((part, downs))
-    downs = send(downs)
     part = exchange(part, MLP)
     gain = lax.dynamic_slice_in_dim(ln_gain, c * half + z * chunk, chunk, 0)
 
@@ -462,15 +460,19 @@
         ),
         compiler_params=params(),
     )(part, res, gain[None])
-    row, downs[1], downs[3] = lax.optimization_barrier((row, downs[1], downs[3]))
     rows = spread(row, MLP, members).reshape(tokens, chunk + HD)
 
     order = jnp.stack(
         [(c + e) % cs * zs + (z + d) % zs for d in range(zs) for e in range(cs)]
     ).astype(jnp.int32)
     gain_up = gain_products(order, ln_gain[None], after(w_up.T, row), chunk)
-    both = jnp.stack(both)
-    rows, downs, gain_up, both = lax.optimization_barrier((rows, downs, gain_up, both))
+    draft_k, draft_v = after((keys_new, values_new), row)
+    both = jnp.broadcast_to(
+        jnp.concatenate([draft_k, draft_v], axis=1)[None], (members, rows_dev, 2 * width)
+    )
+    rows, gain_up, both, downs = lax.optimization_barrier((rows, gain_up, both, downs))
+
+    both = exchange(after(both, rows), MLP)
 
     mine, theirs = up_project(rows, ups)
     theirs = pair(theirs)
@@ -478,8 +480,6 @@
     for d in range(zs):
         term = mine[d].astype(F32) + theirs[d].astype(F32)
         terms.append(shift(term.astype(BF16), -d, zs) if d else term)
-    both = after(both, terms[1])
-    both = jnp.stack([shift(both, d, ys, "y") if d else both for d in range(ys)])
     units = w_down.shape[0]
     act = pl.pallas_call(
         lambda *refs: act_kernel(width, units, zs, *refs),
@@ -488,6 +488,7 @@
     )(*terms, gain_up)
     acts = [shift(act, d, zs) if d else act for d in range(zs)]
     down = down_project(acts, [pair(a) for a in acts], downs)
+    down, both = lax.optimization_barrier((down, both))
     down = exchange(down.reshape(members, block, chunk), MLP)
     mixed = finish(down, hidden)
     mixed = exchange(mixed.reshape(groups, rows_dev, chunk), REQ)
@@ -495,11 +496,7 @@
 
     valid = (accepted >= 0) & (dest_slot == member)[:, None]
     target = jnp.arange(requests, dtype=jnp.int32)[:, None] * tree_len + jnp.maximum(accepted, 0)
-    x, y = lax.axis_index("x"), lax.axis_index("y")
-    at = jnp.arange(group_rows, dtype=jnp.int32)
-    near = at // rows_dev
-    slots = (((x - near % xs) % xs) * ys + (y - near // xs) % ys) * rows_dev + at % rows_dev
-    chooser = jnp.any((target[:, :, None] == slots[None, None, :]) & valid[:, :, None], axis=0)
+    chooser = jnp.any((target[:, :, None] == row_ids[None, None, :]) & valid[:, :, None], axis=0)
     both = both.reshape(group_rows, 2 * width)
     picked = jnp.dot(chooser.astype(BF16), both, preferred_element_type=F32).astype(BF16)
     return (mixed, picked[:, :width][None], picked[:, width:][None])

time: 262 us -> 259 us (0.989)
  waiting for transfers between devices: 64.6 us -> 95.6 us
  starting transfers between devices: 104 us -> 82.9 us
  local copies, waits for them, and re-layouts: 42.7 us -> 34.7 us
  other arithmetic: 10.3 us -> 6.33 us
    ppermute x24 -> x18, waiting for transfers between devices: 50.6 us -> 69.7 us  [shift(): return lax.ppermute(x, 'z', [(i, (i + step) % size) for i in range(size)])]
    ppermute x9, starting transfers between devices: 28 us -> 9.21 us  [pair(): return lax.ppermute(x, 'c', [(0, 1), (1, 0)])]
    all_to_all x6 -> x7, waiting for transfers between devices: 9.96 us -> 21.5 us  [exchange(): return lax.all_to_all(x, axes, split_axis=0, concat_axis=0)]
    ppermute x24 -> x18, starting transfers between devices: 31.4 us -> 21.8 us  [shift(): return lax.ppermute(x, 'z', [(i, (i + step) % size) for i in range(size)])]
    all_to_all x6 -> x7, starting transfers between devices: 38.7 us -> 47.5 us  [exchange(): return lax.all_to_all(x, axes, split_axis=0, concat_axis=0)]
    unnamed x53 -> x41, local copies, waits for them, and re-layouts: 15.3 us -> 8.79 us
    another operation x2 -> x0, other arithmetic: 5.19 us -> none  [the longest x1 2.99 us: local(): jnp.stack([shift(both, d, ys, 'y') if d else both for d in range(ys)])]
    concatenate x2 -> x0, local copies, waits for them, and re-layouts: 3.1 us -> none  [the longest x1 1.64 us: local(): wo_parts = jnp.concatenate(wo_parts, axis=1)]
  transfers between devices with their start and end apart: 40 -> 35, of which waited for: 16 -> 18; matrix products, arithmetic and copies ran while one was open for 14% -> 8% of each run, Pallas kernels for 10% -> 11%
where the time goes in v8:
time: 259 us; the launch traced here: 258 us
  waiting for transfers between devices  95.6 us (37%)
  starting transfers between devices  82.9 us (32%)
  local copies, waits for them, and re-layouts  34.7 us (13%)
  Pallas kernels  32.8 us (13%)
  other arithmetic  6.33 us (2%)
  matrix products  4.24 us (2%)
    ppermute x18, waiting for transfers between devices, shift(): return lax.ppermute(x, 'z', [(i, (i + step) % size) for i in range(size)])  69.7 us
    all_to_all x7, starting transfers between devices, exchange(): return lax.all_to_all(x, axes, split_axis=0, concat_axis=0)  47.5 us
    ppermute x18, starting transfers between devices, shift(): return lax.ppermute(x, 'z', [(i, (i + step) % size) for i in range(size)])  21.8 us
    all_to_all x7, waiting for transfers between devices, exchange(): return lax.all_to_all(x, axes, split_axis=0, concat_axis=0)  21.5 us
    pallas_call x1, Pallas kernels, attend(): pl.pallas_call(body, grid=(steps,), in_specs=[pl.BlockSpec((rows, wide),...  10.2 us
    ppermute x9, starting transfers between devices, pair(): return lax.ppermute(x, 'c', [(0, 1), (1, 0)])  9.21 us
    unnamed x41, local copies, waits for them, and re-layouts  8.79 us
    pallas_call x3, Pallas kernels, cut(): pl.pallas_call(lambda *refs: cut_kernel(n, *refs), grid_spec=pltpu.Prefet...  8.03 us
  transfers between devices with their start and end apart: 35, of which 18 were waited for; matrix products, arithmetic and copies ran while one was open for 8% of the time, Pallas kernels for 11%

profile of v8, /device:TPU:1, one launch (start us, length us, event | category | flops | bytes accessed | tf_op | source)
XLA Modules:
  0.0 257.8 jit_solution(16212370225286181232)
XLA Ops:
  2.6 7.8 %all-to-all-start = ((bf16[16,3,7168]{2,1,0:T(4,128)(2,1)}), bf16[16,3,7168]{2,1,0:T(4,128)(2,1)}, u32[]{:S(2)}, u32[]{:S(2)}) async-start(bf16[16,3,7168]{2,1,0:T(4,128)(2,1)} %broadcast_in_dim.20), calls=%async_computation | async-start | bytes 1835008 | tf_op jit(solution)/shard_map/all_to_all | solution.py:310
  10.5 2.8 %constant_dynamic-slice_fusion.6 = bf16[224,3584]{1,0:T(8,128)(2,1)} fusion(bf16[224,7168]{1,0:T(8,128)(2,1)} %bitcast.85, s32[]{:T(128)S(6)} %select_n.153), kind=kLoop, calls=%fused_computation.76 | loop fusion | bytes 3211268 | tf_op jit(solution)/shard_map/dynamic_slice | solution.py:364
  17.7 4.2 %shard_map.167 = (bf16[2,224,896]{2,1,0:T(8,128)(2,1)S(1)}, bf16[2,224,896]{2,1,0:T(8,128)(2,1)}, bf16[2,224,896]{2,1,0:T(8,128)(2,1)S(1)}, bf16[2,224,896]{2,1,0:T(8,128)(2,1)}) custom-call(s32[8]{0:T(128)S(1)} %get-tuple-element.122.refs_0_, bf16[224,7168]{1,0:T(8,128)(2,1)S(1)} %bitcast.86, bf16[224,3584]{1,0:T(8,128)(2,1)} %collective-permute-done.refs_2_), custom_call_target="tpu_custom_call" | custom-call | tf_op jit(solution)/shard_map/pallas_call | solution.py:218
  31.2 13.8 %collective-permute-done.6 = bf16[6,896]{1,0:T(8,128)(2,1)S(1)} collective-permute-done((bf16[6,896]{1,0:T(8,128)(2,1)S(1)}, bf16[6,896]{1,0:T(8,128)(2,1)S(1)}, u32[]{:S(2)}, u32[]{:S(2)}) %collective-permute-start.6) | collective-permute-done | bytes 10784 | tf_op jit(solution)/shard_map/ppermute | solution.py:88
  46.6 2.4 reshape.202.refs_0_
  49.0 10.2 %shard_map.166 = bf16[48,8192]{1,0:T(8,128)(2,1)} custom-call(bf16[48,7168]{1,0:T(8,128)(2,1)} %reshape.202.refs_0_, bf16[24,16,7168]{2,1,0:T(8,128)(2,1)} %refs_1_.1, bf16[24,16,7168]{2,1,0:T(8,128)(2,1)} %refs_2_.1, bf16[16,7168]{1,0:T(8,128)(2,1)} %pad.7.refs_3_, bf16[16,7168]{1,0:T(8,128)(2,1)} %pad.8.refs_4_, f32[48,400]{1,0:T(8,128)} %pad_maximum_fusion.3.refs_5_), custom_call_target="tpu_custom_call" | custom-call | flops 528482304 | bytes 11010048 | tf_op jit(solution)/shard_map/pallas_call | solution.py:61
  59.2 2.3 reshape.205
  61.5 6.9 %all-to-all-start.1 = ((bf16[16,3,8192]{2,1,0:T(4,128)(2,1)}), bf16[16,3,8192]{2,1,0:T(4,128)(2,1)}, u32[]{:S(2)}, u32[]{:S(2)}) async-start(bf16[16,3,8192]{2,1,0:T(4,128)(2,1)} %reshape.205), calls=%async_computation.1 | async-start | bytes 2097152 | tf_op jit(solution)/shard_map/all_to_all | solution.py:310
  75.1 2.7 %constant_dynamic-slice_fusion = bf16[224,3584]{1,0:T(8,128)(2,1)} fusion(bf16[224,7168]{1,0:T(8,128)(2,1)} %refs_1_.3, s32[]{:T(128)S(6)} %select_n.153), kind=kLoop, calls=%fused_computation.70 | loop fusion | bytes 3211268 | tf_op jit(solution)/shard_map/dynamic_slice | solution.py:364
  77.7 2.5 collective-permute-start.8
  80.2 14.2 %collective-permute-done.11 = bf16[2,56,896]{2,1,0:T(8,128)(2,1)S(1)} collective-permute-done((bf16[2,56,896]{2,1,0:T(8,128)(2,1)S(1)}, bf16[2,56,896]{2,1,0:T(8,128)(2,1)S(1)}, u32[]{:S(2)}, u32[]{:S(2)}) %collective-permute-start.11) | collective-permute-done | bytes 200736 | tf_op jit(solution)/shard_map/ppermute | solution.py:88
  94.4 4.2 %collective-permute-done.9 = bf16[2,56,896]{2,1,0:T(8,128)(2,1)S(1)} collective-permute-done((bf16[2,56,896]{2,1,0:T(8,128)(2,1)S(1)}, bf16[2,56,896]{2,1,0:T(8,128)(2,1)S(1)}, u32[]{:S(2)}, u32[]{:S(2)}) %collective-permute-start.9) | collective-permute-done | bytes 200736 | tf_op jit(solution)/shard_map/ppermute | solution.py:88
  104.2 9.1 %all-to-all-start.2 = ((bf16[128,3,224]{2,1,0:T(4,128)(2,1)}), bf16[128,3,224]{2,1,0:T(4,128)(2,1)}, u32[]{:S(2)}, u32[]{:S(2)}) async-start(bf16[128,3,224]{2,1,0:T(4,128)(2,1)} %copy.69), calls=%async_computation.2 | async-start | bytes 524288 | tf_op jit(solution)/shard_map/all_to_all | solution.py:310
  115.1 3.0 %shard_map.169 = (bf16[2,224,896]{2,1,0:T(8,128)(2,1)S(1)}, bf16[2,224,896]{2,1,0:T(8,128)(2,1)S(1)}, bf16[2,224,896]{2,1,0:T(8,128)(2,1)S(1)}, bf16[2,224,896]{2,1,0:T(8,128)(2,1)S(1)}) custom-call(s32[8]{0:T(128)S(1)} %get-tuple-element.122.refs_0_, bf16[224,7168]{1,0:T(8,128)(2,1)S(1)} %copy-done.1, bf16[224,3584]{1,0:T(8,128)(2,1)} %collective-permute-done.8.refs_2_), custom_call_target="tpu_custom_call" | custom-call | tf_op jit(solution)/shard_map/pallas_call | solution.py:218
  133.4 4.3 %all-to-all-start.3 = ((bf16[16,24,896]{2,1,0:T(8,128)(2,1)}), bf16[16,24,896]{2,1,0:T(8,128)(2,1)}, u32[]{:S(2)}, u32[]{:S(2)}) async-start(bf16[16,24,896]{2,1,0:T(8,128)(2,1)} %bitcast.94), calls=%async_computation.3 | async-start | bytes 1376256 | tf_op jit(solution)/shard_map/all_to_all | solution.py:310
  139.1 2.9 %collective-permute-start.14 = (bf16[2,224,896]{2,1,0:T(8,128)(2,1)}, bf16[2,224,896]{2,1,0:T(8,128)(2,1)}, u32[]{:S(2)}, u32[]{:S(2)}) collective-permute-start(bf16[2,224,896]{2,1,0:T(8,128)(2,1)} %copy-done.10), channel_id=1, source_target_pairs={{0,64},{32,96},{64,0},{96,32},{1,65},{33,97},{65,1},{97,33},{2,66}... | collective-permute-start | bytes 2408456 | tf_op jit(solution)/shard_map/ppermute | solution.py:88
  143.0 6.4 %all-to-all-done.3.parts = bf16[16,24,896]{2,1,0:T(8,128)(2,1)} async-done(((bf16[16,24,896]{2,1,0:T(8,128)(2,1)}), bf16[16,24,896]{2,1,0:T(8,128)(2,1)}, u32[]{:S(2)}, u32[]{:S(2)}) %all-to-all-start.3) | async-done | bytes 688160 | tf_op jit(solution)/shard_map/all_to_all | solution.py:310
  151.7 4.4 %all-to-all-start.4 = ((bf16[16,24,1024]{2,1,0:T(8,128)(2,1)}), bf16[16,24,1024]{2,1,0:T(8,128)(2,1)}, u32[]{:S(2)}, u32[]{:S(2)}) async-start(bf16[16,24,1024]{2,1,0:T(8,128)(2,1)} %broadcast_in_dim.25), calls=%async_computation.4 | async-start | bytes 1572864 | tf_op jit(solution)/shard_map/all_to_all | solution.py:304
  157.0 2.8 %shard_map.171.refs_4_ = f32[8,8,224]{2,1,0:T(8,128)S(1)} custom-call(s32[8]{0:T(128)S(1)} %stack.67.place, f32[1,7168]{1,0:T(1,128)S(1)} %bitcast.88, bf16[224,7168]{1,0:T(8,128)(2,1)S(1)} %bitcast.87), custom_call_target="tpu_custom_call" | custom-call | tf_op jit(solution)/shard_map/pallas_call | solution.py:237
  159.8 17.1 %collective-permute-done.14.refs_10_ = bf16[2,224,896]{2,1,0:T(8,128)(2,1)} collective-permute-done((bf16[2,224,896]{2,1,0:T(8,128)(2,1)}, bf16[2,224,896]{2,1,0:T(8,128)(2,1)}, u32[]{:S(2)}, u32[]{:S(2)}) %collective-permute-start.14) | collective-permute-done | bytes 802848 | tf_op jit(solution)/shard_map/ppermute | solution.py:88
  178.9 5.1 %shard_map.172 = (bf16[4,384,256]{2,1,0:T(8,128)(2,1)S(1)}, bf16[4,384,256]{2,1,0:T(8,128)(2,1)}) custom-call(bf16[384,1024]{1,0:T(8,128)(2,1)} %bitcast.22.refs_0_, bf16[2,224,896]{2,1,0:T(8,128)(2,1)S(1)} %copy-done.4, bf16[2,224,896]{2,1,0:T(8,128)(2,1)} %collective-permute-done.1.refs_2_, bf16[2,224,896]{2,1,0:T(8,128)(2,1)} %collective-permute-done.7.refs_3_, ...), custom_call_target="tpu_custom_call" | custom-call | tf_op jit(solution)/shard_map/pallas_call | solution.py:265
  185.6 6.6 %all-to-all-start.5 = ((bf16[16,3,14336]{2,1,0:T(4,128)(2,1)}), bf16[16,3,14336]{2,1,0:T(4,128)(2,1)}, u32[]{:S(2)}, u32[]{:S(2)}) async-start(bf16[16,3,14336]{2,1,0:T(4,128)(2,1)} %broadcast_in_dim.27), calls=%async_computation.5 | async-start | bytes 3670016 | tf_op jit(solution)/shard_map/all_to_all | solution.py:310
  195.6 3.3 %collective-permute-done.17.refs_1_ = bf16[384,256]{1,0:T(8,128)(2,1)S(1)} collective-permute-done((bf16[384,256]{1,0:T(8,128)(2,1)S(1)}, bf16[384,256]{1,0:T(8,128)(2,1)S(1)}, u32[]{:S(2)}, u32[]{:S(2)}) %collective-permute-start.17) | collective-permute-done | bytes 196640 | tf_op jit(solution)/shard_map/ppermute | solution.py:88
  198.8 3.0 %collective-permute-done.18.refs_2_ = bf16[384,256]{1,0:T(8,128)(2,1)S(1)} collective-permute-done((bf16[384,256]{1,0:T(8,128)(2,1)S(1)}, bf16[384,256]{1,0:T(8,128)(2,1)S(1)}, u32[]{:S(2)}, u32[]{:S(2)}) %collective-permute-start.18) | collective-permute-done | bytes 196640 | tf_op jit(solution)/shard_map/ppermute | solution.py:88
  201.8 5.2 %collective-permute-done.19.refs_3_ = bf16[384,256]{1,0:T(8,128)(2,1)S(1)} collective-permute-done((bf16[384,256]{1,0:T(8,128)(2,1)S(1)}, bf16[384,256]{1,0:T(8,128)(2,1)S(1)}, u32[]{:S(2)}, u32[]{:S(2)}) %collective-permute-start.19) | collective-permute-done | bytes 196640 | tf_op jit(solution)/shard_map/ppermute | solution.py:88
  213.0 7.3 %collective-permute-done.20.refs_1_ = bf16[384,224]{1,0:T(8,128)(2,1)S(1)} collective-permute-done((bf16[384,224]{1,0:T(8,128)(2,1)S(1)}, bf16[384,224]{1,0:T(8,128)(2,1)S(1)}, u32[]{:S(2)}, u32[]{:S(2)}) %collective-permute-start.20) | collective-permute-done | bytes 172064 | tf_op jit(solution)/shard_map/ppermute | solution.py:88
  223.3 3.5 %shard_map.174 = bf16[384,896]{1,0:T(8,128)(2,1)} custom-call(bf16[384,224]{1,0:T(8,128)(2,1)S(1)} %shard_map.173.refs_0_, bf16[384,224]{1,0:T(8,128)(2,1)S(1)} %collective-permute-done.20.refs_1_, bf16[384,224]{1,0:T(8,128)(2,1)S(1)} %collective-permute-done.21.refs_2_, bf16[384,224]{1,0:T(8,128)(2,1)S(1)} %collective-permute-done.22.refs_3_, ...), custom_call_target="tpu_custom_call" | custom-call | tf_op jit(solution)/shard_map/pallas_call | solution.py:277
  226.8 6.5 %all-to-all-start.6 = ((bf16[16,24,896]{2,1,0:T(8,128)(2,1)}), bf16[16,24,896]{2,1,0:T(8,128)(2,1)S(1)}, u32[]{:S(2)}, u32[]{:S(2)}) async-start(bf16[16,24,896]{2,1,0:T(8,128)(2,1)} %bitcast.36), calls=%async_computation.6 | async-start | bytes 1376256 | tf_op jit(solution)/shard_map/all_to_all | solution.py:310
  233.5 2.4 reshape.215
  236.2 8.8 %all-to-all-done.6.parts = bf16[16,24,896]{2,1,0:T(8,128)(2,1)S(1)} async-done(((bf16[16,24,896]{2,1,0:T(8,128)(2,1)}), bf16[16,24,896]{2,1,0:T(8,128)(2,1)S(1)}, u32[]{:S(2)}, u32[]{:S(2)}) %all-to-all-start.6) | async-done | bytes 688160 | tf_op jit(solution)/shard_map/all_to_all | solution.py:310
  245.9 6.4 %all-to-all-start.7 = ((bf16[8,3,896]{2,1,0:T(4,128)(2,1)}), bf16[8,3,896]{2,1,0:T(4,128)(2,1)S(1)}, u32[]{:S(2)}, u32[]{:S(2)}) async-start(bf16[8,3,896]{2,1,0:T(4,128)(2,1)} %reshape.212), calls=%async_computation.7 | async-start | bytes 114688 | tf_op jit(solution)/shard_map/all_to_all | solution.py:310
  253.1 4.0 %all-to-all-done.7 = bf16[8,3,896]{2,1,0:T(4,128)(2,1)S(1)} async-done(((bf16[8,3,896]{2,1,0:T(4,128)(2,1)}), bf16[8,3,896]{2,1,0:T(4,128)(2,1)S(1)}, u32[]{:S(2)}, u32[]{:S(2)}) %all-to-all-start.7) | async-done | bytes 43040 | tf_op jit(solution)/shard_map/all_to_all | solution.py:310
  (157 shorter events, 70.4 us)
Async XLA Ops:
  2.6 44.0 %all-to-all-start = ((bf16[16,3,7168]{2,1,0:T(4,128)(2,1)}), bf16[16,3,7168]{2,1,0:T(4,128)(2,1)}, u32[]{:S(2)}, u32[]{:S(2)}) async-start(bf16[16,3,7168]{2,1,0:T(4,128)(2,1)} %broadcast_in_dim.20), calls=%async_computation | async-start | bytes 1835008 | tf_op jit(solution)/shard_map/all_to_all | solution.py:310
  13.3 4.4 %collective-permute-start = (bf16[224,3584]{1,0:T(8,128)(2,1)}, bf16[224,3584]{1,0:T(8,128)(2,1)}, u32[]{:S(2)}, u32[]{:S(2)}) collective-permute-start(bf16[224,3584]{1,0:T(8,128)(2,1)} %constant_dynamic-slice_fusion.6), channel_id=1, source_target_pairs={{0,16},{16,0},{1,17},{17,1},{2,18},{18,2},{3,19},{19,3},{4,20},{20... | collective-permute-start | bytes 4816904 | tf_op jit(solution)/shard_map/ppermute | solution.py:84
  14.3 13.1 %collective-permute-start.3 = (bf16[3,3584]{1,0:T(4,128)(2,1)S(1)}, bf16[3,3584]{1,0:T(4,128)(2,1)S(1)}, u32[]{:S(2)}, u32[]{:S(2)}) collective-permute-start(bf16[3,3584]{1,0:T(4,128)(2,1)S(1)} %get-tuple-element.120), channel_id=1, source_target_pairs={{0,16},{16,0},{1,17},{17,1},{2,18},{18,2},{3,19},{19,3},{4,20},{20... | collective-permute-start | bytes 64520 | tf_op jit(solution)/shard_map/ppermute | solution.py:84
  23.7 35.6 %collective-permute-start.1 = (bf16[2,224,896]{2,1,0:T(8,128)(2,1)}, bf16[2,224,896]{2,1,0:T(8,128)(2,1)}, u32[]{:S(2)}, u32[]{:S(2)}) collective-permute-start(bf16[2,224,896]{2,1,0:T(8,128)(2,1)} %get-tuple-element.52), channel_id=1, source_target_pairs={{0,32},{32,64},{64,96},{96,0},{1,33},{33,65},{65,97},{97,1},{2,34}... | collective-permute-start | bytes 2408456 | tf_op jit(solution)/shard_map/ppermute | solution.py:88
  25.3 33.9 %collective-permute-start.2 = (bf16[2,224,896]{2,1,0:T(8,128)(2,1)}, bf16[2,224,896]{2,1,0:T(8,128)(2,1)}, u32[]{:S(2)}, u32[]{:S(2)}) collective-permute-start(bf16[2,224,896]{2,1,0:T(8,128)(2,1)} %get-tuple-element.53), channel_id=1, source_target_pairs={{0,96},{32,0},{64,32},{96,64},{1,97},{33,1},{65,33},{97,65},{2,98}... | collective-permute-start | bytes 2408456 | tf_op jit(solution)/shard_map/ppermute | solution.py:88
  27.5 17.5 %collective-permute-start.6 = (bf16[6,896]{1,0:T(8,128)(2,1)S(1)}, bf16[6,896]{1,0:T(8,128)(2,1)S(1)}, u32[]{:S(2)}, u32[]{:S(2)}) collective-permute-start(bf16[6,896]{1,0:T(8,128)(2,1)S(1)} %get-tuple-element.116), channel_id=1, source_target_pairs={{0,96},{32,0},{64,32},{96,64},{1,97},{33,1},{65,33},{97,65},{2,98}... | collective-permute-start | bytes 32264 | tf_op jit(solution)/shard_map/ppermute | solution.py:88
  29.1 17.4 %collective-permute-start.5 = (bf16[6,896]{1,0:T(8,128)(2,1)S(1)}, bf16[6,896]{1,0:T(8,128)(2,1)S(1)}, u32[]{:S(2)}, u32[]{:S(2)}) collective-permute-start(bf16[6,896]{1,0:T(8,128)(2,1)S(1)} %get-tuple-element.117), channel_id=1, source_target_pairs={{0,64},{32,96},{64,0},{96,32},{1,65},{33,97},{65,1},{97,33},{2,66}... | collective-permute-start | bytes 32264 | tf_op jit(solution)/shard_map/ppermute | solution.py:88
  29.1 17.4 %collective-permute-start.4 = (bf16[6,896]{1,0:T(8,128)(2,1)S(1)}, bf16[6,896]{1,0:T(8,128)(2,1)S(1)}, u32[]{:S(2)}, u32[]{:S(2)}) collective-permute-start(bf16[6,896]{1,0:T(8,128)(2,1)S(1)} %get-tuple-element.118), channel_id=1, source_target_pairs={{0,32},{32,64},{64,96},{96,0},{1,33},{33,65},{65,97},{97,1},{2,34}... | collective-permute-start | bytes 32264 | tf_op jit(solution)/shard_map/ppermute | solution.py:88
  61.5 38.1 %all-to-all-start.1 = ((bf16[16,3,8192]{2,1,0:T(4,128)(2,1)}), bf16[16,3,8192]{2,1,0:T(4,128)(2,1)}, u32[]{:S(2)}, u32[]{:S(2)}) async-start(bf16[16,3,8192]{2,1,0:T(4,128)(2,1)} %reshape.205), calls=%async_computation.1 | async-start | bytes 2097152 | tf_op jit(solution)/shard_map/all_to_all | solution.py:310
  68.5 34.8 %collective-permute-start.7 = (bf16[2,224,896]{2,1,0:T(8,128)(2,1)}, bf16[2,224,896]{2,1,0:T(8,128)(2,1)}, u32[]{:S(2)}, u32[]{:S(2)}) collective-permute-start(bf16[2,224,896]{2,1,0:T(8,128)(2,1)} %copy-done.8), channel_id=1, source_target_pairs={{0,64},{32,96},{64,0},{96,32},{1,65},{33,97},{65,1},{97,33},{2,66}... | collective-permute-start | bytes 2408456 | tf_op jit(solution)/shard_map/ppermute | solution.py:88
  72.1 22.3 %collective-permute-start.11 = (bf16[2,56,896]{2,1,0:T(8,128)(2,1)S(1)}, bf16[2,56,896]{2,1,0:T(8,128)(2,1)S(1)}, u32[]{:S(2)}, u32[]{:S(2)}) collective-permute-start(bf16[2,56,896]{2,1,0:T(8,128)(2,1)S(1)} %get-tuple-element.62), channel_id=1, source_target_pairs={{0,96},{32,0},{64,32},{96,64},{1,97},{33,1},{65,33},{97,65},{2,98}... | collective-permute-start | bytes 602120 | tf_op jit(solution)/shard_map/ppermute | solution.py:88
  73.9 20.5 %collective-permute-start.10 = (bf16[2,56,896]{2,1,0:T(8,128)(2,1)S(1)}, bf16[2,56,896]{2,1,0:T(8,128)(2,1)S(1)}, u32[]{:S(2)}, u32[]{:S(2)}) collective-permute-start(bf16[2,56,896]{2,1,0:T(8,128)(2,1)S(1)} %get-tuple-element.61), channel_id=1, source_target_pairs={{0,64},{32,96},{64,0},{96,32},{1,65},{33,97},{65,1},{97,33},{2,66}... | collective-permute-start | bytes 602120 | tf_op jit(solution)/shard_map/ppermute | solution.py:88
  75.1 23.6 %collective-permute-start.9 = (bf16[2,56,896]{2,1,0:T(8,128)(2,1)S(1)}, bf16[2,56,896]{2,1,0:T(8,128)(2,1)S(1)}, u32[]{:S(2)}, u32[]{:S(2)}) collective-permute-start(bf16[2,56,896]{2,1,0:T(8,128)(2,1)S(1)} %get-tuple-element.60), channel_id=1, source_target_pairs={{0,32},{32,64},{64,96},{96,0},{1,33},{33,65},{65,97},{97,1},{2,34}... | collective-permute-start | bytes 602120 | tf_op jit(solution)/shard_map/ppermute | solution.py:88
  77.7 25.5 %collective-permute-start.8 = (bf16[224,3584]{1,0:T(8,128)(2,1)}, bf16[224,3584]{1,0:T(8,128)(2,1)}, u32[]{:S(2)}, u32[]{:S(2)}) collective-permute-start(bf16[224,3584]{1,0:T(8,128)(2,1)} %constant_dynamic-slice_fusion), channel_id=1, source_target_pairs={{0,16},{16,0},{1,17},{17,1},{2,18},{18,2},{3,19},{19,3},{4,20},{20... | collective-permute-start | bytes 4816904 | tf_op jit(solution)/shard_map/ppermute | solution.py:84
  104.2 19.9 %all-to-all-start.2 = ((bf16[128,3,224]{2,1,0:T(4,128)(2,1)}), bf16[128,3,224]{2,1,0:T(4,128)(2,1)}, u32[]{:S(2)}, u32[]{:S(2)}) async-start(bf16[128,3,224]{2,1,0:T(4,128)(2,1)} %copy.69), calls=%async_computation.2 | async-start | bytes 524288 | tf_op jit(solution)/shard_map/all_to_all | solution.py:310
  128.3 2.8 %collective-permute-start.12 = (bf16[384,896]{1,0:T(8,128)(2,1)S(1)}, bf16[384,896]{1,0:T(8,128)(2,1)S(1)}, u32[]{:S(2)}, u32[]{:S(2)}) collective-permute-start(bf16[384,896]{1,0:T(8,128)(2,1)S(1)} %convolution_convert_fusion.1), channel_id=1, source_target_pairs={{0,16},{16,0},{1,17},{17,1},{2,18},{18,2},{3,19},{19,3},{4,20},{20... | collective-permute-start | bytes 2064392 | tf_op jit(solution)/shard_map/ppermute | solution.py:84
  133.4 16.0 %all-to-all-start.3 = ((bf16[16,24,896]{2,1,0:T(8,128)(2,1)}), bf16[16,24,896]{2,1,0:T(8,128)(2,1)}, u32[]{:S(2)}, u32[]{:S(2)}) async-start(bf16[16,24,896]{2,1,0:T(8,128)(2,1)} %bitcast.94), calls=%async_computation.3 | async-start | bytes 1376256 | tf_op jit(solution)/shard_map/all_to_all | solution.py:310
  137.8 22.0 %collective-permute-start.13 = (bf16[2,224,896]{2,1,0:T(8,128)(2,1)}, bf16[2,224,896]{2,1,0:T(8,128)(2,1)}, u32[]{:S(2)}, u32[]{:S(2)}) collective-permute-start(bf16[2,224,896]{2,1,0:T(8,128)(2,1)} %copy-done.11), channel_id=1, source_target_pairs={{0,32},{32,64},{64,96},{96,0},{1,33},{33,65},{65,97},{97,1},{2,34}... | collective-permute-start | bytes 2408456 | tf_op jit(solution)/shard_map/ppermute | solution.py:88
  139.1 37.8 %collective-permute-start.14 = (bf16[2,224,896]{2,1,0:T(8,128)(2,1)}, bf16[2,224,896]{2,1,0:T(8,128)(2,1)}, u32[]{:S(2)}, u32[]{:S(2)}) collective-permute-start(bf16[2,224,896]{2,1,0:T(8,128)(2,1)} %copy-done.10), channel_id=1, source_target_pairs={{0,64},{32,96},{64,0},{96,32},{1,65},{33,97},{65,1},{97,33},{2,66}... | collective-permute-start | bytes 2408456 | tf_op jit(solution)/shard_map/ppermute | solution.py:88
  142.0 34.9 %collective-permute-start.15 = (bf16[2,224,896]{2,1,0:T(8,128)(2,1)}, bf16[2,224,896]{2,1,0:T(8,128)(2,1)}, u32[]{:S(2)}, u32[]{:S(2)}) collective-permute-start(bf16[2,224,896]{2,1,0:T(8,128)(2,1)} %copy-done.9), channel_id=1, source_target_pairs={{0,96},{32,0},{64,32},{96,64},{1,97},{33,1},{65,33},{97,65},{2,98}... | collective-permute-start | bytes 2408456 | tf_op jit(solution)/shard_map/ppermute | solution.py:88
  151.7 25.2 %all-to-all-start.4 = ((bf16[16,24,1024]{2,1,0:T(8,128)(2,1)}), bf16[16,24,1024]{2,1,0:T(8,128)(2,1)}, u32[]{:S(2)}, u32[]{:S(2)}) async-start(bf16[16,24,1024]{2,1,0:T(8,128)(2,1)} %broadcast_in_dim.25), calls=%async_computation.4 | async-start | bytes 1572864 | tf_op jit(solution)/shard_map/all_to_all | solution.py:304
  184.0 8.2 %collective-permute-start.16 = (bf16[4,384,256]{2,1,0:T(8,128)(2,1)}, bf16[4,384,256]{2,1,0:T(8,128)(2,1)S(1)}, u32[]{:S(2)}, u32[]{:S(2)}) collective-permute-start(bf16[4,384,256]{2,1,0:T(8,128)(2,1)} %get-tuple-element.88), channel_id=1, source_target_pairs={{0,16},{16,0},{1,17},{17,1},{2,18},{18,2},{3,19},{19,3},{4,20},{20... | collective-permute-start | bytes 2359304 | tf_op jit(solution)/shard_map/ppermute | solution.py:84
  185.6 41.2 %all-to-all-start.5 = ((bf16[16,3,14336]{2,1,0:T(4,128)(2,1)}), bf16[16,3,14336]{2,1,0:T(4,128)(2,1)}, u32[]{:S(2)}, u32[]{:S(2)}) async-start(bf16[16,3,14336]{2,1,0:T(4,128)(2,1)} %broadcast_in_dim.27), calls=%async_computation.5 | async-start | bytes 3670016 | tf_op jit(solution)/shard_map/all_to_all | solution.py:310
  192.5 6.4 %collective-permute-start.17 = (bf16[384,256]{1,0:T(8,128)(2,1)S(1)}, bf16[384,256]{1,0:T(8,128)(2,1)S(1)}, u32[]{:S(2)}, u32[]{:S(2)}) collective-permute-start(bf16[384,256]{1,0:T(8,128)(2,1)S(1)} %get-tuple-element.103), channel_id=1, source_target_pairs={{0,96},{32,0},{64,32},{96,64},{1,97},{33,1},{65,33},{97,65},{2,98}... | collective-permute-start | bytes 589832 | tf_op jit(solution)/shard_map/ppermute | solution.py:88
  194.4 7.4 %collective-permute-start.18 = (bf16[384,256]{1,0:T(8,128)(2,1)S(1)}, bf16[384,256]{1,0:T(8,128)(2,1)S(1)}, u32[]{:S(2)}, u32[]{:S(2)}) collective-permute-start(bf16[384,256]{1,0:T(8,128)(2,1)S(1)} %get-tuple-element.102), channel_id=1, source_target_pairs={{0,64},{32,96},{64,0},{96,32},{1,65},{33,97},{65,1},{97,33},{2,66}... | collective-permute-start | bytes 589832 | tf_op jit(solution)/shard_map/ppermute | solution.py:88
  195.3 11.8 %collective-permute-start.19 = (bf16[384,256]{1,0:T(8,128)(2,1)S(1)}, bf16[384,256]{1,0:T(8,128)(2,1)S(1)}, u32[]{:S(2)}, u32[]{:S(2)}) collective-permute-start(bf16[384,256]{1,0:T(8,128)(2,1)S(1)} %get-tuple-element.101), channel_id=1, source_target_pairs={{0,32},{32,64},{64,96},{96,0},{1,33},{33,65},{65,97},{97,1},{2,34}... | collective-permute-start | bytes 589832 | tf_op jit(solution)/shard_map/ppermute | solution.py:88
  208.7 11.6 %collective-permute-start.20 = (bf16[384,224]{1,0:T(8,128)(2,1)S(1)}, bf16[384,224]{1,0:T(8,128)(2,1)S(1)}, u32[]{:S(2)}, u32[]{:S(2)}) collective-permute-start(bf16[384,224]{1,0:T(8,128)(2,1)S(1)} %shard_map.173.refs_0_), channel_id=1, source_target_pairs={{0,32},{32,64},{64,96},{96,0},{1,33},{33,65},{65,97},{97,1},{2,34}... | collective-permute-start | bytes 516104 | tf_op jit(solution)/shard_map/ppermute | solution.py:88
  208.8 12.7 %collective-permute-start.21 = (bf16[384,224]{1,0:T(8,128)(2,1)S(1)}, bf16[384,224]{1,0:T(8,128)(2,1)S(1)}, u32[]{:S(2)}, u32[]{:S(2)}) collective-permute-start(bf16[384,224]{1,0:T(8,128)(2,1)S(1)} %shard_map.173.refs_0_), channel_id=1, source_target_pairs={{0,64},{32,96},{64,0},{96,32},{1,65},{33,97},{65,1},{97,33},{2,66}... | collective-permute-start | bytes 516104 | tf_op jit(solution)/shard_map/ppermute | solution.py:88
  209.8 11.8 %collective-permute-start.22 = (bf16[384,224]{1,0:T(8,128)(2,1)S(1)}, bf16[384,224]{1,0:T(8,128)(2,1)S(1)}, u32[]{:S(2)}, u32[]{:S(2)}) collective-permute-start(bf16[384,224]{1,0:T(8,128)(2,1)S(1)} %shard_map.173.refs_0_), channel_id=1, source_target_pairs={{0,96},{32,0},{64,32},{96,64},{1,97},{33,1},{65,33},{97,65},{2,98}... | collective-permute-start | bytes 516104 | tf_op jit(solution)/shard_map/ppermute | solution.py:88
  211.8 10.5 %collective-permute-start.23 = (bf16[384,224]{1,0:T(8,128)(2,1)S(1)}, bf16[384,224]{1,0:T(8,128)(2,1)S(1)}, u32[]{:S(2)}, u32[]{:S(2)}) collective-permute-start(bf16[384,224]{1,0:T(8,128)(2,1)S(1)} %shard_map.173.refs_0_), channel_id=1, source_target_pairs={{0,16},{16,0},{1,17},{17,1},{2,18},{18,2},{3,19},{19,3},{4,20},{20... | collective-permute-start | bytes 516104 | tf_op jit(solution)/shard_map/ppermute | solution.py:84
  226.8 18.2 %all-to-all-start.6 = ((bf16[16,24,896]{2,1,0:T(8,128)(2,1)}), bf16[16,24,896]{2,1,0:T(8,128)(2,1)S(1)}, u32[]{:S(2)}, u32[]{:S(2)}) async-start(bf16[16,24,896]{2,1,0:T(8,128)(2,1)} %bitcast.36), calls=%async_computation.6 | async-start | bytes 1376256 | tf_op jit(solution)/shard_map/all_to_all | solution.py:310
  245.9 11.2 %all-to-all-start.7 = ((bf16[8,3,896]{2,1,0:T(4,128)(2,1)}), bf16[8,3,896]{2,1,0:T(4,128)(2,1)S(1)}, u32[]{:S(2)}, u32[]{:S(2)}) async-start(bf16[8,3,896]{2,1,0:T(4,128)(2,1)} %reshape.212), calls=%async_computation.7 | async-start | bytes 114688 | tf_op jit(solution)/shard_map/all_to_all | solution.py:310
  (23 other events, 178.9 us)

commit v9 on v3

--- a/solution.py
+++ b/solution.py
@@ -18,46 +18,43 @@
 DN = (((1,), (1,)), ((), ()))
 
 
-def attend_kernel(heads, scaling, q, k, v, dk, dv, pool_mask, draft_mask, out):
-    pm = pool_mask[...]
-    dm = draft_mask[...]
+def attend_kernel(heads, scaling, q, k, v, dk, dv, mask, out):
     rows = q.shape[0]
     keys = k.shape[0] * k.shape[1]
-    kk = k[...].reshape(keys, k.shape[2])
-    vv = v[...].reshape(keys, v.shape[2])
+    kk = jnp.concatenate([k[...].reshape(keys, k.shape[2]), dk[...]], axis=0)
+    vv = jnp.concatenate([v[...].reshape(keys, v.shape[2]), dv[...]], axis=0)
+    m = mask[...]
+    span = [slice(h * HD, (h + 1) * HD) for h in range(heads)]
+    scores = [
+        jnp.where(
+            m > 0,
+            lax.dot_general(q[:, cols], kk[:, cols], DN, preferred_element_type=F32) * scaling,
+            NEG,
+        )
+        for cols in span
+    ]
+    tops = [jnp.max(s, axis=1, keepdims=True).astype(BF16).astype(F32) for s in scores]
+    weights = [jnp.exp(s - top) * m for s, top in zip(scores, tops)]
+    totals = [jnp.sum(p, axis=1, keepdims=True) for p in weights]
     lane = lax.broadcasted_iota(jnp.int32, (rows, HD), 1)
     stats = jnp.zeros((rows, HD), F32)
-    for h in range(heads):
-        cols = slice(h * HD, (h + 1) * HD)
-        qh = q[:, cols]
-        s = lax.dot_general(qh, kk[:, cols], DN, preferred_element_type=F32) * scaling
-        sd = lax.dot_general(qh, dk[:, cols], DN, preferred_element_type=F32) * scaling
-        s = jnp.where(pm > 0, s, NEG)
-        sd = jnp.where(dm > 0, sd, NEG)
-        top = jnp.maximum(jnp.max(s, axis=1, keepdims=True), jnp.max(sd, axis=1, keepdims=True))
-        top = top.astype(BF16).astype(F32)
-        p = jnp.exp(s - top) * pm
-        pd = jnp.exp(sd - top) * dm
-        total = jnp.sum(p, axis=1, keepdims=True) + jnp.sum(pd, axis=1, keepdims=True)
-        high = total.astype(BF16).astype(F32)
-        stats = jnp.where(lane == h, top, stats)
+    for h, cols in enumerate(span):
+        w = jnp.dot(weights[h].astype(BF16), vv[:, cols], preferred_element_type=F32)
+        out[:, cols] = w.astype(BF16)
+        high = totals[h].astype(BF16).astype(F32)
+        stats = jnp.where(lane == h, tops[h], stats)
         stats = jnp.where(lane == 8 + h, high, stats)
-        stats = jnp.where(lane == 16 + h, total - high, stats)
-        w = jnp.dot(p.astype(BF16), vv[:, cols], preferred_element_type=F32)
-        w = w + jnp.dot(pd.astype(BF16), dv[:, cols], preferred_element_type=F32)
-        out[:, cols] = w.astype(BF16)
+        stats = jnp.where(lane == 16 + h, totals[h] - high, stats)
     out[:, heads * HD :] = stats.astype(BF16)
 
 
-def attend(q, key_cache, value_cache, dk, dv, pool_mask, draft_mask):
+def attend(q, key_cache, value_cache, dk, dv, mask, steps):
     rows, width = q.shape
     pages, page_len, _ = key_cache.shape
-    heads = 7
-    steps = width // (heads * HD)
-    wide = heads * HD
+    wide = width // steps
+    heads = wide // HD
     col = lambda i: (0, i)
     col3 = lambda i: (0, 0, i)
-    fixed = lambda i: (0, 0)
 
     def body(*refs):
         attend_kernel(heads, 1.0 / math.sqrt(HD), *refs)
@@ -71,8 +68,7 @@
             pl.BlockSpec((pages, page_len, wide), col3),
             pl.BlockSpec((dk.shape[0], wide), col),
             pl.BlockSpec((dv.shape[0], wide), col),
-            pl.BlockSpec(pool_mask.shape, fixed),
-            pl.BlockSpec(draft_mask.shape, fixed),
+            pl.BlockSpec(mask.shape, lambda i: (0, 0)),
         ],
         out_specs=pl.BlockSpec((rows, wide + HD), col),
         out_shape=jax.ShapeDtypeStruct((rows, steps * (wide + HD)), BF16),
@@ -82,15 +78,15 @@
             bytes_accessed=4 * pages * page_len * width,
             transcendentals=rows * pages * page_len * width // HD,
         ),
-    )(q, key_cache, value_cache, dk, dv, pool_mask, draft_mask)
+    )(q, key_cache, value_cache, dk, dv, mask)
 
 
 def pair(x):
     return lax.ppermute(x, "c", [(0, 1), (1, 0)])
 
 
-def shift(x, step, size):
-    return lax.ppermute(x, "z", [(i, (i + step) % size) for i in range(size)])
+def shift(x, step, size, axis="z"):
+    return lax.ppermute(x, axis, [(i, (i + step) % size) for i in range(size)])
 
 
 def after(x, first):
@@ -342,7 +338,8 @@
     chunk = half // zs
     block = tokens // members
 
-    group_q = spread(queries, MLP, members).reshape(group_rows, width)
+    wide_q = jnp.broadcast_to(queries[None], (members,) + queries.shape)
+    group_q = exchange(wide_q, MLP).reshape(group_rows, width)
 
     def piece(w, core, d):
         return lax.dynamic_slice_in_dim(w, core * half + ((z + d) % zs) * chunk, chunk, 1)
@@ -355,14 +352,13 @@
         wo_parts.append(shift(part, d, zs) if d else part)
     wo_parts = jnp.concatenate(wo_parts, axis=1)
 
-    both = spread(
-        after(jnp.concatenate([keys_new, values_new], axis=1), group_q), MLP, members
-    ).reshape(group_rows, 2 * width)
+    both = after(jnp.concatenate([keys_new, values_new], axis=1), wide_q)
+    both = jnp.stack([shift(both, d, xs, "x") if d else both for d in range(xs)])
 
     page_ids = member * pages_dev + jnp.arange(pages_dev, dtype=jnp.int32)
     owners = jnp.any(page_table[:, :, None] == page_ids[None, None, :], axis=1)
     pool_mask = jnp.repeat(jnp.repeat(owners, page_len, axis=1), tree_len, axis=0).astype(F32)
-    draft_pad = 8
+    draft_pad = 16
     slot_ids = member * rows_dev + jnp.arange(draft_pad, dtype=jnp.int32)
     row_ids = jnp.arange(group_rows, dtype=jnp.int32)
     tree_cols = jnp.tile(tree_mask.reshape(group_rows, tree_len), (1, requests))
@@ -383,8 +379,8 @@
         value_cache,
         jnp.pad(keys_new, pad),
         jnp.pad(values_new, pad),
-        pool_mask,
-        draft_mask,
+        jnp.concatenate([pool_mask, draft_mask], axis=1),
+        heads // 7,
     )
 
     parts, both = lax.optimization_barrier((parts, both))
@@ -405,15 +401,6 @@
     source = ((z - at // (cs * rows_dev)) % zs) * cs + (c + at // rows_dev) % cs
     order = at[:, None] == (source * rows_dev + at % rows_dev)[None, :]
     res = jnp.dot(order.astype(BF16), res, preferred_element_type=F32)
-
-    place = c.reshape(1).astype(jnp.int32)
-    up_w = w_up.T
-    up_other = pair(lax.dynamic_slice_in_dim(after(up_w, parts), (1 - c) * half, half, 1))
-    down_other = pair(lax.dynamic_slice_in_dim(after(w_down, parts), (1 - c) * half, half, 1))
-    gw = gain_products(place, ln_gain[None], up_w, up_other, zs, chunk)
-    gain_own = gw[:, 0]
-    gain_other = gw[:, 1]
-    gain_pair = pair(gain_other)
 
     parts = exchange(parts.reshape(members, rows_dev, parts.shape[1]), MLP)
     parts = parts.reshape(members, rows_dev, heads // 7, 8, HD).astype(F32)
@@ -451,7 +438,20 @@
         ),
         compiler_params=params(),
     )(part, res, gain[None])
+
+    place = c.reshape(1).astype(jnp.int32)
+    up_w = w_up.T
+    up_other = pair(lax.dynamic_slice_in_dim(after(up_w, row), (1 - c) * half, half, 1))
+    down_other = pair(lax.dynamic_slice_in_dim(after(w_down, row), (1 - c) * half, half, 1))
+    gw = gain_products(place, ln_gain[None], up_w, up_other, zs, chunk)
+    gain_own = gw[:, 0]
+    gain_other = gw[:, 1]
+    gain_pair = pair(gain_other)
+
+    both = after(both, row)
+    both = jnp.stack([shift(both, d, ys, "y") if d else both for d in range(ys)])
     rows = spread(row, CHIPS, zs * members).reshape(zs, tokens, chunk + HD)
+    rows, both = lax.optimization_barrier((rows, both))
     mine, theirs, stats = up_project(place, rows, up_w, up_other, gain_own, gain_other)
     act = pl.pallas_call(
         lambda *refs: act_kernel(width, *refs),
@@ -466,7 +466,12 @@
 
     valid = (accepted >= 0) & (dest_slot == member)[:, None]
     target = jnp.arange(requests, dtype=jnp.int32)[:, None] * tree_len + jnp.maximum(accepted, 0)
-    chooser = jnp.any((target[:, :, None] == row_ids[None, None, :]) & valid[:, :, None], axis=0)
+    x, y = lax.axis_index("x"), lax.axis_index("y")
+    at = jnp.arange(group_rows, dtype=jnp.int32)
+    near = at // rows_dev
+    slots = (((x - near % xs) % xs) * ys + (y - near // xs) % ys) * rows_dev + at % rows_dev
+    chooser = jnp.any((target[:, :, None] == slots[None, None, :]) & valid[:, :, None], axis=0)
+    both = both.reshape(group_rows, 2 * width)
     picked = jnp.dot(chooser.astype(BF16), both, preferred_element_type=F32).astype(BF16)
     return (mixed, picked[:, :width][None], picked[:, width:][None])
 

time: 245 us -> 252 us (1.029)
  Pallas kernels: 31.1 us -> 22.3 us
  waiting for transfers between devices: 113 us -> 120 us
  starting transfers between devices: 70.1 us -> 74.6 us
  other arithmetic: 2.49 us -> 6.96 us
    ppermute x6 -> x12, waiting for transfers between devices: 1.77 us -> 56.7 us  [shift(): return lax.ppermute(x, axis, [(i, (i + step) % size) for i in range(size)])]
    all_to_all x3 -> x1, waiting for transfers between devices: 44.8 us -> 0.01 us  [spread(): lax.all_to_all(jnp.broadcast_to(x[None], (count,) + x.shape), axes, split...]
    all_to_all x3 -> x1, starting transfers between devices: 18.1 us -> 6.58 us  [spread(): lax.all_to_all(jnp.broadcast_to(x[None], (count,) + x.shape), axes, split...]
    ppermute x6 -> x12, starting transfers between devices: 9 us -> 17.9 us  [shift(): return lax.ppermute(x, axis, [(i, (i + step) % size) for i in range(size)])]
    pallas_call x1, Pallas kernels: 18.9 us -> 10.2 us  [attend(): pl.pallas_call(body, grid=(steps,), in_specs=[pl.BlockSpec((rows, wide),...]
    all_to_all x5 -> x6, starting transfers between devices: 33.2 us -> 41.1 us  [exchange(): return lax.all_to_all(x, axes, split_axis=0, concat_axis=0)]
    broadcast_in_dim x3 -> x1, local copies, waits for them, and re-layouts: 6.1 us -> 2.11 us  [spread(): jnp.broadcast_to(x[None], (count,) + x.shape)]
    another operation x0 -> x2, other arithmetic: none -> 3.82 us  [the longest x1 2.64 us: local(): jnp.stack([shift(both, d, ys, 'y') if d else both for d in range(ys)])]
  transfers between devices with their start and end apart: 22 -> 27, of which waited for: 14 -> 15; matrix products, arithmetic and copies ran while one was open for 5% -> 8% of each run, Pallas kernels for 11% -> 3%
where the time goes in v9:
time: 252 us; the launch traced here: 250 us
  waiting for transfers between devices  120 us (48%)
  starting transfers between devices  74.6 us (30%)
  Pallas kernels  22.3 us (9%)
  local copies, waits for them, and re-layouts  21.5 us (9%)
  other arithmetic  6.96 us (3%)
  matrix products  3.57 us (1%)
    all_to_all x6, waiting for transfers between devices, exchange(): return lax.all_to_all(x, axes, split_axis=0, concat_axis=0)  59.7 us
    ppermute x12, waiting for transfers between devices, shift(): return lax.ppermute(x, axis, [(i, (i + step) % size) for i in range(size)])  56.7 us
    all_to_all x6, starting transfers between devices, exchange(): return lax.all_to_all(x, axes, split_axis=0, concat_axis=0)  41.1 us
    ppermute x12, starting transfers between devices, shift(): return lax.ppermute(x, axis, [(i, (i + step) % size) for i in range(size)])  17.9 us
    pallas_call x1, Pallas kernels, attend(): pl.pallas_call(body, grid=(steps,), in_specs=[pl.BlockSpec((rows, wide),...  10.2 us
    ppermute x8, starting transfers between devices, pair(): return lax.ppermute(x, 'c', [(0, 1), (1, 0)])  8.95 us
    all_to_all x1, starting transfers between devices, spread(): lax.all_to_all(jnp.broadcast_to(x[None], (count,) + x.shape), axes, split...  6.58 us
    pallas_call x1, Pallas kernels, up_project(): pl.pallas_call(up_kernel, grid_spec=pltpu.PrefetchScalarGridSpec(num_scal...  5.44 us
  transfers between devices with their start and end apart: 27, of which 15 were waited for; matrix products, arithmetic and copies ran while one was open for 8% of the time, Pallas kernels for 3%

profile of v9, /device:TPU:1, one launch (start us, length us, event | category | flops | bytes accessed | tf_op | source)
XLA Modules:
  0.0 250.4 jit_solution(5714414749294649846)
XLA Ops:
  0.7 2.1 broadcast_in_dim.18
  2.7 7.6 %all-to-all-start = ((bf16[16,3,7168]{2,1,0:T(4,128)(2,1)}), bf16[16,3,7168]{2,1,0:T(4,128)(2,1)S(1)}, u32[]{:S(2)}, u32[]{:S(2)}) async-start(bf16[16,3,7168]{2,1,0:T(4,128)(2,1)} %broadcast_in_dim.18), calls=%async_computation | async-start | bytes 1835008 | tf_op jit(solution)/shard_map/all_to_all | solution.py:305
  11.8 2.4 collective-permute-start.1
  18.5 5.9 %collective-permute-done = bf16[3,14336]{1,0:T(4,128)(2,1)S(1)} collective-permute-done((bf16[3,14336]{1,0:T(4,128)(2,1)S(1)}, bf16[3,14336]{1,0:T(4,128)(2,1)S(1)}, u32[]{:S(2)}, u32[]{:S(2)}) %collective-permute-start) | collective-permute-done | bytes 86048 | tf_op jit(solution)/shard_map/ppermute | solution.py:89
  24.4 3.3 %collective-permute-done.1 = bf16[3,14336]{1,0:T(4,128)(2,1)S(1)} collective-permute-done((bf16[3,14336]{1,0:T(4,128)(2,1)S(1)}, bf16[3,14336]{1,0:T(4,128)(2,1)S(1)}, u32[]{:S(2)}, u32[]{:S(2)}) %collective-permute-start.1) | collective-permute-done | bytes 86048 | tf_op jit(solution)/shard_map/ppermute | solution.py:89
  30.2 10.2 %shard_map.166 = bf16[48,8192]{1,0:T(8,128)(2,1)} custom-call(bf16[48,7168]{1,0:T(8,128)(2,1)} %reshape.263.refs_0_, bf16[24,16,7168]{2,1,0:T(8,128)(2,1)} %refs_1_.1, bf16[24,16,7168]{2,1,0:T(8,128)(2,1)} %refs_2_.1, bf16[16,7168]{1,0:T(8,128)(2,1)} %pad.7.refs_3_, bf16[16,7168]{1,0:T(8,128)(2,1)} %pad.8.refs_4_, f32[48,400]{1,0:T(8,128)} %pad_maximum_fusion.8.refs_5_), custom_call_target="tpu_custom_call" | custom-call | flops 528482304 | bytes 11010048 | tf_op jit(solution)/shard_map/pallas_call | solution.py:62
  40.4 2.4 reshape.265
  42.7 5.0 %all-to-all-start.1 = ((bf16[16,3,8192]{2,1,0:T(4,128)(2,1)}), bf16[16,3,8192]{2,1,0:T(4,128)(2,1)S(1)}, u32[]{:S(2)}, u32[]{:S(2)}) async-start(bf16[16,3,8192]{2,1,0:T(4,128)(2,1)} %reshape.265), calls=%async_computation.1 | async-start | bytes 2097152 | tf_op jit(solution)/shard_map/all_to_all | solution.py:305
  49.7 3.4 %collective-permute-start.4 = (bf16[2,56,896]{2,1,0:T(8,128)(2,1)S(1)}, bf16[2,56,896]{2,1,0:T(8,128)(2,1)S(1)}, u32[]{:S(2)}, u32[]{:S(2)}) collective-permute-start(bf16[2,56,896]{2,1,0:T(8,128)(2,1)S(1)} %pad_maximum_fusion.4), channel_id=1, source_target_pairs={{0,64},{32,96},{64,0},{96,32},{1,65},{33,97},{65,1},{97,33},{2,66}... | collective-permute-start | bytes 602120 | tf_op jit(solution)/shard_map/ppermute | solution.py:89
  53.9 8.7 %all-to-all-done.1 = bf16[16,3,8192]{2,1,0:T(4,128)(2,1)S(1)} async-done(((bf16[16,3,8192]{2,1,0:T(4,128)(2,1)}), bf16[16,3,8192]{2,1,0:T(4,128)(2,1)S(1)}, u32[]{:S(2)}, u32[]{:S(2)}) %all-to-all-start.1) | async-done | bytes 786464 | tf_op jit(solution)/shard_map/all_to_all | solution.py:305
  65.9 9.8 %all-to-all-start.2 = ((bf16[128,3,224]{2,1,0:T(4,128)(2,1)}), bf16[128,3,224]{2,1,0:T(4,128)(2,1)S(1)}, u32[]{:S(2)}, u32[]{:S(2)}) async-start(bf16[128,3,224]{2,1,0:T(4,128)(2,1)} %copy.79), calls=%async_computation.2 | async-start | bytes 524288 | tf_op jit(solution)/shard_map/all_to_all | solution.py:305
  75.8 11.0 %all-to-all-done.2 = bf16[128,3,224]{2,1,0:T(4,128)(2,1)S(1)} async-done(((bf16[128,3,224]{2,1,0:T(4,128)(2,1)}), bf16[128,3,224]{2,1,0:T(4,128)(2,1)S(1)}, u32[]{:S(2)}, u32[]{:S(2)}) %all-to-all-start.2) | async-done | bytes 172064 | tf_op jit(solution)/shard_map/all_to_all | solution.py:305
  91.4 3.6 %all-to-all-start.3 = ((bf16[16,24,896]{2,1,0:T(8,128)(2,1)}), bf16[16,24,896]{2,1,0:T(8,128)(2,1)S(1)}, u32[]{:S(2)}, u32[]{:S(2)}) async-start(bf16[16,24,896]{2,1,0:T(8,128)(2,1)} %bitcast.31), calls=%async_computation.3 | async-start | bytes 1376256 | tf_op jit(solution)/shard_map/all_to_all | solution.py:305
  97.7 2.1 collective-permute-done.8
  101.0 5.7 %all-to-all-done.3.parts = bf16[16,24,896]{2,1,0:T(8,128)(2,1)S(1)} async-done(((bf16[16,24,896]{2,1,0:T(8,128)(2,1)}), bf16[16,24,896]{2,1,0:T(8,128)(2,1)S(1)}, u32[]{:S(2)}, u32[]{:S(2)}) %all-to-all-start.3) | async-done | bytes 688160 | tf_op jit(solution)/shard_map/all_to_all | solution.py:305
  106.9 2.1 broadcast_in_dim.23
  109.0 6.6 %all-to-all-start.4 = ((bf16[64,24,1024]{2,1,0:T(8,128)(2,1)}), bf16[64,24,1024]{2,1,0:T(8,128)(2,1)}, u32[]{:S(2)}, u32[]{:S(2)}) async-start(bf16[64,24,1024]{2,1,0:T(8,128)(2,1)} %broadcast_in_dim.23), calls=%async_computation.4 | async-start | bytes 6291456 | tf_op jit(solution)/shard_map/all_to_all | solution.py:299
  116.6 2.4 collective-permute-start.12
  120.3 3.2 %collective-permute-start.14 = (bf16[224,3584]{1,0:T(8,128)(2,1)S(1)}, bf16[224,3584]{1,0:T(8,128)(2,1)S(1)}, u32[]{:S(2)}, u32[]{:S(2)}) collective-permute-start(bf16[224,3584]{1,0:T(8,128)(2,1)S(1)} %constant_dynamic-slice_fusion.1), channel_id=1, source_target_pairs={{0,16},{16,0},{1,17},{17,1},{2,18},{18,2},{3,19},{19,3},{4,20},{20... | collective-permute-start | bytes 4816904 | tf_op jit(solution)/shard_map/ppermute | solution.py:85
  124.8 1.7 collective-permute-start.19
  126.5 33.7 %collective-permute-done.11 = bf16[4,3,14336]{2,1,0:T(4,128)(2,1)S(1)} collective-permute-done((bf16[4,3,14336]{2,1,0:T(4,128)(2,1)}, bf16[4,3,14336]{2,1,0:T(4,128)(2,1)S(1)}, u32[]{:S(2)}, u32[]{:S(2)}) %collective-permute-start.11) | collective-permute-done | bytes 344096 | tf_op jit(solution)/shard_map/ppermute | solution.py:89
  160.2 10.6 %collective-permute-done.12 = bf16[4,3,14336]{2,1,0:T(4,128)(2,1)S(1)} collective-permute-done((bf16[4,3,14336]{2,1,0:T(4,128)(2,1)}, bf16[4,3,14336]{2,1,0:T(4,128)(2,1)S(1)}, u32[]{:S(2)}, u32[]{:S(2)}) %collective-permute-start.12) | collective-permute-done | bytes 344096 | tf_op jit(solution)/shard_map/ppermute | solution.py:89
  170.9 2.6 %pad_maximum_fusion = bf16[4,4,3,14336]{3,2,1,0:T(4,128)(2,1)} fusion(bf16[1,4,3,14336]{3,2,1,0:T(4,128)(2,1)S(1)} %bitcast.116, bf16[1,4,3,14336]{3,2,1,0:T(4,128)(2,1)S(1)} %bitcast.115, bf16[1,4,3,14336]{3,2,1,0:T(4,128)(2,1)S(1)} %bitcast.114, bf16[1,4,3,14336]{3,2,1,0:T(4,128)(2,1)S(1)} %bitcast.110), kind=kLoop, calls=%fused_computation.1 | loop fusion | flops 2064384 | bytes 2752512 | tf_op jit(solution)/shard_map/stack | solution.py:452
  173.5 1.7 shard_map.168
  176.7 5.4 %shard_map.169 = (f32[384,224]{1,0:T(8,128)S(1)}, f32[384,224]{1,0:T(8,128)S(1)}, f32[384,128]{1,0:T(8,128)S(1)}) custom-call(s32[1]{0:T(128)} %bitcast.place, bf16[4,384,1024]{2,1,0:T(8,128)(2,1)} %bitcast.34.rows, bf16[224,7168]{1,0:T(8,128)(2,1)S(1)} %bitcast.102, bf16[224,3584]{1,0:T(8,128)(2,1)S(1)} %copy-done.5, ...), custom_call_target="tpu_custom_call" | custom-call | tf_op jit(solution)/shard_map/pallas_call | solution.py:233
  182.1 2.1 collective-permute-start.15
  187.8 3.9 %shard_map.171 = bf16[4,384,896]{2,1,0:T(8,128)(2,1)S(1)} custom-call(s32[1]{0:T(128)} %bitcast.place, bf16[384,224]{1,0:T(8,128)(2,1)S(1)} %shard_map.170.act, bf16[384,224]{1,0:T(8,128)(2,1)S(1)} %collective-permute-done.18.act_pair, bf16[224,7168]{1,0:T(8,128)(2,1)S(1)} %copy-done.3, bf16[224,3584]{1,0:T(8,128)(2,1)} %collective-permute-done.19.other), custom_call_target="tpu_custom_call" | custom-call | tf_op jit(solution)/shard_map/pallas_call | solution.py:263
  193.2 9.4 %all-to-all-start.5 = ((bf16[64,24,896]{2,1,0:T(8,128)(2,1)}), bf16[64,24,896]{2,1,0:T(8,128)(2,1)S(1)}, u32[]{:S(2)}, u32[]{:S(2)}) async-start(bf16[64,24,896]{2,1,0:T(8,128)(2,1)} %bitcast.103), calls=%async_computation.5 | async-start | bytes 5505024 | tf_op jit(solution)/shard_map/all_to_all | solution.py:305
  202.9 3.2 %reshape.276 = bf16[48,14336]{1,0:T(8,128)(2,1)} reshape(bf16[4,4,3,14336]{3,2,1,0:T(4,128)(2,1)} %pad_maximum_fusion) | data formatting | bytes 2752512 | tf_op jit(solution)/shard_map/reshape | solution.py:474
  207.8 30.3 %all-to-all-done.5.parts = bf16[64,24,896]{2,1,0:T(8,128)(2,1)S(1)} async-done(((bf16[64,24,896]{2,1,0:T(8,128)(2,1)}), bf16[64,24,896]{2,1,0:T(8,128)(2,1)S(1)}, u32[]{:S(2)}, u32[]{:S(2)}) %all-to-all-start.5) | async-done | bytes 2752544 | tf_op jit(solution)/shard_map/all_to_all | solution.py:305
  239.2 5.7 %all-to-all-start.6 = ((bf16[8,3,896]{2,1,0:T(4,128)(2,1)}), bf16[8,3,896]{2,1,0:T(4,128)(2,1)S(1)}, u32[]{:S(2)}, u32[]{:S(2)}) async-start(bf16[8,3,896]{2,1,0:T(4,128)(2,1)} %reshape.273), calls=%async_computation.6 | async-start | bytes 114688 | tf_op jit(solution)/shard_map/all_to_all | solution.py:305
  245.7 4.0 %all-to-all-done.6 = bf16[8,3,896]{2,1,0:T(4,128)(2,1)S(1)} async-done(((bf16[8,3,896]{2,1,0:T(4,128)(2,1)}), bf16[8,3,896]{2,1,0:T(4,128)(2,1)S(1)}, u32[]{:S(2)}, u32[]{:S(2)}) %all-to-all-start.6) | async-done | bytes 43040 | tf_op jit(solution)/shard_map/all_to_all | solution.py:305
  (133 shorter events, 37.3 us)
Async XLA Ops:
  0.7 16.2 %copy-start.12 = (s32[3,16,16]{2,1,0:T(8,128)S(1)}, s32[3,16,16]{2,1,0:T(8,128)}, u32[]{:S(2)}) copy-start(s32[3,16,16]{2,1,0:T(8,128)} %param.19) | copy-start | bytes 9220
  0.7 16.3 %copy-start.15 = (s32[3]{0:T(128)S(1)}, s32[3]{0:T(128)}, u32[]{:S(2)}) copy-start(s32[3]{0:T(128)} %param.20) | copy-start | bytes 40
  0.7 16.5 %copy-start.14 = (s32[3,384]{1,0:T(4,128)S(1)}, s32[3,384]{1,0:T(4,128)}, u32[]{:S(2)}) copy-start(s32[3,384]{1,0:T(4,128)} %param.23) | copy-start | bytes 13828
  2.7 26.1 %all-to-all-start = ((bf16[16,3,7168]{2,1,0:T(4,128)(2,1)}), bf16[16,3,7168]{2,1,0:T(4,128)(2,1)S(1)}, u32[]{:S(2)}, u32[]{:S(2)}) async-start(bf16[16,3,7168]{2,1,0:T(4,128)(2,1)} %broadcast_in_dim.18), calls=%async_computation | async-start | bytes 1835008 | tf_op jit(solution)/shard_map/all_to_all | solution.py:305
  10.4 14.0 %collective-permute-start = (bf16[3,14336]{1,0:T(4,128)(2,1)S(1)}, bf16[3,14336]{1,0:T(4,128)(2,1)S(1)}, u32[]{:S(2)}, u32[]{:S(2)}) collective-permute-start(bf16[3,14336]{1,0:T(4,128)(2,1)S(1)} %pad_maximum_fusion.7), channel_id=1, source_target_pairs={{0,4},{4,8},{8,12},{12,0},{1,5},{5,9},{9,13},{13,1},{2,6},{6,10},{... | collective-permute-start | bytes 258056 | tf_op jit(solution)/shard_map/ppermute | solution.py:89
  11.8 15.8 %collective-permute-start.1 = (bf16[3,14336]{1,0:T(4,128)(2,1)S(1)}, bf16[3,14336]{1,0:T(4,128)(2,1)S(1)}, u32[]{:S(2)}, u32[]{:S(2)}) collective-permute-start(bf16[3,14336]{1,0:T(4,128)(2,1)S(1)} %pad_maximum_fusion.7), channel_id=1, source_target_pairs={{0,8},{4,12},{8,0},{12,4},{1,9},{5,13},{9,1},{13,5},{2,10},{6,14},... | collective-permute-start | bytes 258056 | tf_op jit(solution)/shard_map/ppermute | solution.py:89
  14.2 13.4 %collective-permute-start.2 = (bf16[3,14336]{1,0:T(4,128)(2,1)S(1)}, bf16[3,14336]{1,0:T(4,128)(2,1)S(1)}, u32[]{:S(2)}, u32[]{:S(2)}) collective-permute-start(bf16[3,14336]{1,0:T(4,128)(2,1)S(1)} %pad_maximum_fusion.7), channel_id=1, source_target_pairs={{0,12},{4,0},{8,4},{12,8},{1,13},{5,1},{9,5},{13,9},{2,14},{6,2},{... | collective-permute-start | bytes 258056 | tf_op jit(solution)/shard_map/ppermute | solution.py:89
  42.7 19.9 %all-to-all-start.1 = ((bf16[16,3,8192]{2,1,0:T(4,128)(2,1)}), bf16[16,3,8192]{2,1,0:T(4,128)(2,1)S(1)}, u32[]{:S(2)}, u32[]{:S(2)}) async-start(bf16[16,3,8192]{2,1,0:T(4,128)(2,1)} %reshape.265), calls=%async_computation.1 | async-start | bytes 2097152 | tf_op jit(solution)/shard_map/all_to_all | solution.py:305
  48.0 27.7 %collective-permute-start.3 = (bf16[2,56,896]{2,1,0:T(8,128)(2,1)S(1)}, bf16[2,56,896]{2,1,0:T(8,128)(2,1)S(1)}, u32[]{:S(2)}, u32[]{:S(2)}) collective-permute-start(bf16[2,56,896]{2,1,0:T(8,128)(2,1)S(1)} %pad_maximum_fusion.3), channel_id=1, source_target_pairs={{0,32},{32,64},{64,96},{96,0},{1,33},{33,65},{65,97},{97,1},{2,34}... | collective-permute-start | bytes 602120 | tf_op jit(solution)/shard_map/ppermute | solution.py:89
  49.7 25.9 %collective-permute-start.4 = (bf16[2,56,896]{2,1,0:T(8,128)(2,1)S(1)}, bf16[2,56,896]{2,1,0:T(8,128)(2,1)S(1)}, u32[]{:S(2)}, u32[]{:S(2)}) collective-permute-start(bf16[2,56,896]{2,1,0:T(8,128)(2,1)S(1)} %pad_maximum_fusion.4), channel_id=1, source_target_pairs={{0,64},{32,96},{64,0},{96,32},{1,65},{33,97},{65,1},{97,33},{2,66}... | collective-permute-start | bytes 602120 | tf_op jit(solution)/shard_map/ppermute | solution.py:89
  53.2 22.5 %collective-permute-start.5 = (bf16[2,56,896]{2,1,0:T(8,128)(2,1)S(1)}, bf16[2,56,896]{2,1,0:T(8,128)(2,1)S(1)}, u32[]{:S(2)}, u32[]{:S(2)}) collective-permute-start(bf16[2,56,896]{2,1,0:T(8,128)(2,1)S(1)} %pad_maximum_fusion.5), channel_id=1, source_target_pairs={{0,96},{32,0},{64,32},{96,64},{1,97},{33,1},{65,33},{97,65},{2,98}... | collective-permute-start | bytes 602120 | tf_op jit(solution)/shard_map/ppermute | solution.py:89
  65.9 21.0 %all-to-all-start.2 = ((bf16[128,3,224]{2,1,0:T(4,128)(2,1)}), bf16[128,3,224]{2,1,0:T(4,128)(2,1)S(1)}, u32[]{:S(2)}, u32[]{:S(2)}) async-start(bf16[128,3,224]{2,1,0:T(4,128)(2,1)} %copy.79), calls=%async_computation.2 | async-start | bytes 524288 | tf_op jit(solution)/shard_map/all_to_all | solution.py:305
  75.7 12.7 %copy-start.11 = (bf16[3,7168]{1,0:T(4,128)(2,1)S(1)}, bf16[3,7168]{1,0:T(4,128)(2,1)}, u32[]{:S(2)}) copy-start(bf16[3,7168]{1,0:T(4,128)(2,1)} %param.18) | copy-start | bytes 129028
  87.5 2.6 %collective-permute-start.6 = (bf16[384,896]{1,0:T(8,128)(2,1)S(1)}, bf16[384,896]{1,0:T(8,128)(2,1)S(1)}, u32[]{:S(2)}, u32[]{:S(2)}) collective-permute-start(bf16[384,896]{1,0:T(8,128)(2,1)S(1)} %convolution_convert_fusion.1), channel_id=1, source_target_pairs={{0,16},{16,0},{1,17},{17,1},{2,18},{18,2},{3,19},{19,3},{4,20},{20... | collective-permute-start | bytes 2064392 | tf_op jit(solution)/shard_map/ppermute | solution.py:85
  88.4 6.6 %collective-permute-start.7 = (bf16[3,3584]{1,0:T(4,128)(2,1)S(1)}, bf16[3,3584]{1,0:T(4,128)(2,1)S(1)}, u32[]{:S(2)}, u32[]{:S(2)}) collective-permute-start(bf16[3,3584]{1,0:T(4,128)(2,1)S(1)} %get-tuple-element.60), channel_id=1, source_target_pairs={{0,16},{16,0},{1,17},{17,1},{2,18},{18,2},{3,19},{19,3},{4,20},{20... | collective-permute-start | bytes 64520 | tf_op jit(solution)/shard_map/ppermute | solution.py:85
  91.4 15.3 %all-to-all-start.3 = ((bf16[16,24,896]{2,1,0:T(8,128)(2,1)}), bf16[16,24,896]{2,1,0:T(8,128)(2,1)S(1)}, u32[]{:S(2)}, u32[]{:S(2)}) async-start(bf16[16,24,896]{2,1,0:T(8,128)(2,1)} %bitcast.31), calls=%async_computation.3 | async-start | bytes 1376256 | tf_op jit(solution)/shard_map/all_to_all | solution.py:305
  95.1 2.6 %collective-permute-start.10 = (bf16[6,896]{1,0:T(8,128)(2,1)S(1)}, bf16[6,896]{1,0:T(8,128)(2,1)S(1)}, u32[]{:S(2)}, u32[]{:S(2)}) collective-permute-start(bf16[6,896]{1,0:T(8,128)(2,1)S(1)} %get-tuple-element.56), channel_id=1, source_target_pairs={{0,96},{32,0},{64,32},{96,64},{1,97},{33,1},{65,33},{97,65},{2,98}... | collective-permute-start | bytes 32264 | tf_op jit(solution)/shard_map/ppermute | solution.py:89
  95.8 4.1 %collective-permute-start.8 = (bf16[6,896]{1,0:T(8,128)(2,1)S(1)}, bf16[6,896]{1,0:T(8,128)(2,1)S(1)}, u32[]{:S(2)}, u32[]{:S(2)}) collective-permute-start(bf16[6,896]{1,0:T(8,128)(2,1)S(1)} %get-tuple-element.58), channel_id=1, source_target_pairs={{0,32},{32,64},{64,96},{96,0},{1,33},{33,65},{65,97},{97,1},{2,34}... | collective-permute-start | bytes 32264 | tf_op jit(solution)/shard_map/ppermute | solution.py:89
  96.6 4.2 %collective-permute-start.9 = (bf16[6,896]{1,0:T(8,128)(2,1)S(1)}, bf16[6,896]{1,0:T(8,128)(2,1)S(1)}, u32[]{:S(2)}, u32[]{:S(2)}) collective-permute-start(bf16[6,896]{1,0:T(8,128)(2,1)S(1)} %get-tuple-element.57), channel_id=1, source_target_pairs={{0,64},{32,96},{64,0},{96,32},{1,65},{33,97},{65,1},{97,33},{2,66}... | collective-permute-start | bytes 32264 | tf_op jit(solution)/shard_map/ppermute | solution.py:89
  109.0 66.2 %all-to-all-start.4 = ((bf16[64,24,1024]{2,1,0:T(8,128)(2,1)}), bf16[64,24,1024]{2,1,0:T(8,128)(2,1)}, u32[]{:S(2)}, u32[]{:S(2)}) async-start(bf16[64,24,1024]{2,1,0:T(8,128)(2,1)} %broadcast_in_dim.23), calls=%async_computation.4 | async-start | bytes 6291456 | tf_op jit(solution)/shard_map/all_to_all | solution.py:299
  115.6 44.6 %collective-permute-start.11 = (bf16[4,3,14336]{2,1,0:T(4,128)(2,1)}, bf16[4,3,14336]{2,1,0:T(4,128)(2,1)S(1)}, u32[]{:S(2)}, u32[]{:S(2)}) collective-permute-start(bf16[4,3,14336]{2,1,0:T(4,128)(2,1)} %pad_maximum_fusion.2), channel_id=1, source_target_pairs={{0,1},{1,2},{2,3},{3,0},{4,5},{5,6},{6,7},{7,4},{8,9},{9,10},{10,1... | collective-permute-start | bytes 1032200 | tf_op jit(solution)/shard_map/ppermute | solution.py:89
  116.6 54.2 %collective-permute-start.12 = (bf16[4,3,14336]{2,1,0:T(4,128)(2,1)}, bf16[4,3,14336]{2,1,0:T(4,128)(2,1)S(1)}, u32[]{:S(2)}, u32[]{:S(2)}) collective-permute-start(bf16[4,3,14336]{2,1,0:T(4,128)(2,1)} %pad_maximum_fusion.2), channel_id=1, source_target_pairs={{0,2},{1,3},{2,0},{3,1},{4,6},{5,7},{6,4},{7,5},{8,10},{9,11},{10,... | collective-permute-start | bytes 1032200 | tf_op jit(solution)/shard_map/ppermute | solution.py:89
  119.0 51.9 %collective-permute-start.13 = (bf16[4,3,14336]{2,1,0:T(4,128)(2,1)}, bf16[4,3,14336]{2,1,0:T(4,128)(2,1)S(1)}, u32[]{:S(2)}, u32[]{:S(2)}) collective-permute-start(bf16[4,3,14336]{2,1,0:T(4,128)(2,1)} %pad_maximum_fusion.2), channel_id=1, source_target_pairs={{0,3},{1,0},{2,1},{3,2},{4,7},{5,4},{6,5},{7,6},{8,11},{9,8},{10,9... | collective-permute-start | bytes 1032200 | tf_op jit(solution)/shard_map/ppermute | solution.py:89
  120.3 50.6 %copy-start.7 = (bf16[4,3,14336]{2,1,0:T(4,128)(2,1)S(1)}, bf16[4,3,14336]{2,1,0:T(4,128)(2,1)}, u32[]{:S(2)}) copy-start(bf16[4,3,14336]{2,1,0:T(4,128)(2,1)} %pad_maximum_fusion.2) | copy-start | bytes 1032196
  120.3 53.2 %collective-permute-start.14 = (bf16[224,3584]{1,0:T(8,128)(2,1)S(1)}, bf16[224,3584]{1,0:T(8,128)(2,1)S(1)}, u32[]{:S(2)}, u32[]{:S(2)}) collective-permute-start(bf16[224,3584]{1,0:T(8,128)(2,1)S(1)} %constant_dynamic-slice_fusion.1), channel_id=1, source_target_pairs={{0,16},{16,0},{1,17},{17,1},{2,18},{18,2},{3,19},{19,3},{4,20},{20... | collective-permute-start | bytes 4816904 | tf_op jit(solution)/shard_map/ppermute | solution.py:85
  124.8 61.9 %collective-permute-start.19 = (bf16[224,3584]{1,0:T(8,128)(2,1)}, bf16[224,3584]{1,0:T(8,128)(2,1)}, u32[]{:S(2)}, u32[]{:S(2)}) collective-permute-start(bf16[224,3584]{1,0:T(8,128)(2,1)} %constant_dynamic-slice_fusion), channel_id=1, source_target_pairs={{0,16},{16,0},{1,17},{17,1},{2,18},{18,2},{3,19},{19,3},{4,20},{20... | collective-permute-start | bytes 4816904 | tf_op jit(solution)/shard_map/ppermute | solution.py:85
  182.1 3.7 %collective-permute-start.15 = (f32[384,224]{1,0:T(8,128)S(1)}, f32[384,224]{1,0:T(8,128)S(1)}, u32[]{:S(2)}, u32[]{:S(2)}) collective-permute-start(f32[384,224]{1,0:T(8,128)S(1)} %get-tuple-element.28), channel_id=1, source_target_pairs={{0,16},{16,0},{1,17},{17,1},{2,18},{18,2},{3,19},{19,3},{4,20},{20... | collective-permute-start | bytes 1032200 | tf_op jit(solution)/shard_map/ppermute | solution.py:85
  184.2 1.7 collective-permute-start.16
  184.3 1.6 collective-permute-start.17
  186.3 1.5 collective-permute-start.18
  193.2 44.8 %all-to-all-start.5 = ((bf16[64,24,896]{2,1,0:T(8,128)(2,1)}), bf16[64,24,896]{2,1,0:T(8,128)(2,1)S(1)}, u32[]{:S(2)}, u32[]{:S(2)}) async-start(bf16[64,24,896]{2,1,0:T(8,128)(2,1)} %bitcast.103), calls=%async_computation.5 | async-start | bytes 5505024 | tf_op jit(solution)/shard_map/all_to_all | solution.py:305
  239.2 10.6 %all-to-all-start.6 = ((bf16[8,3,896]{2,1,0:T(4,128)(2,1)}), bf16[8,3,896]{2,1,0:T(4,128)(2,1)S(1)}, u32[]{:S(2)}, u32[]{:S(2)}) async-start(bf16[8,3,896]{2,1,0:T(4,128)(2,1)} %reshape.273), calls=%async_computation.6 | async-start | bytes 114688 | tf_op jit(solution)/shard_map/all_to_all | solution.py:305
  (12 other events, 85.2 us)

commit v10 on v9

--- a/solution.py
+++ b/solution.py
@@ -402,6 +402,7 @@
     order = at[:, None] == (source * rows_dev + at % rows_dev)[None, :]
     res = jnp.dot(order.astype(BF16), res, preferred_element_type=F32)
 
+    sent_parts = parts
     parts = exchange(parts.reshape(members, rows_dev, parts.shape[1]), MLP)
     parts = parts.reshape(members, rows_dev, heads // 7, 8, HD).astype(F32)
     st = parts[:, :, :, 7]
@@ -418,7 +419,11 @@
             for to in range(zs)
         ]
     ).reshape(groups * members, rows_dev, zs * k_dev)
-    feats = exchange(feats, ALL)
+    far = shift(after(both, sent_parts), ys // 2, ys, "y")
+    feats, far = lax.optimization_barrier((feats, far))
+    both = after(both, feats)
+    both = [far if d == ys // 2 else shift(both, d, ys, "y") if d else both for d in range(ys)]
+    feats, both = lax.optimization_barrier((exchange(feats, ALL), both))
     feats = (
         feats.reshape(groups, members, rows_dev, zs * k_dev)
         .transpose(1, 0, 2, 3)
@@ -448,10 +453,7 @@
     gain_other = gw[:, 1]
     gain_pair = pair(gain_other)
 
-    both = after(both, row)
-    both = jnp.stack([shift(both, d, ys, "y") if d else both for d in range(ys)])
     rows = spread(row, CHIPS, zs * members).reshape(zs, tokens, chunk + HD)
-    rows, both = lax.optimization_barrier((rows, both))
     mine, theirs, stats = up_project(place, rows, up_w, up_other, gain_own, gain_other)
     act = pl.pallas_call(
         lambda *refs: act_kernel(width, *refs),
@@ -471,7 +473,7 @@
     near = at // rows_dev
     slots = (((x - near % xs) % xs) * ys + (y - near // xs) % ys) * rows_dev + at % rows_dev
     chooser = jnp.any((target[:, :, None] == slots[None, None, :]) & valid[:, :, None], axis=0)
-    both = both.reshape(group_rows, 2 * width)
+    both = jnp.stack(both).reshape(group_rows, 2 * width)
     picked = jnp.dot(chooser.astype(BF16), both, preferred_element_type=F32).astype(BF16)
     return (mixed, picked[:, :width][None], picked[:, width:][None])
 

time: 252 us -> 240 us (0.952)
  waiting for transfers between devices: 120 us -> 105 us
  other arithmetic: 6.96 us -> 9.84 us
    ppermute x12, waiting for transfers between devices: 56.7 us -> 19.5 us  [shift(): return lax.ppermute(x, axis, [(i, (i + step) % size) for i in range(size)])]
    all_to_all x1, waiting for transfers between devices: 0.01 us -> 30.6 us  [spread(): lax.all_to_all(jnp.broadcast_to(x[None], (count,) + x.shape), axes, split...]
    all_to_all x6, waiting for transfers between devices: 59.7 us -> 51.1 us  [exchange(): return lax.all_to_all(x, axes, split_axis=0, concat_axis=0)]
  transfers between devices with their start and end apart: 27 -> 27, of which waited for: 15 -> 17; matrix products, arithmetic and copies ran while one was open for 8% -> 10% of each run, Pallas kernels for 3% -> 3%
where the time goes in v10:
time: 240 us; the launch traced here: 239 us
  waiting for transfers between devices  105 us (44%)
  starting transfers between devices  73.2 us (30%)
  local copies, waits for them, and re-layouts  23.5 us (10%)
  Pallas kernels  22.3 us (9%)
  other arithmetic  9.84 us (4%)
  matrix products  3.59 us (1%)
    all_to_all x6, waiting for transfers between devices, exchange(): return lax.all_to_all(x, axes, split_axis=0, concat_axis=0)  51.1 us
    all_to_all x6, starting transfers between devices, exchange(): return lax.all_to_all(x, axes, split_axis=0, concat_axis=0)  39.9 us
    all_to_all x1, waiting for transfers between devices, spread(): lax.all_to_all(jnp.broadcast_to(x[None], (count,) + x.shape), axes, split...  30.6 us
    ppermute x12, waiting for transfers between devices, shift(): return lax.ppermute(x, axis, [(i, (i + step) % size) for i in range(size)])  19.5 us
    ppermute x12, starting transfers between devices, shift(): return lax.ppermute(x, axis, [(i, (i + step) % size) for i in range(size)])  17.1 us
    pallas_call x1, Pallas kernels, attend(): pl.pallas_call(body, grid=(steps,), in_specs=[pl.BlockSpec((rows, wide),...  10.2 us
    ppermute x8, starting transfers between devices, pair(): return lax.ppermute(x, 'c', [(0, 1), (1, 0)])  9.76 us
    all_to_all x1, starting transfers between devices, spread(): lax.all_to_all(jnp.broadcast_to(x[None], (count,) + x.shape), axes, split...  6.4 us
  transfers between devices with their start and end apart: 27, of which 17 were waited for; matrix products, arithmetic and copies ran while one was open for 10% of the time, Pallas kernels for 3%

profile of v10, /device:TPU:1, one launch (start us, length us, event | category | flops | bytes accessed | tf_op | source)
XLA Modules:
  0.0 238.8 jit_solution(4849097010861516607)
XLA Ops:
  0.7 2.1 broadcast_in_dim.18
  2.8 7.6 %all-to-all-start = ((bf16[16,3,7168]{2,1,0:T(4,128)(2,1)}), bf16[16,3,7168]{2,1,0:T(4,128)(2,1)S(1)}, u32[]{:S(2)}, u32[]{:S(2)}) async-start(bf16[16,3,7168]{2,1,0:T(4,128)(2,1)} %broadcast_in_dim.18), calls=%async_computation | async-start | bytes 1835008 | tf_op jit(solution)/shard_map/all_to_all | solution.py:305
  10.4 2.6 %collective-permute-start.2 = (bf16[3,14336]{1,0:T(4,128)(2,1)S(1)}, bf16[3,14336]{1,0:T(4,128)(2,1)S(1)}, u32[]{:S(2)}, u32[]{:S(2)}) collective-permute-start(bf16[3,14336]{1,0:T(4,128)(2,1)S(1)} %pad_maximum_fusion.7), channel_id=1, source_target_pairs={{0,12},{4,0},{8,4},{12,8},{1,13},{5,1},{9,5},{13,9},{2,14},{6,2},{... | collective-permute-start | bytes 258056 | tf_op jit(solution)/shard_map/ppermute | solution.py:89
  17.3 6.7 %collective-permute-done.2 = bf16[3,14336]{1,0:T(4,128)(2,1)S(1)} collective-permute-done((bf16[3,14336]{1,0:T(4,128)(2,1)S(1)}, bf16[3,14336]{1,0:T(4,128)(2,1)S(1)}, u32[]{:S(2)}, u32[]{:S(2)}) %collective-permute-start.2) | collective-permute-done | bytes 86048 | tf_op jit(solution)/shard_map/ppermute | solution.py:89
  28.7 10.2 %shard_map.166 = bf16[48,8192]{1,0:T(8,128)(2,1)} custom-call(bf16[48,7168]{1,0:T(8,128)(2,1)} %reshape.263.refs_0_, bf16[24,16,7168]{2,1,0:T(8,128)(2,1)} %refs_1_.1, bf16[24,16,7168]{2,1,0:T(8,128)(2,1)} %refs_2_.1, bf16[16,7168]{1,0:T(8,128)(2,1)} %pad.7.refs_3_, bf16[16,7168]{1,0:T(8,128)(2,1)} %pad.8.refs_4_, f32[48,400]{1,0:T(8,128)} %pad_maximum_fusion.8.refs_5_), custom_call_target="tpu_custom_call" | custom-call | flops 528482304 | bytes 11010048 | tf_op jit(solution)/shard_map/pallas_call | solution.py:62
  38.9 2.3 reshape.265
  41.2 5.8 %all-to-all-start.1 = ((bf16[16,3,8192]{2,1,0:T(4,128)(2,1)}), bf16[16,3,8192]{2,1,0:T(4,128)(2,1)S(1)}, u32[]{:S(2)}, u32[]{:S(2)}) async-start(bf16[16,3,8192]{2,1,0:T(4,128)(2,1)} %reshape.265), calls=%async_computation.1 | async-start | bytes 2097152 | tf_op jit(solution)/shard_map/all_to_all | solution.py:305
  47.2 2.8 %collective-permute-start.3 = (bf16[4,3,14336]{2,1,0:T(4,128)(2,1)S(1)}, bf16[4,3,14336]{2,1,0:T(4,128)(2,1)S(1)}, u32[]{:S(2)}, u32[]{:S(2)}) collective-permute-start(bf16[4,3,14336]{2,1,0:T(4,128)(2,1)S(1)} %pad_maximum_fusion.2), channel_id=1, source_target_pairs={{0,2},{1,3},{2,0},{3,1},{4,6},{5,7},{6,4},{7,5},{8,10},{9,11},{10,... | collective-permute-start | bytes 1032200 | tf_op jit(solution)/shard_map/ppermute | solution.py:89
  51.3 3.8 %collective-permute-start.8 = (bf16[2,56,896]{2,1,0:T(8,128)(2,1)}, bf16[2,56,896]{2,1,0:T(8,128)(2,1)}, u32[]{:S(2)}, u32[]{:S(2)}) collective-permute-start(bf16[2,56,896]{2,1,0:T(8,128)(2,1)} %pad_maximum_fusion.5), channel_id=1, source_target_pairs={{0,96},{32,0},{64,32},{96,64},{1,97},{33,1},{65,33},{97,65},{2,98}... | collective-permute-start | bytes 602120 | tf_op jit(solution)/shard_map/ppermute | solution.py:89
  55.8 6.1 %all-to-all-done.1 = bf16[16,3,8192]{2,1,0:T(4,128)(2,1)S(1)} async-done(((bf16[16,3,8192]{2,1,0:T(4,128)(2,1)}), bf16[16,3,8192]{2,1,0:T(4,128)(2,1)S(1)}, u32[]{:S(2)}, u32[]{:S(2)}) %all-to-all-start.1) | async-done | bytes 786464 | tf_op jit(solution)/shard_map/all_to_all | solution.py:305
  64.3 6.3 %collective-permute-done.3 = bf16[4,3,14336]{2,1,0:T(4,128)(2,1)S(1)} collective-permute-done((bf16[4,3,14336]{2,1,0:T(4,128)(2,1)S(1)}, bf16[4,3,14336]{2,1,0:T(4,128)(2,1)S(1)}, u32[]{:S(2)}, u32[]{:S(2)}) %collective-permute-start.3) | collective-permute-done | bytes 344096 | tf_op jit(solution)/shard_map/ppermute | solution.py:89
  71.2 2.1 collective-permute-start.5
  73.4 1.7 collective-permute-start.6
  75.9 10.1 %all-to-all-start.2 = ((bf16[128,3,224]{2,1,0:T(4,128)(2,1)}), bf16[128,3,224]{2,1,0:T(4,128)(2,1)S(1)}, u32[]{:S(2)}, u32[]{:S(2)}) async-start(bf16[128,3,224]{2,1,0:T(4,128)(2,1)} %copy.79), calls=%async_computation.2 | async-start | bytes 524288 | tf_op jit(solution)/shard_map/all_to_all | solution.py:305
  87.9 9.3 %all-to-all-done.2 = bf16[128,3,224]{2,1,0:T(4,128)(2,1)S(1)} async-done(((bf16[128,3,224]{2,1,0:T(4,128)(2,1)}), bf16[128,3,224]{2,1,0:T(4,128)(2,1)S(1)}, u32[]{:S(2)}, u32[]{:S(2)}) %all-to-all-start.2) | async-done | bytes 172064 | tf_op jit(solution)/shard_map/all_to_all | solution.py:305
  102.4 3.6 %all-to-all-start.3 = ((bf16[16,24,896]{2,1,0:T(8,128)(2,1)}), bf16[16,24,896]{2,1,0:T(8,128)(2,1)S(1)}, u32[]{:S(2)}, u32[]{:S(2)}) async-start(bf16[16,24,896]{2,1,0:T(8,128)(2,1)} %bitcast.31), calls=%async_computation.3 | async-start | bytes 1376256 | tf_op jit(solution)/shard_map/all_to_all | solution.py:305
  106.8 1.7 collective-permute-start.12
  108.7 2.4 %collective-permute-done.12 = bf16[6,896]{1,0:T(8,128)(2,1)S(1)} collective-permute-done((bf16[6,896]{1,0:T(8,128)(2,1)S(1)}, bf16[6,896]{1,0:T(8,128)(2,1)S(1)}, u32[]{:S(2)}, u32[]{:S(2)}) %collective-permute-start.12) | collective-permute-done | bytes 10784 | tf_op jit(solution)/shard_map/ppermute | solution.py:89
  112.5 5.2 %all-to-all-done.3.parts = bf16[16,24,896]{2,1,0:T(8,128)(2,1)S(1)} async-done(((bf16[16,24,896]{2,1,0:T(8,128)(2,1)}), bf16[16,24,896]{2,1,0:T(8,128)(2,1)S(1)}, u32[]{:S(2)}, u32[]{:S(2)}) %all-to-all-start.3) | async-done | bytes 688160 | tf_op jit(solution)/shard_map/all_to_all | solution.py:305
  117.9 2.1 broadcast_in_dim.23
  120.0 6.4 %all-to-all-start.4 = ((bf16[64,24,1024]{2,1,0:T(8,128)(2,1)}), bf16[64,24,1024]{2,1,0:T(8,128)(2,1)}, u32[]{:S(2)}, u32[]{:S(2)}) async-start(bf16[64,24,1024]{2,1,0:T(8,128)(2,1)} %broadcast_in_dim.23), calls=%async_computation.4 | async-start | bytes 6291456 | tf_op jit(solution)/shard_map/all_to_all | solution.py:299
  126.6 2.2 collective-permute-start.14
  133.6 30.6 %all-to-all-done.4 = bf16[64,24,1024]{2,1,0:T(8,128)(2,1)} async-done(((bf16[64,24,1024]{2,1,0:T(8,128)(2,1)}), bf16[64,24,1024]{2,1,0:T(8,128)(2,1)}, u32[]{:S(2)}, u32[]{:S(2)}) %all-to-all-start.4) | async-done | bytes 3145760 | tf_op jit(solution)/shard_map/all_to_all | solution.py:299
  165.6 5.4 %shard_map.169 = (f32[384,224]{1,0:T(8,128)S(1)}, f32[384,224]{1,0:T(8,128)S(1)}, f32[384,128]{1,0:T(8,128)S(1)}) custom-call(s32[1]{0:T(128)} %bitcast.place, bf16[4,384,1024]{2,1,0:T(8,128)(2,1)} %bitcast.34.rows, bf16[224,7168]{1,0:T(8,128)(2,1)S(1)} %bitcast.102, bf16[224,3584]{1,0:T(8,128)(2,1)S(1)} %copy-done.5, ...), custom_call_target="tpu_custom_call" | custom-call | tf_op jit(solution)/shard_map/pallas_call | solution.py:233
  171.0 3.9 %collective-permute-start.15 = (f32[384,224]{1,0:T(8,128)S(1)}, f32[384,224]{1,0:T(8,128)S(1)}, u32[]{:S(2)}, u32[]{:S(2)}) collective-permute-start(f32[384,224]{1,0:T(8,128)S(1)} %get-tuple-element.37), channel_id=1, source_target_pairs={{0,16},{16,0},{1,17},{17,1},{2,18},{18,2},{3,19},{19,3},{4,20},{20... | collective-permute-start | bytes 1032200 | tf_op jit(solution)/shard_map/ppermute | solution.py:85
  178.5 3.9 %shard_map.171 = bf16[4,384,896]{2,1,0:T(8,128)(2,1)S(1)} custom-call(s32[1]{0:T(128)} %bitcast.place, bf16[384,224]{1,0:T(8,128)(2,1)S(1)} %shard_map.170.act, bf16[384,224]{1,0:T(8,128)(2,1)S(1)} %collective-permute-done.18.act_pair, bf16[224,7168]{1,0:T(8,128)(2,1)S(1)} %copy-done.3, bf16[224,3584]{1,0:T(8,128)(2,1)} %collective-permute-done.19.other), custom_call_target="tpu_custom_call" | custom-call | tf_op jit(solution)/shard_map/pallas_call | solution.py:263
  183.9 7.1 %all-to-all-start.5 = ((bf16[64,24,896]{2,1,0:T(8,128)(2,1)}), bf16[64,24,896]{2,1,0:T(8,128)(2,1)S(1)}, u32[]{:S(2)}, u32[]{:S(2)}) async-start(bf16[64,24,896]{2,1,0:T(8,128)(2,1)} %bitcast.103), calls=%async_computation.5 | async-start | bytes 5505024 | tf_op jit(solution)/shard_map/all_to_all | solution.py:305
  191.3 3.8 %pad_maximum_fusion = bf16[4,4,3,14336]{3,2,1,0:T(4,128)(2,1)} fusion(bf16[1,4,3,14336]{3,2,1,0:T(4,128)(2,1)} %bitcast.116, bf16[1,4,3,14336]{3,2,1,0:T(4,128)(2,1)} %bitcast.114, bf16[1,4,3,14336]{3,2,1,0:T(4,128)(2,1)} %bitcast.115, bf16[1,4,3,14336]{3,2,1,0:T(4,128)(2,1)S(1)} %bitcast.110), kind=kLoop, calls=%fused_computation.1 | loop fusion | flops 2064384 | bytes 2752512 | tf_op jit(solution)/shard_map/stack | solution.py:476
  195.1 3.2 %reshape.276 = bf16[48,14336]{1,0:T(8,128)(2,1)} reshape(bf16[4,4,3,14336]{3,2,1,0:T(4,128)(2,1)} %pad_maximum_fusion) | data formatting | bytes 2752512 | tf_op jit(solution)/shard_map/reshape | solution.py:476
  200.0 26.5 %all-to-all-done.5.parts = bf16[64,24,896]{2,1,0:T(8,128)(2,1)S(1)} async-done(((bf16[64,24,896]{2,1,0:T(8,128)(2,1)}), bf16[64,24,896]{2,1,0:T(8,128)(2,1)S(1)}, u32[]{:S(2)}, u32[]{:S(2)}) %all-to-all-start.5) | async-done | bytes 2752544 | tf_op jit(solution)/shard_map/all_to_all | solution.py:305
  227.5 5.7 %all-to-all-start.6 = ((bf16[8,3,896]{2,1,0:T(4,128)(2,1)}), bf16[8,3,896]{2,1,0:T(4,128)(2,1)S(1)}, u32[]{:S(2)}, u32[]{:S(2)}) async-start(bf16[8,3,896]{2,1,0:T(4,128)(2,1)} %reshape.273), calls=%async_computation.6 | async-start | bytes 114688 | tf_op jit(solution)/shard_map/all_to_all | solution.py:305
  234.0 4.0 %all-to-all-done.6 = bf16[8,3,896]{2,1,0:T(4,128)(2,1)S(1)} async-done(((bf16[8,3,896]{2,1,0:T(4,128)(2,1)}), bf16[8,3,896]{2,1,0:T(4,128)(2,1)S(1)}, u32[]{:S(2)}, u32[]{:S(2)}) %all-to-all-start.6) | async-done | bytes 43040 | tf_op jit(solution)/shard_map/all_to_all | solution.py:305
  (145 shorter events, 40.2 us)
Async XLA Ops:
  0.7 15.0 %copy-start.21 = (s32[3]{0:T(128)S(1)}, s32[3]{0:T(128)}, u32[]{:S(2)}) copy-start(s32[3]{0:T(128)} %param.20) | copy-start | bytes 40
  0.7 15.2 %copy-start.18 = (s32[3,16,16]{2,1,0:T(8,128)S(1)}, s32[3,16,16]{2,1,0:T(8,128)}, u32[]{:S(2)}) copy-start(s32[3,16,16]{2,1,0:T(8,128)} %param.19) | copy-start | bytes 9220
  0.7 15.3 %copy-start.20 = (s32[3,384]{1,0:T(4,128)S(1)}, s32[3,384]{1,0:T(4,128)}, u32[]{:S(2)}) copy-start(s32[3,384]{1,0:T(4,128)} %param.23) | copy-start | bytes 13828
  2.8 24.5 %all-to-all-start = ((bf16[16,3,7168]{2,1,0:T(4,128)(2,1)}), bf16[16,3,7168]{2,1,0:T(4,128)(2,1)S(1)}, u32[]{:S(2)}, u32[]{:S(2)}) async-start(bf16[16,3,7168]{2,1,0:T(4,128)(2,1)} %broadcast_in_dim.18), calls=%async_computation | async-start | bytes 1835008 | tf_op jit(solution)/shard_map/all_to_all | solution.py:305
  10.4 13.6 %collective-permute-start.2 = (bf16[3,14336]{1,0:T(4,128)(2,1)S(1)}, bf16[3,14336]{1,0:T(4,128)(2,1)S(1)}, u32[]{:S(2)}, u32[]{:S(2)}) collective-permute-start(bf16[3,14336]{1,0:T(4,128)(2,1)S(1)} %pad_maximum_fusion.7), channel_id=1, source_target_pairs={{0,12},{4,0},{8,4},{12,8},{1,13},{5,1},{9,5},{13,9},{2,14},{6,2},{... | collective-permute-start | bytes 258056 | tf_op jit(solution)/shard_map/ppermute | solution.py:89
  13.1 12.4 %collective-permute-start.1 = (bf16[3,14336]{1,0:T(4,128)(2,1)S(1)}, bf16[3,14336]{1,0:T(4,128)(2,1)S(1)}, u32[]{:S(2)}, u32[]{:S(2)}) collective-permute-start(bf16[3,14336]{1,0:T(4,128)(2,1)S(1)} %pad_maximum_fusion.7), channel_id=1, source_target_pairs={{0,8},{4,12},{8,0},{12,4},{1,9},{5,13},{9,1},{13,5},{2,10},{6,14},... | collective-permute-start | bytes 258056 | tf_op jit(solution)/shard_map/ppermute | solution.py:89
  13.6 13.2 %collective-permute-start = (bf16[3,14336]{1,0:T(4,128)(2,1)S(1)}, bf16[3,14336]{1,0:T(4,128)(2,1)S(1)}, u32[]{:S(2)}, u32[]{:S(2)}) collective-permute-start(bf16[3,14336]{1,0:T(4,128)(2,1)S(1)} %pad_maximum_fusion.7), channel_id=1, source_target_pairs={{0,4},{4,8},{8,12},{12,0},{1,5},{5,9},{9,13},{13,1},{2,6},{6,10},{... | collective-permute-start | bytes 258056 | tf_op jit(solution)/shard_map/ppermute | solution.py:89
  27.3 43.9 %copy-start.7 = (bf16[4,3,14336]{2,1,0:T(4,128)(2,1)}, bf16[4,3,14336]{2,1,0:T(4,128)(2,1)S(1)}, u32[]{:S(2)}) copy-start(bf16[4,3,14336]{2,1,0:T(4,128)(2,1)S(1)} %pad_maximum_fusion.2) | copy-start | bytes 1032196
  41.2 20.7 %all-to-all-start.1 = ((bf16[16,3,8192]{2,1,0:T(4,128)(2,1)}), bf16[16,3,8192]{2,1,0:T(4,128)(2,1)S(1)}, u32[]{:S(2)}, u32[]{:S(2)}) async-start(bf16[16,3,8192]{2,1,0:T(4,128)(2,1)} %reshape.265), calls=%async_computation.1 | async-start | bytes 2097152 | tf_op jit(solution)/shard_map/all_to_all | solution.py:305
  47.2 23.5 %collective-permute-start.3 = (bf16[4,3,14336]{2,1,0:T(4,128)(2,1)S(1)}, bf16[4,3,14336]{2,1,0:T(4,128)(2,1)S(1)}, u32[]{:S(2)}, u32[]{:S(2)}) collective-permute-start(bf16[4,3,14336]{2,1,0:T(4,128)(2,1)S(1)} %pad_maximum_fusion.2), channel_id=1, source_target_pairs={{0,2},{1,3},{2,0},{3,1},{4,6},{5,7},{6,4},{7,5},{8,10},{9,11},{10,... | collective-permute-start | bytes 1032200 | tf_op jit(solution)/shard_map/ppermute | solution.py:89
  51.3 34.7 %collective-permute-start.8 = (bf16[2,56,896]{2,1,0:T(8,128)(2,1)}, bf16[2,56,896]{2,1,0:T(8,128)(2,1)}, u32[]{:S(2)}, u32[]{:S(2)}) collective-permute-start(bf16[2,56,896]{2,1,0:T(8,128)(2,1)} %pad_maximum_fusion.5), channel_id=1, source_target_pairs={{0,96},{32,0},{64,32},{96,64},{1,97},{33,1},{65,33},{97,65},{2,98}... | collective-permute-start | bytes 602120 | tf_op jit(solution)/shard_map/ppermute | solution.py:89
  55.8 30.2 %collective-permute-start.7 = (bf16[2,56,896]{2,1,0:T(8,128)(2,1)}, bf16[2,56,896]{2,1,0:T(8,128)(2,1)}, u32[]{:S(2)}, u32[]{:S(2)}) collective-permute-start(bf16[2,56,896]{2,1,0:T(8,128)(2,1)} %pad_maximum_fusion.4), channel_id=1, source_target_pairs={{0,64},{32,96},{64,0},{96,32},{1,65},{33,97},{65,1},{97,33},{2,66}... | collective-permute-start | bytes 602120 | tf_op jit(solution)/shard_map/ppermute | solution.py:89
  70.6 26.7 %copy-start.10 = (bf16[4,3,14336]{2,1,0:T(4,128)(2,1)}, bf16[4,3,14336]{2,1,0:T(4,128)(2,1)S(1)}, u32[]{:S(2)}) copy-start(bf16[4,3,14336]{2,1,0:T(4,128)(2,1)S(1)} %collective-permute-done.3) | copy-start | bytes 1032196
  70.6 26.5 %collective-permute-start.4 = (bf16[4,3,14336]{2,1,0:T(4,128)(2,1)S(1)}, bf16[4,3,14336]{2,1,0:T(4,128)(2,1)S(1)}, u32[]{:S(2)}, u32[]{:S(2)}) collective-permute-start(bf16[4,3,14336]{2,1,0:T(4,128)(2,1)S(1)} %pad_maximum_fusion.2), channel_id=1, source_target_pairs={{0,1},{1,2},{2,3},{3,0},{4,5},{5,6},{6,7},{7,4},{8,9},{9,10},{10,1... | collective-permute-start | bytes 1032200 | tf_op jit(solution)/shard_map/ppermute | solution.py:89
  71.2 26.0 %collective-permute-start.5 = (bf16[4,3,14336]{2,1,0:T(4,128)(2,1)S(1)}, bf16[4,3,14336]{2,1,0:T(4,128)(2,1)S(1)}, u32[]{:S(2)}, u32[]{:S(2)}) collective-permute-start(bf16[4,3,14336]{2,1,0:T(4,128)(2,1)S(1)} %pad_maximum_fusion.2), channel_id=1, source_target_pairs={{0,3},{1,0},{2,1},{3,2},{4,7},{5,4},{6,5},{7,6},{8,11},{9,8},{10,9... | collective-permute-start | bytes 1032200 | tf_op jit(solution)/shard_map/ppermute | solution.py:89
  73.4 12.7 %collective-permute-start.6 = (bf16[2,56,896]{2,1,0:T(8,128)(2,1)S(1)}, bf16[2,56,896]{2,1,0:T(8,128)(2,1)S(1)}, u32[]{:S(2)}, u32[]{:S(2)}) collective-permute-start(bf16[2,56,896]{2,1,0:T(8,128)(2,1)S(1)} %pad_maximum_fusion.3), channel_id=1, source_target_pairs={{0,32},{32,64},{64,96},{96,0},{1,33},{33,65},{65,97},{97,1},{2,34}... | collective-permute-start | bytes 602120 | tf_op jit(solution)/shard_map/ppermute | solution.py:89
  75.9 21.2 %all-to-all-start.2 = ((bf16[128,3,224]{2,1,0:T(4,128)(2,1)}), bf16[128,3,224]{2,1,0:T(4,128)(2,1)S(1)}, u32[]{:S(2)}, u32[]{:S(2)}) async-start(bf16[128,3,224]{2,1,0:T(4,128)(2,1)} %copy.79), calls=%async_computation.2 | async-start | bytes 524288 | tf_op jit(solution)/shard_map/all_to_all | solution.py:305
  98.5 2.6 %collective-permute-start.9 = (bf16[384,896]{1,0:T(8,128)(2,1)S(1)}, bf16[384,896]{1,0:T(8,128)(2,1)S(1)}, u32[]{:S(2)}, u32[]{:S(2)}) collective-permute-start(bf16[384,896]{1,0:T(8,128)(2,1)S(1)} %convolution_convert_fusion.1), channel_id=1, source_target_pairs={{0,16},{16,0},{1,17},{17,1},{2,18},{18,2},{3,19},{19,3},{4,20},{20... | collective-permute-start | bytes 2064392 | tf_op jit(solution)/shard_map/ppermute | solution.py:85
  99.4 6.6 %collective-permute-start.10 = (bf16[3,3584]{1,0:T(4,128)(2,1)S(1)}, bf16[3,3584]{1,0:T(4,128)(2,1)S(1)}, u32[]{:S(2)}, u32[]{:S(2)}) collective-permute-start(bf16[3,3584]{1,0:T(4,128)(2,1)S(1)} %get-tuple-element.72), channel_id=1, source_target_pairs={{0,16},{16,0},{1,17},{17,1},{2,18},{18,2},{3,19},{19,3},{4,20},{20... | collective-permute-start | bytes 64520 | tf_op jit(solution)/shard_map/ppermute | solution.py:85
  102.4 15.3 %all-to-all-start.3 = ((bf16[16,24,896]{2,1,0:T(8,128)(2,1)}), bf16[16,24,896]{2,1,0:T(8,128)(2,1)S(1)}, u32[]{:S(2)}, u32[]{:S(2)}) async-start(bf16[16,24,896]{2,1,0:T(8,128)(2,1)} %bitcast.31), calls=%async_computation.3 | async-start | bytes 1376256 | tf_op jit(solution)/shard_map/all_to_all | solution.py:305
  106.1 2.6 %collective-permute-start.13 = (bf16[6,896]{1,0:T(8,128)(2,1)S(1)}, bf16[6,896]{1,0:T(8,128)(2,1)S(1)}, u32[]{:S(2)}, u32[]{:S(2)}) collective-permute-start(bf16[6,896]{1,0:T(8,128)(2,1)S(1)} %get-tuple-element.68), channel_id=1, source_target_pairs={{0,96},{32,0},{64,32},{96,64},{1,97},{33,1},{65,33},{97,65},{2,98}... | collective-permute-start | bytes 32264 | tf_op jit(solution)/shard_map/ppermute | solution.py:89
  106.8 4.4 %collective-permute-start.12 = (bf16[6,896]{1,0:T(8,128)(2,1)S(1)}, bf16[6,896]{1,0:T(8,128)(2,1)S(1)}, u32[]{:S(2)}, u32[]{:S(2)}) collective-permute-start(bf16[6,896]{1,0:T(8,128)(2,1)S(1)} %get-tuple-element.69), channel_id=1, source_target_pairs={{0,64},{32,96},{64,0},{96,32},{1,65},{33,97},{65,1},{97,33},{2,66}... | collective-permute-start | bytes 32264 | tf_op jit(solution)/shard_map/ppermute | solution.py:89
  108.5 3.8 %collective-permute-start.11 = (bf16[6,896]{1,0:T(8,128)(2,1)S(1)}, bf16[6,896]{1,0:T(8,128)(2,1)S(1)}, u32[]{:S(2)}, u32[]{:S(2)}) collective-permute-start(bf16[6,896]{1,0:T(8,128)(2,1)S(1)} %get-tuple-element.70), channel_id=1, source_target_pairs={{0,32},{32,64},{64,96},{96,0},{1,33},{33,65},{65,97},{97,1},{2,34}... | collective-permute-start | bytes 32264 | tf_op jit(solution)/shard_map/ppermute | solution.py:89
  120.0 44.1 %all-to-all-start.4 = ((bf16[64,24,1024]{2,1,0:T(8,128)(2,1)}), bf16[64,24,1024]{2,1,0:T(8,128)(2,1)}, u32[]{:S(2)}, u32[]{:S(2)}) async-start(bf16[64,24,1024]{2,1,0:T(8,128)(2,1)} %broadcast_in_dim.23), calls=%async_computation.4 | async-start | bytes 6291456 | tf_op jit(solution)/shard_map/all_to_all | solution.py:299
  126.6 5.3 %collective-permute-start.14 = (bf16[224,3584]{1,0:T(8,128)(2,1)S(1)}, bf16[224,3584]{1,0:T(8,128)(2,1)S(1)}, u32[]{:S(2)}, u32[]{:S(2)}) collective-permute-start(bf16[224,3584]{1,0:T(8,128)(2,1)S(1)} %constant_dynamic-slice_fusion.1), channel_id=1, source_target_pairs={{0,16},{16,0},{1,17},{17,1},{2,18},{18,2},{3,19},{19,3},{4,20},{20... | collective-permute-start | bytes 4816904 | tf_op jit(solution)/shard_map/ppermute | solution.py:85
  130.1 47.4 %collective-permute-start.19 = (bf16[224,3584]{1,0:T(8,128)(2,1)}, bf16[224,3584]{1,0:T(8,128)(2,1)}, u32[]{:S(2)}, u32[]{:S(2)}) collective-permute-start(bf16[224,3584]{1,0:T(8,128)(2,1)} %constant_dynamic-slice_fusion), channel_id=1, source_target_pairs={{0,16},{16,0},{1,17},{17,1},{2,18},{18,2},{3,19},{19,3},{4,20},{20... | collective-permute-start | bytes 4816904 | tf_op jit(solution)/shard_map/ppermute | solution.py:85
  171.0 5.6 %collective-permute-start.15 = (f32[384,224]{1,0:T(8,128)S(1)}, f32[384,224]{1,0:T(8,128)S(1)}, u32[]{:S(2)}, u32[]{:S(2)}) collective-permute-start(f32[384,224]{1,0:T(8,128)S(1)} %get-tuple-element.37), channel_id=1, source_target_pairs={{0,16},{16,0},{1,17},{17,1},{2,18},{18,2},{3,19},{19,3},{4,20},{20... | collective-permute-start | bytes 1032200 | tf_op jit(solution)/shard_map/ppermute | solution.py:85
  174.9 1.7 collective-permute-start.16
  175.0 1.6 collective-permute-start.17
  177.0 1.5 collective-permute-start.18
  183.9 42.5 %all-to-all-start.5 = ((bf16[64,24,896]{2,1,0:T(8,128)(2,1)}), bf16[64,24,896]{2,1,0:T(8,128)(2,1)S(1)}, u32[]{:S(2)}, u32[]{:S(2)}) async-start(bf16[64,24,896]{2,1,0:T(8,128)(2,1)} %bitcast.103), calls=%async_computation.5 | async-start | bytes 5505024 | tf_op jit(solution)/shard_map/all_to_all | solution.py:305
  227.5 10.6 %all-to-all-start.6 = ((bf16[8,3,896]{2,1,0:T(4,128)(2,1)}), bf16[8,3,896]{2,1,0:T(4,128)(2,1)S(1)}, u32[]{:S(2)}, u32[]{:S(2)}) async-start(bf16[8,3,896]{2,1,0:T(4,128)(2,1)} %reshape.273), calls=%async_computation.6 | async-start | bytes 114688 | tf_op jit(solution)/shard_map/all_to_all | solution.py:305
  (18 other events, 117.0 us)

commit v11 on v9

--- a/solution.py
+++ b/solution.py
@@ -383,7 +383,9 @@
         heads // 7,
     )
 
-    parts, both = lax.optimization_barrier((parts, both))
+    far = shift(both, ys // 2, ys, "y")
+    parts, both, far = lax.optimization_barrier((parts, both, far))
+    both = [far if d == ys // 2 else shift(both, d, ys, "y") if d else both for d in range(ys)]
 
     res = after(resid, parts)
     res = jnp.stack(
@@ -418,6 +420,7 @@
             for to in range(zs)
         ]
     ).reshape(groups * members, rows_dev, zs * k_dev)
+    feats, both = lax.optimization_barrier((feats, both))
     feats = exchange(feats, ALL)
     feats = (
         feats.reshape(groups, members, rows_dev, zs * k_dev)
@@ -448,10 +451,7 @@
     gain_other = gw[:, 1]
     gain_pair = pair(gain_other)
 
-    both = after(both, row)
-    both = jnp.stack([shift(both, d, ys, "y") if d else both for d in range(ys)])
     rows = spread(row, CHIPS, zs * members).reshape(zs, tokens, chunk + HD)
-    rows, both = lax.optimization_barrier((rows, both))
     mine, theirs, stats = up_project(place, rows, up_w, up_other, gain_own, gain_other)
     act = pl.pallas_call(
         lambda *refs: act_kernel(width, *refs),
@@ -471,7 +471,7 @@
     near = at // rows_dev
     slots = (((x - near % xs) % xs) * ys + (y - near // xs) % ys) * rows_dev + at % rows_dev
     chooser = jnp.any((target[:, :, None] == slots[None, None, :]) & valid[:, :, None], axis=0)
-    both = both.reshape(group_rows, 2 * width)
+    both = jnp.stack(both).reshape(group_rows, 2 * width)
     picked = jnp.dot(chooser.astype(BF16), both, preferred_element_type=F32).astype(BF16)
     return (mixed, picked[:, :width][None], picked[:, width:][None])
 

time: 252 us -> 237 us (0.940)
  waiting for transfers between devices: 120 us -> 106 us
  starting transfers between devices: 74.6 us -> 71.3 us
    ppermute x12, waiting for transfers between devices: 56.7 us -> 19.9 us  [shift(): return lax.ppermute(x, axis, [(i, (i + step) % size) for i in range(size)])]
    all_to_all x1, waiting for transfers between devices: 0.01 us -> 30.6 us  [spread(): lax.all_to_all(jnp.broadcast_to(x[None], (count,) + x.shape), axes, split...]
    all_to_all x6, waiting for transfers between devices: 59.7 us -> 52.1 us  [exchange(): return lax.all_to_all(x, axes, split_axis=0, concat_axis=0)]
    all_to_all x6, starting transfers between devices: 41.1 us -> 38.1 us  [exchange(): return lax.all_to_all(x, axes, split_axis=0, concat_axis=0)]
  transfers between devices with their start and end apart: 27 -> 27, of which waited for: 15 -> 17; matrix products, arithmetic and copies ran while one was open for 8% -> 10% of each run, Pallas kernels for 3% -> 8%
where the time goes in v11:
time: 237 us; the launch traced here: 236 us
  waiting for transfers between devices  106 us (45%)
  starting transfers between devices  71.3 us (30%)
  Pallas kernels  22.3 us (9%)
  local copies, waits for them, and re-layouts  21.9 us (9%)
  other arithmetic  9.39 us (4%)
  matrix products  3.58 us (2%)
    all_to_all x6, waiting for transfers between devices, exchange(): return lax.all_to_all(x, axes, split_axis=0, concat_axis=0)  52.1 us
    all_to_all x6, starting transfers between devices, exchange(): return lax.all_to_all(x, axes, split_axis=0, concat_axis=0)  38.1 us
    all_to_all x1, waiting for transfers between devices, spread(): lax.all_to_all(jnp.broadcast_to(x[None], (count,) + x.shape), axes, split...  30.6 us
    ppermute x12, waiting for transfers between devices, shift(): return lax.ppermute(x, axis, [(i, (i + step) % size) for i in range(size)])  19.9 us
    ppermute x12, starting transfers between devices, shift(): return lax.ppermute(x, axis, [(i, (i + step) % size) for i in range(size)])  17 us
    pallas_call x1, Pallas kernels, attend(): pl.pallas_call(body, grid=(steps,), in_specs=[pl.BlockSpec((rows, wide),...  10.2 us
    ppermute x8, starting transfers between devices, pair(): return lax.ppermute(x, 'c', [(0, 1), (1, 0)])  9.76 us
    all_to_all x1, starting transfers between devices, spread(): lax.all_to_all(jnp.broadcast_to(x[None], (count,) + x.shape), axes, split...  6.4 us
  transfers between devices with their start and end apart: 27, of which 17 were waited for; matrix products, arithmetic and copies ran while one was open for 10% of the time, Pallas kernels for 8%

profile of v11, /device:TPU:1, one launch (start us, length us, event | category | flops | bytes accessed | tf_op | source)
XLA Modules:
  0.0 236.1 jit_solution(265285641845176006)
XLA Ops:
  0.7 2.1 broadcast_in_dim.18
  2.7 7.6 %all-to-all-start = ((bf16[16,3,7168]{2,1,0:T(4,128)(2,1)}), bf16[16,3,7168]{2,1,0:T(4,128)(2,1)S(1)}, u32[]{:S(2)}, u32[]{:S(2)}) async-start(bf16[16,3,7168]{2,1,0:T(4,128)(2,1)} %broadcast_in_dim.18), calls=%async_computation | async-start | bytes 1835008 | tf_op jit(solution)/shard_map/all_to_all | solution.py:305
  10.4 2.6 %collective-permute-start.2 = (bf16[3,14336]{1,0:T(4,128)(2,1)S(1)}, bf16[3,14336]{1,0:T(4,128)(2,1)S(1)}, u32[]{:S(2)}, u32[]{:S(2)}) collective-permute-start(bf16[3,14336]{1,0:T(4,128)(2,1)S(1)} %pad_maximum_fusion.7), channel_id=1, source_target_pairs={{0,12},{4,0},{8,4},{12,8},{1,13},{5,1},{9,5},{13,9},{2,14},{6,2},{... | collective-permute-start | bytes 258056 | tf_op jit(solution)/shard_map/ppermute | solution.py:89
  16.5 7.6 %collective-permute-done.2 = bf16[3,14336]{1,0:T(4,128)(2,1)S(1)} collective-permute-done((bf16[3,14336]{1,0:T(4,128)(2,1)S(1)}, bf16[3,14336]{1,0:T(4,128)(2,1)S(1)}, u32[]{:S(2)}, u32[]{:S(2)}) %collective-permute-start.2) | collective-permute-done | bytes 86048 | tf_op jit(solution)/shard_map/ppermute | solution.py:89
  27.3 3.6 %collective-permute-start.3 = (bf16[4,3,14336]{2,1,0:T(4,128)(2,1)S(1)}, bf16[4,3,14336]{2,1,0:T(4,128)(2,1)S(1)}, u32[]{:S(2)}, u32[]{:S(2)}) collective-permute-start(bf16[4,3,14336]{2,1,0:T(4,128)(2,1)S(1)} %pad_maximum_fusion.2), channel_id=1, source_target_pairs={{0,2},{1,3},{2,0},{3,1},{4,6},{5,7},{6,4},{7,5},{8,10},{9,11},{10,... | collective-permute-start | bytes 1032200 | tf_op jit(solution)/shard_map/ppermute | solution.py:89
  33.1 10.2 %shard_map.166 = bf16[48,8192]{1,0:T(8,128)(2,1)} custom-call(bf16[48,7168]{1,0:T(8,128)(2,1)} %reshape.263.refs_0_, bf16[24,16,7168]{2,1,0:T(8,128)(2,1)} %refs_1_.1, bf16[24,16,7168]{2,1,0:T(8,128)(2,1)} %refs_2_.1, bf16[16,7168]{1,0:T(8,128)(2,1)} %pad.7.refs_3_, bf16[16,7168]{1,0:T(8,128)(2,1)} %pad.8.refs_4_, f32[48,400]{1,0:T(8,128)} %pad_maximum_fusion.8.refs_5_), custom_call_target="tpu_custom_call" | custom-call | flops 528482304 | bytes 11010048 | tf_op jit(solution)/shard_map/pallas_call | solution.py:62
  43.3 2.5 %reshape.265 = bf16[16,3,8192]{2,1,0:T(4,128)(2,1)} reshape(bf16[48,8192]{1,0:T(8,128)(2,1)} %shard_map.166) | data formatting | bytes 1572864 | tf_op jit(solution)/shard_map/reshape | solution.py:407
  45.8 3.7 %all-to-all-start.1 = ((bf16[16,3,8192]{2,1,0:T(4,128)(2,1)}), bf16[16,3,8192]{2,1,0:T(4,128)(2,1)S(1)}, u32[]{:S(2)}, u32[]{:S(2)}) async-start(bf16[16,3,8192]{2,1,0:T(4,128)(2,1)} %reshape.265), calls=%async_computation.1 | async-start | bytes 2097152 | tf_op jit(solution)/shard_map/all_to_all | solution.py:305
  53.0 3.8 %collective-permute-start.8 = (bf16[2,56,896]{2,1,0:T(8,128)(2,1)}, bf16[2,56,896]{2,1,0:T(8,128)(2,1)S(1)}, u32[]{:S(2)}, u32[]{:S(2)}) collective-permute-start(bf16[2,56,896]{2,1,0:T(8,128)(2,1)} %pad_maximum_fusion.5), channel_id=1, source_target_pairs={{0,96},{32,0},{64,32},{96,64},{1,97},{33,1},{65,33},{97,65},{2,98}... | collective-permute-start | bytes 602120 | tf_op jit(solution)/shard_map/ppermute | solution.py:89
  58.9 5.4 %all-to-all-done.1 = bf16[16,3,8192]{2,1,0:T(4,128)(2,1)S(1)} async-done(((bf16[16,3,8192]{2,1,0:T(4,128)(2,1)}), bf16[16,3,8192]{2,1,0:T(4,128)(2,1)S(1)}, u32[]{:S(2)}, u32[]{:S(2)}) %all-to-all-start.1) | async-done | bytes 786464 | tf_op jit(solution)/shard_map/all_to_all | solution.py:305
  66.6 5.8 %collective-permute-done.4 = bf16[4,3,14336]{2,1,0:T(4,128)(2,1)S(1)} collective-permute-done((bf16[4,3,14336]{2,1,0:T(4,128)(2,1)S(1)}, bf16[4,3,14336]{2,1,0:T(4,128)(2,1)S(1)}, u32[]{:S(2)}, u32[]{:S(2)}) %collective-permute-start.4) | collective-permute-done | bytes 344096 | tf_op jit(solution)/shard_map/ppermute | solution.py:89
  73.5 10.5 %all-to-all-start.2 = ((bf16[128,3,224]{2,1,0:T(4,128)(2,1)}), bf16[128,3,224]{2,1,0:T(4,128)(2,1)S(1)}, u32[]{:S(2)}, u32[]{:S(2)}) async-start(bf16[128,3,224]{2,1,0:T(4,128)(2,1)} %copy.79), calls=%async_computation.2 | async-start | bytes 524288 | tf_op jit(solution)/shard_map/all_to_all | solution.py:305
  84.1 11.0 %all-to-all-done.2 = bf16[128,3,224]{2,1,0:T(4,128)(2,1)S(1)} async-done(((bf16[128,3,224]{2,1,0:T(4,128)(2,1)}), bf16[128,3,224]{2,1,0:T(4,128)(2,1)S(1)}, u32[]{:S(2)}, u32[]{:S(2)}) %all-to-all-start.2) | async-done | bytes 172064 | tf_op jit(solution)/shard_map/all_to_all | solution.py:305
  99.7 3.6 %all-to-all-start.3 = ((bf16[16,24,896]{2,1,0:T(8,128)(2,1)}), bf16[16,24,896]{2,1,0:T(8,128)(2,1)S(1)}, u32[]{:S(2)}, u32[]{:S(2)}) async-start(bf16[16,24,896]{2,1,0:T(8,128)(2,1)} %bitcast.31), calls=%async_computation.3 | async-start | bytes 1376256 | tf_op jit(solution)/shard_map/all_to_all | solution.py:305
  104.2 1.7 collective-permute-start.12
  106.1 2.4 %collective-permute-done.12 = bf16[6,896]{1,0:T(8,128)(2,1)S(1)} collective-permute-done((bf16[6,896]{1,0:T(8,128)(2,1)S(1)}, bf16[6,896]{1,0:T(8,128)(2,1)S(1)}, u32[]{:S(2)}, u32[]{:S(2)}) %collective-permute-start.12) | collective-permute-done | bytes 10784 | tf_op jit(solution)/shard_map/ppermute | solution.py:89
  109.8 5.2 %all-to-all-done.3.parts = bf16[16,24,896]{2,1,0:T(8,128)(2,1)S(1)} async-done(((bf16[16,24,896]{2,1,0:T(8,128)(2,1)}), bf16[16,24,896]{2,1,0:T(8,128)(2,1)S(1)}, u32[]{:S(2)}, u32[]{:S(2)}) %all-to-all-start.3) | async-done | bytes 688160 | tf_op jit(solution)/shard_map/all_to_all | solution.py:305
  115.3 2.1 broadcast_in_dim.23
  117.4 6.4 %all-to-all-start.4 = ((bf16[64,24,1024]{2,1,0:T(8,128)(2,1)}), bf16[64,24,1024]{2,1,0:T(8,128)(2,1)}, u32[]{:S(2)}, u32[]{:S(2)}) async-start(bf16[64,24,1024]{2,1,0:T(8,128)(2,1)} %broadcast_in_dim.23), calls=%async_computation.4 | async-start | bytes 6291456 | tf_op jit(solution)/shard_map/all_to_all | solution.py:299
  123.9 2.2 collective-permute-start.14
  127.4 1.7 collective-permute-start.19
  129.2 1.7 shard_map.168
  130.9 30.6 %all-to-all-done.4 = bf16[64,24,1024]{2,1,0:T(8,128)(2,1)} async-done(((bf16[64,24,1024]{2,1,0:T(8,128)(2,1)}), bf16[64,24,1024]{2,1,0:T(8,128)(2,1)}, u32[]{:S(2)}, u32[]{:S(2)}) %all-to-all-start.4) | async-done | bytes 3145760 | tf_op jit(solution)/shard_map/all_to_all | solution.py:299
  162.9 5.4 %shard_map.169 = (f32[384,224]{1,0:T(8,128)S(1)}, f32[384,224]{1,0:T(8,128)S(1)}, f32[384,128]{1,0:T(8,128)S(1)}) custom-call(s32[1]{0:T(128)} %bitcast.place, bf16[4,384,1024]{2,1,0:T(8,128)(2,1)} %bitcast.34.rows, bf16[224,7168]{1,0:T(8,128)(2,1)S(1)} %bitcast.102, bf16[224,3584]{1,0:T(8,128)(2,1)S(1)} %copy-done.5, ...), custom_call_target="tpu_custom_call" | custom-call | tf_op jit(solution)/shard_map/pallas_call | solution.py:233
  168.4 3.9 %collective-permute-start.15 = (f32[384,224]{1,0:T(8,128)S(1)}, f32[384,224]{1,0:T(8,128)S(1)}, u32[]{:S(2)}, u32[]{:S(2)}) collective-permute-start(f32[384,224]{1,0:T(8,128)S(1)} %get-tuple-element.31), channel_id=1, source_target_pairs={{0,16},{16,0},{1,17},{17,1},{2,18},{18,2},{3,19},{19,3},{4,20},{20... | collective-permute-start | bytes 1032200 | tf_op jit(solution)/shard_map/ppermute | solution.py:85
  175.9 3.9 %shard_map.171 = bf16[4,384,896]{2,1,0:T(8,128)(2,1)S(1)} custom-call(s32[1]{0:T(128)} %bitcast.place, bf16[384,224]{1,0:T(8,128)(2,1)S(1)} %shard_map.170.act, bf16[384,224]{1,0:T(8,128)(2,1)S(1)} %collective-permute-done.18.act_pair, bf16[224,7168]{1,0:T(8,128)(2,1)S(1)} %copy-done.3, bf16[224,3584]{1,0:T(8,128)(2,1)} %collective-permute-done.19.other), custom_call_target="tpu_custom_call" | custom-call | tf_op jit(solution)/shard_map/pallas_call | solution.py:263
  181.3 7.1 %all-to-all-start.5 = ((bf16[64,24,896]{2,1,0:T(8,128)(2,1)}), bf16[64,24,896]{2,1,0:T(8,128)(2,1)S(1)}, u32[]{:S(2)}, u32[]{:S(2)}) async-start(bf16[64,24,896]{2,1,0:T(8,128)(2,1)} %bitcast.103), calls=%async_computation.5 | async-start | bytes 5505024 | tf_op jit(solution)/shard_map/all_to_all | solution.py:305
  188.7 3.8 %pad_maximum_fusion = bf16[4,4,3,14336]{3,2,1,0:T(4,128)(2,1)} fusion(bf16[1,4,3,14336]{3,2,1,0:T(4,128)(2,1)} %bitcast.116, bf16[1,4,3,14336]{3,2,1,0:T(4,128)(2,1)} %bitcast.114, bf16[1,4,3,14336]{3,2,1,0:T(4,128)(2,1)} %bitcast.115, bf16[1,4,3,14336]{3,2,1,0:T(4,128)(2,1)S(1)} %bitcast.110), kind=kLoop, calls=%fused_computation.1 | loop fusion | flops 2064384 | bytes 2752512 | tf_op jit(solution)/shard_map/stack | solution.py:474
  192.5 3.2 %reshape.276 = bf16[48,14336]{1,0:T(8,128)(2,1)} reshape(bf16[4,4,3,14336]{3,2,1,0:T(4,128)(2,1)} %pad_maximum_fusion) | data formatting | bytes 2752512 | tf_op jit(solution)/shard_map/reshape | solution.py:474
  197.3 26.5 %all-to-all-done.5.parts = bf16[64,24,896]{2,1,0:T(8,128)(2,1)S(1)} async-done(((bf16[64,24,896]{2,1,0:T(8,128)(2,1)}), bf16[64,24,896]{2,1,0:T(8,128)(2,1)S(1)}, u32[]{:S(2)}, u32[]{:S(2)}) %all-to-all-start.5) | async-done | bytes 2752544 | tf_op jit(solution)/shard_map/all_to_all | solution.py:305
  224.9 5.7 %all-to-all-start.6 = ((bf16[8,3,896]{2,1,0:T(4,128)(2,1)}), bf16[8,3,896]{2,1,0:T(4,128)(2,1)S(1)}, u32[]{:S(2)}, u32[]{:S(2)}) async-start(bf16[8,3,896]{2,1,0:T(4,128)(2,1)} %reshape.273), calls=%async_computation.6 | async-start | bytes 114688 | tf_op jit(solution)/shard_map/all_to_all | solution.py:305
  231.4 4.0 %all-to-all-done.6 = bf16[8,3,896]{2,1,0:T(4,128)(2,1)S(1)} async-done(((bf16[8,3,896]{2,1,0:T(4,128)(2,1)}), bf16[8,3,896]{2,1,0:T(4,128)(2,1)S(1)}, u32[]{:S(2)}, u32[]{:S(2)}) %all-to-all-start.6) | async-done | bytes 43040 | tf_op jit(solution)/shard_map/all_to_all | solution.py:305
  (141 shorter events, 37.5 us)
Async XLA Ops:
  0.7 15.1 %copy-start.16 = (s32[3,16,16]{2,1,0:T(8,128)S(1)}, s32[3,16,16]{2,1,0:T(8,128)}, u32[]{:S(2)}) copy-start(s32[3,16,16]{2,1,0:T(8,128)} %param.19) | copy-start | bytes 9220
  0.7 15.3 %copy-start.18 = (s32[3,384]{1,0:T(4,128)S(1)}, s32[3,384]{1,0:T(4,128)}, u32[]{:S(2)}) copy-start(s32[3,384]{1,0:T(4,128)} %param.23) | copy-start | bytes 13828
  2.7 29.0 %all-to-all-start = ((bf16[16,3,7168]{2,1,0:T(4,128)(2,1)}), bf16[16,3,7168]{2,1,0:T(4,128)(2,1)S(1)}, u32[]{:S(2)}, u32[]{:S(2)}) async-start(bf16[16,3,7168]{2,1,0:T(4,128)(2,1)} %broadcast_in_dim.18), calls=%async_computation | async-start | bytes 1835008 | tf_op jit(solution)/shard_map/all_to_all | solution.py:305
  10.4 13.6 %collective-permute-start.2 = (bf16[3,14336]{1,0:T(4,128)(2,1)S(1)}, bf16[3,14336]{1,0:T(4,128)(2,1)S(1)}, u32[]{:S(2)}, u32[]{:S(2)}) collective-permute-start(bf16[3,14336]{1,0:T(4,128)(2,1)S(1)} %pad_maximum_fusion.7), channel_id=1, source_target_pairs={{0,12},{4,0},{8,4},{12,8},{1,13},{5,1},{9,5},{13,9},{2,14},{6,2},{... | collective-permute-start | bytes 258056 | tf_op jit(solution)/shard_map/ppermute | solution.py:89
  13.1 12.4 %collective-permute-start.1 = (bf16[3,14336]{1,0:T(4,128)(2,1)S(1)}, bf16[3,14336]{1,0:T(4,128)(2,1)S(1)}, u32[]{:S(2)}, u32[]{:S(2)}) collective-permute-start(bf16[3,14336]{1,0:T(4,128)(2,1)S(1)} %pad_maximum_fusion.7), channel_id=1, source_target_pairs={{0,8},{4,12},{8,0},{12,4},{1,9},{5,13},{9,1},{13,5},{2,10},{6,14},... | collective-permute-start | bytes 258056 | tf_op jit(solution)/shard_map/ppermute | solution.py:89
  13.6 13.2 %collective-permute-start = (bf16[3,14336]{1,0:T(4,128)(2,1)S(1)}, bf16[3,14336]{1,0:T(4,128)(2,1)S(1)}, u32[]{:S(2)}, u32[]{:S(2)}) collective-permute-start(bf16[3,14336]{1,0:T(4,128)(2,1)S(1)} %pad_maximum_fusion.7), channel_id=1, source_target_pairs={{0,4},{4,8},{8,12},{12,0},{1,5},{5,9},{9,13},{13,1},{2,6},{6,10},{... | collective-permute-start | bytes 258056 | tf_op jit(solution)/shard_map/ppermute | solution.py:89
  27.3 23.4 %copy-start.7 = (bf16[4,3,14336]{2,1,0:T(4,128)(2,1)}, bf16[4,3,14336]{2,1,0:T(4,128)(2,1)S(1)}, u32[]{:S(2)}) copy-start(bf16[4,3,14336]{2,1,0:T(4,128)(2,1)S(1)} %pad_maximum_fusion.2) | copy-start | bytes 1032196
  27.3 16.0 %collective-permute-start.3 = (bf16[4,3,14336]{2,1,0:T(4,128)(2,1)S(1)}, bf16[4,3,14336]{2,1,0:T(4,128)(2,1)S(1)}, u32[]{:S(2)}, u32[]{:S(2)}) collective-permute-start(bf16[4,3,14336]{2,1,0:T(4,128)(2,1)S(1)} %pad_maximum_fusion.2), channel_id=1, source_target_pairs={{0,2},{1,3},{2,0},{3,1},{4,6},{5,7},{6,4},{7,5},{8,10},{9,11},{10,... | collective-permute-start | bytes 1032200 | tf_op jit(solution)/shard_map/ppermute | solution.py:89
  45.8 18.5 %all-to-all-start.1 = ((bf16[16,3,8192]{2,1,0:T(4,128)(2,1)}), bf16[16,3,8192]{2,1,0:T(4,128)(2,1)S(1)}, u32[]{:S(2)}, u32[]{:S(2)}) async-start(bf16[16,3,8192]{2,1,0:T(4,128)(2,1)} %reshape.265), calls=%async_computation.1 | async-start | bytes 2097152 | tf_op jit(solution)/shard_map/all_to_all | solution.py:305
  49.5 23.0 %collective-permute-start.4 = (bf16[4,3,14336]{2,1,0:T(4,128)(2,1)S(1)}, bf16[4,3,14336]{2,1,0:T(4,128)(2,1)S(1)}, u32[]{:S(2)}, u32[]{:S(2)}) collective-permute-start(bf16[4,3,14336]{2,1,0:T(4,128)(2,1)S(1)} %pad_maximum_fusion.2), channel_id=1, source_target_pairs={{0,1},{1,2},{2,3},{3,0},{4,5},{5,6},{6,7},{7,4},{8,9},{9,10},{10,1... | collective-permute-start | bytes 1032200 | tf_op jit(solution)/shard_map/ppermute | solution.py:89
  50.7 21.8 %collective-permute-start.5 = (bf16[4,3,14336]{2,1,0:T(4,128)(2,1)S(1)}, bf16[4,3,14336]{2,1,0:T(4,128)(2,1)S(1)}, u32[]{:S(2)}, u32[]{:S(2)}) collective-permute-start(bf16[4,3,14336]{2,1,0:T(4,128)(2,1)S(1)} %pad_maximum_fusion.2), channel_id=1, source_target_pairs={{0,3},{1,0},{2,1},{3,2},{4,7},{5,4},{6,5},{7,6},{8,11},{9,8},{10,9... | collective-permute-start | bytes 1032200 | tf_op jit(solution)/shard_map/ppermute | solution.py:89
  53.0 31.0 %collective-permute-start.8 = (bf16[2,56,896]{2,1,0:T(8,128)(2,1)}, bf16[2,56,896]{2,1,0:T(8,128)(2,1)S(1)}, u32[]{:S(2)}, u32[]{:S(2)}) collective-permute-start(bf16[2,56,896]{2,1,0:T(8,128)(2,1)} %pad_maximum_fusion.5), channel_id=1, source_target_pairs={{0,96},{32,0},{64,32},{96,64},{1,97},{33,1},{65,33},{97,65},{2,98}... | collective-permute-start | bytes 602120 | tf_op jit(solution)/shard_map/ppermute | solution.py:89
  57.5 26.5 %collective-permute-start.7 = (bf16[2,56,896]{2,1,0:T(8,128)(2,1)}, bf16[2,56,896]{2,1,0:T(8,128)(2,1)S(1)}, u32[]{:S(2)}, u32[]{:S(2)}) collective-permute-start(bf16[2,56,896]{2,1,0:T(8,128)(2,1)} %pad_maximum_fusion.4), channel_id=1, source_target_pairs={{0,64},{32,96},{64,0},{96,32},{1,65},{33,97},{65,1},{97,33},{2,66}... | collective-permute-start | bytes 602120 | tf_op jit(solution)/shard_map/ppermute | solution.py:89
  58.2 25.8 %collective-permute-start.6 = (bf16[2,56,896]{2,1,0:T(8,128)(2,1)}, bf16[2,56,896]{2,1,0:T(8,128)(2,1)S(1)}, u32[]{:S(2)}, u32[]{:S(2)}) collective-permute-start(bf16[2,56,896]{2,1,0:T(8,128)(2,1)} %pad_maximum_fusion.3), channel_id=1, source_target_pairs={{0,32},{32,64},{64,96},{96,0},{1,33},{33,65},{65,97},{97,1},{2,34}... | collective-permute-start | bytes 602120 | tf_op jit(solution)/shard_map/ppermute | solution.py:89
  72.5 23.0 %copy-start.11 = (bf16[4,3,14336]{2,1,0:T(4,128)(2,1)}, bf16[4,3,14336]{2,1,0:T(4,128)(2,1)S(1)}, u32[]{:S(2)}) copy-start(bf16[4,3,14336]{2,1,0:T(4,128)(2,1)S(1)} %collective-permute-done.4) | copy-start | bytes 1032196
  72.5 23.0 %copy-start.12 = (bf16[4,3,14336]{2,1,0:T(4,128)(2,1)}, bf16[4,3,14336]{2,1,0:T(4,128)(2,1)S(1)}, u32[]{:S(2)}) copy-start(bf16[4,3,14336]{2,1,0:T(4,128)(2,1)S(1)} %collective-permute-done.5) | copy-start | bytes 1032196
  73.5 21.6 %all-to-all-start.2 = ((bf16[128,3,224]{2,1,0:T(4,128)(2,1)}), bf16[128,3,224]{2,1,0:T(4,128)(2,1)S(1)}, u32[]{:S(2)}, u32[]{:S(2)}) async-start(bf16[128,3,224]{2,1,0:T(4,128)(2,1)} %copy.79), calls=%async_computation.2 | async-start | bytes 524288 | tf_op jit(solution)/shard_map/all_to_all | solution.py:305
  95.9 2.6 %collective-permute-start.9 = (bf16[384,896]{1,0:T(8,128)(2,1)S(1)}, bf16[384,896]{1,0:T(8,128)(2,1)S(1)}, u32[]{:S(2)}, u32[]{:S(2)}) collective-permute-start(bf16[384,896]{1,0:T(8,128)(2,1)S(1)} %convolution_convert_fusion.1), channel_id=1, source_target_pairs={{0,16},{16,0},{1,17},{17,1},{2,18},{18,2},{3,19},{19,3},{4,20},{20... | collective-permute-start | bytes 2064392 | tf_op jit(solution)/shard_map/ppermute | solution.py:85
  96.8 6.6 %collective-permute-start.10 = (bf16[3,3584]{1,0:T(4,128)(2,1)S(1)}, bf16[3,3584]{1,0:T(4,128)(2,1)S(1)}, u32[]{:S(2)}, u32[]{:S(2)}) collective-permute-start(bf16[3,3584]{1,0:T(4,128)(2,1)S(1)} %get-tuple-element.66), channel_id=1, source_target_pairs={{0,16},{16,0},{1,17},{17,1},{2,18},{18,2},{3,19},{19,3},{4,20},{20... | collective-permute-start | bytes 64520 | tf_op jit(solution)/shard_map/ppermute | solution.py:85
  99.7 15.3 %all-to-all-start.3 = ((bf16[16,24,896]{2,1,0:T(8,128)(2,1)}), bf16[16,24,896]{2,1,0:T(8,128)(2,1)S(1)}, u32[]{:S(2)}, u32[]{:S(2)}) async-start(bf16[16,24,896]{2,1,0:T(8,128)(2,1)} %bitcast.31), calls=%async_computation.3 | async-start | bytes 1376256 | tf_op jit(solution)/shard_map/all_to_all | solution.py:305
  103.5 2.6 %collective-permute-start.13 = (bf16[6,896]{1,0:T(8,128)(2,1)S(1)}, bf16[6,896]{1,0:T(8,128)(2,1)S(1)}, u32[]{:S(2)}, u32[]{:S(2)}) collective-permute-start(bf16[6,896]{1,0:T(8,128)(2,1)S(1)} %get-tuple-element.62), channel_id=1, source_target_pairs={{0,96},{32,0},{64,32},{96,64},{1,97},{33,1},{65,33},{97,65},{2,98}... | collective-permute-start | bytes 32264 | tf_op jit(solution)/shard_map/ppermute | solution.py:89
  104.2 4.4 %collective-permute-start.12 = (bf16[6,896]{1,0:T(8,128)(2,1)S(1)}, bf16[6,896]{1,0:T(8,128)(2,1)S(1)}, u32[]{:S(2)}, u32[]{:S(2)}) collective-permute-start(bf16[6,896]{1,0:T(8,128)(2,1)S(1)} %get-tuple-element.63), channel_id=1, source_target_pairs={{0,64},{32,96},{64,0},{96,32},{1,65},{33,97},{65,1},{97,33},{2,66}... | collective-permute-start | bytes 32264 | tf_op jit(solution)/shard_map/ppermute | solution.py:89
  105.9 3.8 %collective-permute-start.11 = (bf16[6,896]{1,0:T(8,128)(2,1)S(1)}, bf16[6,896]{1,0:T(8,128)(2,1)S(1)}, u32[]{:S(2)}, u32[]{:S(2)}) collective-permute-start(bf16[6,896]{1,0:T(8,128)(2,1)S(1)} %get-tuple-element.64), channel_id=1, source_target_pairs={{0,32},{32,64},{64,96},{96,0},{1,33},{33,65},{65,97},{97,1},{2,34}... | collective-permute-start | bytes 32264 | tf_op jit(solution)/shard_map/ppermute | solution.py:89
  117.4 44.1 %all-to-all-start.4 = ((bf16[64,24,1024]{2,1,0:T(8,128)(2,1)}), bf16[64,24,1024]{2,1,0:T(8,128)(2,1)}, u32[]{:S(2)}, u32[]{:S(2)}) async-start(bf16[64,24,1024]{2,1,0:T(8,128)(2,1)} %broadcast_in_dim.23), calls=%async_computation.4 | async-start | bytes 6291456 | tf_op jit(solution)/shard_map/all_to_all | solution.py:299
  123.9 5.3 %collective-permute-start.14 = (bf16[224,3584]{1,0:T(8,128)(2,1)S(1)}, bf16[224,3584]{1,0:T(8,128)(2,1)S(1)}, u32[]{:S(2)}, u32[]{:S(2)}) collective-permute-start(bf16[224,3584]{1,0:T(8,128)(2,1)S(1)} %constant_dynamic-slice_fusion.1), channel_id=1, source_target_pairs={{0,16},{16,0},{1,17},{17,1},{2,18},{18,2},{3,19},{19,3},{4,20},{20... | collective-permute-start | bytes 4816904 | tf_op jit(solution)/shard_map/ppermute | solution.py:85
  127.4 47.4 %collective-permute-start.19 = (bf16[224,3584]{1,0:T(8,128)(2,1)}, bf16[224,3584]{1,0:T(8,128)(2,1)}, u32[]{:S(2)}, u32[]{:S(2)}) collective-permute-start(bf16[224,3584]{1,0:T(8,128)(2,1)} %constant_dynamic-slice_fusion), channel_id=1, source_target_pairs={{0,16},{16,0},{1,17},{17,1},{2,18},{18,2},{3,19},{19,3},{4,20},{20... | collective-permute-start | bytes 4816904 | tf_op jit(solution)/shard_map/ppermute | solution.py:85
  168.4 5.6 %collective-permute-start.15 = (f32[384,224]{1,0:T(8,128)S(1)}, f32[384,224]{1,0:T(8,128)S(1)}, u32[]{:S(2)}, u32[]{:S(2)}) collective-permute-start(f32[384,224]{1,0:T(8,128)S(1)} %get-tuple-element.31), channel_id=1, source_target_pairs={{0,16},{16,0},{1,17},{17,1},{2,18},{18,2},{3,19},{19,3},{4,20},{20... | collective-permute-start | bytes 1032200 | tf_op jit(solution)/shard_map/ppermute | solution.py:85
  172.3 1.7 collective-permute-start.16
  172.4 1.6 collective-permute-start.17
  174.4 1.5 collective-permute-start.18
  181.3 42.5 %all-to-all-start.5 = ((bf16[64,24,896]{2,1,0:T(8,128)(2,1)}), bf16[64,24,896]{2,1,0:T(8,128)(2,1)S(1)}, u32[]{:S(2)}, u32[]{:S(2)}) async-start(bf16[64,24,896]{2,1,0:T(8,128)(2,1)} %bitcast.103), calls=%async_computation.5 | async-start | bytes 5505024 | tf_op jit(solution)/shard_map/all_to_all | solution.py:305
  224.9 10.6 %all-to-all-start.6 = ((bf16[8,3,896]{2,1,0:T(4,128)(2,1)}), bf16[8,3,896]{2,1,0:T(4,128)(2,1)S(1)}, u32[]{:S(2)}, u32[]{:S(2)}) async-start(bf16[8,3,896]{2,1,0:T(4,128)(2,1)} %reshape.273), calls=%async_computation.6 | async-start | bytes 114688 | tf_op jit(solution)/shard_map/all_to_all | solution.py:305
  (16 other events, 115.7 us)
